TPU v7x, 32 devices: a whole 2x2x4 slice. The times are simulated.
32 devices in a mesh: rows: 8 (over y, x, core), feat: 4 (over z).
Axes of the slice: x: 2, y: 2, z: 4, core: 2. Of those that a mesh axis runs over, the one named last changes fastest.
Arguments:
- tokens: bfloat16 [32, 128, 768], P(('rows', 'feat')), may hold values from -6 to 6
- cotangent: bfloat16 [32, 128, 768], P(('rows', 'feat')), may hold values from -6 to 6
- seg_ids: int32 [32, 128], P(('rows', 'feat')), may hold values from 0 to 7, as said below
- pad_mask: int32 [32, 128], P(('rows', 'feat')), may hold values from 0 to 1, as said below
- norm1_gain: bfloat16 [768], replicated, may hold values from 0.5 to 1.5
- w_query: bfloat16 [768, 768], replicated, may hold values from -0.21875 to 0.21875
- w_key: bfloat16 [768, 768], replicated, may hold values from -0.21875 to 0.21875
- w_value: bfloat16 [768, 768], replicated, may hold values from -0.21875 to 0.21875
- w_gate: bfloat16 [768, 768], replicated, may hold values from -0.21875 to 0.21875
- w_rate: bfloat16 [768, 12], replicated, may hold values from -0.21875 to 0.21875
- b_rate: bfloat16 [12], replicated, may hold values from -3 to 3
- inner_w1: bfloat16 [12, 64, 256], replicated, may hold values from -0.75 to 0.75
- inner_b1: bfloat16 [12, 256], replicated, may hold values from -2 to 2
- inner_w2: bfloat16 [12, 256, 64], replicated, may hold values from -0.375 to 0.375
- inner_b2: bfloat16 [12, 64], replicated, may hold values from -2 to 2
- inner_gain: bfloat16 [12, 64], replicated, may hold values from 0.5 to 1.5
- inner_bias: bfloat16 [12, 64], replicated, may hold values from -2 to 2
- w_out: bfloat16 [768, 768], replicated, may hold values from -0.21875 to 0.21875
- norm2_gain: bfloat16 [768], replicated, may hold values from 0.5 to 1.5
- ffn_gate: bfloat16 [768, 2048], P(None, 'feat'), may hold values from -0.21875 to 0.21875
- ffn_up: bfloat16 [768, 2048], P(None, 'feat'), may hold values from -0.21875 to 0.21875
- ffn_down: bfloat16 [2048, 768], P('feat'), may hold values from -0.125 to 0.125
Outputs:
- mixed: bfloat16 [32, 128, 768], P(('rows', 'feat'))
- grad_tokens: float32 [32, 128, 768], P(('rows', 'feat'))
- grad_norm1_gain: float32 [768], P('feat')
- grad_w_query: float32 [768, 768], P('feat')
- grad_w_key: float32 [768, 768], P('feat')
- grad_w_value: float32 [768, 768], P('feat')
- grad_w_gate: float32 [768, 768], P('feat')
- grad_w_rate: float32 [768, 12], P('feat')
- grad_b_rate: float32 [12], replicated
- grad_inner_w1: float32 [12, 64, 256], replicated
- grad_inner_b1: float32 [12, 256], replicated
- grad_inner_w2: float32 [12, 256, 64], replicated
- grad_inner_b2: float32 [12, 64], replicated
- grad_inner_gain: float32 [12, 64], replicated
- grad_inner_bias: float32 [12, 64], replicated
- grad_w_out: float32 [768, 768], P('feat')
- grad_norm2_gain: float32 [768], P('feat')
- grad_ffn_gate: float32 [768, 2048], P(None, 'feat')
- grad_ffn_up: float32 [768, 2048], P(None, 'feat')
- grad_ffn_down: float32 [2048, 768], P('feat')
Inputs may be any that keep to these rules, and one draw needn't show every extreme that they name: Within a row seg_ids start at 0, never fall, rise by one at each new document and change only at multiples of 16 positions; padding is a tail of whole mini-batches with its own id. In some row every mini-batch begins a new document. `pad_mask`: zeros form the tail of a row, a multiple of 16 tokens long and at most half the row; the first mini-batch of every row is live.
All inputs are finite; a program needn't handle non-finite values.
Results may differ from a plain program's by a relative error of at most 0.018.
Values may be sent and summed in bfloat16 or wider, within the bound.
No kernel may reach another device: no remote copies, remote signals or barrier semaphores. Data moves between devices by JAX's collectives and lax.ppermute only.
A program may use at most 128 MiB of HBM per device.

v0:
```python
from functools import partial

import jax
import jax.numpy as jnp
from jax import lax
from jax.experimental import pallas as pl
from jax.experimental.pallas import tpu as pltpu
from jax.sharding import PartitionSpec as P

MB = 16
EPSILON = 1e-06
BASE_RATE = 0.1
F32 = jnp.float32
BF16 = jnp.bfloat16
VMEM_BYTES = 56 * 2**20


def dot(left, right, left_dim=1, right_dim=0):
    return lax.dot_general(
        left, right, (((left_dim,), (right_dim,)), ((), ())), preferred_element_type=F32
    )


def low(values):
    return values.astype(BF16)


def gelu_parts(values):
    phi = 0.5 + 0.5 * lax.erf(values * 0.7071067811865476)
    density = jnp.exp(-0.5 * values * values) * 0.3989422804014327
    return (values * phi, phi + values * density, density * (2.0 - values * values))


def mean_last(values):
    return jnp.sum(values, -1, keepdims=True) * (1.0 / values.shape[-1])


def sum_rows(values):
    return jnp.sum(values, 0, keepdims=True)


def column_of(row):
    size = row.shape[1]
    return jnp.transpose(jnp.broadcast_to(row, (size, size)))[:, 0:1]


def segment_masks(seg_row):
    size = seg_row.shape[1]
    rows = lax.broadcasted_iota(jnp.int32, (size, size), 0)
    cols = lax.broadcasted_iota(jnp.int32, (size, size), 1)
    same = column_of(seg_row) == seg_row
    block = MB.bit_length() - 1
    later = lax.shift_right_logical(rows, block) > lax.shift_right_logical(cols, block)
    inclusive = jnp.where(same & (cols <= rows), 1.0, 0.0)
    strict = jnp.where(same & later, 1.0, 0.0)
    return (inclusive, strict)


def forward_kernel(
    seg_smem,
    seg_ref,
    live_ref,
    tok_ref,
    gain1_ref,
    wq_ref,
    wk_ref,
    wv_ref,
    wg_ref,
    wr_ref,
    br_ref,
    w1_ref,
    b1_ref,
    w2_ref,
    b2_ref,
    ig_ref,
    ib_ref,
    wo_ref,
    gain2_ref,
    normed_ref,
    normed_two_ref,
    resid_ref,
    gated_ref,
    gelu_ref,
    slope_ref,
    qk_ref,
    ecol_ref,
    erow_ref,
    fcol_ref,
    w2t_ref,
    slope1_ref,
    curve1_ref,
    act_ref,
    d1_ref,
    d2_ref,
    n_ref,
    s_ref,
    fit_ref,
    w2s_ref,
    p1_ref,
    p2_ref,
    slopeq_ref,
    nq_ref,
    sq_ref,
    q_s,
    k_s,
    v_s,
    out_s,
    w1_s,
    w1b_s,
    b1_s,
    w2_s,
    b2_s,
    b1f,
    b2f,
    igf,
    ibf,
):
    length, width = tok_ref.shape[1], tok_ref.shape[2]
    heads, head = w1_ref.shape[0], w1_ref.shape[1]
    blocks = length // MB
    tok = tok_ref[0].astype(F32)
    spread = lax.rsqrt(mean_last(tok * tok) + EPSILON)
    normed = low(tok * spread * gain1_ref[...].astype(F32))
    normed_ref[...] = normed
    seg_row = seg_ref[...].astype(F32)
    live = column_of(live_ref[...].astype(F32))
    rate_pre = dot(normed, wr_ref[...]) + br_ref[...].astype(F32)
    sig = jax.nn.sigmoid(rate_pre)
    rates = (BASE_RATE / head) * sig * live
    ecol_ref[...] = jnp.zeros(ecol_ref.shape, F32)
    ecol_ref[:, 0:heads] = rates
    fcol_ref[...] = jnp.zeros(fcol_ref.shape, F32)
    fcol_ref[:, 0:heads] = rates * (1.0 - sig)
    erow_ref[...] = jnp.transpose(ecol_ref[...])[0 : erow_ref.shape[0]]
    for w_ref, to in ((wq_ref, q_s), (wk_ref, k_s), (wv_ref, v_s)):
        whole = dot(normed, w_ref[...])
        for h in range(heads):
            to[h] = whole[:, h * head : (h + 1) * head]
    b1f[...] = b1_ref[...].astype(F32)
    b2f[...] = b2_ref[...].astype(F32)
    igf[...] = ig_ref[...].astype(F32)
    ibf[...] = ib_ref[...].astype(F32)
    for h in range(heads):
        qk_ref[h, 0:length] = low(q_s[h])
        qk_ref[h, length : 2 * length] = low(k_s[h])
        w2t_ref[h] = low(jnp.transpose(w2_ref[h].astype(F32)))

    def step(b, carry):
        here = pl.multiple_of(b * MB, MB)
        before = jnp.maximum(here - 1, 0)
        fresh = (b == 0) | (seg_smem[0, here] != seg_smem[0, before])

        @pl.when(fresh)
        def _():
            for h in range(heads):
                first = w1_ref[h]
                second = w2t_ref[h]
                w1_s[h] = first.astype(F32)
                w1b_s[h] = first
                w2_s[h] = second.astype(F32)
                w2s_ref[b, h] = second
                b1_s[h] = b1f[h : h + 1]
                b2_s[h] = b2f[h : h + 1]

        @pl.when(jnp.logical_not(fresh))
        def _():
            for h in range(heads):
                w2s_ref[b, h] = low(w2_s[h])

        ds = pl.ds(here, MB)
        rng = range(heads)
        k = [k_s[h, ds, :] for h in rng]
        v = [v_s[h, ds, :] for h in rng]
        e = [ecol_ref[ds, h : h + 1] for h in rng]
        w1 = [w1b_s[h] for h in rng]
        w2 = [w2s_ref[b, h] for h in rng]
        w1f = [w1_s[h] for h in rng]
        w2f = [w2_s[h] for h in rng]
        b1 = [b1_s[h] for h in rng]
        b2 = [b2_s[h] for h in rng]
        g = [igf[h : h + 1] for h in rng]
        gb = [ibf[h : h + 1] for h in rng]
        parts = [gelu_parts(dot(low(k[h]), w1[h]) + b1[h]) for h in rng]
        act = [low(parts[h][0]) for h in rng]
        z2 = [dot(act[h], w2[h], 1, 1) + b2[h] for h in rng]
        c = [z - mean_last(z) for z in z2]
        s = [lax.rsqrt(mean_last(x * x) + EPSILON) for x in c]
        n = [c[h] * s[h] for h in rng]
        fit = [g[h] * n[h] + gb[h] - (v[h] - k[h]) for h in rng]
        share = [g[h] * fit[h] for h in rng]
        m1 = [mean_last(share[h]) for h in rng]
        m2 = [mean_last(share[h] * n[h]) for h in rng]
        d2 = [s[h] * (share[h] - m1[h] - n[h] * m2[h]) for h in rng]
        back = [dot(low(d2[h]), w2[h]) for h in rng]
        d1 = [back[h] * parts[h][1] for h in rng]
        d1b = [low(d1[h]) for h in rng]
        ed2 = [d2[h] * e[h] for h in rng]
        up1 = [dot(low(k[h] * e[h]), d1b[h], 0, 0) for h in rng]
        up2 = [dot(low(ed2[h]), act[h], 0, 0) for h in rng]
        for h in rng:
            w1n = w1f[h] - up1[h]
            w1_s[h] = w1n
            w1b_s[h] = low(w1n)
            w2_s[h] = w2f[h] - up2[h]
            b1_s[h] = b1[h] - sum_rows(d1[h] * e[h])
            b2_s[h] = b2[h] - sum_rows(ed2[h])
            act_ref[h, pl.ds(length + here, MB), :] = act[h]
            slope1_ref[h, ds, :] = low(parts[h][1])
            curve1_ref[h, ds, :] = low(back[h] * parts[h][2])
            d1_ref[h, ds, :] = d1b[h]
            d2_ref[h, ds, :] = d2[h]
            n_ref[h, ds, :] = n[h]
            s_ref[h, ds, :] = s[h]
            fit_ref[h, ds, :] = fit[h]
        return carry

    lax.fori_loop(0, blocks, step, 0)
    inclusive, _ = segment_masks(seg_row)
    for h in range(heads):
        queries = qk_ref[h, 0:length]
        keys = qk_ref[h, length : 2 * length]
        key_act = act_ref[h, length : 2 * length]
        er = erow_ref[h : h + 1, :]
        p1 = (dot(queries, keys, 1, 1) + 1.0) * inclusive
        p1_ref[h] = low(p1)
        zq1 = dot(queries, w1_ref[h]) + b1f[h : h + 1] - dot(low(p1 * er), d1_ref[h])
        aq, slope, _ = gelu_parts(zq1)
        aqb = low(aq)
        act_ref[h, 0:length] = aqb
        slopeq_ref[h] = low(slope)
        p2 = (dot(aqb, key_act, 1, 1) + 1.0) * inclusive
        p2_ref[h] = low(p2)
        zq2 = dot(aqb, w2t_ref[h], 1, 1) + b2f[h : h + 1] - dot(low(p2 * er), low(d2_ref[h]))
        c = zq2 - mean_last(zq2)
        s = lax.rsqrt(mean_last(c * c) + EPSILON)
        n = c * s
        nq_ref[h] = n
        sq_ref[h] = s
        out_s[:, h * head : (h + 1) * head] = q_s[h] + igf[h : h + 1] * n + ibf[h : h + 1]
    inner_out = out_s[...]
    gate, slope, _ = gelu_parts(dot(normed, wg_ref[...]))
    gelu_ref[...] = gate
    slope_ref[...] = inner_out * slope
    gated = low(inner_out * gate)
    gated_ref[...] = gated
    resid = tok + dot(gated, wo_ref[...])
    resid_ref[...] = resid
    spread_two = lax.rsqrt(mean_last(resid * resid) + EPSILON)
    normed_two_ref[...] = low(resid * spread_two * gain2_ref[...].astype(F32))


def ffn_kernel(x_ref, c_ref, wg_ref, wu_ref, wd_ref, act_ref, gg_ref, gu_ref, gx_ref):
    x = x_ref[...]
    gate = dot(x, wg_ref[...])
    up = dot(x, wu_ref[...])
    grad_act = dot(c_ref[...], wd_ref[...], 1, 1)
    sigma = jax.nn.sigmoid(gate)
    silu = gate * sigma
    act_ref[...] = low(silu * up)
    gg = low(grad_act * up * sigma * (1.0 + gate * (1.0 - sigma)))
    gu = low(grad_act * silu)
    gg_ref[...] = gg
    gu_ref[...] = gu
    gx_ref[...] = low(dot(gg, wg_ref[...], 1, 1) + dot(gu, wu_ref[...], 1, 1))


def ffn_weights_kernel(parts, *refs):
    x_refs, c_refs, act_refs, gg_refs, gu_refs = (
        refs[i * parts : (i + 1) * parts] for i in range(5)
    )
    wd_ref = refs[5 * parts]
    grad_gate_ref, grad_up_ref, grad_down_ref = refs[5 * parts + 1 : 5 * parts + 4]
    out_refs = refs[5 * parts + 4 : 6 * parts + 4]
    x_s, c_s, act_s, gg_s, gu_s = refs[6 * parts + 4 :]
    rows = x_refs[0].shape[0]
    for i in range(parts):
        at = slice(i * rows, (i + 1) * rows)
        x_s[at] = x_refs[i][...]
        c_s[at] = c_refs[i][...]
        act_s[at] = act_refs[i][...]
        gg_s[at] = gg_refs[i][...]
        gu_s[at] = gu_refs[i][...]
        out_refs[i][...] = low(dot(act_refs[i][...], wd_ref[...]))
    grad_gate_ref[...] = low(dot(x_s[...], gg_s[...], 0, 0))
    grad_up_ref[...] = low(dot(x_s[...], gu_s[...], 0, 0))
    grad_down_ref[...] = low(dot(act_s[...], c_s[...], 0, 0))


def between_kernel(parts, *refs):
    pieces = refs[0:parts]
    resid_ref, cot_ref, gain2_ref, wo_ref, gelu_ref, slope_ref, gated_ref, normed_ref = refs[
        parts : parts + 8
    ]
    resid_grad_ref, go_ref, gg_ref, gwo_ref, gwg_ref, gain_grad_ref = refs[parts + 8 :]
    grad = pieces[0][...].astype(F32)
    for piece in pieces[1:]:
        grad = grad + piece[...].astype(F32)
    resid = resid_ref[...]
    spread = lax.rsqrt(mean_last(resid * resid) + EPSILON)
    scaled = gain2_ref[...].astype(F32) * grad
    grad_resid = (
        cot_ref[0].astype(F32)
        + spread * scaled
        - resid * (spread * spread * spread * mean_last(scaled * resid))
    )
    gain_grad_ref[...] = sum_rows(grad * resid * spread)
    resid_grad_ref[...] = grad_resid
    grad_branch = low(grad_resid)
    grad_gated = dot(grad_branch, wo_ref[...], 1, 1)
    go_ref[...] = grad_gated * gelu_ref[...]
    grad_gates = low(grad_gated * slope_ref[...])
    gg_ref[...] = grad_gates
    gwo_ref[...] = low(dot(gated_ref[...], grad_branch, 0, 0))
    gwg_ref[...] = low(dot(normed_ref[...], grad_gates, 0, 0))


def backward_kernel(
    seg_smem,
    seg_ref,
    go_ref,
    normed_ref,
    qk_ref,
    ecol_ref,
    erow_ref,
    fcol_ref,
    w1_ref,
    w2t_ref,
    ig_ref,
    slope1_ref,
    curve1_ref,
    act_ref,
    d1_ref,
    d2_ref,
    n_ref,
    s_ref,
    fit_ref,
    w2s_ref,
    p1_ref,
    p2_ref,
    slopeq_ref,
    nq_ref,
    sq_ref,
    gq_ref,
    gk_ref,
    gv_ref,
    gr_ref,
    gw_ref,
    ginner_ref,
    small_ref,
    igf,
    t1_s,
    t2_s,
    ga_s,
    hh1_s,
    hh2_s,
    u_s,
    share_s,
    ge_s,
    gw1_s,
    gw1b_s,
    gb1_s,
    gw2_s,
    gw2b_s,
    gb2_s,
):
    length = go_ref.shape[0]
    heads, head, inner = w1_ref.shape
    blocks = length // MB
    top, bottom = slice(0, length), slice(length, 2 * length)
    igf[...] = ig_ref[...].astype(F32)
    inclusive, strict = segment_masks(seg_ref[...].astype(F32))
    for h in range(heads):
        g = igf[h : h + 1]
        er = erow_ref[h : h + 1, :]
        go = go_ref[:, h * head : (h + 1) * head]
        n = nq_ref[h]
        x = go * g
        hq2 = low(sq_ref[h] * (x - mean_last(x) - n * mean_last(x * n)))
        hh2_s[h, top] = hq2
        t2_s[h] = dot(p2_ref[h], hq2, 0, 0)
        mix = low(-dot(hq2, low(d2_ref[h]), 1, 1) * (inclusive * er))
        aq = act_ref[h, top]
        gaq = dot(hq2, w2t_ref[h]) + dot(mix, act_ref[h, bottom])
        ga_s[h] = dot(mix, aq, 0, 0)
        hq1 = low(gaq * slopeq_ref[h].astype(F32))
        hh1_s[h, top] = hq1
        t1_s[h] = dot(p1_ref[h], hq1, 0, 0)
    ge_s[...] = jnp.zeros(ge_s.shape, F32)

    def step(i, carry):
        b = blocks - 1 - i
        here = pl.multiple_of(b * MB, MB)
        after = jnp.minimum(here + MB, length - 1)
        fresh = (i == 0) | (seg_smem[0, after] != seg_smem[0, after - 1])

        @pl.when(fresh)
        def _():
            for ref in (gw1_s, gw1b_s, gb1_s, gw2_s, gw2b_s, gb2_s):
                ref[...] = jnp.zeros(ref.shape, ref.dtype)

        ds = pl.ds(here, MB)
        ds_low = pl.ds(length + here, MB)
        rng = range(heads)
        k = [qk_ref[h, ds_low, :] for h in rng]
        act = [act_ref[h, ds_low, :] for h in rng]
        e = [ecol_ref[ds, h : h + 1] for h in rng]
        w2 = [w2s_ref[b, h] for h in rng]
        gw1b = [gw1b_s[h] for h in rng]
        gw2b = [gw2b_s[h] for h in rng]
        gw1 = [gw1_s[h] for h in rng]
        gw2 = [gw2_s[h] for h in rng]
        gb1 = [gb1_s[h] for h in rng]
        gb2 = [gb2_s[h] for h in rng]
        d1 = [d1_ref[h, ds, :].astype(F32) for h in rng]
        d2 = [d2_ref[h, ds, :] for h in rng]
        n = [n_ref[h, ds, :] for h in rng]
        s = [s_ref[h, ds, :] for h in rng]
        fit = [fit_ref[h, ds, :] for h in rng]
        slope = [slope1_ref[h, ds, :].astype(F32) for h in rng]
        curve = [curve1_ref[h, ds, :].astype(F32) for h in rng]
        g = [igf[h : h + 1] for h in rng]
        share = [g[h] * fit[h] for h in rng]
        t1 = [t1_s[h, ds, :] + dot(k[h], gw1b[h]) + gb1[h] for h in rng]
        t2 = [t2_s[h, ds, :] + dot(act[h], gw2b[h], 1, 1) + gb2[h] for h in rng]
        g1 = [-e[h] * t1[h] for h in rng]
        u = [low(g1[h] * slope[h]) for h in rng]
        ed2 = [low(-e[h] * d2[h]) for h in rng]
        ga = [ga_s[h, ds, :] + dot(ed2[h], gw2b[h]) for h in rng]
        g2 = [dot(u[h], w2[h], 1, 1) - e[h] * t2[h] for h in rng]
        y = [s[h] * g2[h] for h in rng]
        my = [mean_last(y[h]) for h in rng]
        myn = [mean_last(y[h] * n[h]) for h in rng]
        msn = [mean_last(share[h] * n[h]) for h in rng]
        mgd = [mean_last(g2[h] * d2[h]) for h in rng]
        gshare = [y[h] - my[h] - n[h] * myn[h] for h in rng]
        gn = [g[h] * (g[h] * gshare[h]) - y[h] * msn[h] - share[h] * myn[h] for h in rng]
        mn = [mean_last(gn[h]) for h in rng]
        mnn = [mean_last(gn[h] * n[h]) for h in rng]
        h2 = [
            low(s[h] * (gn[h] - mn[h] - n[h] * (mnn[h] + mgd[h]))) for h in rng
        ]
        ga = [ga[h] + dot(h2[h], w2[h]) for h in rng]
        h1f = [ga[h] * slope[h] + g1[h] * curve[h] for h in rng]
        h1 = [low(x) for x in h1f]
        up1 = [dot(k[h], h1[h], 0, 0) for h in rng]
        up2 = [
            dot(low(d2[h]), u[h], 0, 0) + dot(h2[h], act[h], 0, 0) for h in rng
        ]
        for h in rng:
            w1n = gw1[h] + up1[h]
            w2n = gw2[h] + up2[h]
            gw1_s[h] = w1n
            gw1b_s[h] = low(w1n)
            gw2_s[h] = w2n
            gw2b_s[h] = low(w2n)
            gb1_s[h] = gb1[h] + sum_rows(h1f[h])
            gb2_s[h] = gb2[h] + sum_rows(h2[h].astype(F32))
            u_s[h, ds, :] = u[h]
            hh1_s[h, ds_low, :] = h1[h]
            hh2_s[h, ds_low, :] = h2[h]
            share_s[h, ds, :] = gshare[h]
            ge_s[ds, h : h + 1] = -jnp.sum(d1[h] * t1[h], -1, keepdims=True) - jnp.sum(
                d2[h] * t2[h], -1, keepdims=True
            )
        return carry

    lax.fori_loop(0, blocks, step, 0)
    small_ref[...] = jnp.zeros(small_ref.shape, F32)
    per_row = small_ref.shape[1] // inner
    for h in range(heads):
        cols = slice(h * head, (h + 1) * head)
        g = igf[h : h + 1]
        er = erow_ref[h : h + 1, :]
        hh1 = hh1_s[h]
        hh2 = hh2_s[h]
        qk = qk_ref[h]
        keys = qk_ref[h, bottom]
        both = dot(hh1, d1_ref[h], 1, 1)
        mixq = low(-both[top] * (inclusive * er))
        mixk = low(-both[bottom] * (strict * er))
        direct = dot(hh1, w1_ref[h], 1, 1)
        share = share_s[h]
        spread = dot(mixq, qk_ref[h, top], 0, 0) + dot(mixk, keys, 0, 0)
        go = go_ref[:, cols]
        gq_ref[:, cols] = low(go + direct[top] + dot(mixq, keys))
        gk_ref[:, cols] = low(g * share + direct[bottom] + dot(mixk, keys) + spread)
        gv_ref[:, cols] = low(-g * share)
        ginner_ref[h] = low(dot(qk, hh1, 0, 0))
        ginner_ref[heads + h] = low(
            dot(hh2, act_ref[h], 0, 0) + dot(low(d2_ref[h]), u_s[h], 0, 0)
        )
        row, lane = 14 + h // per_row, (h % per_row) * inner
        small_ref[row : row + 1, lane : lane + inner] = sum_rows(hh1.astype(F32))
        row = 14 + heads // per_row
        small_ref[row : row + 1, cols] = sum_rows(hh2.astype(F32))
        small_ref[row + 1 : row + 2, cols] = sum_rows(go * nq_ref[h]) + sum_rows(
            share * (fit_ref[h] + g * n_ref[h])
        )
        small_ref[row + 2 : row + 3, cols] = sum_rows(go) + g * sum_rows(share)
    grad_rates = ge_s[...] * fcol_ref[...]
    row = 17 + heads // per_row
    small_ref[row : row + 1, 0 : grad_rates.shape[1]] = sum_rows(grad_rates)
    gr_ref[...] = low(grad_rates)
    normed = normed_ref[...]
    small_ref[2 : 2 + heads] = dot(low(grad_rates), normed, 0, 0)[0:heads]
    for i, ref in enumerate((gq_ref, gk_ref, gv_ref)):
        gw_ref[i] = low(dot(normed, ref[...], 0, 0))


def input_kernel(
    gq_ref,
    gk_ref,
    gv_ref,
    gg_ref,
    gr_ref,
    wq_ref,
    wk_ref,
    wv_ref,
    wg_ref,
    wr_ref,
    tok_ref,
    gain1_ref,
    resid_grad_ref,
    small_ref,
    gain_two_ref,
    grad_ref,
    small_out,
):
    heads = wr_ref.shape[1]
    grad = dot(gq_ref[...], wq_ref[...], 1, 1) + dot(gk_ref[...], wk_ref[...], 1, 1)
    grad = grad + dot(gv_ref[...], wv_ref[...], 1, 1) + dot(gg_ref[...], wg_ref[...], 1, 1)
    grad = grad + dot(gr_ref[:, 0:heads], wr_ref[...], 1, 1)
    tok = tok_ref[0].astype(F32)
    spread = lax.rsqrt(mean_last(tok * tok) + EPSILON)
    scaled = gain1_ref[...].astype(F32) * grad
    grad_ref[0] = (
        resid_grad_ref[...]
        + spread * scaled
        - tok * (spread * spread * spread * mean_last(scaled * tok))
    )
    small_out[...] = small_ref[...]
    small_out[0:1] = sum_rows(grad * tok * spread)
    small_out[1:2] = gain_two_ref[...]


def call(kernel, outs, inputs, scratch=(), smem=0):
    specs = [pl.BlockSpec(memory_space=pltpu.SMEM)] * smem
    specs += [pl.BlockSpec(memory_space=pltpu.VMEM)] * (len(inputs) - smem)
    return pl.pallas_call(
        kernel,
        out_shape=[jax.ShapeDtypeStruct(s, d) for s, d in outs],
        in_specs=specs,
        out_specs=[pl.BlockSpec(memory_space=pltpu.VMEM)] * len(outs),
        scratch_shapes=[pltpu.VMEM(s, d) for s, d in scratch],
        compiler_params=pltpu.CompilerParams(vmem_limit_bytes=VMEM_BYTES),
    )(*inputs)


def exchange(values, axis, size, distance):
    return lax.ppermute(values, axis, [(i, i ^ distance) for i in range(size)])


def add_low(left, right):
    return low(left.astype(F32) + right.astype(F32))


def halve(values, axis, size, distance, dim):
    side = lax.bitwise_and(lax.axis_index(axis) // distance, 1)
    half = values.shape[dim] // 2
    kept = lax.dynamic_slice_in_dim(values, side * half, half, dim)
    sent = lax.dynamic_slice_in_dim(values, (1 - side) * half, half, dim)
    return add_low(kept, exchange(sent, axis, size, distance))


def double(values, axis, size, distance, dim):
    side = lax.bitwise_and(lax.axis_index(axis) // distance, 1)
    other = exchange(values, axis, size, distance)
    return jnp.where(
        side == 0,
        jnp.concatenate([values, other], dim),
        jnp.concatenate([other, values], dim),
    )


def distances(size):
    found = []
    step = 1
    while step < size:
        found.append(step)
        step *= 2
    return found


def scatter_rows(values, size, dim):
    for d in distances(size):
        values = halve(values, "rows", size, d, dim)
    return values


def gather_rows(values, size, dim):
    for d in reversed(distances(size)):
        values = double(values, "rows", size, d, dim)
    return values


def scatter_feat(values, size, dim):
    me = lax.axis_index("feat")
    total = lax.dynamic_index_in_dim(values, me, dim, keepdims=False).astype(F32)
    for s in range(1, size):
        piece = lax.dynamic_index_in_dim(values, lax.bitwise_xor(me, s), dim, keepdims=False)
        total = total + exchange(piece, "feat", size, s).astype(F32)
    return low(total)


def on_device(
    rows,
    feats,
    tokens,
    cotangent,
    seg_ids,
    pad_mask,
    norm1_gain,
    w_query,
    w_key,
    w_value,
    w_gate,
    w_rate,
    b_rate,
    inner_w1,
    inner_b1,
    inner_w2,
    inner_b2,
    inner_gain,
    inner_bias,
    w_out,
    norm2_gain,
    ffn_gate,
    ffn_up,
    ffn_down,
):
    _, length, width = tokens.shape
    heads, head, inner = inner_w1.shape
    hidden = ffn_gate.shape[1]
    blocks = length // MB
    gain_one = norm1_gain[None]
    gain_two = norm2_gain[None]
    line = (length, width)
    wide = (heads, length, inner)
    slim = (heads, length, head)
    thin = (heads, length, 1)
    square = (heads, length, length)
    state = (heads, head, inner)
    cots = [cotangent[0]]
    for s in range(1, feats):
        cots.append(exchange(cots[0], "feat", feats, s))
    saved = call(
        forward_kernel,
        [
            (line, BF16),
            (line, BF16),
            (line, F32),
            (line, BF16),
            (line, F32),
            (line, F32),
            ((heads, 2 * length, head), BF16),
            ((length, 128), F32),
            ((16, length), F32),
            ((length, 128), F32),
            (state, BF16),
            (wide, BF16),
            (wide, BF16),
            ((heads, 2 * length, inner), BF16),
            (wide, BF16),
            (slim, F32),
            (slim, F32),
            (thin, F32),
            (slim, F32),
            ((blocks,) + state, BF16),
            (square, BF16),
            (square, BF16),
            (wide, BF16),
            (slim, F32),
            (thin, F32),
        ],
        [
            seg_ids,
            seg_ids,
            pad_mask,
            tokens,
            gain_one,
            w_query,
            w_key,
            w_value,
            w_gate,
            w_rate,
            b_rate[None],
            inner_w1,
            inner_b1,
            inner_w2,
            inner_b2,
            inner_gain,
            inner_bias,
            w_out,
            gain_two,
        ],
        [
            (slim, F32),
            (slim, F32),
            (slim, F32),
            (line, F32),
            (state, F32),
            (state, BF16),
            ((heads, 1, inner), F32),
            (state, F32),
            ((heads, 1, head), F32),
            ((heads, inner), F32),
            ((heads, head), F32),
            ((heads, head), F32),
            ((heads, head), F32),
        ],
        smem=1,
    )
    normed, normed_two, resid, gated, gelu_gate, gate_slope = saved[0:6]
    qk, ecol, erow, fcol, w2t = saved[6:11]
    rest = saved[11:]
    blocks_in = [normed_two]
    for s in range(1, feats):
        blocks_in.append(exchange(normed_two, "feat", feats, s))
    acts, ggs, gus, pieces = [], [], [], []
    for s in range(feats):
        act, gg, gu, gx = call(
            ffn_kernel,
            [((length, hidden), BF16)] * 3 + [(line, BF16)],
            [blocks_in[s], cots[s], ffn_gate, ffn_up, ffn_down],
        )
        acts.append(act)
        ggs.append(gg)
        gus.append(gu)
        pieces.append(gx if s == 0 else exchange(gx, "feat", feats, s))
    whole = feats * length
    ffn_grads = call(
        partial(ffn_weights_kernel, feats),
        [((width, hidden), BF16), ((width, hidden), BF16), ((hidden, width), BF16)]
        + [(line, BF16)] * feats,
        blocks_in + cots + acts + ggs + gus + [ffn_down],
        [((whole, width), BF16), ((whole, width), BF16)] + [((whole, hidden), BF16)] * 3,
    )
    ffn_out = ffn_grads[3].astype(F32)
    for s in range(1, feats):
        ffn_out = ffn_out + exchange(ffn_grads[3 + s], "feat", feats, s).astype(F32)
    mixed = low(resid + ffn_out)
    grad_resid, grad_inner_out, grad_gates, grad_w_out, grad_w_gate, grad_gain_two = call(
        partial(between_kernel, feats),
        [
            (line, F32),
            (line, F32),
            (line, BF16),
            ((width, width), BF16),
            ((width, width), BF16),
            ((1, width), F32),
        ],
        pieces
        + [resid, cotangent, gain_two, w_out, gelu_gate, gate_slope, gated, normed],
    )

    def shares(values):
        return values.reshape((feats, width // feats, width))

    def reduced_by_features(values):
        values = scatter_rows(values, rows, 1)
        values = scatter_feat(values, feats, 0)
        return gather_rows(values, rows, 0).astype(F32)

    def reduced_over_rows(values):
        return gather_rows(scatter_rows(values, rows, 0), rows, 0).astype(F32)

    total_ffn = [reduced_over_rows(x) for x in ffn_grads[0:3]]
    total_out = reduced_by_features(shares(grad_w_out))
    total_gate = reduced_by_features(shares(grad_w_gate))
    gq, gk, gv, gr, gw, ginner, small = call(
        backward_kernel,
        [
            (line, BF16),
            (line, BF16),
            (line, BF16),
            ((length, 128), BF16),
            ((3, width, width), BF16),
            ((2 * heads, head, inner), BF16),
            ((24, width), F32),
        ],
        [seg_ids, seg_ids, grad_inner_out, normed, qk, ecol, erow, fcol, inner_w1, w2t]
        + [inner_gain]
        + list(rest),
        [
            ((heads, head), F32),
            (wide, F32),
            (slim, F32),
            (wide, F32),
            ((heads, 2 * length, inner), BF16),
            ((heads, 2 * length, head), BF16),
            (wide, BF16),
            (slim, F32),
            ((length, 128), F32),
            (state, F32),
            (state, BF16),
            ((heads, 1, inner), F32),
            (state, F32),
            (state, BF16),
            ((heads, 1, head), F32),
        ],
        smem=1,
    )
    grad_tokens, small = call(
        input_kernel,
        [((1,) + line, F32), ((24, width), F32)],
        [gq, gk, gv, grad_gates, gr, w_query, w_key, w_value, w_gate, w_rate]
        + [tokens, gain_one, grad_resid, small, grad_gain_two],
    )
    totals = [reduced_by_features(shares(gw[i])) for i in range(3)]
    inner_sum = scatter_rows(ginner.reshape((-1, inner)), rows, 0)
    for d in distances(feats):
        inner_sum = add_low(inner_sum, exchange(inner_sum, "feat", feats, d))
    inner_sum = gather_rows(inner_sum, rows, 0).astype(F32).reshape((2,) + state)
    for d in distances(rows):
        small = small + exchange(small, "rows", rows, d)
    for d in distances(feats):
        small = small + exchange(small, "feat", feats, d)
    me = lax.axis_index("feat")
    mine = lax.dynamic_slice_in_dim(small, me * (width // feats), width // feats, 1)
    bias_rows = heads * inner // width
    at = 14 + bias_rows
    return (
        mixed[None],
        grad_tokens,
        mine[0],
        totals[0],
        totals[1],
        totals[2],
        total_gate,
        jnp.transpose(mine[2 : 2 + heads]),
        small[at + 3, 0:heads],
        inner_sum[0],
        small[14:at].reshape((heads, inner)),
        jnp.transpose(inner_sum[1], (0, 2, 1)),
        small[at].reshape((heads, head)),
        small[at + 1].reshape((heads, head)),
        small[at + 2].reshape((heads, head)),
        total_out,
        mine[1],
        total_ffn[0],
        total_ffn[1],
        total_ffn[2],
    )


def solution(mesh):
    batch = ("rows", "feat")
    placed = (
        (P(batch, None, None), P(batch, None, None), P(batch, None), P(batch, None))
        + (P(),) * 15
        + (P(None, "feat"), P(None, "feat"), P("feat", None))
    )
    return jax.shard_map(
        partial(on_device, mesh.shape["rows"], mesh.shape["feat"]),
        mesh=mesh,
        in_specs=placed,
        out_specs=(
            P(batch, None, None),
            P(batch, None, None),
            P("feat"),
            P("feat", None),
            P("feat", None),
            P("feat", None),
            P("feat", None),
            P("feat", None),
            P(),
            P(),
            P(),
            P(),
            P(),
            P(),
            P(),
            P("feat", None),
            P("feat"),
            P(None, "feat"),
            P(None, "feat"),
            P("feat", None),
        ),
        check_vma=False,
    )
```

profile of v0, /device:TPU:0, one launch (start us, length us, event | category | flops | bytes accessed | tf_op | source)
XLA Modules:
  0.0 361.4 jit_solution(9899824052792580188)
XLA Ops:
  6.2 25.7 %shard_map.365 = (bf16[128,768]{1,0:T(8,128)(2,1)}, bf16[128,768]{1,0:T(8,128)(2,1)}, f32[128,768]{1,0:T(8,128)}, bf16[128,768]{1,0:T(8,128)(2,1)}, f32[128,768]...) custom-call(s32[1,128]{1,0:T(1,128)} %seg_ref.3, ...), custom_call_target="tpu_custom_call" | custom-call | tf_op jit(solution)/shard_map/pallas_call | solution.py:549
  37.3 4.0 %collective-permute-start.2 = (bf16[128,768]{1,0:T(8,128)(2,1)}, bf16[128,768]{1,0:T(8,128)(2,1)S(1)}, u32[]{:S(2)}, u32[]{:S(2)}) collective-permute-start(bf16[128,768]{1,0:T(8,128)(2,1)} %get-tuple-element.84.x_ref.refs_0_), channel_id=1, source_target_pairs={{0,3},{1,2},{2,1},{3,0},{4,7},{5,6},{6,5},{7,4},{8,11},{9,10},{10,... | collective-permute-start | bytes 589832 | tf_op jit(solution)/shard_map/ppermute | solution.py:560
  41.4 6.5 %collective-permute-done.x_ref.refs_1_ = bf16[128,768]{1,0:T(8,128)(2,1)S(1)} collective-permute-done((bf16[128,768]{1,0:T(8,128)(2,1)}, bf16[128,768]{1,0:T(8,128)(2,1)S(1)}, u32[]{:S(2)}, u32[]{:S(2)}) %collective-permute-start) | collective-permute-done | bytes 196640 | tf_op jit(solution)/shard_map/ppermute | solution.py:560
  50.1 3.8 %shard_map.366 = (bf16[128,512]{1,0:T(8,128)(2,1)}, bf16[128,512]{1,0:T(8,128)(2,1)}, bf16[128,512]{1,0:T(8,128)(2,1)}, bf16[128,768]{1,0:T(8,128)(2,1)}) custom-call(bf16[128,768]{1,0:T(8,128)(2,1)} %get-tuple-element.84.x_ref.refs_0_, bf16[128,768]{1,0:T(8,128)(2,1)} %bitcast.71, bf16[768,512]{1,0:T(8,128)(2,1)} %wg_ref.10, bf16[768,512]{1,0:T(8,128)(2,1)} %wu_ref.7, ...), custom_call_target="tpu_custom_call" | custom-call | tf_op jit(solution)/shard_map/pallas_call | solution.py:549
  54.6 3.8 %shard_map.367 = (bf16[128,512]{1,0:T(8,128)(2,1)}, bf16[128,512]{1,0:T(8,128)(2,1)}, bf16[128,512]{1,0:T(8,128)(2,1)}, bf16[128,768]{1,0:T(8,128)(2,1)}) custom-call(bf16[128,768]{1,0:T(8,128)(2,1)} %copy-done.15, bf16[128,768]{1,0:T(8,128)(2,1)} %copy-done.16, bf16[768,512]{1,0:T(8,128)(2,1)} %wg_ref.10, bf16[768,512]{1,0:T(8,128)(2,1)} %wu_ref.7, ...), custom_call_target="tpu_custom_call" | custom-call | tf_op jit(solution)/shard_map/pallas_call | solution.py:549
  58.4 6.0 %collective-permute-done.4.c_ref.refs_6_ = bf16[128,768]{1,0:T(8,128)(2,1)S(1)} collective-permute-done((bf16[128,768]{1,0:T(8,128)(2,1)S(1)}, bf16[128,768]{1,0:T(8,128)(2,1)S(1)}, u32[]{:S(2)}, u32[]{:S(2)}) %collective-permute-start.4) | collective-permute-done | bytes 196640 | tf_op jit(solution)/shard_map/ppermute | solution.py:560
  65.1 3.8 %shard_map.368 = (bf16[128,512]{1,0:T(8,128)(2,1)}, bf16[128,512]{1,0:T(8,128)(2,1)}, bf16[128,512]{1,0:T(8,128)(2,1)}, bf16[128,768]{1,0:T(8,128)(2,1)}) custom-call(bf16[128,768]{1,0:T(8,128)(2,1)} %copy-done.17, bf16[128,768]{1,0:T(8,128)(2,1)} %copy-done.18, bf16[768,512]{1,0:T(8,128)(2,1)} %wg_ref.10, bf16[768,512]{1,0:T(8,128)(2,1)} %wu_ref.7, ...), custom_call_target="tpu_custom_call" | custom-call | tf_op jit(solution)/shard_map/pallas_call | solution.py:549
  70.2 3.8 %shard_map.369 = (bf16[128,512]{1,0:T(8,128)(2,1)}, bf16[128,512]{1,0:T(8,128)(2,1)}, bf16[128,512]{1,0:T(8,128)(2,1)}, bf16[128,768]{1,0:T(8,128)(2,1)}) custom-call(bf16[128,768]{1,0:T(8,128)(2,1)} %copy-done.19, bf16[128,768]{1,0:T(8,128)(2,1)} %copy-done.20, bf16[768,512]{1,0:T(8,128)(2,1)} %wg_ref.10, bf16[768,512]{1,0:T(8,128)(2,1)} %wu_ref.7, ...), custom_call_target="tpu_custom_call" | custom-call | tf_op jit(solution)/shard_map/pallas_call | solution.py:549
  74.0 5.0 %shard_map.370 = (bf16[768,512]{1,0:T(8,128)(2,1)}, bf16[768,512]{1,0:T(8,128)(2,1)}, bf16[512,768]{1,0:T(8,128)(2,1)}, bf16[128,768]{1,0:T(8,128)(2,1)}, bf16[1...) custom-call(bf16[128,768]{1,0:T(8,128)(2,1)} %get-tuple-element.84.x_ref.refs_0_, ...), custom_call_target="tpu_custom_call" | custom-call | tf_op jit(solution)/shard_map/pallas_call | solution.py:549
  79.0 4.2 %collective-permute-start.8 = (bf16[128,768]{1,0:T(8,128)(2,1)}, bf16[128,768]{1,0:T(8,128)(2,1)S(1)}, u32[]{:S(2)}, u32[]{:S(2)}) collective-permute-start(bf16[128,768]{1,0:T(8,128)(2,1)} %get-tuple-element.100), channel_id=1, source_target_pairs={{0,3},{1,2},{2,1},{3,0},{4,7},{5,6},{6,5},{7,4},{8,11},{9,10},{10,... | collective-permute-start | bytes 589832 | tf_op jit(solution)/shard_map/ppermute | solution.py:560
  91.8 5.3 %collective-permute-done.9.refs_1_ = bf16[128,768]{1,0:T(8,128)(2,1)S(1)} collective-permute-done((bf16[128,768]{1,0:T(8,128)(2,1)S(1)}, bf16[128,768]{1,0:T(8,128)(2,1)S(1)}, u32[]{:S(2)}, u32[]{:S(2)}) %collective-permute-start.9) | collective-permute-done | bytes 196640 | tf_op jit(solution)/shard_map/ppermute | solution.py:560
  99.7 12.9 %collective-permute-done.10.refs_2_ = bf16[128,768]{1,0:T(8,128)(2,1)S(1)} collective-permute-done((bf16[128,768]{1,0:T(8,128)(2,1)S(1)}, bf16[128,768]{1,0:T(8,128)(2,1)S(1)}, u32[]{:S(2)}, u32[]{:S(2)}) %collective-permute-start.10) | collective-permute-done | bytes 196640 | tf_op jit(solution)/shard_map/ppermute | solution.py:560
  113.3 4.5 %shard_map.371 = (f32[128,768]{1,0:T(8,128)}, f32[128,768]{1,0:T(8,128)}, bf16[128,768]{1,0:T(8,128)(2,1)}, bf16[768,768]{1,0:T(8,128)(2,1)}, bf16[768,768]{1,0:T(8,128)(2,1)}, /*index=5*/f32[1,768]{1,0:T(1,128)}) custom-call(bf16[128,768]{1,0:T(8,128)(2,1)} %get-tuple-element.101.refs_0_, bf16[128,768]{1,0:T(8,128)(2,1)} %copy-done.24, ...), custom_call_target="tpu_custom_call" | custom-call | tf_op jit(solution)/shard_map/pallas_call | solution.py:549
  117.8 28.8 %shard_map.372 = (bf16[128,768]{1,0:T(8,128)(2,1)}, bf16[128,768]{1,0:T(8,128)(2,1)}, bf16[128,768]{1,0:T(8,128)(2,1)}, bf16[128,128]{1,0:T(8,128)(2,1)}, bf16[3...) custom-call(s32[1,128]{1,0:T(1,128)} %seg_ref.3, s32[1,128]{1,0:T(1,128)} %seg_ref.3, ...), custom_call_target="tpu_custom_call" | custom-call | tf_op jit(solution)/shard_map/pallas_call | solution.py:549
  148.9 5.5 %shard_map.373 = (f32[1,128,768]{2,1,0:T(8,128)}, f32[24,768]{1,0:T(8,128)}) custom-call(bf16[128,768]{1,0:T(8,128)(2,1)} %get-tuple-element.129.gq_ref, bf16[128,768]{1,0:T(8,128)(2,1)} %get-tuple-element.130.gk_ref, bf16[128,768]{1,0:T(8,128)(2,1)} %get-tuple-element.131.gv_ref, bf16[128,768]{1,0:T(8,128)(2,1)} %get-tuple-element.132.gg_ref, ...), custom_call_target="tpu_custom_call" | custom-call | tf_op jit(solution)/shard_map/pallas_call | solution.py:549
  176.9 3.6 collective-permute-start.16
  194.0 4.1 %collective-permute-done.77 = bf16[192,512]{1,0:T(8,128)(2,1)S(1)} collective-permute-done((bf16[192,512]{1,0:T(8,128)(2,1)}, bf16[192,512]{1,0:T(8,128)(2,1)S(1)}, u32[]{:S(2)}, u32[]{:S(2)}) %collective-permute-start.77) | collective-permute-done | bytes 196640 | tf_op jit(solution)/shard_map/ppermute | solution.py:560
  201.0 5.5 %collective-permute-done.83 = bf16[128,768]{1,0:T(8,128)(2,1)S(1)} collective-permute-done((bf16[128,768]{1,0:T(8,128)(2,1)S(1)}, bf16[128,768]{1,0:T(8,128)(2,1)S(1)}, u32[]{:S(2)}, u32[]{:S(2)}) %collective-permute-start.83) | collective-permute-done | bytes 196640 | tf_op jit(solution)/shard_map/ppermute | solution.py:560
  234.2 3.5 collective-permute-done.55
  238.0 17.5 %collective-permute-done.74 = bf16[192,512]{1,0:T(8,128)(2,1)S(1)} collective-permute-done((bf16[192,512]{1,0:T(8,128)(2,1)S(1)}, bf16[192,512]{1,0:T(8,128)(2,1)S(1)}, u32[]{:S(2)}, u32[]{:S(2)}) %collective-permute-start.74) | collective-permute-done | bytes 196640 | tf_op jit(solution)/shard_map/ppermute | solution.py:560
  264.4 4.2 %collective-permute-done.56 = bf16[192,256]{1,0:T(8,128)(2,1)S(1)} collective-permute-done((bf16[192,256]{1,0:T(8,128)(2,1)S(1)}, bf16[192,256]{1,0:T(8,128)(2,1)S(1)}, u32[]{:S(2)}, u32[]{:S(2)}) %collective-permute-start.56) | collective-permute-done | bytes 98336 | tf_op jit(solution)/shard_map/ppermute | solution.py:560
  279.3 5.1 %collective-permute-done.58 = bf16[192,256]{1,0:T(8,128)(2,1)S(1)} collective-permute-done((bf16[192,256]{1,0:T(8,128)(2,1)S(1)}, bf16[192,256]{1,0:T(8,128)(2,1)S(1)}, u32[]{:S(2)}, u32[]{:S(2)}) %collective-permute-start.58) | collective-permute-done | bytes 98336 | tf_op jit(solution)/shard_map/ppermute | solution.py:560
  287.1 4.1 %collective-permute-done.37 = bf16[4,24,768]{2,1,0:T(8,128)(2,1)S(1)} collective-permute-done((bf16[4,24,768]{2,1,0:T(8,128)(2,1)S(1)}, bf16[4,24,768]{2,1,0:T(8,128)(2,1)S(1)}, u32[]{:S(2)}, u32[]{:S(2)}) %collective-permute-start.37) | collective-permute-done | bytes 147488 | tf_op jit(solution)/shard_map/ppermute | solution.py:560
  326.7 3.6 collective-permute-done.32
  (343 shorter events, 185.1 us)
Async XLA Ops:
  34.4 24.0 %collective-permute-start.1 = (bf16[128,768]{1,0:T(8,128)(2,1)}, bf16[128,768]{1,0:T(8,128)(2,1)S(1)}, u32[]{:S(2)}, u32[]{:S(2)}) collective-permute-start(bf16[128,768]{1,0:T(8,128)(2,1)} %get-tuple-element.84.x_ref.refs_0_), channel_id=1, source_target_pairs={{0,2},{1,3},{2,0},{3,1},{4,6},{5,7},{6,4},{7,5},{8,10},{9,11},{10,... | collective-permute-start | bytes 589832 | tf_op jit(solution)/shard_map/ppermute | solution.py:560
  37.3 27.1 %collective-permute-start.4 = (bf16[128,768]{1,0:T(8,128)(2,1)S(1)}, bf16[128,768]{1,0:T(8,128)(2,1)S(1)}, u32[]{:S(2)}, u32[]{:S(2)}) collective-permute-start(bf16[128,768]{1,0:T(8,128)(2,1)S(1)} %bitcast.74), channel_id=1, source_target_pairs={{0,2},{1,3},{2,0},{3,1},{4,6},{5,7},{6,4},{7,5},{8,10},{9,11},{10,... | collective-permute-start | bytes 589832 | tf_op jit(solution)/shard_map/ppermute | solution.py:560
  37.3 31.5 %collective-permute-start.2 = (bf16[128,768]{1,0:T(8,128)(2,1)}, bf16[128,768]{1,0:T(8,128)(2,1)S(1)}, u32[]{:S(2)}, u32[]{:S(2)}) collective-permute-start(bf16[128,768]{1,0:T(8,128)(2,1)} %get-tuple-element.84.x_ref.refs_0_), channel_id=1, source_target_pairs={{0,3},{1,2},{2,1},{3,0},{4,7},{5,6},{6,5},{7,4},{8,11},{9,10},{10,... | collective-permute-start | bytes 589832 | tf_op jit(solution)/shard_map/ppermute | solution.py:560
  79.0 77.1 %collective-permute-start.8 = (bf16[128,768]{1,0:T(8,128)(2,1)}, bf16[128,768]{1,0:T(8,128)(2,1)S(1)}, u32[]{:S(2)}, u32[]{:S(2)}) collective-permute-start(bf16[128,768]{1,0:T(8,128)(2,1)} %get-tuple-element.100), channel_id=1, source_target_pairs={{0,3},{1,2},{2,1},{3,0},{4,7},{5,6},{6,5},{7,4},{8,11},{9,10},{10,... | collective-permute-start | bytes 589832 | tf_op jit(solution)/shard_map/ppermute | solution.py:560
  83.2 73.0 %collective-permute-start.7 = (bf16[128,768]{1,0:T(8,128)(2,1)}, bf16[128,768]{1,0:T(8,128)(2,1)S(1)}, u32[]{:S(2)}, u32[]{:S(2)}) collective-permute-start(bf16[128,768]{1,0:T(8,128)(2,1)} %get-tuple-element.99), channel_id=1, source_target_pairs={{0,2},{1,3},{2,0},{3,1},{4,6},{5,7},{6,4},{7,5},{8,10},{9,11},{10,... | collective-permute-start | bytes 589832 | tf_op jit(solution)/shard_map/ppermute | solution.py:560
  84.3 28.2 %collective-permute-start.10 = (bf16[128,768]{1,0:T(8,128)(2,1)S(1)}, bf16[128,768]{1,0:T(8,128)(2,1)S(1)}, u32[]{:S(2)}, u32[]{:S(2)}) collective-permute-start(bf16[128,768]{1,0:T(8,128)(2,1)S(1)} %copy-done.32), channel_id=1, source_target_pairs={{0,2},{1,3},{2,0},{3,1},{4,6},{5,7},{6,4},{7,5},{8,10},{9,11},{10,... | collective-permute-start | bytes 589832 | tf_op jit(solution)/shard_map/ppermute | solution.py:560
  87.2 25.3 %collective-permute-start.11 = (bf16[128,768]{1,0:T(8,128)(2,1)S(1)}, bf16[128,768]{1,0:T(8,128)(2,1)S(1)}, u32[]{:S(2)}, u32[]{:S(2)}) collective-permute-start(bf16[128,768]{1,0:T(8,128)(2,1)S(1)} %copy-done.33), channel_id=1, source_target_pairs={{0,3},{1,2},{2,1},{3,0},{4,7},{5,6},{6,5},{7,4},{8,11},{9,10},{10,... | collective-permute-start | bytes 589832 | tf_op jit(solution)/shard_map/ppermute | solution.py:560
  97.2 59.5 %collective-permute-start.6 = (bf16[128,768]{1,0:T(8,128)(2,1)S(1)}, bf16[128,768]{1,0:T(8,128)(2,1)S(1)}, u32[]{:S(2)}, u32[]{:S(2)}) collective-permute-start(bf16[128,768]{1,0:T(8,128)(2,1)S(1)} %copy-done.30), channel_id=1, source_target_pairs={{0,1},{1,0},{2,3},{3,2},{4,5},{5,4},{6,7},{7,6},{8,9},{9,8},{10,11... | collective-permute-start | bytes 589832 | tf_op jit(solution)/shard_map/ppermute | solution.py:560
  112.5 52.3 %collective-permute-start.70 = (bf16[384,512]{1,0:T(8,128)(2,1)}, bf16[384,512]{1,0:T(8,128)(2,1)}, u32[]{:S(2)}, u32[]{:S(2)}) collective-permute-start(bf16[384,512]{1,0:T(8,128)(2,1)} %constant_dynamic-slice_fusion.9), channel_id=1, source_target_pairs={{0,4},{4,0},{8,12},{12,8},{16,20},{20,16},{24,28},{28,24},{1,5},{5... | collective-permute-start | bytes 1179656 | tf_op jit(solution)/shard_map/ppermute | solution.py:560
  112.5 54.0 %collective-permute-start.76 = (bf16[384,512]{1,0:T(8,128)(2,1)}, bf16[384,512]{1,0:T(8,128)(2,1)}, u32[]{:S(2)}, u32[]{:S(2)}) collective-permute-start(bf16[384,512]{1,0:T(8,128)(2,1)} %constant_dynamic-slice_fusion.6), channel_id=1, source_target_pairs={{0,4},{4,0},{8,12},{12,8},{16,20},{20,16},{24,28},{28,24},{1,5},{5... | collective-permute-start | bytes 1179656 | tf_op jit(solution)/shard_map/ppermute | solution.py:560
  156.6 63.7 %collective-permute-start.17 = (bf16[4,96,768]{2,1,0:T(8,128)(2,1)}, bf16[4,96,768]{2,1,0:T(8,128)(2,1)}, u32[]{:S(2)}, u32[]{:S(2)}) collective-permute-start(bf16[4,96,768]{2,1,0:T(8,128)(2,1)} %constant_dynamic-slice_fusion.27), channel_id=1, source_target_pairs={{0,4},{4,0},{8,12},{12,8},{16,20},{20,16},{24,28},{28,24},{1,5},{5... | collective-permute-start | bytes 1769480 | tf_op jit(solution)/shard_map/ppermute | solution.py:560
  164.8 57.5 %collective-permute-start.26 = (bf16[4,96,768]{2,1,0:T(8,128)(2,1)}, bf16[4,96,768]{2,1,0:T(8,128)(2,1)}, u32[]{:S(2)}, u32[]{:S(2)}) collective-permute-start(bf16[4,96,768]{2,1,0:T(8,128)(2,1)} %constant_dynamic-slice_fusion.24), channel_id=1, source_target_pairs={{0,4},{4,0},{8,12},{12,8},{16,20},{20,16},{24,28},{28,24},{1,5},{5... | collective-permute-start | bytes 1769480 | tf_op jit(solution)/shard_map/ppermute | solution.py:560
  164.8 60.2 %collective-permute-start.35 = (bf16[4,96,768]{2,1,0:T(8,128)(2,1)}, bf16[4,96,768]{2,1,0:T(8,128)(2,1)}, u32[]{:S(2)}, u32[]{:S(2)}) collective-permute-start(bf16[4,96,768]{2,1,0:T(8,128)(2,1)} %constant_dynamic-slice_fusion.21), channel_id=1, source_target_pairs={{0,4},{4,0},{8,12},{12,8},{16,20},{20,16},{24,28},{28,24},{1,5},{5... | collective-permute-start | bytes 1769480 | tf_op jit(solution)/shard_map/ppermute | solution.py:560
  166.5 32.6 %collective-permute-start.53 = (bf16[768,256]{1,0:T(8,128)(2,1)}, bf16[768,256]{1,0:T(8,128)(2,1)}, u32[]{:S(2)}, u32[]{:S(2)}) collective-permute-start(bf16[768,256]{1,0:T(8,128)(2,1)} %constant_dynamic-slice_fusion.15), channel_id=1, source_target_pairs={{0,4},{4,0},{8,12},{12,8},{16,20},{20,16},{24,28},{28,24},{1,5},{5... | collective-permute-start | bytes 1179656 | tf_op jit(solution)/shard_map/ppermute | solution.py:560
  198.1 28.9 %collective-permute-start.44 = (bf16[4,96,768]{2,1,0:T(8,128)(2,1)}, bf16[4,96,768]{2,1,0:T(8,128)(2,1)S(1)}, u32[]{:S(2)}, u32[]{:S(2)}) collective-permute-start(bf16[4,96,768]{2,1,0:T(8,128)(2,1)} %constant_dynamic-slice_fusion.18), channel_id=1, source_target_pairs={{0,4},{4,0},{8,12},{12,8},{16,20},{20,16},{24,28},{28,24},{1,5},{5... | collective-permute-start | bytes 1769480 | tf_op jit(solution)/shard_map/ppermute | solution.py:560
  228.7 41.7 %collective-permute-start.18 = (bf16[4,48,768]{2,1,0:T(8,128)(2,1)S(1)}, bf16[4,48,768]{2,1,0:T(8,128)(2,1)S(1)}, u32[]{:S(2)}, u32[]{:S(2)}) collective-permute-start(bf16[4,48,768]{2,1,0:T(8,128)(2,1)S(1)} %constant_dynamic-slice_fusion.26), channel_id=1, source_target_pairs={{0,8},{4,12},{8,0},{12,4},{16,24},{20,28},{24,16},{28,20},{1,9},{5... | collective-permute-start | bytes 884744 | tf_op jit(solution)/shard_map/ppermute | solution.py:560
  230.7 39.9 %collective-permute-start.27 = (bf16[4,48,768]{2,1,0:T(8,128)(2,1)S(1)}, bf16[4,48,768]{2,1,0:T(8,128)(2,1)S(1)}, u32[]{:S(2)}, u32[]{:S(2)}) collective-permute-start(bf16[4,48,768]{2,1,0:T(8,128)(2,1)S(1)} %constant_dynamic-slice_fusion.23), channel_id=1, source_target_pairs={{0,8},{4,12},{8,0},{12,4},{16,24},{20,28},{24,16},{28,20},{1,9},{5... | collective-permute-start | bytes 884744 | tf_op jit(solution)/shard_map/ppermute | solution.py:560
  231.1 40.1 %collective-permute-start.36 = (bf16[4,48,768]{2,1,0:T(8,128)(2,1)S(1)}, bf16[4,48,768]{2,1,0:T(8,128)(2,1)S(1)}, u32[]{:S(2)}, u32[]{:S(2)}) collective-permute-start(bf16[4,48,768]{2,1,0:T(8,128)(2,1)S(1)} %constant_dynamic-slice_fusion.20), channel_id=1, source_target_pairs={{0,8},{4,12},{8,0},{12,4},{16,24},{20,28},{24,16},{28,20},{1,9},{5... | collective-permute-start | bytes 884744 | tf_op jit(solution)/shard_map/ppermute | solution.py:560
  233.4 22.1 %collective-permute-start.74 = (bf16[192,512]{1,0:T(8,128)(2,1)S(1)}, bf16[192,512]{1,0:T(8,128)(2,1)S(1)}, u32[]{:S(2)}, u32[]{:S(2)}) collective-permute-start(bf16[192,512]{1,0:T(8,128)(2,1)S(1)} %maximum_select_fusion.14), channel_id=1, source_target_pairs={{0,8},{4,12},{8,0},{12,4},{16,24},{20,28},{24,16},{28,20},{1,9},{5... | collective-permute-start | bytes 589832 | tf_op jit(solution)/shard_map/ppermute | solution.py:560
  237.7 22.1 %collective-permute-start.80 = (bf16[192,512]{1,0:T(8,128)(2,1)S(1)}, bf16[192,512]{1,0:T(8,128)(2,1)S(1)}, u32[]{:S(2)}, u32[]{:S(2)}) collective-permute-start(bf16[192,512]{1,0:T(8,128)(2,1)S(1)} %maximum_select_fusion.15), channel_id=1, source_target_pairs={{0,8},{4,12},{8,0},{12,4},{16,24},{20,28},{24,16},{28,20},{1,9},{5... | collective-permute-start | bytes 589832 | tf_op jit(solution)/shard_map/ppermute | solution.py:560
  270.4 73.1 %collective-permute-start.75 = (bf16[384,512]{1,0:T(8,128)(2,1)S(1)}, bf16[384,512]{1,0:T(8,128)(2,1)S(1)}, u32[]{:S(2)}, u32[]{:S(2)}) collective-permute-start(bf16[384,512]{1,0:T(8,128)(2,1)S(1)} %maximum_select_fusion.5), channel_id=1, source_target_pairs={{0,4},{4,0},{8,12},{12,8},{16,20},{20,16},{24,28},{28,24},{1,5},{5... | collective-permute-start | bytes 1179656 | tf_op jit(solution)/shard_map/ppermute | solution.py:560
  270.6 75.0 %collective-permute-start.81 = (bf16[384,512]{1,0:T(8,128)(2,1)S(1)}, bf16[384,512]{1,0:T(8,128)(2,1)S(1)}, u32[]{:S(2)}, u32[]{:S(2)}) collective-permute-start(bf16[384,512]{1,0:T(8,128)(2,1)S(1)} %maximum_select_fusion.6), channel_id=1, source_target_pairs={{0,4},{4,0},{8,12},{12,8},{16,20},{20,16},{24,28},{28,24},{1,5},{5... | collective-permute-start | bytes 1179656 | tf_op jit(solution)/shard_map/ppermute | solution.py:560
  320.3 28.0 %collective-permute-start.87 = (bf16[256,768]{1,0:T(8,128)(2,1)S(1)}, bf16[256,768]{1,0:T(8,128)(2,1)S(1)}, u32[]{:S(2)}, u32[]{:S(2)}) collective-permute-start(bf16[256,768]{1,0:T(8,128)(2,1)S(1)} %maximum_select_fusion.7), channel_id=1, source_target_pairs={{0,4},{4,0},{8,12},{12,8},{16,20},{20,16},{24,28},{28,24},{1,5},{5... | collective-permute-start | bytes 1179656 | tf_op jit(solution)/shard_map/ppermute | solution.py:560
  321.6 33.3 %collective-permute-start.59 = (bf16[384,256]{1,0:T(8,128)(2,1)S(1)}, bf16[384,256]{1,0:T(8,128)(2,1)S(1)}, u32[]{:S(2)}, u32[]{:S(2)}) collective-permute-start(bf16[384,256]{1,0:T(8,128)(2,1)S(1)} %maximum_select_fusion.13), channel_id=1, source_target_pairs={{0,8},{4,12},{8,0},{12,4},{16,24},{20,28},{24,16},{28,20},{1,9},{5... | collective-permute-start | bytes 589832 | tf_op jit(solution)/shard_map/ppermute | solution.py:560
  (98 other events, 670.3 us)
where the time goes:
time: 363 us; the launch traced here: 361 us
  waiting for transfers between devices  133 us (37%)
  starting transfers between devices  90.9 us (25%)
  Pallas kernels  84.6 us (23%)
  local copies, waits for them, and re-layouts  30.6 us (8%)
  other arithmetic  20.7 us (6%)
    ppermute x88, waiting for transfers between devices, exchange(): return lax.ppermute(values, axis, [(i, i ^ distance) for i in range(size)])  133 us
    ppermute x88, starting transfers between devices, exchange(): return lax.ppermute(values, axis, [(i, i ^ distance) for i in range(size)])  90.9 us
    pallas_call x9, Pallas kernels, call(): pl.pallas_call(kernel, out_shape=[jax.ShapeDtypeStruct(s, d) for s, d in...  84.6 us
    dynamic_slice x27, local copies, waits for them, and re-layouts, halve(): sent = lax.dynamic_slice_in_dim(values, (1 - side) * half, half, dim)  11.1 us
    convert_element_type x34, other arithmetic, low(): return values.astype(BF16)  10.4 us
  transfers between devices with their start and end apart: 88, of which 39 were waited for; matrix products, arithmetic and copies ran while one was open for 11% of the time, Pallas kernels for 14%

commit v1 on v0

--- a/solution.py
+++ b/solution.py
@@ -70,23 +70,21 @@
     br_ref,
     w1_ref,
     b1_ref,
-    w2_ref,
+    w2t_ref,
     b2_ref,
     ig_ref,
     ib_ref,
     wo_ref,
     gain2_ref,
-    normed_ref,
+    pair_ref,
     normed_two_ref,
     resid_ref,
-    gated_ref,
     gelu_ref,
     slope_ref,
     qk_ref,
     ecol_ref,
     erow_ref,
     fcol_ref,
-    w2t_ref,
     slope1_ref,
     curve1_ref,
     act_ref,
@@ -121,10 +119,10 @@
     tok = tok_ref[0].astype(F32)
     spread = lax.rsqrt(mean_last(tok * tok) + EPSILON)
     normed = low(tok * spread * gain1_ref[...].astype(F32))
-    normed_ref[...] = normed
+    pair_ref[0] = normed
     seg_row = seg_ref[...].astype(F32)
     live = column_of(live_ref[...].astype(F32))
-    rate_pre = dot(normed, wr_ref[...]) + br_ref[...].astype(F32)
+    rate_pre = dot(normed, wr_ref[...], 1, 1) + br_ref[...].astype(F32)
     sig = jax.nn.sigmoid(rate_pre)
     rates = (BASE_RATE / head) * sig * live
     ecol_ref[...] = jnp.zeros(ecol_ref.shape, F32)
@@ -143,7 +141,6 @@
     for h in range(heads):
         qk_ref[h, 0:length] = low(q_s[h])
         qk_ref[h, length : 2 * length] = low(k_s[h])
-        w2t_ref[h] = low(jnp.transpose(w2_ref[h].astype(F32)))
 
     def step(b, carry):
         here = pl.multiple_of(b * MB, MB)
@@ -242,7 +239,7 @@
     gelu_ref[...] = gate
     slope_ref[...] = inner_out * slope
     gated = low(inner_out * gate)
-    gated_ref[...] = gated
+    pair_ref[1] = gated
     resid = tok + dot(gated, wo_ref[...])
     resid_ref[...] = resid
     spread_two = lax.rsqrt(mean_last(resid * resid) + EPSILON)
@@ -264,14 +261,13 @@
     gx_ref[...] = low(dot(gg, wg_ref[...], 1, 1) + dot(gu, wu_ref[...], 1, 1))
 
 
-def ffn_weights_kernel(parts, *refs):
+def ffn_weights_kernel(parts, ids_smem, *refs):
     x_refs, c_refs, act_refs, gg_refs, gu_refs = (
         refs[i * parts : (i + 1) * parts] for i in range(5)
     )
-    wd_ref = refs[5 * parts]
-    grad_gate_ref, grad_up_ref, grad_down_ref = refs[5 * parts + 1 : 5 * parts + 4]
-    out_refs = refs[5 * parts + 4 : 6 * parts + 4]
-    x_s, c_s, act_s, gg_s, gu_s = refs[6 * parts + 4 :]
+    wd_ref, kept_ref, sent_ref = refs[5 * parts : 5 * parts + 3]
+    out_refs = refs[5 * parts + 3 : 6 * parts + 3]
+    x_s, c_s, act_s, gg_s, gu_s = refs[6 * parts + 3 :]
     rows = x_refs[0].shape[0]
     for i in range(parts):
         at = slice(i * rows, (i + 1) * rows)
@@ -281,17 +277,34 @@
         gg_s[at] = gg_refs[i][...]
         gu_s[at] = gu_refs[i][...]
         out_refs[i][...] = low(dot(act_refs[i][...], wd_ref[...]))
-    grad_gate_ref[...] = low(dot(x_s[...], gg_s[...], 0, 0))
-    grad_up_ref[...] = low(dot(x_s[...], gu_s[...], 0, 0))
-    grad_down_ref[...] = low(dot(act_s[...], c_s[...], 0, 0))
+    half = kept_ref.shape[2]
+    core = ids_smem[0]
+    for i, (left, right) in enumerate(((x_s, gg_s), (x_s, gu_s), (c_s, act_s))):
+        whole = low(dot(left[...], right[...], 0, 0))
+
+        @pl.when(core == 0)
+        def _(whole=whole, i=i):
+            kept_ref[i] = whole[:, 0:half]
+            sent_ref[i] = whole[:, half:]
+
+        @pl.when(core != 0)
+        def _(whole=whole, i=i):
+            kept_ref[i] = whole[:, half:]
+            sent_ref[i] = whole[:, 0:half]
+
+
+def cut_rows_kernel(ids_smem, kept_ref, got_ref, *out_refs):
+    chip = ids_smem[1]
+    rows = out_refs[0].shape[1]
+    for s, out in enumerate(out_refs):
+        at = pl.ds(pl.multiple_of(lax.bitwise_xor(chip, s) * rows, rows), rows)
+        out[...] = low(kept_ref[:, at, :].astype(F32) + got_ref[:, at, :].astype(F32))
 
 
 def between_kernel(parts, *refs):
     pieces = refs[0:parts]
-    resid_ref, cot_ref, gain2_ref, wo_ref, gelu_ref, slope_ref, gated_ref, normed_ref = refs[
-        parts : parts + 8
-    ]
-    resid_grad_ref, go_ref, gg_ref, gwo_ref, gwg_ref, gain_grad_ref = refs[parts + 8 :]
+    resid_ref, cot_ref, gain2_ref, wo_ref, gelu_ref, slope_ref = refs[parts : parts + 6]
+    resid_grad_ref, go_ref, pair_ref, gain_grad_ref = refs[parts + 6 :]
     grad = pieces[0][...].astype(F32)
     for piece in pieces[1:]:
         grad = grad + piece[...].astype(F32)
@@ -308,17 +321,15 @@
     grad_branch = low(grad_resid)
     grad_gated = dot(grad_branch, wo_ref[...], 1, 1)
     go_ref[...] = grad_gated * gelu_ref[...]
-    grad_gates = low(grad_gated * slope_ref[...])
-    gg_ref[...] = grad_gates
-    gwo_ref[...] = low(dot(gated_ref[...], grad_branch, 0, 0))
-    gwg_ref[...] = low(dot(normed_ref[...], grad_gates, 0, 0))
+    pair_ref[0] = low(grad_gated * slope_ref[...])
+    pair_ref[1] = grad_branch
 
 
 def backward_kernel(
+    ids_smem,
     seg_smem,
     seg_ref,
     go_ref,
-    normed_ref,
     qk_ref,
     ecol_ref,
     erow_ref,
@@ -340,12 +351,10 @@
     slopeq_ref,
     nq_ref,
     sq_ref,
-    gq_ref,
-    gk_ref,
-    gv_ref,
+    triple_ref,
     gr_ref,
-    gw_ref,
-    ginner_ref,
+    kept_ref,
+    sent_ref,
     small_ref,
     igf,
     t1_s,
@@ -466,9 +475,11 @@
 
     lax.fori_loop(0, blocks, step, 0)
     small_ref[...] = jnp.zeros(small_ref.shape, F32)
-    per_row = small_ref.shape[1] // inner
+    core = ids_smem[0]
+    pad = small_ref.shape[0] // 2
     for h in range(heads):
         cols = slice(h * head, (h + 1) * head)
+        rows = slice(h * head, (h + 1) * head)
         g = igf[h : h + 1]
         er = erow_ref[h : h + 1, :]
         hh1 = hh1_s[h]
@@ -482,42 +493,82 @@
         share = share_s[h]
         spread = dot(mixq, qk_ref[h, top], 0, 0) + dot(mixk, keys, 0, 0)
         go = go_ref[:, cols]
-        gq_ref[:, cols] = low(go + direct[top] + dot(mixq, keys))
-        gk_ref[:, cols] = low(g * share + direct[bottom] + dot(mixk, keys) + spread)
-        gv_ref[:, cols] = low(-g * share)
-        ginner_ref[h] = low(dot(qk, hh1, 0, 0))
-        ginner_ref[heads + h] = low(
-            dot(hh2, act_ref[h], 0, 0) + dot(low(d2_ref[h]), u_s[h], 0, 0)
-        )
-        row, lane = 14 + h // per_row, (h % per_row) * inner
-        small_ref[row : row + 1, lane : lane + inner] = sum_rows(hh1.astype(F32))
-        row = 14 + heads // per_row
-        small_ref[row : row + 1, cols] = sum_rows(hh2.astype(F32))
-        small_ref[row + 1 : row + 2, cols] = sum_rows(go * nq_ref[h]) + sum_rows(
+        triple_ref[0, :, cols] = low(go + direct[top] + dot(mixq, keys))
+        triple_ref[1, :, cols] = low(g * share + direct[bottom] + dot(mixk, keys) + spread)
+        triple_ref[2, :, cols] = low(-g * share)
+        first = low(dot(qk, hh1, 0, 0))
+        second = low(dot(hh2, act_ref[h], 0, 0) + dot(low(d2_ref[h]), u_s[h], 0, 0))
+
+        @pl.when(core == 0)
+        def _(first=first, second=second, rows=rows):
+            kept_ref[rows] = first
+            sent_ref[rows] = second
+
+        @pl.when(core != 0)
+        def _(first=first, second=second, rows=rows):
+            kept_ref[rows] = second
+            sent_ref[rows] = first
+
+        small_ref[h : h + 1] = sum_rows(hh1.astype(F32))
+        row = slice(pad + h, pad + h + 1)
+        small_ref[row, 0:head] = sum_rows(hh2.astype(F32))
+        small_ref[row, head : 2 * head] = sum_rows(go * nq_ref[h]) + sum_rows(
             share * (fit_ref[h] + g * n_ref[h])
         )
-        small_ref[row + 2 : row + 3, cols] = sum_rows(go) + g * sum_rows(share)
+        small_ref[row, 2 * head : 3 * head] = sum_rows(go) + g * sum_rows(share)
     grad_rates = ge_s[...] * fcol_ref[...]
-    row = 17 + heads // per_row
-    small_ref[row : row + 1, 0 : grad_rates.shape[1]] = sum_rows(grad_rates)
     gr_ref[...] = low(grad_rates)
-    normed = normed_ref[...]
-    small_ref[2 : 2 + heads] = dot(low(grad_rates), normed, 0, 0)[0:heads]
-    for i, ref in enumerate((gq_ref, gk_ref, gv_ref)):
-        gw_ref[i] = low(dot(normed, ref[...], 0, 0))
+    total = jnp.broadcast_to(sum_rows(grad_rates), (grad_rates.shape[1], grad_rates.shape[1]))
+    small_ref[pad : pad + heads, 3 * head : 3 * head + 1] = jnp.transpose(total)[0:heads, 0:1]
+
+
+def put_matrix(to_ref, values, index, count, feats):
+    chips = to_ref.shape[0]
+    rows = values.shape[0] // (feats * chips)
+    chunks = values.shape[1] // 128
+    for f in range(feats):
+        for l in range(chunks):
+            row = ((f * count + index) * chunks + l) * rows
+            for j in range(chips):
+                at = (f * chips + j) * rows
+                to_ref[j, row : row + rows, :] = values[at : at + rows, l * 128 : (l + 1) * 128]
+
+
+def core_columns(core, values):
+    half = values.shape[1] // 2
+    return jnp.where(core == 0, values[:, 0:half], values[:, half:])
+
+
+def gate_weights_kernel(
+    feats, ids_smem, mine_ref, other_ref, grads_ref, other_grads_ref, wg_ref, *refs
+):
+    part_ref = refs[0]
+    pieces_s, left_s, right_s = refs[-3:]
+    outs = refs[1:-3]
+    core, chip = ids_smem[0], ids_smem[1]
+    length = mine_ref.shape[1]
+    for i in range(2):
+        left_s[i, 0:length] = mine_ref[i]
+        left_s[i, length : 2 * length] = other_ref[i]
+        right_s[i, 0:length] = core_columns(core, grads_ref[i])
+        right_s[i, length : 2 * length] = core_columns(core, other_grads_ref[i])
+    for i in range(2):
+        put_matrix(pieces_s, low(dot(left_s[i], right_s[i], 0, 0)), i, 2, feats)
+    for s, out in enumerate(outs):
+        out[...] = pieces_s[lax.bitwise_xor(chip, s)]
+    part_ref[...] = dot(grads_ref[0], wg_ref[...], 1, 1)
 
 
 def input_kernel(
-    gq_ref,
-    gk_ref,
-    gv_ref,
-    gg_ref,
+    feats,
+    triple_ref,
     gr_ref,
+    pair_ref,
     wq_ref,
     wk_ref,
     wv_ref,
-    wg_ref,
     wr_ref,
+    part_ref,
     tok_ref,
     gain1_ref,
     resid_grad_ref,
@@ -526,10 +577,11 @@
     grad_ref,
     small_out,
 ):
-    heads = wr_ref.shape[1]
-    grad = dot(gq_ref[...], wq_ref[...], 1, 1) + dot(gk_ref[...], wk_ref[...], 1, 1)
-    grad = grad + dot(gv_ref[...], wv_ref[...], 1, 1) + dot(gg_ref[...], wg_ref[...], 1, 1)
-    grad = grad + dot(gr_ref[:, 0:heads], wr_ref[...], 1, 1)
+    heads = wr_ref.shape[0]
+    grad = part_ref[...] + dot(triple_ref[0], wq_ref[...], 1, 1)
+    grad = grad + dot(triple_ref[1], wk_ref[...], 1, 1) + dot(triple_ref[2], wv_ref[...], 1, 1)
+    gr = gr_ref[...]
+    grad = grad + dot(gr[:, 0:heads], wr_ref[...])
     tok = tok_ref[0].astype(F32)
     spread = lax.rsqrt(mean_last(tok * tok) + EPSILON)
     scaled = gain1_ref[...].astype(F32) * grad
@@ -538,12 +590,189 @@
         + spread * scaled
         - tok * (spread * spread * spread * mean_last(scaled * tok))
     )
-    small_out[...] = small_ref[...]
-    small_out[0:1] = sum_rows(grad * tok * spread)
-    small_out[1:2] = gain_two_ref[...]
-
-
-def call(kernel, outs, inputs, scratch=(), smem=0):
+    rate_rows = dot(gr, pair_ref[0], 0, 0)
+    gain_row = sum_rows(grad * tok * spread)
+    small_out[...] = jnp.zeros(small_out.shape, BF16)
+    share = tok.shape[1] // feats
+    for f in range(feats):
+        cols = slice(f * share, (f + 1) * share)
+        small_out[f * 16 : f * 16 + 16, 0:share] = low(
+            jnp.concatenate(
+                [rate_rows[0:heads, cols], gain_row[:, cols], gain_two_ref[:, cols]]
+                + [jnp.zeros((14 - heads, share), F32)],
+                0,
+            )
+        )
+    at = feats * 16
+    small_out[at : at + small_ref.shape[0]] = low(small_ref[...])
+
+
+def late_weights_kernel(
+    feats,
+    ids_smem,
+    mine_ref,
+    other_ref,
+    triple_ref,
+    other_triple_ref,
+    kept_ref,
+    got_ref,
+    small_ref,
+    *refs,
+):
+    pieces_s, left_s, right_s = refs[-3:]
+    outs = refs[:-3]
+    core, chip = ids_smem[0], ids_smem[1]
+    length = mine_ref.shape[1]
+    chips = pieces_s.shape[0]
+    left_s[0:length] = mine_ref[0]
+    left_s[length : 2 * length] = other_ref[0]
+    for i in range(3):
+        right_s[i, 0:length] = core_columns(core, triple_ref[i])
+        right_s[i, length : 2 * length] = core_columns(core, other_triple_ref[i])
+    for i in range(3):
+        put_matrix(pieces_s, low(dot(left_s[...], right_s[i], 0, 0)), i, 3, feats)
+    inner = low(kept_ref[...].astype(F32) + got_ref[...].astype(F32))
+    rows = inner.shape[0] // chips
+    extra = small_ref.shape[0] // chips
+    start = pieces_s.shape[1] - 2 * (rows + extra)
+    for j in range(chips):
+        at = start
+        for l in range(2):
+            cols = slice(l * 128, (l + 1) * 128)
+            pieces_s[j, at : at + rows] = inner[j * rows : (j + 1) * rows, cols]
+            at += rows
+            pieces_s[j, at : at + extra] = small_ref[j * extra : (j + 1) * extra, cols]
+            at += extra
+    for s, out in enumerate(outs):
+        out[...] = pieces_s[lax.bitwise_xor(chip, s)]
+
+
+def cut_feat_kernel(parts, ids_smem, *refs):
+    outs = refs[parts:]
+    feat = ids_smem[2]
+    total_rows = refs[0].shape[0]
+    each = outs[0].shape[0]
+    common = (len(outs) * each - total_rows) // (len(outs) - 1)
+    own = each - common
+
+    def total(at):
+        value = refs[0][at].astype(F32)
+        for ref in refs[1:parts]:
+            value = value + ref[at].astype(F32)
+        return low(value)
+
+    for s, out in enumerate(outs):
+        at = pl.ds(pl.multiple_of(lax.bitwise_xor(feat, s) * own, 16), own)
+        out[0:own] = total((at, slice(None)))
+    if common:
+        shared = total((slice(own * len(outs), total_rows), slice(None)))
+        for out in outs:
+            out[own:each] = shared
+
+
+def take_matrices(ids_smem, pieces, outs):
+    core, chip = ids_smem[0], ids_smem[1]
+    count = len(outs)
+    chunks = outs[0].shape[1] // 256
+    rows = outs[0].shape[0] // len(pieces)
+    for s, both in enumerate(pieces):
+        at = pl.ds(pl.multiple_of(lax.bitwise_xor(chip, s) * rows, 16), rows)
+        for i, out in enumerate(outs):
+            for l in range(chunks):
+                row = (i * chunks + l) * rows
+                mine = both[0][row : row + rows, :].astype(F32)
+                other = both[1][row : row + rows, :].astype(F32)
+
+                @pl.when(core == 0)
+                def _(out=out, at=at, l=l, mine=mine, other=other):
+                    out[at, l * 128 : (l + 1) * 128] = mine
+                    out[at, (chunks + l) * 128 : (chunks + l + 1) * 128] = other
+
+                @pl.when(core != 0)
+                def _(out=out, at=at, l=l, mine=mine, other=other):
+                    out[at, l * 128 : (l + 1) * 128] = other
+                    out[at, (chunks + l) * 128 : (chunks + l + 1) * 128] = mine
+
+
+def early_totals_kernel(chips, ids_smem, *refs):
+    ffn = [(refs[s], refs[chips + s]) for s in range(chips)]
+    pair = [(refs[2 * chips + s], refs[3 * chips + s]) for s in range(chips)]
+    gate_ref, up_ref, down_ref, wg_ref, wo_ref, down_s = refs[4 * chips :]
+    core, chip = ids_smem[0], ids_smem[1]
+    half = ffn[0][0].shape[2]
+    rows = ffn[0][0].shape[1]
+    for s, both in enumerate(ffn):
+        at = pl.ds(pl.multiple_of(lax.bitwise_xor(chip, s) * rows, 16), rows)
+        for i, out in enumerate((gate_ref, up_ref, down_s)):
+            mine = both[0][i].astype(F32)
+            other = both[1][i].astype(F32)
+
+            @pl.when(core == 0)
+            def _(out=out, at=at, mine=mine, other=other):
+                out[at, 0:half] = mine
+                out[at, half : 2 * half] = other
+
+            @pl.when(core != 0)
+            def _(out=out, at=at, mine=mine, other=other):
+                out[at, 0:half] = other
+                out[at, half : 2 * half] = mine
+
+    down_ref[...] = jnp.transpose(down_s[...])
+    take_matrices(ids_smem, pair, (wg_ref, wo_ref))
+
+
+def late_totals_kernel(chips, feats, heads, head, ids_smem, *refs):
+    pieces = [(refs[s], refs[chips + s]) for s in range(chips)]
+    (wq_ref, wk_ref, wv_ref, first_ref, second_ref) = refs[2 * chips : 2 * chips + 5]
+    (rate_ref, norm1_ref, norm2_ref, b1_ref, b2_ref, ig_ref, ib_ref, br_ref) = refs[
+        2 * chips + 5 : 2 * chips + 13
+    ]
+    small_s = refs[2 * chips + 13]
+    core, chip, feat = ids_smem[0], ids_smem[1], ids_smem[2]
+    take_matrices(ids_smem, pieces, (wq_ref, wk_ref, wv_ref))
+    rows = first_ref.shape[0] // chips
+    extra = small_s.shape[0] // chips
+    start = refs[0].shape[0] - 2 * (rows + extra)
+    for s, both in enumerate(pieces):
+        place = lax.bitwise_xor(chip, s)
+        at = pl.ds(pl.multiple_of(place * rows, 16), rows)
+        at_small = pl.ds(pl.multiple_of(place * extra, 16), extra)
+        row = start
+        for l in range(2):
+            cols = slice(l * 128, (l + 1) * 128)
+            mine = both[0][row : row + rows].astype(F32)
+            other = both[1][row : row + rows].astype(F32)
+            row += rows
+
+            @pl.when(core == 0)
+            def _(at=at, cols=cols, mine=mine, other=other):
+                first_ref[at, cols] = mine
+                second_ref[at, cols] = other
+
+            @pl.when(core != 0)
+            def _(at=at, cols=cols, mine=mine, other=other):
+                first_ref[at, cols] = other
+                second_ref[at, cols] = mine
+
+            small_s[at_small, cols] = both[0][row : row + extra].astype(F32) + both[1][
+                row : row + extra
+            ].astype(F32)
+            row += extra
+    share = rate_ref.shape[1]
+    block = small_s[pl.ds(pl.multiple_of(feat * 16, 16), 16), :]
+    rate_ref[...] = block[0:heads, 0:share]
+    norm1_ref[...] = block[heads : heads + 1, 0:share]
+    norm2_ref[...] = block[heads + 1 : heads + 2, 0:share]
+    at = feats * 16
+    b1_ref[...] = small_s[at : at + heads, :]
+    packed = small_s[at + 16 : at + 16 + heads, :]
+    b2_ref[...] = packed[:, 0:head]
+    ig_ref[...] = packed[:, head : 2 * head]
+    ib_ref[...] = packed[:, 2 * head : 3 * head]
+    br_ref[...] = packed[:, 3 * head : 3 * head + 1]
+
+
+def call(kernel, outs, inputs, scratch=(), smem=0, us=1.0):
     specs = [pl.BlockSpec(memory_space=pltpu.SMEM)] * smem
     specs += [pl.BlockSpec(memory_space=pltpu.VMEM)] * (len(inputs) - smem)
     return pl.pallas_call(
@@ -552,6 +781,9 @@
         in_specs=specs,
         out_specs=[pl.BlockSpec(memory_space=pltpu.VMEM)] * len(outs),
         scratch_shapes=[pltpu.VMEM(s, d) for s, d in scratch],
+        cost_estimate=pl.CostEstimate(
+            flops=int(us * 1e9), bytes_accessed=int(us * 1e6), transcendentals=0
+        ),
         compiler_params=pltpu.CompilerParams(vmem_limit_bytes=VMEM_BYTES),
     )(*inputs)
 
@@ -589,6 +821,27 @@
         found.append(step)
         step *= 2
     return found
+
+
+def across_chips(values, rows):
+    return [values[0]] + [
+        exchange(values[s], "rows", rows, 2 * s) for s in range(1, len(values))
+    ]
+
+
+def across_feats(values, feats):
+    return [values[0]] + [exchange(values[s], "feat", feats, s) for s in range(1, feats)]
+
+
+def other_core(values, rows):
+    return exchange(values, "rows", rows, 1)
+
+
+def sum_low(values):
+    values = [v.astype(F32) for v in values]
+    while len(values) > 1:
+        values = [values[i] + values[i + 1] for i in range(0, len(values), 2)]
+    return low(values[0])
 
 
 def scatter_rows(values, size, dim):
@@ -642,6 +895,7 @@
     heads, head, inner = inner_w1.shape
     hidden = ffn_gate.shape[1]
     blocks = length // MB
+    chips = rows // 2
     gain_one = norm1_gain[None]
     gain_two = norm2_gain[None]
     line = (length, width)
@@ -650,23 +904,24 @@
     thin = (heads, length, 1)
     square = (heads, length, length)
     state = (heads, head, inner)
-    cots = [cotangent[0]]
-    for s in range(1, feats):
-        cots.append(exchange(cots[0], "feat", feats, s))
+    w2t = jnp.transpose(inner_w2, (0, 2, 1))
+    w_rate_t = jnp.transpose(w_rate)
+    place = lax.axis_index("rows")
+    me = lax.axis_index("feat")
+    ids = jnp.stack([lax.bitwise_and(place, 1), lax.shift_right_logical(place, 1), me])
+    cots = across_feats([cotangent[0]] * feats, feats)
     saved = call(
         forward_kernel,
         [
-            (line, BF16),
+            ((2,) + line, BF16),
             (line, BF16),
             (line, F32),
-            (line, BF16),
             (line, F32),
             (line, F32),
             ((heads, 2 * length, head), BF16),
             ((length, 128), F32),
             ((16, length), F32),
             ((length, 128), F32),
-            (state, BF16),
             (wide, BF16),
             (wide, BF16),
             ((heads, 2 * length, inner), BF16),
@@ -692,11 +947,11 @@
             w_key,
             w_value,
             w_gate,
-            w_rate,
+            w_rate_t,
             b_rate[None],
             inner_w1,
             inner_b1,
-            inner_w2,
+            w2t,
             inner_b2,
             inner_gain,
             inner_bias,
@@ -719,76 +974,40 @@
             ((heads, head), F32),
         ],
         smem=1,
-    )
-    normed, normed_two, resid, gated, gelu_gate, gate_slope = saved[0:6]
-    qk, ecol, erow, fcol, w2t = saved[6:11]
-    rest = saved[11:]
-    blocks_in = [normed_two]
-    for s in range(1, feats):
-        blocks_in.append(exchange(normed_two, "feat", feats, s))
+        us=25,
+    )
+    pair, normed_two, resid, gelu_gate, gate_slope = saved[0:5]
+    qk, ecol, erow, fcol = saved[5:9]
+    rest = saved[9:]
+    blocks_in = across_feats([normed_two] * feats, feats)
     acts, ggs, gus, pieces = [], [], [], []
     for s in range(feats):
         act, gg, gu, gx = call(
             ffn_kernel,
             [((length, hidden), BF16)] * 3 + [(line, BF16)],
             [blocks_in[s], cots[s], ffn_gate, ffn_up, ffn_down],
+            us=3,
         )
         acts.append(act)
         ggs.append(gg)
         gus.append(gu)
         pieces.append(gx if s == 0 else exchange(gx, "feat", feats, s))
-    whole = feats * length
-    ffn_grads = call(
-        partial(ffn_weights_kernel, feats),
-        [((width, hidden), BF16), ((width, hidden), BF16), ((hidden, width), BF16)]
-        + [(line, BF16)] * feats,
-        blocks_in + cots + acts + ggs + gus + [ffn_down],
-        [((whole, width), BF16), ((whole, width), BF16)] + [((whole, hidden), BF16)] * 3,
-    )
-    ffn_out = ffn_grads[3].astype(F32)
-    for s in range(1, feats):
-        ffn_out = ffn_out + exchange(ffn_grads[3 + s], "feat", feats, s).astype(F32)
-    mixed = low(resid + ffn_out)
-    grad_resid, grad_inner_out, grad_gates, grad_w_out, grad_w_gate, grad_gain_two = call(
+    grad_resid, grad_inner_out, grad_pair, grad_gain_two = call(
         partial(between_kernel, feats),
-        [
-            (line, F32),
-            (line, F32),
-            (line, BF16),
-            ((width, width), BF16),
-            ((width, width), BF16),
-            ((1, width), F32),
-        ],
-        pieces
-        + [resid, cotangent, gain_two, w_out, gelu_gate, gate_slope, gated, normed],
-    )
-
-    def shares(values):
-        return values.reshape((feats, width // feats, width))
-
-    def reduced_by_features(values):
-        values = scatter_rows(values, rows, 1)
-        values = scatter_feat(values, feats, 0)
-        return gather_rows(values, rows, 0).astype(F32)
-
-    def reduced_over_rows(values):
-        return gather_rows(scatter_rows(values, rows, 0), rows, 0).astype(F32)
-
-    total_ffn = [reduced_over_rows(x) for x in ffn_grads[0:3]]
-    total_out = reduced_by_features(shares(grad_w_out))
-    total_gate = reduced_by_features(shares(grad_w_gate))
-    gq, gk, gv, gr, gw, ginner, small = call(
+        [(line, F32), (line, F32), ((2,) + line, BF16), ((1, width), F32)],
+        pieces + [resid, cotangent, gain_two, w_out, gelu_gate, gate_slope],
+        us=4,
+    )
+    triple, grad_rates, kept, sent, small = call(
         backward_kernel,
         [
-            (line, BF16),
-            (line, BF16),
-            (line, BF16),
+            ((3,) + line, BF16),
             ((length, 128), BF16),
-            ((3, width, width), BF16),
-            ((2 * heads, head, inner), BF16),
-            ((24, width), F32),
+            ((heads * head, inner), BF16),
+            ((heads * head, inner), BF16),
+            ((32, inner), F32),
         ],
-        [seg_ids, seg_ids, grad_inner_out, normed, qk, ecol, erow, fcol, inner_w1, w2t]
+        [ids, seg_ids, seg_ids, grad_inner_out, qk, ecol, erow, fcol, inner_w1, w2t]
         + [inner_gain]
         + list(rest),
         [
@@ -808,49 +1027,212 @@
             (state, BF16),
             ((heads, 1, head), F32),
         ],
+        smem=2,
+        us=28,
+    )
+    step = 16 * chips
+    small_rows = -(-(16 * feats + 32) // step) * step
+
+    def finish(part):
+        return call(
+            partial(input_kernel, feats),
+            [((1,) + line, F32), ((small_rows, inner), BF16)],
+            [triple, grad_rates, pair, w_query, w_key, w_value, w_rate_t, part]
+            + [tokens, gain_one, grad_resid, small, grad_gain_two],
+            us=4,
+        )
+
+    if (width // feats) % step or hidden % 256 or width % 256:
+        out, grads = plain_totals(
+            rows, feats, blocks_in, cots, acts, ggs, gus, ffn_down, pair, grad_pair, w_gate
+        )
+        grad_tokens, small = finish(grads.pop())
+        late = plain_late_totals(rows, feats, pair, triple, kept, sent, small, state)
+        mixed = low(resid + sum(x.astype(F32) for x in across_feats(out, feats)))
+        return arrange(mixed, grad_tokens, grads, late, state)
+    ffn = call(
+        partial(ffn_weights_kernel, feats),
+        [((3, width, hidden // 2), BF16)] * 2 + [(line, BF16)] * feats,
+        [ids] + blocks_in + cots + acts + ggs + gus + [ffn_down],
+        [((feats * length, width), BF16)] * 2 + [((feats * length, hidden), BF16)] * 3,
         smem=1,
-    )
-    grad_tokens, small = call(
-        input_kernel,
-        [((1,) + line, F32), ((24, width), F32)],
-        [gq, gk, gv, grad_gates, gr, w_query, w_key, w_value, w_gate, w_rate]
-        + [tokens, gain_one, grad_resid, small, grad_gain_two],
-    )
-    totals = [reduced_by_features(shares(gw[i])) for i in range(3)]
-    inner_sum = scatter_rows(ginner.reshape((-1, inner)), rows, 0)
-    for d in distances(feats):
-        inner_sum = add_low(inner_sum, exchange(inner_sum, "feat", feats, d))
-    inner_sum = gather_rows(inner_sum, rows, 0).astype(F32).reshape((2,) + state)
-    for d in distances(rows):
-        small = small + exchange(small, "rows", rows, d)
-    for d in distances(feats):
-        small = small + exchange(small, "feat", feats, d)
-    me = lax.axis_index("feat")
-    mine = lax.dynamic_slice_in_dim(small, me * (width // feats), width // feats, 1)
-    bias_rows = heads * inner // width
-    at = 14 + bias_rows
+        us=6,
+    )
+    out = across_feats(ffn[2:], feats)
+    mixed = low(resid + sum(x.astype(F32) for x in out))
+    ffn_pieces = call(
+        cut_rows_kernel,
+        [((3, width // chips, hidden // 2), BF16)] * chips,
+        [ids, ffn[0], other_core(ffn[1], rows)],
+        smem=1,
+        us=2,
+    )
+    ffn_total = sum_low(across_chips(ffn_pieces, rows))
+    ffn_all = across_chips([ffn_total] * chips, rows)
+    ffn_others = [other_core(x, rows) for x in ffn_all]
+    pair_other = other_core(pair, rows)
+    half = width // 2
+    per = width // (feats * chips) * (half // 128)
+    gate = call(
+        partial(gate_weights_kernel, feats),
+        [(line, F32)] + [((feats * 2 * per, 128), BF16)] * chips,
+        [ids, pair, pair_other, grad_pair, other_core(grad_pair, rows), w_gate],
+        [
+            ((chips, feats * 2 * per, 128), BF16),
+            ((2, 2 * length, width), BF16),
+            ((2, 2 * length, half), BF16),
+        ],
+        smem=1,
+        us=4,
+    )
+    gate_cut = call(
+        partial(cut_feat_kernel, chips),
+        [((2 * per, 128), BF16)] * feats,
+        [ids] + across_chips(gate[1:], rows),
+        smem=1,
+        us=2,
+    )
+    gate_total = sum_low(across_feats(gate_cut, feats))
+    gate_all = across_chips([gate_total] * chips, rows)
+    gate_others = [other_core(x, rows) for x in gate_all]
+    share = (width // feats, width)
+    early = call(
+        partial(early_totals_kernel, chips),
+        [((width, hidden), F32)] * 2 + [((hidden, width), F32)] + [(share, F32)] * 2,
+        [ids] + ffn_all + ffn_others + gate_all + gate_others,
+        [((width, hidden), F32)],
+        smem=1,
+        us=4,
+    )
+    triple_other = other_core(triple, rows)
+    got = other_core(sent, rows)
+    grad_tokens, small = finish(gate[0])
+    tail = 2 * (heads * head + small_rows) // chips
+    late = call(
+        partial(late_weights_kernel, feats),
+        [((feats * 3 * per + tail, 128), BF16)] * chips,
+        [ids, pair, pair_other, triple, triple_other, kept, got, small],
+        [
+            ((chips, feats * 3 * per + tail, 128), BF16),
+            ((2 * length, width), BF16),
+            ((3, 2 * length, half), BF16),
+        ],
+        smem=1,
+        us=4,
+    )
+    late_cut = call(
+        partial(cut_feat_kernel, chips),
+        [((3 * per + tail, 128), BF16)] * feats,
+        [ids] + across_chips(late, rows),
+        smem=1,
+        us=2,
+    )
+    late_total = sum_low(across_feats(late_cut, feats))
+    late_all = across_chips([late_total] * chips, rows)
+    late_others = [other_core(x, rows) for x in late_all]
+    late = call(
+        partial(late_totals_kernel, chips, feats, heads, head),
+        [(share, F32)] * 3
+        + [((heads * head, inner), F32)] * 2
+        + [((heads, width // feats), F32)]
+        + [((1, width // feats), F32)] * 2
+        + [((heads, inner), F32)]
+        + [((heads, head), F32)] * 3
+        + [((heads, 1), F32)],
+        [ids] + late_all + late_others,
+        [((small_rows, inner), F32)],
+        smem=1,
+        us=4,
+    )
+    return arrange(mixed, grad_tokens, early, late, state)
+
+
+def arrange(mixed, grad_tokens, early, late, state):
     return (
         mixed[None],
         grad_tokens,
-        mine[0],
-        totals[0],
-        totals[1],
-        totals[2],
-        total_gate,
-        jnp.transpose(mine[2 : 2 + heads]),
-        small[at + 3, 0:heads],
-        inner_sum[0],
-        small[14:at].reshape((heads, inner)),
-        jnp.transpose(inner_sum[1], (0, 2, 1)),
-        small[at].reshape((heads, head)),
-        small[at + 1].reshape((heads, head)),
-        small[at + 2].reshape((heads, head)),
-        total_out,
-        mine[1],
-        total_ffn[0],
-        total_ffn[1],
-        total_ffn[2],
-    )
+        late[6][0],
+        late[0],
+        late[1],
+        late[2],
+        early[3],
+        jnp.transpose(late[5]),
+        late[12][:, 0],
+        late[3].reshape(state),
+        late[8],
+        jnp.transpose(late[4].reshape(state), (0, 2, 1)),
+        late[9],
+        late[10],
+        late[11],
+        early[4],
+        late[7][0],
+        early[0],
+        early[1],
+        early[2],
+    )
+
+
+def contract(left, right):
+    return low(dot(left, right, 0, 0))
+
+
+def plain_features(values, rows, feats):
+    width = values.shape[0]
+    values = values.reshape((feats, width // feats, width))
+    values = scatter_feat(scatter_rows(values, rows, 1), feats, 0)
+    return gather_rows(values, rows, 0).astype(F32)
+
+
+def plain_totals(
+    rows, feats, blocks_in, cots, acts, ggs, gus, ffn_down, pair, grad_pair, w_gate
+):
+    def joined(parts):
+        return jnp.concatenate(parts, 0)
+
+    def over_rows(values):
+        return gather_rows(scatter_rows(values, rows, 0), rows, 0).astype(F32)
+
+    x, c, act = joined(blocks_in), joined(cots), joined(acts)
+    out = [low(dot(a, ffn_down)) for a in acts]
+    grads = [contract(x, joined(ggs)), contract(x, joined(gus)), contract(act, c)]
+    grads = [over_rows(g) for g in grads]
+    for i in range(2):
+        grads.append(plain_features(contract(pair[i], grad_pair[i]), rows, feats))
+    grads.append(dot(grad_pair[0], w_gate, 1, 1))
+    return out, grads
+
+
+def plain_late_totals(rows, feats, pair, triple, kept, sent, small, state):
+    heads, head, _ = state
+    me = lax.axis_index("feat")
+    core = lax.bitwise_and(lax.axis_index("rows"), 1)
+    late = [plain_features(contract(pair[0], triple[i]), rows, feats) for i in range(3)]
+    both = jnp.where(core == 0, jnp.stack([kept, sent]), jnp.stack([sent, kept]))
+    both = scatter_rows(both, rows, 1)
+    for d in distances(feats):
+        both = add_low(both, exchange(both, "feat", feats, d))
+    both = gather_rows(both, rows, 1).astype(F32)
+    for d in distances(rows):
+        small = add_low(small, exchange(small, "rows", rows, d))
+    for d in distances(feats):
+        small = add_low(small, exchange(small, "feat", feats, d))
+    small = small.astype(F32)
+    share = pair.shape[2] // feats
+    block = lax.dynamic_slice_in_dim(small, me * 16, 16, 0)[:, 0:share]
+    at = feats * 16
+    packed = small[at + 16 : at + 16 + heads]
+    return late + [
+        both[0],
+        both[1],
+        block[0:heads],
+        block[heads : heads + 1],
+        block[heads + 1 : heads + 2],
+        small[at : at + heads],
+        packed[:, 0:head],
+        packed[:, head : 2 * head],
+        packed[:, 2 * head : 3 * head],
+        packed[:, 3 * head : 3 * head + 1],
+    ]
 
 
 def solution(mesh):

time: 363 us -> 226 us (0.62)
  waiting for transfers between devices: 133 us -> 44.9 us
  starting transfers between devices: 90.9 us -> 57.6 us
  Pallas kernels: 84.6 us -> 107 us
  local copies, waits for them, and re-layouts: 30.6 us -> 10.1 us
  other arithmetic: 20.7 us -> 3.08 us
    ppermute x88 -> x53, waiting for transfers between devices: 133 us -> 44.9 us  [exchange(): return lax.ppermute(values, axis, [(i, i ^ distance) for i in range(size)])]
    ppermute x88 -> x53, starting transfers between devices: 90.9 us -> 57.6 us  [exchange(): return lax.ppermute(values, axis, [(i, i ^ distance) for i in range(size)])]
    pallas_call x9 -> x16, Pallas kernels: 84.6 us -> 107 us  [call(): pl.pallas_call(kernel, out_shape=[jax.ShapeDtypeStruct(s, d) for s, d in...]
    dynamic_slice x27 -> x0, local copies, waits for them, and re-layouts: 11.1 us -> none  [halve(): sent = lax.dynamic_slice_in_dim(values, (1 - side) * half, half, dim)]
    convert_element_type x34 -> x3, other arithmetic: 10.4 us -> 0.31 us  [low(): return values.astype(BF16)]
    convert_element_type x9 -> x0, other arithmetic: 8.62 us -> none  [the longest x5 4.29 us: reduced_by_features(): return gather_rows(values, rows, 0).astype(F32)]
    slice x5 -> x0, local copies, waits for them, and re-layouts: 4.72 us -> none  [the longest x1 2.21 us: on_device(): totals = [reduced_by_features(shares(gw[i])) for i in range(3)]]
    unnamed x70 -> x110, local copies, waits for them, and re-layouts: 6.82 us -> 7.6 us
  transfers between devices with their start and end apart: 88 -> 53, of which waited for: 39 -> 12; matrix products, arithmetic and copies ran while one was open for 11% -> 3% of each run, Pallas kernels for 14% -> 45%
where the time goes in v1:
time: 226 us; the launch traced here: 223 us
  Pallas kernels  107 us (47%)
  starting transfers between devices  57.6 us (25%)
  waiting for transfers between devices  44.9 us (20%)
  local copies, waits for them, and re-layouts  10.1 us (4%)
  other arithmetic  3.08 us (1%)
    pallas_call x16, Pallas kernels, call(): pl.pallas_call(kernel, out_shape=[jax.ShapeDtypeStruct(s, d) for s, d in...  107 us
    ppermute x53, starting transfers between devices, exchange(): return lax.ppermute(values, axis, [(i, i ^ distance) for i in range(size)])  57.6 us
    ppermute x53, waiting for transfers between devices, exchange(): return lax.ppermute(values, axis, [(i, i ^ distance) for i in range(size)])  44.9 us
    unnamed x110, local copies, waits for them, and re-layouts  7.6 us
  transfers between devices with their start and end apart: 53, of which 12 were waited for; matrix products, arithmetic and copies ran while one was open for 3% of the time, Pallas kernels for 45%

profile of v1, /device:TPU:0, one launch (start us, length us, event | category | flops | bytes accessed | tf_op | source)
XLA Modules:
  0.0 223.3 jit_solution(18298804277158734291)
XLA Ops:
  0.7 5.1 %collective-permute-start.5 = (bf16[128,768]{1,0:T(8,128)(2,1)}, bf16[128,768]{1,0:T(8,128)(2,1)S(1)}, u32[]{:S(2)}, u32[]{:S(2)}) collective-permute-start(bf16[128,768]{1,0:T(8,128)(2,1)} %bitcast.18), channel_id=1, source_target_pairs={{0,3},{1,2},{2,1},{3,0},{4,7},{5,6},{6,5},{7,4},{8,11},{9,10},{10,... | collective-permute-start | bytes 589832 | tf_op jit(solution)/shard_map/ppermute | solution.py:792
  8.9 23.8 %shard_map.365 = (bf16[2,128,768]{2,1,0:T(8,128)(2,1)}, bf16[128,768]{1,0:T(8,128)(2,1)}, f32[128,768]{1,0:T(8,128)}, f32[128,768]{1,0:T(8,128)}, f32[128,768]{1...) custom-call(s32[1,128]{1,0:T(1,128)} %seg_ref.3, ...), custom_call_target="tpu_custom_call" | custom-call | flops 24999999488 | bytes 25000000 | tf_op jit(solution)/shard_map/pallas_call | solution.py:778
  32.7 3.4 %collective-permute-start.2 = (bf16[128,768]{1,0:T(8,128)(2,1)}, bf16[128,768]{1,0:T(8,128)(2,1)S(1)}, u32[]{:S(2)}, u32[]{:S(2)}) collective-permute-start(bf16[128,768]{1,0:T(8,128)(2,1)} %get-tuple-element.116.x_ref.refs_0_), channel_id=1, source_target_pairs={{0,3},{1,2},{2,1},{3,0},{4,7},{5,6},{6,5},{7,4},{8,11},{9,10},{10,... | collective-permute-start | bytes 589832 | tf_op jit(solution)/shard_map/ppermute | solution.py:792
  36.2 3.8 %shard_map.366 = (bf16[128,512]{1,0:T(8,128)(2,1)}, bf16[128,512]{1,0:T(8,128)(2,1)}, bf16[128,512]{1,0:T(8,128)(2,1)}, bf16[128,768]{1,0:T(8,128)(2,1)}) custom-call(bf16[128,768]{1,0:T(8,128)(2,1)} %get-tuple-element.116.x_ref.refs_0_, bf16[128,768]{1,0:T(8,128)(2,1)} %bitcast.21, bf16[768,512]{1,0:T(8,128)(2,1)} %wg_ref.10, bf16[768,512]{1,0:T(8,128)(2,1)} %wu_ref.7, ...), custom_call_target="tpu_custom_call" | custom-call | flops 3000000000 | bytes 3000000 | tf_op jit(solution)/shard_map/pallas_call | solution.py:778
  41.6 4.6 %collective-permute-done.x_ref.refs_1_ = bf16[128,768]{1,0:T(8,128)(2,1)S(1)} collective-permute-done((bf16[128,768]{1,0:T(8,128)(2,1)}, bf16[128,768]{1,0:T(8,128)(2,1)S(1)}, u32[]{:S(2)}, u32[]{:S(2)}) %collective-permute-start) | collective-permute-done | bytes 196640 | tf_op jit(solution)/shard_map/ppermute | solution.py:792
  46.9 3.8 %shard_map.367 = (bf16[128,512]{1,0:T(8,128)(2,1)}, bf16[128,512]{1,0:T(8,128)(2,1)}, bf16[128,512]{1,0:T(8,128)(2,1)}, bf16[128,768]{1,0:T(8,128)(2,1)}) custom-call(bf16[128,768]{1,0:T(8,128)(2,1)} %copy-done.43, bf16[128,768]{1,0:T(8,128)(2,1)} %copy-done.40, bf16[768,512]{1,0:T(8,128)(2,1)} %wg_ref.10, bf16[768,512]{1,0:T(8,128)(2,1)} %wu_ref.7, ...), custom_call_target="tpu_custom_call" | custom-call | flops 3000000000 | bytes 3000000 | tf_op jit(solution)/shard_map/pallas_call | solution.py:778
  53.6 3.8 %shard_map.368 = (bf16[128,512]{1,0:T(8,128)(2,1)}, bf16[128,512]{1,0:T(8,128)(2,1)}, bf16[128,512]{1,0:T(8,128)(2,1)}, bf16[128,768]{1,0:T(8,128)(2,1)}) custom-call(bf16[128,768]{1,0:T(8,128)(2,1)} %copy-done.46, bf16[128,768]{1,0:T(8,128)(2,1)} %copy-done.39, bf16[768,512]{1,0:T(8,128)(2,1)} %wg_ref.10, bf16[768,512]{1,0:T(8,128)(2,1)} %wu_ref.7, ...), custom_call_target="tpu_custom_call" | custom-call | flops 3000000000 | bytes 3000000 | tf_op jit(solution)/shard_map/pallas_call | solution.py:778
  58.8 3.8 %shard_map.369 = (bf16[128,512]{1,0:T(8,128)(2,1)}, bf16[128,512]{1,0:T(8,128)(2,1)}, bf16[128,512]{1,0:T(8,128)(2,1)}, bf16[128,768]{1,0:T(8,128)(2,1)}) custom-call(bf16[128,768]{1,0:T(8,128)(2,1)} %copy-done.42, bf16[128,768]{1,0:T(8,128)(2,1)} %copy-done.38, bf16[768,512]{1,0:T(8,128)(2,1)} %wg_ref.10, bf16[768,512]{1,0:T(8,128)(2,1)} %wu_ref.7, ...), custom_call_target="tpu_custom_call" | custom-call | flops 3000000000 | bytes 3000000 | tf_op jit(solution)/shard_map/pallas_call | solution.py:778
  62.5 2.9 %collective-permute-start.11 = (bf16[128,768]{1,0:T(8,128)(2,1)}, bf16[128,768]{1,0:T(8,128)(2,1)S(1)}, u32[]{:S(2)}, u32[]{:S(2)}) collective-permute-start(bf16[128,768]{1,0:T(8,128)(2,1)} %get-tuple-element.136), channel_id=1, source_target_pairs={{0,3},{1,2},{2,1},{3,0},{4,7},{5,6},{6,5},{7,4},{8,11},{9,10},{10,... | collective-permute-start | bytes 589832 | tf_op jit(solution)/shard_map/ppermute | solution.py:792
  65.5 6.6 %shard_map.370 = (bf16[3,768,256]{2,1,0:T(8,128)(2,1)}, bf16[3,768,256]{2,1,0:T(8,128)(2,1)}, bf16[128,768]{1,0:T(8,128)(2,1)}, bf16[128,768]{1,0:T(8,128)(2,1)}...) custom-call(s32[3]{0:T(128)} %pad_add_fusion.ids_smem, bf16[128,768]{1,0:T(8,128)(2,1)} %get-tuple-element.116.x_ref.refs_0_, ...), custom_call_target="tpu_custom_call" | custom-call | flops 6000000000 | bytes 6000000 | tf_op jit(solution)/shard_map/pallas_call | solution.py:778
  74.5 3.6 %shard_map.371 = (f32[128,768]{1,0:T(8,128)}, f32[128,768]{1,0:T(8,128)}, bf16[2,128,768]{2,1,0:T(8,128)(2,1)}, f32[1,768]{1,0:T(1,128)}) custom-call(bf16[128,768]{1,0:T(8,128)(2,1)} %get-tuple-element.133.refs_0_, bf16[128,768]{1,0:T(8,128)(2,1)} %copy-done.44, bf16[128,768]{1,0:T(8,128)(2,1)} %copy-done.45, bf16[128,768]{1,0:T(8,128)(2,1)} %copy-done.47, ...), custom_call_target="tpu_custom_call" | custom-call | flops 4000000000 | bytes 4000000 | tf_op jit(solution)/shard_map/pallas_call | solution.py:778
  78.1 28.1 %shard_map.372 = (bf16[3,128,768]{2,1,0:T(8,128)(2,1)}, bf16[128,128]{1,0:T(8,128)(2,1)}, bf16[768,256]{1,0:T(8,128)(2,1)}, bf16[768,256]{1,0:T(8,128)(2,1)}, f32[32,256]{1,0:T(8,128)}) custom-call(s32[3]{0:T(128)} %pad_add_fusion.ids_smem, s32[1,128]{1,0:T(1,128)} %seg_ref.3, s32[1,128]{1,0:T(1,128)} %seg_ref.3, f32[128,768]{1,0:T(8,128)} %get-tuple-element.139.go_ref, ...), custom_call_target="tpu_custom_call" | custom-call | flops 28000000000 | bytes 28000000 | tf_op jit(solution)/shard_map/pallas_call | solution.py:778
  107.9 3.8 %shard_map.373 = (f32[128,768]{1,0:T(8,128)}, bf16[1152,128]{1,0:T(8,128)(2,1)}, bf16[1152,128]{1,0:T(8,128)(2,1)}, bf16[1152,128]{1,0:T(8,128)(2,1)}, bf16[1152,128]{1,0:T(8,128)(2,1)}) custom-call(s32[3]{0:T(128)} %pad_add_fusion.ids_smem, bf16[2,128,768]{2,1,0:T(8,128)(2,1)} %get-tuple-element.160.mine_ref.pair_ref, bf16[2,128,768]{2,1,0:T(8,128)(2,1)} %copy-done.14, ...), custom_call_target="tpu_custom_call" | custom-call | flops 4000000000 | bytes 4000000 | tf_op jit(solution)/shard_map/pallas_call | solution.py:778
  114.5 4.9 %shard_map.374 = (f32[1,128,768]{2,1,0:T(8,128)}, bf16[128,256]{1,0:T(8,128)(2,1)}) custom-call(bf16[3,128,768]{2,1,0:T(8,128)(2,1)} %get-tuple-element.158.triple_ref, bf16[128,128]{1,0:T(8,128)(2,1)} %get-tuple-element.159.gr_ref, bf16[2,128,768]{2,1,0:T(8,128)(2,1)} %get-tuple-element.160.mine_ref.pair_ref, bf16[768,768]{1,0:T(8,128)(2,1)} %wq_ref.3, ...), custom_call_target="tpu_custom_call" | custom-call | flops 4000000000 | bytes 4000000 | tf_op jit(solution)/shard_map/pallas_call | solution.py:778
  121.0 4.1 %shard_map.375 = (bf16[2176,128]{1,0:T(8,128)(2,1)}, bf16[2176,128]{1,0:T(8,128)(2,1)}, bf16[2176,128]{1,0:T(8,128)(2,1)}, bf16[2176,128]{1,0:T(8,128)(2,1)}) custom-call(s32[3]{0:T(128)} %pad_add_fusion.ids_smem, bf16[2,128,768]{2,1,0:T(8,128)(2,1)} %get-tuple-element.160.mine_ref.pair_ref, bf16[2,128,768]{2,1,0:T(8,128)(2,1)} %copy-done.14, ...), custom_call_target="tpu_custom_call" | custom-call | flops 4000000000 | bytes 4000000 | tf_op jit(solution)/shard_map/pallas_call | solution.py:778
  127.6 8.1 %collective-permute-done.41.refs_2_ = bf16[1152,128]{1,0:T(8,128)(2,1)S(1)} collective-permute-done((bf16[1152,128]{1,0:T(8,128)(2,1)S(1)}, bf16[1152,128]{1,0:T(8,128)(2,1)S(1)}, u32[]{:S(2)}, u32[]{:S(2)}) %collective-permute-start.41) | collective-permute-done | bytes 294944 | tf_op jit(solution)/shard_map/ppermute | solution.py:792
  135.7 3.0 %collective-permute-start.7 = (bf16[128,768]{1,0:T(8,128)(2,1)S(1)}, bf16[128,768]{1,0:T(8,128)(2,1)S(1)}, u32[]{:S(2)}, u32[]{:S(2)}) collective-permute-start(bf16[128,768]{1,0:T(8,128)(2,1)S(1)} %copy-done.37), channel_id=1, source_target_pairs={{0,2},{1,3},{2,0},{3,1},{4,6},{5,7},{6,4},{7,5},{8,10},{9,11},{10,... | collective-permute-start | bytes 589832 | tf_op jit(solution)/shard_map/ppermute | solution.py:792
  141.8 4.2 %collective-permute-done.7 = bf16[128,768]{1,0:T(8,128)(2,1)S(1)} collective-permute-done((bf16[128,768]{1,0:T(8,128)(2,1)S(1)}, bf16[128,768]{1,0:T(8,128)(2,1)S(1)}, u32[]{:S(2)}, u32[]{:S(2)}) %collective-permute-start.7) | collective-permute-done | bytes 196640 | tf_op jit(solution)/shard_map/ppermute | solution.py:792
  146.0 5.4 %collective-permute-done.43 = bf16[288,128]{1,0:T(8,128)(2,1)S(1)} collective-permute-done((bf16[288,128]{1,0:T(8,128)(2,1)}, bf16[288,128]{1,0:T(8,128)(2,1)S(1)}, u32[]{:S(2)}, u32[]{:S(2)}) %collective-permute-start.43) | collective-permute-done | bytes 73760 | tf_op jit(solution)/shard_map/ppermute | solution.py:792
  153.4 2.9 %shard_map.378 = (bf16[3,192,256]{2,1,0:T(8,128)(2,1)}, bf16[3,192,256]{2,1,0:T(8,128)(2,1)}, bf16[3,192,256]{2,1,0:T(8,128)(2,1)}, bf16[3,192,256]{2,1,0:T(8,128)(2,1)}) custom-call(s32[3]{0:T(128)} %pad_add_fusion.ids_smem, bf16[3,768,256]{2,1,0:T(8,128)(2,1)} %get-tuple-element.182.kept_ref, bf16[3,768,256]{2,1,0:T(8,128)(2,1)} %copy-done.8), custom_call_target="tpu_custom_call" | custom-call | flops 2000000000 | bytes 2000000 | tf_op jit(solution)/shard_map/pallas_call | solution.py:778
  180.1 10.3 %collective-permute-done.20 = bf16[880,128]{1,0:T(8,128)(2,1)S(1)} collective-permute-done((bf16[880,128]{1,0:T(8,128)(2,1)}, bf16[880,128]{1,0:T(8,128)(2,1)S(1)}, u32[]{:S(2)}, u32[]{:S(2)}) %collective-permute-start.20) | collective-permute-done | bytes 225312 | tf_op jit(solution)/shard_map/ppermute | solution.py:792
  197.6 3.7 %collective-permute-done.35.refs_3_ = bf16[3,192,256]{2,1,0:T(8,128)(2,1)S(1)} collective-permute-done((bf16[3,192,256]{2,1,0:T(8,128)(2,1)S(1)}, bf16[3,192,256]{2,1,0:T(8,128)(2,1)S(1)}, u32[]{:S(2)}, u32[]{:S(2)}) %collective-permute-start.35) | collective-permute-done | bytes 294944 | tf_op jit(solution)/shard_map/ppermute | solution.py:792
  211.1 3.8 %shard_map.377 = (f32[192,768]{1,0:T(8,128)}, f32[192,768]{1,0:T(8,128)}, f32[192,768]{1,0:T(8,128)}, f32[768,256]{1,0:T(8,128)}, f32[768,256]{1,0:T(8,128)}, /*...) custom-call(s32[3]{0:T(128)} %pad_add_fusion.ids_smem, ...), custom_call_target="tpu_custom_call" | custom-call | flops 4000000000 | bytes 4000000 | tf_op jit(solution)/shard_map/pallas_call | solution.py:778
  217.9 5.4 %shard_map.380 = (f32[768,512]{1,0:T(8,128)}, f32[768,512]{1,0:T(8,128)}, f32[512,768]{1,0:T(8,128)}, f32[192,768]{1,0:T(8,128)}, f32[192,768]{1,0:T(8,128)}) custom-call(s32[3]{0:T(128)} %pad_add_fusion.ids_smem, bf16[3,192,256]{2,1,0:T(8,128)(2,1)} %copy-done.1, bf16[3,192,256]{2,1,0:T(8,128)(2,1)} %copy-done.19, bf16[3,192,256]{2,1,0:T(8,128)(2,1)} %copy-done.18, ...), custom_call_target="tpu_custom_call" | custom-call | flops 4000000000 | bytes 4000000 | tf_op jit(solution)/shard_map/pallas_call | solution.py:778
  (216 shorter events, 69.6 us)
Async XLA Ops:
  0.7 56.8 %collective-permute-start.5 = (bf16[128,768]{1,0:T(8,128)(2,1)}, bf16[128,768]{1,0:T(8,128)(2,1)S(1)}, u32[]{:S(2)}, u32[]{:S(2)}) collective-permute-start(bf16[128,768]{1,0:T(8,128)(2,1)} %bitcast.18), channel_id=1, source_target_pairs={{0,3},{1,2},{2,1},{3,0},{4,7},{5,6},{6,5},{7,4},{8,11},{9,10},{10,... | collective-permute-start | bytes 589832 | tf_op jit(solution)/shard_map/ppermute | solution.py:792
  5.8 44.9 %collective-permute-start.4 = (bf16[128,768]{1,0:T(8,128)(2,1)}, bf16[128,768]{1,0:T(8,128)(2,1)S(1)}, u32[]{:S(2)}, u32[]{:S(2)}) collective-permute-start(bf16[128,768]{1,0:T(8,128)(2,1)} %bitcast.19), channel_id=1, source_target_pairs={{0,2},{1,3},{2,0},{3,1},{4,6},{5,7},{6,4},{7,5},{8,10},{9,11},{10,... | collective-permute-start | bytes 589832 | tf_op jit(solution)/shard_map/ppermute | solution.py:792
  5.8 34.8 %collective-permute-start.3 = (bf16[128,768]{1,0:T(8,128)(2,1)}, bf16[128,768]{1,0:T(8,128)(2,1)S(1)}, u32[]{:S(2)}, u32[]{:S(2)}) collective-permute-start(bf16[128,768]{1,0:T(8,128)(2,1)} %bitcast.20), channel_id=1, source_target_pairs={{0,1},{1,0},{2,3},{3,2},{4,5},{5,4},{6,7},{7,6},{8,9},{9,8},{10,11... | collective-permute-start | bytes 589832 | tf_op jit(solution)/shard_map/ppermute | solution.py:792
  32.7 24.7 %collective-permute-start.2 = (bf16[128,768]{1,0:T(8,128)(2,1)}, bf16[128,768]{1,0:T(8,128)(2,1)S(1)}, u32[]{:S(2)}, u32[]{:S(2)}) collective-permute-start(bf16[128,768]{1,0:T(8,128)(2,1)} %get-tuple-element.116.x_ref.refs_0_), channel_id=1, source_target_pairs={{0,3},{1,2},{2,1},{3,0},{4,7},{5,6},{6,5},{7,4},{8,11},{9,10},{10,... | collective-permute-start | bytes 589832 | tf_op jit(solution)/shard_map/ppermute | solution.py:792
  46.2 60.2 %collective-permute-start.12 = (bf16[2,128,768]{2,1,0:T(8,128)(2,1)S(1)}, bf16[2,128,768]{2,1,0:T(8,128)(2,1)S(1)}, u32[]{:S(2)}, u32[]{:S(2)}) collective-permute-start(bf16[2,128,768]{2,1,0:T(8,128)(2,1)S(1)} %copy-done.13), channel_id=1, source_target_pairs={{0,4},{4,0},{8,12},{12,8},{16,20},{20,16},{24,28},{28,24},{1,5},{5... | collective-permute-start | bytes 1179656 | tf_op jit(solution)/shard_map/ppermute | solution.py:792
  50.7 21.9 %collective-permute-start.9 = (bf16[128,768]{1,0:T(8,128)(2,1)}, bf16[128,768]{1,0:T(8,128)(2,1)S(1)}, u32[]{:S(2)}, u32[]{:S(2)}) collective-permute-start(bf16[128,768]{1,0:T(8,128)(2,1)} %get-tuple-element.134), channel_id=1, source_target_pairs={{0,1},{1,0},{2,3},{3,2},{4,5},{5,4},{6,7},{7,6},{8,9},{9,8},{10,11... | collective-permute-start | bytes 589832 | tf_op jit(solution)/shard_map/ppermute | solution.py:792
  57.4 16.4 %collective-permute-start.10 = (bf16[128,768]{1,0:T(8,128)(2,1)}, bf16[128,768]{1,0:T(8,128)(2,1)S(1)}, u32[]{:S(2)}, u32[]{:S(2)}) collective-permute-start(bf16[128,768]{1,0:T(8,128)(2,1)} %get-tuple-element.135), channel_id=1, source_target_pairs={{0,2},{1,3},{2,0},{3,1},{4,6},{5,7},{6,4},{7,5},{8,10},{9,11},{10,... | collective-permute-start | bytes 589832 | tf_op jit(solution)/shard_map/ppermute | solution.py:792
  72.0 53.1 %collective-permute-start.6 = (bf16[128,768]{1,0:T(8,128)(2,1)}, bf16[128,768]{1,0:T(8,128)(2,1)S(1)}, u32[]{:S(2)}, u32[]{:S(2)}) collective-permute-start(bf16[128,768]{1,0:T(8,128)(2,1)} %get-tuple-element.130), channel_id=1, source_target_pairs={{0,1},{1,0},{2,3},{3,2},{4,5},{5,4},{6,7},{7,6},{8,9},{9,8},{10,11... | collective-permute-start | bytes 589832 | tf_op jit(solution)/shard_map/ppermute | solution.py:792
  72.6 78.7 %collective-permute-start.29 = (bf16[3,768,256]{2,1,0:T(8,128)(2,1)}, bf16[3,768,256]{2,1,0:T(8,128)(2,1)S(1)}, u32[]{:S(2)}, u32[]{:S(2)}) collective-permute-start(bf16[3,768,256]{2,1,0:T(8,128)(2,1)} %get-tuple-element.183), channel_id=1, source_target_pairs={{0,4},{4,0},{8,12},{12,8},{16,20},{20,16},{24,28},{28,24},{1,5},{5... | collective-permute-start | bytes 3538952 | tf_op jit(solution)/shard_map/ppermute | solution.py:792
  78.1 28.7 %collective-permute-start.13 = (bf16[2,128,768]{2,1,0:T(8,128)(2,1)}, bf16[2,128,768]{2,1,0:T(8,128)(2,1)S(1)}, u32[]{:S(2)}, u32[]{:S(2)}) collective-permute-start(bf16[2,128,768]{2,1,0:T(8,128)(2,1)} %get-tuple-element.161.grads_ref), channel_id=1, source_target_pairs={{0,4},{4,0},{8,12},{12,8},{16,20},{20,16},{24,28},{28,24},{1,5},{5... | collective-permute-start | bytes 1179656 | tf_op jit(solution)/shard_map/ppermute | solution.py:792
  106.2 13.2 %collective-permute-start.15 = (bf16[768,256]{1,0:T(8,128)(2,1)}, bf16[768,256]{1,0:T(8,128)(2,1)S(1)}, u32[]{:S(2)}, u32[]{:S(2)}) collective-permute-start(bf16[768,256]{1,0:T(8,128)(2,1)} %get-tuple-element.168), channel_id=1, source_target_pairs={{0,4},{4,0},{8,12},{12,8},{16,20},{20,16},{24,28},{28,24},{1,5},{5... | collective-permute-start | bytes 1179656 | tf_op jit(solution)/shard_map/ppermute | solution.py:792
  106.4 13.5 %collective-permute-start.14 = (bf16[3,128,768]{2,1,0:T(8,128)(2,1)}, bf16[3,128,768]{2,1,0:T(8,128)(2,1)S(1)}, u32[]{:S(2)}, u32[]{:S(2)}) collective-permute-start(bf16[3,128,768]{2,1,0:T(8,128)(2,1)} %get-tuple-element.158.triple_ref), channel_id=1, source_target_pairs={{0,4},{4,0},{8,12},{12,8},{16,20},{20,16},{24,28},{28,24},{1,5},{5... | collective-permute-start | bytes 1769480 | tf_op jit(solution)/shard_map/ppermute | solution.py:792
  111.7 15.4 %collective-permute-start.40 = (bf16[1152,128]{1,0:T(8,128)(2,1)}, bf16[1152,128]{1,0:T(8,128)(2,1)S(1)}, u32[]{:S(2)}, u32[]{:S(2)}) collective-permute-start(bf16[1152,128]{1,0:T(8,128)(2,1)} %get-tuple-element.189), channel_id=1, source_target_pairs={{0,8},{4,12},{8,0},{12,4},{16,24},{20,28},{24,16},{28,20},{1,9},{5... | collective-permute-start | bytes 884744 | tf_op jit(solution)/shard_map/ppermute | solution.py:792
  119.4 16.3 %collective-permute-start.41 = (bf16[1152,128]{1,0:T(8,128)(2,1)S(1)}, bf16[1152,128]{1,0:T(8,128)(2,1)S(1)}, u32[]{:S(2)}, u32[]{:S(2)}) collective-permute-start(bf16[1152,128]{1,0:T(8,128)(2,1)S(1)} %copy-done.25), channel_id=1, source_target_pairs={{0,16},{4,20},{8,24},{12,28},{16,0},{20,4},{24,8},{28,12},{1,17},{... | collective-permute-start | bytes 884744 | tf_op jit(solution)/shard_map/ppermute | solution.py:792
  120.0 18.7 %collective-permute-start.42 = (bf16[1152,128]{1,0:T(8,128)(2,1)S(1)}, bf16[1152,128]{1,0:T(8,128)(2,1)S(1)}, u32[]{:S(2)}, u32[]{:S(2)}) collective-permute-start(bf16[1152,128]{1,0:T(8,128)(2,1)S(1)} %copy-done.23), channel_id=1, source_target_pairs={{0,24},{4,28},{8,16},{12,20},{16,8},{20,12},{24,0},{28,4},{1,25},{... | collective-permute-start | bytes 884744 | tf_op jit(solution)/shard_map/ppermute | solution.py:792
  125.1 35.1 %collective-permute-start.16 = (bf16[2176,128]{1,0:T(8,128)(2,1)}, bf16[2176,128]{1,0:T(8,128)(2,1)S(1)}, u32[]{:S(2)}, u32[]{:S(2)}) collective-permute-start(bf16[2176,128]{1,0:T(8,128)(2,1)} %get-tuple-element.171), channel_id=1, source_target_pairs={{0,8},{4,12},{8,0},{12,4},{16,24},{20,28},{24,16},{28,20},{1,9},{5... | collective-permute-start | bytes 1671176 | tf_op jit(solution)/shard_map/ppermute | solution.py:792
  127.1 34.9 %collective-permute-start.17 = (bf16[2176,128]{1,0:T(8,128)(2,1)}, bf16[2176,128]{1,0:T(8,128)(2,1)S(1)}, u32[]{:S(2)}, u32[]{:S(2)}) collective-permute-start(bf16[2176,128]{1,0:T(8,128)(2,1)} %get-tuple-element.172), channel_id=1, source_target_pairs={{0,16},{4,20},{8,24},{12,28},{16,0},{20,4},{24,8},{28,12},{1,17},{... | collective-permute-start | bytes 1671176 | tf_op jit(solution)/shard_map/ppermute | solution.py:792
  138.7 24.2 %collective-permute-start.18 = (bf16[2176,128]{1,0:T(8,128)(2,1)}, bf16[2176,128]{1,0:T(8,128)(2,1)S(1)}, u32[]{:S(2)}, u32[]{:S(2)}) collective-permute-start(bf16[2176,128]{1,0:T(8,128)(2,1)} %get-tuple-element.173), channel_id=1, source_target_pairs={{0,24},{4,28},{8,16},{12,20},{16,8},{20,12},{24,0},{28,4},{1,25},{... | collective-permute-start | bytes 1671176 | tf_op jit(solution)/shard_map/ppermute | solution.py:792
  162.0 13.9 %collective-permute-start.32 = (bf16[3,192,256]{2,1,0:T(8,128)(2,1)}, bf16[3,192,256]{2,1,0:T(8,128)(2,1)S(1)}, u32[]{:S(2)}, u32[]{:S(2)}) collective-permute-start(bf16[3,192,256]{2,1,0:T(8,128)(2,1)} %get-tuple-element.187), channel_id=1, source_target_pairs={{0,24},{4,28},{8,16},{12,20},{16,8},{20,12},{24,0},{28,4},{1,25},{... | collective-permute-start | bytes 884744 | tf_op jit(solution)/shard_map/ppermute | solution.py:792
  173.3 17.1 %collective-permute-start.20 = (bf16[880,128]{1,0:T(8,128)(2,1)}, bf16[880,128]{1,0:T(8,128)(2,1)S(1)}, u32[]{:S(2)}, u32[]{:S(2)}) collective-permute-start(bf16[880,128]{1,0:T(8,128)(2,1)} %get-tuple-element.176), channel_id=1, source_target_pairs={{0,2},{1,3},{2,0},{3,1},{4,6},{5,7},{6,4},{7,5},{8,10},{9,11},{10,... | collective-permute-start | bytes 675848 | tf_op jit(solution)/shard_map/ppermute | solution.py:792
  175.9 16.4 %collective-permute-start.21 = (bf16[880,128]{1,0:T(8,128)(2,1)}, bf16[880,128]{1,0:T(8,128)(2,1)S(1)}, u32[]{:S(2)}, u32[]{:S(2)}) collective-permute-start(bf16[880,128]{1,0:T(8,128)(2,1)} %get-tuple-element.177), channel_id=1, source_target_pairs={{0,3},{1,2},{2,1},{3,0},{4,7},{5,6},{6,5},{7,4},{8,11},{9,10},{10,... | collective-permute-start | bytes 675848 | tf_op jit(solution)/shard_map/ppermute | solution.py:792
  178.6 15.4 %collective-permute-start.46 = (bf16[288,128]{1,0:T(8,128)(2,1)S(1)}, bf16[288,128]{1,0:T(8,128)(2,1)S(1)}, u32[]{:S(2)}, u32[]{:S(2)}) collective-permute-start(bf16[288,128]{1,0:T(8,128)(2,1)S(1)} %add_convert_fusion.3.refs_8_), channel_id=1, source_target_pairs={{0,8},{4,12},{8,0},{12,4},{16,24},{20,28},{24,16},{28,20},{1,9},{5... | collective-permute-start | bytes 221192 | tf_op jit(solution)/shard_map/ppermute | solution.py:792
  179.6 15.0 %collective-permute-start.52 = (bf16[288,128]{1,0:T(8,128)(2,1)S(1)}, bf16[288,128]{1,0:T(8,128)(2,1)S(1)}, u32[]{:S(2)}, u32[]{:S(2)}) collective-permute-start(bf16[288,128]{1,0:T(8,128)(2,1)S(1)} %collective-permute-done.48.refs_11_), channel_id=1, source_target_pairs={{0,4},{4,0},{8,12},{12,8},{16,20},{20,16},{24,28},{28,24},{1,5},{5... | collective-permute-start | bytes 221192 | tf_op jit(solution)/shard_map/ppermute | solution.py:792
  179.6 16.0 %collective-permute-start.51 = (bf16[288,128]{1,0:T(8,128)(2,1)S(1)}, bf16[288,128]{1,0:T(8,128)(2,1)S(1)}, u32[]{:S(2)}, u32[]{:S(2)}) collective-permute-start(bf16[288,128]{1,0:T(8,128)(2,1)S(1)} %collective-permute-done.47.refs_10_), channel_id=1, source_target_pairs={{0,4},{4,0},{8,12},{12,8},{16,20},{20,16},{24,28},{28,24},{1,5},{5... | collective-permute-start | bytes 221192 | tf_op jit(solution)/shard_map/ppermute | solution.py:792
  (84 other events, 707.2 us)

commit v2 on v1

--- a/solution.py
+++ b/solution.py
@@ -12,7 +12,6 @@
 BASE_RATE = 0.1
 F32 = jnp.float32
 BF16 = jnp.bfloat16
-VMEM_BYTES = 56 * 2**20
 
 
 def dot(left, right, left_dim=1, right_dim=0):
@@ -61,11 +60,11 @@
     seg_ref,
     live_ref,
     tok_ref,
-    gain1_ref,
-    wq_ref,
-    wk_ref,
-    wv_ref,
-    wg_ref,
+    gains_ref,
+    wq_hbm,
+    wk_hbm,
+    wv_hbm,
+    wg_hbm,
     wr_ref,
     br_ref,
     w1_ref,
@@ -74,51 +73,57 @@
     b2_ref,
     ig_ref,
     ib_ref,
-    wo_ref,
-    gain2_ref,
+    wo_hbm,
     pair_ref,
     normed_two_ref,
-    resid_ref,
-    gelu_ref,
-    slope_ref,
-    qk_ref,
-    ecol_ref,
-    erow_ref,
-    fcol_ref,
-    slope1_ref,
-    curve1_ref,
-    act_ref,
-    d1_ref,
-    d2_ref,
-    n_ref,
-    s_ref,
-    fit_ref,
-    w2s_ref,
-    p1_ref,
-    p2_ref,
-    slopeq_ref,
-    nq_ref,
-    sq_ref,
-    q_s,
-    k_s,
-    v_s,
-    out_s,
-    w1_s,
-    w1b_s,
-    b1_s,
-    w2_s,
-    b2_s,
-    b1f,
-    b2f,
-    igf,
-    ibf,
+    *refs,
 ):
+    saved = (len(refs) - 15) // 2
+    outs, kept, scratch = refs[0:saved], refs[saved : 2 * saved], refs[2 * saved :]
+    (
+        resid_ref,
+        gelu_ref,
+        slope_ref,
+        qk_ref,
+        ecol_ref,
+        erow_ref,
+        fcol_ref,
+        slope1_ref,
+        curve1_ref,
+        act_ref,
+        d1_ref,
+        d2_ref,
+        n_ref,
+        s_ref,
+        fit_ref,
+        w2s_ref,
+        p1_ref,
+        p2_ref,
+        slopeq_ref,
+        nq_ref,
+        sq_ref,
+    ) = kept
+    q_s, k_s, v_s, out_s, w1_s, w1b_s, b1_s, w2_s, b2_s, b1f, b2f, igf, ibf, weights_s, sems = scratch
     length, width = tok_ref.shape[1], tok_ref.shape[2]
+    copies = [
+        pltpu.make_async_copy(w, weights_s.at[i], sems.at[i])
+        for i, w in enumerate((wq_hbm, wk_hbm, wv_hbm, wg_hbm, wo_hbm))
+    ]
+    for copy in copies:
+        copy.start()
+    saves = [
+        pltpu.make_async_copy(kept[i], outs[i], sems.at[len(copies) + i]) for i in range(saved)
+    ]
+
+    def save(*indices):
+        for i in indices:
+            saves[i].start()
+
     heads, head = w1_ref.shape[0], w1_ref.shape[1]
     blocks = length // MB
     tok = tok_ref[0].astype(F32)
     spread = lax.rsqrt(mean_last(tok * tok) + EPSILON)
-    normed = low(tok * spread * gain1_ref[...].astype(F32))
+    normed = low(tok * spread * gains_ref[0:1].astype(F32))
     pair_ref[0] = normed
     seg_row = seg_ref[...].astype(F32)
     live = column_of(live_ref[...].astype(F32))
@@ -130,8 +135,9 @@
     fcol_ref[...] = jnp.zeros(fcol_ref.shape, F32)
     fcol_ref[:, 0:heads] = rates * (1.0 - sig)
     erow_ref[...] = jnp.transpose(ecol_ref[...])[0 : erow_ref.shape[0]]
-    for w_ref, to in ((wq_ref, q_s), (wk_ref, k_s), (wv_ref, v_s)):
-        whole = dot(normed, w_ref[...])
+    for i, to in enumerate((q_s, k_s, v_s)):
+        copies[i].wait()
+        whole = dot(normed, weights_s[i])
         for h in range(heads):
             to[h] = whole[:, h * head : (h + 1) * head]
     b1f[...] = b1_ref[...].astype(F32)
@@ -211,7 +217,9 @@
             fit_ref[h, ds, :] = fit[h]
         return carry
 
+    save(3, 4, 5, 6)
     lax.fori_loop(0, blocks, step, 0)
+    save(7, 8, 10, 11, 12, 13, 14, 15)
     inclusive, _ = segment_masks(seg_row)
     for h in range(heads):
         queries = qk_ref[h, 0:length]
@@ -234,16 +242,22 @@
         nq_ref[h] = n
         sq_ref[h] = s
         out_s[:, h * head : (h + 1) * head] = q_s[h] + igf[h : h + 1] * n + ibf[h : h + 1]
+    save(9, 16, 17, 18, 19, 20)
     inner_out = out_s[...]
-    gate, slope, _ = gelu_parts(dot(normed, wg_ref[...]))
+    copies[3].wait()
+    gate, slope, _ = gelu_parts(dot(normed, weights_s[3]))
     gelu_ref[...] = gate
     slope_ref[...] = inner_out * slope
     gated = low(inner_out * gate)
     pair_ref[1] = gated
-    resid = tok + dot(gated, wo_ref[...])
+    copies[4].wait()
+    resid = tok + dot(gated, weights_s[4])
     resid_ref[...] = resid
     spread_two = lax.rsqrt(mean_last(resid * resid) + EPSILON)
-    normed_two_ref[...] = low(resid * spread_two * gain2_ref[...].astype(F32))
+    normed_two_ref[...] = low(resid * spread_two * gains_ref[1:2].astype(F32))
+    save(0, 1, 2)
+    for copy in saves:
+        copy.wait()
 
 
 def ffn_kernel(x_ref, c_ref, wg_ref, wu_ref, wd_ref, act_ref, gg_ref, gu_ref, gx_ref):
@@ -293,24 +307,16 @@
             sent_ref[i] = whole[:, 0:half]
 
 
-def cut_rows_kernel(ids_smem, kept_ref, got_ref, *out_refs):
-    chip = ids_smem[1]
-    rows = out_refs[0].shape[1]
-    for s, out in enumerate(out_refs):
-        at = pl.ds(pl.multiple_of(lax.bitwise_xor(chip, s) * rows, rows), rows)
-        out[...] = low(kept_ref[:, at, :].astype(F32) + got_ref[:, at, :].astype(F32))
-
-
 def between_kernel(parts, *refs):
     pieces = refs[0:parts]
-    resid_ref, cot_ref, gain2_ref, wo_ref, gelu_ref, slope_ref = refs[parts : parts + 6]
+    resid_ref, cot_ref, gains_ref, wo_ref, gelu_ref, slope_ref = refs[parts : parts + 6]
     resid_grad_ref, go_ref, pair_ref, gain_grad_ref = refs[parts + 6 :]
     grad = pieces[0][...].astype(F32)
     for piece in pieces[1:]:
         grad = grad + piece[...].astype(F32)
     resid = resid_ref[...]
     spread = lax.rsqrt(mean_last(resid * resid) + EPSILON)
-    scaled = gain2_ref[...].astype(F32) * grad
+    scaled = gains_ref[1:2].astype(F32) * grad
     grad_resid = (
         cot_ref[0].astype(F32)
         + spread * scaled
@@ -540,11 +546,21 @@
 
 
 def gate_weights_kernel(
-    feats, ids_smem, mine_ref, other_ref, grads_ref, other_grads_ref, wg_ref, *refs
+    feats,
+    chips,
+    ids_smem,
+    mine_ref,
+    other_ref,
+    grads_ref,
+    other_grads_ref,
+    wg_ref,
+    kept_ref,
+    got_ref,
+    part_ref,
+    *refs,
 ):
-    part_ref = refs[0]
-    pieces_s, left_s, right_s = refs[-3:]
-    outs = refs[1:-3]
+    outs = refs[0:chips]
+    pieces_s, left_s, right_s = refs[chips:]
     core, chip = ids_smem[0], ids_smem[1]
     length = mine_ref.shape[1]
     for i in range(2):
@@ -554,8 +570,19 @@
         right_s[i, length : 2 * length] = core_columns(core, other_grads_ref[i])
     for i in range(2):
         put_matrix(pieces_s, low(dot(left_s[i], right_s[i], 0, 0)), i, 2, feats)
+    count, _, half = kept_ref.shape
+    chunks = half // 128
+    before = outs[0].shape[0] - pieces_s.shape[1]
+    rows = before // (count * chunks)
     for s, out in enumerate(outs):
-        out[...] = pieces_s[lax.bitwise_xor(chip, s)]
+        place = lax.bitwise_xor(chip, s)
+        at = pl.ds(pl.multiple_of(place * rows, 16), rows)
+        for i in range(count):
+            both = low(kept_ref[i, at, :].astype(F32) + got_ref[i, at, :].astype(F32))
+            for l in range(chunks):
+                row = (i * chunks + l) * rows
+                out[row : row + rows] = both[:, l * 128 : (l + 1) * 128]
+        out[before:] = pieces_s[place]
     part_ref[...] = dot(grads_ref[0], wg_ref[...], 1, 1)
 
 
@@ -570,7 +597,7 @@
     wr_ref,
     part_ref,
     tok_ref,
-    gain1_ref,
+    gains_ref,
     resid_grad_ref,
     small_ref,
     gain_two_ref,
@@ -584,7 +611,7 @@
     grad = grad + dot(gr[:, 0:heads], wr_ref[...])
     tok = tok_ref[0].astype(F32)
     spread = lax.rsqrt(mean_last(tok * tok) + EPSILON)
-    scaled = gain1_ref[...].astype(F32) * grad
+    scaled = gains_ref[0:1].astype(F32) * grad
     grad_ref[0] = (
         resid_grad_ref[...]
         + spread * scaled
@@ -607,23 +634,31 @@
     small_out[at : at + small_ref.shape[0]] = low(small_ref[...])
 
 
+def tails_kernel(ids_smem, kept_ref, got_ref, small_ref, *refs):
+    outs, tails_s = refs[:-1], refs[-1]
+    chips = len(outs)
+    inner = low(kept_ref[...].astype(F32) + got_ref[...].astype(F32))
+    rows = inner.shape[0] // chips
+    extra = small_ref.shape[0] // chips
+    for j in range(chips):
+        at = 0
+        for l in range(2):
+            cols = slice(l * 128, (l + 1) * 128)
+            tails_s[j, at : at + rows] = inner[j * rows : (j + 1) * rows, cols]
+            at += rows
+            tails_s[j, at : at + extra] = small_ref[j * extra : (j + 1) * extra, cols]
+            at += extra
+    for s, out in enumerate(outs):
+        out[...] = tails_s[lax.bitwise_xor(ids_smem[1], s)]
+
+
 def late_weights_kernel(
-    feats,
-    ids_smem,
-    mine_ref,
-    other_ref,
-    triple_ref,
-    other_triple_ref,
-    kept_ref,
-    got_ref,
-    small_ref,
-    *refs,
+    feats, ids_smem, mine_ref, other_ref, triple_ref, other_triple_ref, *refs
 ):
     pieces_s, left_s, right_s = refs[-3:]
     outs = refs[:-3]
     core, chip = ids_smem[0], ids_smem[1]
     length = mine_ref.shape[1]
-    chips = pieces_s.shape[0]
     left_s[0:length] = mine_ref[0]
     left_s[length : 2 * length] = other_ref[0]
     for i in range(3):
@@ -631,55 +666,47 @@
         right_s[i, length : 2 * length] = core_columns(core, other_triple_ref[i])
     for i in range(3):
         put_matrix(pieces_s, low(dot(left_s[...], right_s[i], 0, 0)), i, 3, feats)
-    inner = low(kept_ref[...].astype(F32) + got_ref[...].astype(F32))
-    rows = inner.shape[0] // chips
-    extra = small_ref.shape[0] // chips
-    start = pieces_s.shape[1] - 2 * (rows + extra)
-    for j in range(chips):
-        at = start
-        for l in range(2):
-            cols = slice(l * 128, (l + 1) * 128)
-            pieces_s[j, at : at + rows] = inner[j * rows : (j + 1) * rows, cols]
-            at += rows
-            pieces_s[j, at : at + extra] = small_ref[j * extra : (j + 1) * extra, cols]
-            at += extra
     for s, out in enumerate(outs):
         out[...] = pieces_s[lax.bitwise_xor(chip, s)]
 
 
-def cut_feat_kernel(parts, ids_smem, *refs):
-    outs = refs[parts:]
-    feat = ids_smem[2]
-    total_rows = refs[0].shape[0]
-    each = outs[0].shape[0]
-    common = (len(outs) * each - total_rows) // (len(outs) - 1)
-    own = each - common
-
-    def total(at):
-        value = refs[0][at].astype(F32)
-        for ref in refs[1:parts]:
-            value = value + ref[at].astype(F32)
-        return low(value)
-
+def sum_at(refs, at):
+    value = refs[0][at].astype(F32)
+    for ref in refs[1:]:
+        value = value + ref[at].astype(F32)
+    return low(value)
+
+
+def cut_feat_kernel(chips, ids_smem, *refs):
+    parts, outs = refs[0:chips], refs[chips:]
+    rows = outs[0].shape[0]
     for s, out in enumerate(outs):
-        at = pl.ds(pl.multiple_of(lax.bitwise_xor(feat, s) * own, 16), own)
-        out[0:own] = total((at, slice(None)))
-    if common:
-        shared = total((slice(own * len(outs), total_rows), slice(None)))
-        for out in outs:
-            out[own:each] = shared
-
-
-def take_matrices(ids_smem, pieces, outs):
+        at = pl.ds(pl.multiple_of(lax.bitwise_xor(ids_smem[2], s) * rows, 16), rows)
+        out[...] = sum_at(parts, (at, slice(None)))
+
+
+def middle_kernel(chips, ids_smem, *refs):
+    pair, tail = refs[0:chips], refs[chips : 2 * chips]
+    total_ref, outs = refs[2 * chips], refs[2 * chips + 1 :]
+    before = total_ref.shape[0]
+    rows = (pair[0].shape[0] - before) // len(outs)
+    shared = sum_at(tail, (slice(None), slice(None)))
+    for s, out in enumerate(outs):
+        at = pl.multiple_of(before + lax.bitwise_xor(ids_smem[2], s) * rows, 16)
+        out[0:rows] = sum_at(pair, (pl.ds(at, rows), slice(None)))
+        out[rows:] = shared
+    total_ref[...] = sum_at(pair, (slice(0, before), slice(None)))
+
+
+def take_matrices(ids_smem, pieces, outs, start=0):
     core, chip = ids_smem[0], ids_smem[1]
-    count = len(outs)
     chunks = outs[0].shape[1] // 256
     rows = outs[0].shape[0] // len(pieces)
     for s, both in enumerate(pieces):
         at = pl.ds(pl.multiple_of(lax.bitwise_xor(chip, s) * rows, 16), rows)
         for i, out in enumerate(outs):
             for l in range(chunks):
-                row = (i * chunks + l) * rows
+                row = start + (i * chunks + l) * rows
                 mine = both[0][row : row + rows, :].astype(F32)
                 other = both[1][row : row + rows, :].astype(F32)
 
@@ -694,45 +721,24 @@
                     out[at, (chunks + l) * 128 : (chunks + l + 1) * 128] = mine
 
 
-def early_totals_kernel(chips, ids_smem, *refs):
-    ffn = [(refs[s], refs[chips + s]) for s in range(chips)]
-    pair = [(refs[2 * chips + s], refs[3 * chips + s]) for s in range(chips)]
-    gate_ref, up_ref, down_ref, wg_ref, wo_ref, down_s = refs[4 * chips :]
-    core, chip = ids_smem[0], ids_smem[1]
-    half = ffn[0][0].shape[2]
-    rows = ffn[0][0].shape[1]
-    for s, both in enumerate(ffn):
-        at = pl.ds(pl.multiple_of(lax.bitwise_xor(chip, s) * rows, 16), rows)
-        for i, out in enumerate((gate_ref, up_ref, down_s)):
-            mine = both[0][i].astype(F32)
-            other = both[1][i].astype(F32)
-
-            @pl.when(core == 0)
-            def _(out=out, at=at, mine=mine, other=other):
-                out[at, 0:half] = mine
-                out[at, half : 2 * half] = other
-
-            @pl.when(core != 0)
-            def _(out=out, at=at, mine=mine, other=other):
-                out[at, 0:half] = other
-                out[at, half : 2 * half] = mine
-
+def ffn_totals_kernel(chips, ids_smem, *refs):
+    pieces = [(refs[s], refs[chips + s]) for s in range(chips)]
+    gate_ref, up_ref, down_ref, down_s = refs[2 * chips :]
+    take_matrices(ids_smem, pieces, (gate_ref, up_ref, down_s))
     down_ref[...] = jnp.transpose(down_s[...])
-    take_matrices(ids_smem, pair, (wg_ref, wo_ref))
-
-
-def late_totals_kernel(chips, feats, heads, head, ids_smem, *refs):
+
+
+def early_totals_kernel(chips, feats, heads, head, ids_smem, *refs):
     pieces = [(refs[s], refs[chips + s]) for s in range(chips)]
-    (wq_ref, wk_ref, wv_ref, first_ref, second_ref) = refs[2 * chips : 2 * chips + 5]
-    (rate_ref, norm1_ref, norm2_ref, b1_ref, b2_ref, ig_ref, ib_ref, br_ref) = refs[
-        2 * chips + 5 : 2 * chips + 13
+    wg_ref, wo_ref, first_ref, second_ref = refs[2 * chips : 2 * chips + 4]
+    (rate_ref, norm1_ref, norm2_ref, b1_ref, b2_ref, ig_ref, ib_ref, br_ref, small_s) = refs[
+        2 * chips + 4 :
     ]
-    small_s = refs[2 * chips + 13]
     core, chip, feat = ids_smem[0], ids_smem[1], ids_smem[2]
-    take_matrices(ids_smem, pieces, (wq_ref, wk_ref, wv_ref))
+    take_matrices(ids_smem, pieces, (wg_ref, wo_ref))
     rows = first_ref.shape[0] // chips
     extra = small_s.shape[0] // chips
-    start = refs[0].shape[0] - 2 * (rows + extra)
+    start = 2 * (wg_ref.shape[0] // chips) * (wg_ref.shape[1] // 256)
     for s, both in enumerate(pieces):
         place = lax.bitwise_xor(chip, s)
         at = pl.ds(pl.multiple_of(place * rows, 16), rows)
@@ -772,20 +778,46 @@
     br_ref[...] = packed[:, 3 * head : 3 * head + 1]
 
 
-def call(kernel, outs, inputs, scratch=(), smem=0, us=1.0):
-    specs = [pl.BlockSpec(memory_space=pltpu.SMEM)] * smem
-    specs += [pl.BlockSpec(memory_space=pltpu.VMEM)] * (len(inputs) - smem)
+def late_totals_kernel(chips, ids_smem, *refs):
+    pieces = [(refs[s], refs[chips + s]) for s in range(chips)]
+    take_matrices(ids_smem, pieces, refs[2 * chips : 2 * chips + 3])
+
+
+def held(values):
+    return pltpu.with_memory_space_constraint(values, pltpu.VMEM)
+
+
+def call(kernel, outs, inputs, scratch=(), smem=0, us=1.0, plain=(), loose=(), keep=True, mib=24):
+    specs, placed = [], []
+    for i, x in enumerate(inputs):
+        if i < smem:
+            specs.append(pl.BlockSpec(memory_space=pltpu.SMEM))
+            placed.append(x)
+        elif i in loose:
+            specs.append(pl.BlockSpec(memory_space=pltpu.HBM))
+            placed.append(pltpu.with_memory_space_constraint(x, pltpu.HBM))
+        elif i in plain:
+            specs.append(pl.BlockSpec(memory_space=pltpu.VMEM))
+            placed.append(pltpu.with_memory_space_constraint(x, pltpu.HBM))
+        else:
+            specs.append(pl.BlockSpec(memory_space=pltpu.VMEM))
+            placed.append(held(x))
+    kept = [keep] * len(outs) if isinstance(keep, bool) else list(keep)
     return pl.pallas_call(
         kernel,
-        out_shape=[jax.ShapeDtypeStruct(s, d) for s, d in outs],
+        out_shape=[
+            pltpu.VMEM(s, d) if k else pltpu.HBM(s, d) for (s, d), k in zip(outs, kept)
+        ],
         in_specs=specs,
-        out_specs=[pl.BlockSpec(memory_space=pltpu.VMEM)] * len(outs),
-        scratch_shapes=[pltpu.VMEM(s, d) for s, d in scratch],
+        out_specs=[
+            pl.BlockSpec(memory_space=pltpu.HBM if k is None else pltpu.VMEM) for k in kept
+        ],
+        scratch_shapes=[pltpu.VMEM(*x) if isinstance(x, tuple) else x for x in scratch],
         cost_estimate=pl.CostEstimate(
-            flops=int(us * 1e9), bytes_accessed=int(us * 1e6), transcendentals=0
+            flops=int(us * 1e10), bytes_accessed=int(us * 3e7), transcendentals=0
         ),
-        compiler_params=pltpu.CompilerParams(vmem_limit_bytes=VMEM_BYTES),
-    )(*inputs)
+        compiler_params=pltpu.CompilerParams(vmem_limit_bytes=mib * 2**20),
+    )(*placed)
 
 
 def exchange(values, axis, size, distance):
@@ -896,8 +928,7 @@
     hidden = ffn_gate.shape[1]
     blocks = length // MB
     chips = rows // 2
-    gain_one = norm1_gain[None]
-    gain_two = norm2_gain[None]
+    gains = jnp.stack([norm1_gain, norm2_gain])
     line = (length, width)
     wide = (heads, length, inner)
     slim = (heads, length, head)
@@ -910,39 +941,38 @@
     me = lax.axis_index("feat")
     ids = jnp.stack([lax.bitwise_and(place, 1), lax.shift_right_logical(place, 1), me])
     cots = across_feats([cotangent[0]] * feats, feats)
+    kept = [
+        (line, F32),
+        (line, F32),
+        (line, F32),
+        ((heads, 2 * length, head), BF16),
+        ((length, 128), F32),
+        ((16, length), F32),
+        ((length, 128), F32),
+        (wide, BF16),
+        (wide, BF16),
+        ((heads, 2 * length, inner), BF16),
+        (wide, BF16),
+        (slim, F32),
+        (slim, F32),
+        (thin, F32),
+        (slim, F32),
+        ((blocks,) + state, BF16),
+        (square, BF16),
+        (square, BF16),
+        (wide, BF16),
+        (slim, F32),
+        (thin, F32),
+    ]
     saved = call(
         forward_kernel,
-        [
-            ((2,) + line, BF16),
-            (line, BF16),
-            (line, F32),
-            (line, F32),
-            (line, F32),
-            ((heads, 2 * length, head), BF16),
-            ((length, 128), F32),
-            ((16, length), F32),
-            ((length, 128), F32),
-            (wide, BF16),
-            (wide, BF16),
-            ((heads, 2 * length, inner), BF16),
-            (wide, BF16),
-            (slim, F32),
-            (slim, F32),
-            (thin, F32),
-            (slim, F32),
-            ((blocks,) + state, BF16),
-            (square, BF16),
-            (square, BF16),
-            (wide, BF16),
-            (slim, F32),
-            (thin, F32),
-        ],
+        [((2,) + line, BF16), (line, BF16)] + kept,
         [
             seg_ids,
             seg_ids,
             pad_mask,
             tokens,
-            gain_one,
+            gains,
             w_query,
             w_key,
             w_value,
@@ -956,9 +986,9 @@
             inner_gain,
             inner_bias,
             w_out,
-            gain_two,
         ],
-        [
+        kept
+        + [
             (slim, F32),
             (slim, F32),
             (slim, F32),
@@ -972,81 +1002,98 @@
             ((heads, head), F32),
             ((heads, head), F32),
             ((heads, head), F32),
+            ((5, width, width), BF16),
+            pltpu.SemaphoreType.DMA((5 + len(kept),)),
         ],
         smem=1,
-        us=25,
+        us=20,
+        plain=range(18),
+        loose=(5, 6, 7, 8, 17),
+        keep=[True, True] + [None] * len(kept),
+        mib=48,
     )
     pair, normed_two, resid, gelu_gate, gate_slope = saved[0:5]
     qk, ecol, erow, fcol = saved[5:9]
     rest = saved[9:]
-    blocks_in = across_feats([normed_two] * feats, feats)
+    normed_two, *cots = lax.optimization_barrier([normed_two] + cots)
+    blocks_in = [normed_two]
+    for s in range(1, feats):
+        nearest = s & -s
+        blocks_in.append(exchange(blocks_in[s ^ nearest], "feat", feats, nearest))
     acts, ggs, gus, pieces = [], [], [], []
     for s in range(feats):
         act, gg, gu, gx = call(
             ffn_kernel,
             [((length, hidden), BF16)] * 3 + [(line, BF16)],
             [blocks_in[s], cots[s], ffn_gate, ffn_up, ffn_down],
-            us=3,
+            us=1.5,
         )
         acts.append(act)
         ggs.append(gg)
         gus.append(gu)
         pieces.append(gx if s == 0 else exchange(gx, "feat", feats, s))
-    grad_resid, grad_inner_out, grad_pair, grad_gain_two = call(
-        partial(between_kernel, feats),
-        [(line, F32), (line, F32), ((2,) + line, BF16), ((1, width), F32)],
-        pieces + [resid, cotangent, gain_two, w_out, gelu_gate, gate_slope],
-        us=4,
-    )
-    triple, grad_rates, kept, sent, small = call(
-        backward_kernel,
-        [
-            ((3,) + line, BF16),
-            ((length, 128), BF16),
-            ((heads * head, inner), BF16),
-            ((heads * head, inner), BF16),
-            ((32, inner), F32),
-        ],
-        [ids, seg_ids, seg_ids, grad_inner_out, qk, ecol, erow, fcol, inner_w1, w2t]
-        + [inner_gain]
-        + list(rest),
-        [
-            ((heads, head), F32),
-            (wide, F32),
-            (slim, F32),
-            (wide, F32),
-            ((heads, 2 * length, inner), BF16),
-            ((heads, 2 * length, head), BF16),
-            (wide, BF16),
-            (slim, F32),
-            ((length, 128), F32),
-            (state, F32),
-            (state, BF16),
-            ((heads, 1, inner), F32),
-            (state, F32),
-            (state, BF16),
-            ((heads, 1, head), F32),
-        ],
-        smem=2,
-        us=28,
-    )
+    def between(pieces):
+        return call(
+            partial(between_kernel, feats),
+            [(line, F32), (line, F32), ((2,) + line, BF16), ((1, width), F32)],
+            pieces + [resid, cotangent, gains, w_out, gelu_gate, gate_slope],
+            us=1,
+        )
+
+    def inner_backward(grad_inner_out):
+        return call(
+            backward_kernel,
+            [
+                ((3,) + line, BF16),
+                ((length, 128), BF16),
+                ((heads * head, inner), BF16),
+                ((heads * head, inner), BF16),
+                ((32, inner), F32),
+            ],
+            [ids, seg_ids, seg_ids, grad_inner_out, qk, ecol, erow, fcol, inner_w1, w2t]
+            + [inner_gain]
+            + list(rest),
+            [
+                ((heads, head), F32),
+                (wide, F32),
+                (slim, F32),
+                (wide, F32),
+                ((heads, 2 * length, inner), BF16),
+                ((heads, 2 * length, head), BF16),
+                (wide, BF16),
+                (slim, F32),
+                ((length, 128), F32),
+                (state, F32),
+                (state, BF16),
+                ((heads, 1, inner), F32),
+                (state, F32),
+                (state, BF16),
+                ((heads, 1, head), F32),
+            ],
+            smem=2,
+            us=22,
+        )
+
     step = 16 * chips
     small_rows = -(-(16 * feats + 32) // step) * step
 
-    def finish(part):
+    def finish(triple, grad_rates, small, part, grad_resid, grad_gain_two):
         return call(
             partial(input_kernel, feats),
             [((1,) + line, F32), ((small_rows, inner), BF16)],
             [triple, grad_rates, pair, w_query, w_key, w_value, w_rate_t, part]
-            + [tokens, gain_one, grad_resid, small, grad_gain_two],
-            us=4,
+            + [tokens, gains, grad_resid, small, grad_gain_two],
+            us=2,
+            keep=(False, True),
         )
 
     if (width // feats) % step or hidden % 256 or width % 256:
+        grad_resid, grad_inner_out, grad_pair, grad_gain_two = between(pieces)
         out, grads = plain_totals(
             rows, feats, blocks_in, cots, acts, ggs, gus, ffn_down, pair, grad_pair, w_gate
         )
-        grad_tokens, small = finish(grads.pop())
+        triple, grad_rates, kept, sent, small = inner_backward(grad_inner_out)
+        grad_tokens, small = finish(triple, grad_rates, small, grads.pop(), grad_resid, grad_gain_two)
         late = plain_late_totals(rows, feats, pair, triple, kept, sent, small, state)
         mixed = low(resid + sum(x.astype(F32) for x in across_feats(out, feats)))
         return arrange(mixed, grad_tokens, grads, late, state)
@@ -1056,95 +1103,120 @@
         [ids] + blocks_in + cots + acts + ggs + gus + [ffn_down],
         [((feats * length, width), BF16)] * 2 + [((feats * length, hidden), BF16)] * 3,
         smem=1,
-        us=6,
-    )
-    out = across_feats(ffn[2:], feats)
-    mixed = low(resid + sum(x.astype(F32) for x in out))
-    ffn_pieces = call(
-        cut_rows_kernel,
-        [((3, width // chips, hidden // 2), BF16)] * chips,
-        [ids, ffn[0], other_core(ffn[1], rows)],
-        smem=1,
-        us=2,
-    )
-    ffn_total = sum_low(across_chips(ffn_pieces, rows))
-    ffn_all = across_chips([ffn_total] * chips, rows)
-    ffn_others = [other_core(x, rows) for x in ffn_all]
+        us=4,
+    )
+    pieces, ffn_kept = lax.optimization_barrier((pieces, ffn[0]))
+    grad_resid, grad_inner_out, grad_pair, grad_gain_two = between(pieces)
     pair_other = other_core(pair, rows)
     half = width // 2
     per = width // (feats * chips) * (half // 128)
-    gate = call(
-        partial(gate_weights_kernel, feats),
-        [(line, F32)] + [((feats * 2 * per, 128), BF16)] * chips,
-        [ids, pair, pair_other, grad_pair, other_core(grad_pair, rows), w_gate],
+    ffn_rows = 3 * (width // chips) * (hidden // 256)
+    part, *early = call(
+        partial(gate_weights_kernel, feats, chips),
+        [(line, F32)] + [((ffn_rows + feats * 2 * per, 128), BF16)] * chips,
+        [ids, pair, pair_other, grad_pair, other_core(grad_pair, rows), w_gate]
+        + [ffn_kept, other_core(ffn[1], rows)],
         [
             ((chips, feats * 2 * per, 128), BF16),
             ((2, 2 * length, width), BF16),
             ((2, 2 * length, half), BF16),
         ],
         smem=1,
-        us=4,
-    )
-    gate_cut = call(
-        partial(cut_feat_kernel, chips),
-        [((2 * per, 128), BF16)] * feats,
-        [ids] + across_chips(gate[1:], rows),
-        smem=1,
         us=2,
     )
-    gate_total = sum_low(across_feats(gate_cut, feats))
-    gate_all = across_chips([gate_total] * chips, rows)
-    gate_others = [other_core(x, rows) for x in gate_all]
-    share = (width // feats, width)
-    early = call(
-        partial(early_totals_kernel, chips),
-        [((width, hidden), F32)] * 2 + [((hidden, width), F32)] + [(share, F32)] * 2,
-        [ids] + ffn_all + ffn_others + gate_all + gate_others,
-        [((width, hidden), F32)],
-        smem=1,
-        us=4,
-    )
+    grad_inner_out, early, out = lax.optimization_barrier((grad_inner_out, early, ffn[2:]))
+    early = across_chips(early, rows)
+    out = across_feats(out, feats)
+    triple, grad_rates, kept, sent, small = inner_backward(grad_inner_out)
     triple_other = other_core(triple, rows)
     got = other_core(sent, rows)
-    grad_tokens, small = finish(gate[0])
+    small, early, out = lax.optimization_barrier((small, early, out))
+    grad_tokens, small = finish(
+        triple, grad_rates, small, part, grad_resid, grad_gain_two
+    )
+    mixed = low(resid + sum(x.astype(F32) for x in out))
     tail = 2 * (heads * head + small_rows) // chips
+    tails = call(
+        tails_kernel,
+        [((tail, 128), BF16)] * chips,
+        [ids, kept, got, small],
+        [((chips, tail, 128), BF16)],
+        smem=1,
+        us=1,
+    )
+    tails, triple = lax.optimization_barrier((tails, triple))
+    tails = across_chips(tails, rows)
     late = call(
         partial(late_weights_kernel, feats),
-        [((feats * 3 * per + tail, 128), BF16)] * chips,
-        [ids, pair, pair_other, triple, triple_other, kept, got, small],
+        [((feats * 3 * per, 128), BF16)] * chips,
+        [ids, pair, pair_other, triple, triple_other],
         [
-            ((chips, feats * 3 * per + tail, 128), BF16),
+            ((chips, feats * 3 * per, 128), BF16),
             ((2 * length, width), BF16),
             ((3, 2 * length, half), BF16),
         ],
         smem=1,
-        us=4,
-    )
+        us=2,
+    )
+    late = across_chips(late, rows)
+    ffn_total, *cut = call(
+        partial(middle_kernel, chips),
+        [((ffn_rows, 128), BF16)] + [((2 * per + tail, 128), BF16)] * feats,
+        [ids] + early + tails,
+        smem=1,
+        us=1,
+    )
+    ffn_total = across_chips([ffn_total] * chips, rows)
+    ffn_total += [other_core(x, rows) for x in ffn_total]
+    joined = sum_low(across_feats(cut, feats))
+    joined = across_chips([joined] * chips, rows)
+    joined += [other_core(x, rows) for x in joined]
     late_cut = call(
         partial(cut_feat_kernel, chips),
-        [((3 * per + tail, 128), BF16)] * feats,
-        [ids] + across_chips(late, rows),
+        [((3 * per, 128), BF16)] * feats,
+        [ids] + late,
         smem=1,
-        us=2,
+        us=1,
     )
     late_total = sum_low(across_feats(late_cut, feats))
-    late_all = across_chips([late_total] * chips, rows)
-    late_others = [other_core(x, rows) for x in late_all]
-    late = call(
-        partial(late_totals_kernel, chips, feats, heads, head),
-        [(share, F32)] * 3
+    late = across_chips([late_total] * chips, rows)
+    late += [other_core(x, rows) for x in late]
+    share = (width // feats, width)
+    ffn = call(
+        partial(ffn_totals_kernel, chips),
+        [((width, hidden), F32)] * 2 + [((hidden, width), F32)],
+        [ids] + ffn_total,
+        [((width, hidden), F32)],
+        smem=1,
+        us=3,
+        keep=False,
+    )
+    early = call(
+        partial(early_totals_kernel, chips, feats, heads, head),
+        [(share, F32)] * 2
         + [((heads * head, inner), F32)] * 2
         + [((heads, width // feats), F32)]
         + [((1, width // feats), F32)] * 2
         + [((heads, inner), F32)]
         + [((heads, head), F32)] * 3
         + [((heads, 1), F32)],
-        [ids] + late_all + late_others,
+        [ids] + joined,
         [((small_rows, inner), F32)],
         smem=1,
-        us=4,
-    )
-    return arrange(mixed, grad_tokens, early, late, state)
+        us=3,
+        keep=False,
+    )
+    late = call(
+        partial(late_totals_kernel, chips),
+        [(share, F32)] * 3,
+        [ids] + late,
+        smem=1,
+        us=2,
+        keep=False,
+    )
+    return arrange(
+        mixed, grad_tokens, list(ffn) + list(early[0:2]), list(late) + list(early[2:]), state
+    )
 
 
 def arrange(mixed, grad_tokens, early, late, state):

time: 226 us -> 190 us (0.84); the launches traced: 223 us -> 190 us
  Pallas kernels: 107 us -> 76.8 us
  local copies, waits for them, and re-layouts: 10.1 us -> 1.58 us
  waiting for transfers between devices: 44.9 us -> 50.3 us
    pallas_call x16 -> x17, Pallas kernels: 107 us -> 76.8 us  [call(): pl.pallas_call(kernel, out_shape=[pltpu.VMEM(s, d) if k else pltpu.HBM(s,...]
    unnamed x110 -> x82, local copies, waits for them, and re-layouts: 7.6 us -> 0.21 us
    ppermute x53, waiting for transfers between devices: 44.9 us -> 50.3 us  [exchange(): return lax.ppermute(values, axis, [(i, i ^ distance) for i in range(size)])]
    broadcast_in_dim x2 -> x0, local copies, waits for them, and re-layouts: 2.52 us -> none  [the longest x1 1.26 us: on_device(): gain_one = norm1_gain[None]]
  transfers between devices with their start and end apart: 53 -> 53, of which waited for: 12 -> 14; matrix products, arithmetic and copies ran while one was open for 3% -> 3% of each run, Pallas kernels for 45% -> 38%
where the time goes in v2:
time: 190 us
  Pallas kernels  76.8 us (40%)
  starting transfers between devices  55.8 us (29%)
  waiting for transfers between devices  50.3 us (26%)
  other arithmetic  3.99 us (2%)
    pallas_call x17, Pallas kernels, call(): pl.pallas_call(kernel, out_shape=[pltpu.VMEM(s, d) if k else pltpu.HBM(s,...  76.8 us
    ppermute x53, starting transfers between devices, exchange(): return lax.ppermute(values, axis, [(i, i ^ distance) for i in range(size)])  55.8 us
    ppermute x53, waiting for transfers between devices, exchange(): return lax.ppermute(values, axis, [(i, i ^ distance) for i in range(size)])  50.3 us
  transfers between devices with their start and end apart: 53, of which 14 were waited for; matrix products, arithmetic and copies ran while one was open for 3% of the time, Pallas kernels for 38%

profile of v2, /device:TPU:0, one launch (start us, length us, event | category | flops | bytes accessed | tf_op | source)
XLA Modules:
  0.0 189.8 jit_solution(15116898750376577331)
XLA Ops:
  0.7 3.1 %collective-permute-start = (bf16[128,768]{1,0:T(8,128)(2,1)}, bf16[128,768]{1,0:T(8,128)(2,1)}, u32[]{:S(2)}, u32[]{:S(2)}) collective-permute-start(bf16[128,768]{1,0:T(8,128)(2,1)} %bitcast.18), channel_id=1, source_target_pairs={{0,1},{1,0},{2,3},{3,2},{4,5},{5,4},{6,7},{7,6},{8,9},{9,8},{10,11... | collective-permute-start | bytes 589832 | tf_op jit(solution)/shard_map/ppermute | solution.py:824
  3.7 2.6 %collective-permute-start.1 = (bf16[128,768]{1,0:T(8,128)(2,1)}, bf16[128,768]{1,0:T(8,128)(2,1)}, u32[]{:S(2)}, u32[]{:S(2)}) collective-permute-start(bf16[128,768]{1,0:T(8,128)(2,1)} %bitcast.19), channel_id=1, source_target_pairs={{0,2},{1,3},{2,0},{3,1},{4,6},{5,7},{6,4},{7,5},{8,10},{9,11},{10,... | collective-permute-start | bytes 589832 | tf_op jit(solution)/shard_map/ppermute | solution.py:824
  8.3 22.3 %shard_map.365 = (bf16[2,128,768]{2,1,0:T(8,128)(2,1)S(1)}, bf16[128,768]{1,0:T(8,128)(2,1)}, f32[128,768]{1,0:T(8,128)}, f32[128,768]{1,0:T(8,128)}, f32[128,76...) custom-call(s32[1,128]{1,0:T(1,128)} %seg_ref.3, ...), custom_call_target="tpu_custom_call" | custom-call | flops 199999995904 | bytes 600000000 | tf_op jit(solution)/shard_map/pallas_call | solution.py:806
  32.5 2.5 %collective-permute-start.3 = (bf16[128,768]{1,0:T(8,128)(2,1)}, bf16[128,768]{1,0:T(8,128)(2,1)S(1)}, u32[]{:S(2)}, u32[]{:S(2)}) collective-permute-start(bf16[128,768]{1,0:T(8,128)(2,1)} %get-tuple-element.151.x_ref.refs_0_), channel_id=1, source_target_pairs={{0,1},{1,0},{2,3},{3,2},{4,5},{5,4},{6,7},{7,6},{8,9},{9,8},{10,11... | collective-permute-start | bytes 589832 | tf_op jit(solution)/shard_map/ppermute | solution.py:824
  35.0 2.2 %shard_map.366 = (bf16[128,512]{1,0:T(8,128)(2,1)S(1)}, bf16[128,512]{1,0:T(8,128)(2,1)S(1)}, bf16[128,512]{1,0:T(8,128)(2,1)S(1)}, bf16[128,768]{1,0:T(8,128)(2,1)S(1)}) custom-call(bf16[128,768]{1,0:T(8,128)(2,1)} %get-tuple-element.151.x_ref.refs_0_, bf16[128,768]{1,0:T(8,128)(2,1)S(1)} %bitcast.21, bf16[768,512]{1,0:T(8,128)(2,1)S(1)} %copy-done.9, ...), custom_call_target="tpu_custom_call" | custom-call | flops 15000000512 | bytes 45000000 | tf_op jit(solution)/shard_map/pallas_call | solution.py:806
  37.3 6.3 %collective-permute-done.5.x_ref.refs_2_ = bf16[128,768]{1,0:T(8,128)(2,1)S(1)} collective-permute-done((bf16[128,768]{1,0:T(8,128)(2,1)}, bf16[128,768]{1,0:T(8,128)(2,1)S(1)}, u32[]{:S(2)}, u32[]{:S(2)}) %collective-permute-start.5) | collective-permute-done | bytes 196640 | tf_op jit(solution)/shard_map/ppermute | solution.py:824
  45.9 3.1 %collective-permute-start.7 = (bf16[128,768]{1,0:T(8,128)(2,1)S(1)}, bf16[128,768]{1,0:T(8,128)(2,1)S(1)}, u32[]{:S(2)}, u32[]{:S(2)}) collective-permute-start(bf16[128,768]{1,0:T(8,128)(2,1)S(1)} %collective-permute-done.5.x_ref.refs_2_), channel_id=1, source_target_pairs={{0,1},{1,0},{2,3},{3,2},{4,5},{5,4},{6,7},{7,6},{8,9},{9,8},{10,11... | collective-permute-start | bytes 589832 | tf_op jit(solution)/shard_map/ppermute | solution.py:824
  49.0 2.2 %shard_map.367 = (bf16[128,512]{1,0:T(8,128)(2,1)S(1)}, bf16[128,512]{1,0:T(8,128)(2,1)S(1)}, bf16[128,512]{1,0:T(8,128)(2,1)S(1)}, bf16[128,768]{1,0:T(8,128)(2,1)S(1)}) custom-call(bf16[128,768]{1,0:T(8,128)(2,1)S(1)} %collective-permute-done.3.x_ref.refs_1_, bf16[128,768]{1,0:T(8,128)(2,1)} %collective-permute-done.c_ref.refs_5_, ...), custom_call_target="tpu_custom_call" | custom-call | flops 15000000512 | bytes 45000000 | tf_op jit(solution)/shard_map/pallas_call | solution.py:806
  51.3 6.9 %collective-permute-done.7.x_ref.refs_3_ = bf16[128,768]{1,0:T(8,128)(2,1)S(1)} collective-permute-done((bf16[128,768]{1,0:T(8,128)(2,1)S(1)}, bf16[128,768]{1,0:T(8,128)(2,1)S(1)}, u32[]{:S(2)}, u32[]{:S(2)}) %collective-permute-start.7) | collective-permute-done | bytes 196640 | tf_op jit(solution)/shard_map/ppermute | solution.py:824
  58.2 2.2 %shard_map.369 = (bf16[128,512]{1,0:T(8,128)(2,1)S(1)}, bf16[128,512]{1,0:T(8,128)(2,1)S(1)}, bf16[128,512]{1,0:T(8,128)(2,1)S(1)}, bf16[128,768]{1,0:T(8,128)(2,1)S(1)}) custom-call(bf16[128,768]{1,0:T(8,128)(2,1)S(1)} %collective-permute-done.7.x_ref.refs_3_, bf16[128,768]{1,0:T(8,128)(2,1)} %collective-permute-done.2.c_ref.refs_7_, ...), custom_call_target="tpu_custom_call" | custom-call | flops 15000000512 | bytes 45000000 | tf_op jit(solution)/shard_map/pallas_call | solution.py:806
  60.4 2.4 %collective-permute-start.8 = (bf16[128,768]{1,0:T(8,128)(2,1)S(1)}, bf16[128,768]{1,0:T(8,128)(2,1)S(1)}, u32[]{:S(2)}, u32[]{:S(2)}) collective-permute-start(bf16[128,768]{1,0:T(8,128)(2,1)S(1)} %get-tuple-element.159), channel_id=1, source_target_pairs={{0,3},{1,2},{2,1},{3,0},{4,7},{5,6},{6,5},{7,4},{8,11},{9,10},{10,... | collective-permute-start | bytes 589832 | tf_op jit(solution)/shard_map/ppermute | solution.py:824
  62.8 4.9 %shard_map.370 = (bf16[3,768,256]{2,1,0:T(8,128)(2,1)S(1)}, bf16[3,768,256]{2,1,0:T(8,128)(2,1)S(1)}, bf16[128,768]{1,0:T(8,128)(2,1)S(1)}, bf16[128,768]{1,0:T(...) custom-call(s32[3]{0:T(128)S(1)} %pad_add_fusion.ids_smem, ...), custom_call_target="tpu_custom_call" | custom-call | flops 40000000000 | bytes 120000000 | tf_op jit(solution)/shard_map/pallas_call | solution.py:806
  71.2 2.8 %shard_map.372 = (f32[128,768]{1,0:T(8,128)S(1)}, bf16[2304,128]{1,0:T(8,128)(2,1)S(1)}, bf16[2304,128]{1,0:T(8,128)(2,1)}, bf16[2304,128]{1,0:T(8,128)(2,1)}, bf16[2304,128]{1,0:T(8,128)(2,1)}) custom-call(s32[3]{0:T(128)S(1)} %pad_add_fusion.ids_smem, bf16[2,128,768]{2,1,0:T(8,128)(2,1)S(1)} %get-tuple-element.180.mine_ref.pair_ref, ...), custom_call_target="tpu_custom_call" | custom-call | flops 20000000000 | bytes 60000000 | tf_op jit(solution)/shard_map/pallas_call | solution.py:806
  80.9 2.4 %collective-permute-start.17 = (bf16[128,768]{1,0:T(8,128)(2,1)}, bf16[128,768]{1,0:T(8,128)(2,1)}, u32[]{:S(2)}, u32[]{:S(2)}) collective-permute-start(bf16[128,768]{1,0:T(8,128)(2,1)} %get-tuple-element.219), channel_id=1, source_target_pairs={{0,3},{1,2},{2,1},{3,0},{4,7},{5,6},{6,5},{7,4},{8,11},{9,10},{10,... | collective-permute-start | bytes 589832 | tf_op jit(solution)/shard_map/ppermute | solution.py:824
  83.6 22.2 %shard_map.373 = (bf16[3,128,768]{2,1,0:T(8,128)(2,1)S(1)}, bf16[128,128]{1,0:T(8,128)(2,1)S(1)}, bf16[768,256]{1,0:T(8,128)(2,1)S(1)}, bf16[768,256]{1,0:T(8,128)(2,1)S(1)}, f32[32,256]{1,0:T(8,128)S(1)}) custom-call(s32[3]{0:T(128)S(1)} %pad_add_fusion.ids_smem, s32[1,128]{1,0:T(1,128)S(1)} %copy-done.18, s32[1,128]{1,0:T(1,128)S(1)} %copy-done.18, ...), custom_call_target="tpu_custom_call" | custom-call | flops 219999993856 | bytes 660000000 | tf_op jit(solution)/shard_map/pallas_call | solution.py:806
  106.4 2.2 %shard_map.374 = (f32[1,128,768]{2,1,0:T(8,128)}, bf16[128,256]{1,0:T(8,128)(2,1)S(1)}) custom-call(bf16[3,128,768]{2,1,0:T(8,128)(2,1)S(1)} %get-tuple-element.251.triple_ref, bf16[128,128]{1,0:T(8,128)(2,1)S(1)} %get-tuple-element.225.gr_ref, bf16[2,128,768]{2,1,0:T(8,128)(2,1)S(1)} %get-tuple-element.180.mine_ref.pair_ref, ...), custom_call_target="tpu_custom_call" | custom-call | flops 20000000000 | bytes 60000000 | tf_op jit(solution)/shard_map/pallas_call | solution.py:806
  122.7 4.9 %collective-permute-done.33.refs_1_ = bf16[1728,128]{1,0:T(8,128)(2,1)S(1)} collective-permute-done((bf16[1728,128]{1,0:T(8,128)(2,1)S(1)}, bf16[1728,128]{1,0:T(8,128)(2,1)S(1)}, u32[]{:S(2)}, u32[]{:S(2)}) %collective-permute-start.33) | collective-permute-done | bytes 442400 | tf_op jit(solution)/shard_map/ppermute | solution.py:824
  128.9 9.7 %collective-permute-done.34.refs_2_ = bf16[1728,128]{1,0:T(8,128)(2,1)S(1)} collective-permute-done((bf16[1728,128]{1,0:T(8,128)(2,1)S(1)}, bf16[1728,128]{1,0:T(8,128)(2,1)S(1)}, u32[]{:S(2)}, u32[]{:S(2)}) %collective-permute-start.34) | collective-permute-done | bytes 442400 | tf_op jit(solution)/shard_map/ppermute | solution.py:824
  144.6 5.2 %collective-permute-done.23 = bf16[736,128]{1,0:T(8,128)(2,1)S(1)} collective-permute-done((bf16[736,128]{1,0:T(8,128)(2,1)S(1)}, bf16[736,128]{1,0:T(8,128)(2,1)S(1)}, u32[]{:S(2)}, u32[]{:S(2)}) %collective-permute-start.23) | collective-permute-done | bytes 188448 | tf_op jit(solution)/shard_map/ppermute | solution.py:824
  149.9 2.6 %collective-permute-start.36 = (bf16[432,128]{1,0:T(8,128)(2,1)S(1)}, bf16[432,128]{1,0:T(8,128)(2,1)S(1)}, u32[]{:S(2)}, u32[]{:S(2)}) collective-permute-start(bf16[432,128]{1,0:T(8,128)(2,1)S(1)} %get-tuple-element.257), channel_id=1, source_target_pairs={{0,1},{1,0},{2,3},{3,2},{4,5},{5,4},{6,7},{7,6},{8,9},{9,8},{10,11... | collective-permute-start | bytes 331784 | tf_op jit(solution)/shard_map/ppermute | solution.py:824
  157.7 4.6 %collective-permute-done.37 = bf16[432,128]{1,0:T(8,128)(2,1)S(1)} collective-permute-done((bf16[432,128]{1,0:T(8,128)(2,1)S(1)}, bf16[432,128]{1,0:T(8,128)(2,1)S(1)}, u32[]{:S(2)}, u32[]{:S(2)}) %collective-permute-start.37) | collective-permute-done | bytes 110624 | tf_op jit(solution)/shard_map/ppermute | solution.py:824
  165.6 4.3 %collective-permute-done.26.refs_2_ = bf16[736,128]{1,0:T(8,128)(2,1)S(1)} collective-permute-done((bf16[736,128]{1,0:T(8,128)(2,1)S(1)}, bf16[736,128]{1,0:T(8,128)(2,1)S(1)}, u32[]{:S(2)}, u32[]{:S(2)}) %collective-permute-start.26) | collective-permute-done | bytes 188448 | tf_op jit(solution)/shard_map/ppermute | solution.py:824
  178.6 2.5 %shard_map.377 = (f32[192,768]{1,0:T(8,128)}, f32[192,768]{1,0:T(8,128)}, f32[768,256]{1,0:T(8,128)}, f32[768,256]{1,0:T(8,128)}, f32[12,192]{1,0:T(8,128)}, /*i...) custom-call(s32[3]{0:T(128)S(1)} %pad_add_fusion.ids_smem, ...), custom_call_target="tpu_custom_call" | custom-call | flops 30000001024 | bytes 90000000 | tf_op jit(solution)/shard_map/pallas_call | solution.py:806
  184.4 3.3 %shard_map.381 = (f32[768,512]{1,0:T(8,128)}, f32[768,512]{1,0:T(8,128)}, f32[512,768]{1,0:T(8,128)}) custom-call(s32[3]{0:T(128)S(1)} %pad_add_fusion.ids_smem, bf16[1152,128]{1,0:T(8,128)(2,1)S(1)} %get-tuple-element.274.refs_0_, bf16[1152,128]{1,0:T(8,128)(2,1)S(1)} %collective-permute-done.46.refs_1_, ...), custom_call_target="tpu_custom_call" | custom-call | flops 30000001024 | bytes 90000000 | tf_op jit(solution)/shard_map/pallas_call | solution.py:806
  (189 shorter events, 60.9 us)
Async XLA Ops:
  0.7 30.2 %collective-permute-start = (bf16[128,768]{1,0:T(8,128)(2,1)}, bf16[128,768]{1,0:T(8,128)(2,1)}, u32[]{:S(2)}, u32[]{:S(2)}) collective-permute-start(bf16[128,768]{1,0:T(8,128)(2,1)} %bitcast.18), channel_id=1, source_target_pairs={{0,1},{1,0},{2,3},{3,2},{4,5},{5,4},{6,7},{7,6},{8,9},{9,8},{10,11... | collective-permute-start | bytes 589832 | tf_op jit(solution)/shard_map/ppermute | solution.py:824
  3.7 27.1 %collective-permute-start.1 = (bf16[128,768]{1,0:T(8,128)(2,1)}, bf16[128,768]{1,0:T(8,128)(2,1)}, u32[]{:S(2)}, u32[]{:S(2)}) collective-permute-start(bf16[128,768]{1,0:T(8,128)(2,1)} %bitcast.19), channel_id=1, source_target_pairs={{0,2},{1,3},{2,0},{3,1},{4,6},{5,7},{6,4},{7,5},{8,10},{9,11},{10,... | collective-permute-start | bytes 589832 | tf_op jit(solution)/shard_map/ppermute | solution.py:824
  6.3 24.5 %collective-permute-start.2 = (bf16[128,768]{1,0:T(8,128)(2,1)}, bf16[128,768]{1,0:T(8,128)(2,1)}, u32[]{:S(2)}, u32[]{:S(2)}) collective-permute-start(bf16[128,768]{1,0:T(8,128)(2,1)} %bitcast.20), channel_id=1, source_target_pairs={{0,3},{1,2},{2,1},{3,0},{4,7},{5,6},{6,5},{7,4},{8,11},{9,10},{10,... | collective-permute-start | bytes 589832 | tf_op jit(solution)/shard_map/ppermute | solution.py:824
  30.7 38.7 %collective-permute-start.9 = (bf16[2,128,768]{2,1,0:T(8,128)(2,1)S(1)}, bf16[2,128,768]{2,1,0:T(8,128)(2,1)S(1)}, u32[]{:S(2)}, u32[]{:S(2)}) collective-permute-start(bf16[2,128,768]{2,1,0:T(8,128)(2,1)S(1)} %get-tuple-element.180.mine_ref.pair_ref), channel_id=1, source_target_pairs={{0,4},{4,0},{8,12},{12,8},{16,20},{20,16},{24,28},{28,24},{1,5},{5... | collective-permute-start | bytes 1179656 | tf_op jit(solution)/shard_map/ppermute | solution.py:824
  30.8 12.8 %collective-permute-start.5 = (bf16[128,768]{1,0:T(8,128)(2,1)}, bf16[128,768]{1,0:T(8,128)(2,1)S(1)}, u32[]{:S(2)}, u32[]{:S(2)}) collective-permute-start(bf16[128,768]{1,0:T(8,128)(2,1)} %get-tuple-element.151.x_ref.refs_0_), channel_id=1, source_target_pairs={{0,2},{1,3},{2,0},{3,1},{4,6},{5,7},{6,4},{7,5},{8,10},{9,11},{10,... | collective-permute-start | bytes 589832 | tf_op jit(solution)/shard_map/ppermute | solution.py:824
  32.5 16.5 %collective-permute-start.3 = (bf16[128,768]{1,0:T(8,128)(2,1)}, bf16[128,768]{1,0:T(8,128)(2,1)S(1)}, u32[]{:S(2)}, u32[]{:S(2)}) collective-permute-start(bf16[128,768]{1,0:T(8,128)(2,1)} %get-tuple-element.151.x_ref.refs_0_), channel_id=1, source_target_pairs={{0,1},{1,0},{2,3},{3,2},{4,5},{5,4},{6,7},{7,6},{8,9},{9,8},{10,11... | collective-permute-start | bytes 589832 | tf_op jit(solution)/shard_map/ppermute | solution.py:824
  45.9 21.9 %collective-permute-start.6 = (bf16[128,768]{1,0:T(8,128)(2,1)S(1)}, bf16[128,768]{1,0:T(8,128)(2,1)S(1)}, u32[]{:S(2)}, u32[]{:S(2)}) collective-permute-start(bf16[128,768]{1,0:T(8,128)(2,1)S(1)} %get-tuple-element.157), channel_id=1, source_target_pairs={{0,2},{1,3},{2,0},{3,1},{4,6},{5,7},{6,4},{7,5},{8,10},{9,11},{10,... | collective-permute-start | bytes 589832 | tf_op jit(solution)/shard_map/ppermute | solution.py:824
  45.9 12.3 %collective-permute-start.7 = (bf16[128,768]{1,0:T(8,128)(2,1)S(1)}, bf16[128,768]{1,0:T(8,128)(2,1)S(1)}, u32[]{:S(2)}, u32[]{:S(2)}) collective-permute-start(bf16[128,768]{1,0:T(8,128)(2,1)S(1)} %collective-permute-done.5.x_ref.refs_2_), channel_id=1, source_target_pairs={{0,1},{1,0},{2,3},{3,2},{4,5},{5,4},{6,7},{7,6},{8,9},{9,8},{10,11... | collective-permute-start | bytes 589832 | tf_op jit(solution)/shard_map/ppermute | solution.py:824
  51.3 16.5 %collective-permute-start.4 = (bf16[128,768]{1,0:T(8,128)(2,1)S(1)}, bf16[128,768]{1,0:T(8,128)(2,1)S(1)}, u32[]{:S(2)}, u32[]{:S(2)}) collective-permute-start(bf16[128,768]{1,0:T(8,128)(2,1)S(1)} %get-tuple-element.155), channel_id=1, source_target_pairs={{0,1},{1,0},{2,3},{3,2},{4,5},{5,4},{6,7},{7,6},{8,9},{9,8},{10,11... | collective-permute-start | bytes 589832 | tf_op jit(solution)/shard_map/ppermute | solution.py:824
  75.6 30.8 %collective-permute-start.12 = (bf16[2304,128]{1,0:T(8,128)(2,1)}, bf16[2304,128]{1,0:T(8,128)(2,1)}, u32[]{:S(2)}, u32[]{:S(2)}) collective-permute-start(bf16[2304,128]{1,0:T(8,128)(2,1)} %get-tuple-element.213), channel_id=1, source_target_pairs={{0,8},{4,12},{8,0},{12,4},{16,24},{20,28},{24,16},{28,20},{1,9},{5... | collective-permute-start | bytes 1769480 | tf_op jit(solution)/shard_map/ppermute | solution.py:824
  77.1 29.3 %collective-permute-start.13 = (bf16[2304,128]{1,0:T(8,128)(2,1)}, bf16[2304,128]{1,0:T(8,128)(2,1)}, u32[]{:S(2)}, u32[]{:S(2)}) collective-permute-start(bf16[2304,128]{1,0:T(8,128)(2,1)} %get-tuple-element.214), channel_id=1, source_target_pairs={{0,16},{4,20},{8,24},{12,28},{16,0},{20,4},{24,8},{28,12},{1,17},{... | collective-permute-start | bytes 1769480 | tf_op jit(solution)/shard_map/ppermute | solution.py:824
  78.7 27.7 %collective-permute-start.14 = (bf16[2304,128]{1,0:T(8,128)(2,1)}, bf16[2304,128]{1,0:T(8,128)(2,1)}, u32[]{:S(2)}, u32[]{:S(2)}) collective-permute-start(bf16[2304,128]{1,0:T(8,128)(2,1)} %get-tuple-element.215), channel_id=1, source_target_pairs={{0,24},{4,28},{8,16},{12,20},{16,8},{20,12},{24,0},{28,4},{1,25},{... | collective-permute-start | bytes 1769480 | tf_op jit(solution)/shard_map/ppermute | solution.py:824
  79.0 26.8 %collective-permute-start.16 = (bf16[128,768]{1,0:T(8,128)(2,1)}, bf16[128,768]{1,0:T(8,128)(2,1)}, u32[]{:S(2)}, u32[]{:S(2)}) collective-permute-start(bf16[128,768]{1,0:T(8,128)(2,1)} %get-tuple-element.218), channel_id=1, source_target_pairs={{0,2},{1,3},{2,0},{3,1},{4,6},{5,7},{6,4},{7,5},{8,10},{9,11},{10,... | collective-permute-start | bytes 589832 | tf_op jit(solution)/shard_map/ppermute | solution.py:824
  80.9 25.0 %collective-permute-start.17 = (bf16[128,768]{1,0:T(8,128)(2,1)}, bf16[128,768]{1,0:T(8,128)(2,1)}, u32[]{:S(2)}, u32[]{:S(2)}) collective-permute-start(bf16[128,768]{1,0:T(8,128)(2,1)} %get-tuple-element.219), channel_id=1, source_target_pairs={{0,3},{1,2},{2,1},{3,0},{4,7},{5,6},{6,5},{7,4},{8,11},{9,10},{10,... | collective-permute-start | bytes 589832 | tf_op jit(solution)/shard_map/ppermute | solution.py:824
  114.5 13.1 %collective-permute-start.33 = (bf16[1728,128]{1,0:T(8,128)(2,1)S(1)}, bf16[1728,128]{1,0:T(8,128)(2,1)S(1)}, u32[]{:S(2)}, u32[]{:S(2)}) collective-permute-start(bf16[1728,128]{1,0:T(8,128)(2,1)S(1)} %get-tuple-element.253), channel_id=1, source_target_pairs={{0,8},{4,12},{8,0},{12,4},{16,24},{20,28},{24,16},{28,20},{1,9},{5... | collective-permute-start | bytes 1327112 | tf_op jit(solution)/shard_map/ppermute | solution.py:824
  116.0 22.6 %collective-permute-start.34 = (bf16[1728,128]{1,0:T(8,128)(2,1)S(1)}, bf16[1728,128]{1,0:T(8,128)(2,1)S(1)}, u32[]{:S(2)}, u32[]{:S(2)}) collective-permute-start(bf16[1728,128]{1,0:T(8,128)(2,1)S(1)} %get-tuple-element.254), channel_id=1, source_target_pairs={{0,16},{4,20},{8,24},{12,28},{16,0},{20,4},{24,8},{28,12},{1,17},{... | collective-permute-start | bytes 1327112 | tf_op jit(solution)/shard_map/ppermute | solution.py:824
  117.4 22.6 %collective-permute-start.35 = (bf16[1728,128]{1,0:T(8,128)(2,1)S(1)}, bf16[1728,128]{1,0:T(8,128)(2,1)S(1)}, u32[]{:S(2)}, u32[]{:S(2)}) collective-permute-start(bf16[1728,128]{1,0:T(8,128)(2,1)S(1)} %get-tuple-element.255), channel_id=1, source_target_pairs={{0,24},{4,28},{8,16},{12,20},{16,8},{20,12},{24,0},{28,4},{1,25},{... | collective-permute-start | bytes 1327112 | tf_op jit(solution)/shard_map/ppermute | solution.py:824
  120.8 31.7 %collective-permute-start.46 = (bf16[1152,128]{1,0:T(8,128)(2,1)S(1)}, bf16[1152,128]{1,0:T(8,128)(2,1)S(1)}, u32[]{:S(2)}, u32[]{:S(2)}) collective-permute-start(bf16[1152,128]{1,0:T(8,128)(2,1)S(1)} %get-tuple-element.274.refs_0_), channel_id=1, source_target_pairs={{0,8},{4,12},{8,0},{12,4},{16,24},{20,28},{24,16},{28,20},{1,9},{5... | collective-permute-start | bytes 884744 | tf_op jit(solution)/shard_map/ppermute | solution.py:824
  121.8 30.8 %collective-permute-start.47 = (bf16[1152,128]{1,0:T(8,128)(2,1)S(1)}, bf16[1152,128]{1,0:T(8,128)(2,1)S(1)}, u32[]{:S(2)}, u32[]{:S(2)}) collective-permute-start(bf16[1152,128]{1,0:T(8,128)(2,1)S(1)} %get-tuple-element.274.refs_0_), channel_id=1, source_target_pairs={{0,16},{4,20},{8,24},{12,28},{16,0},{20,4},{24,8},{28,12},{1,17},{... | collective-permute-start | bytes 884744 | tf_op jit(solution)/shard_map/ppermute | solution.py:824
  127.6 15.3 %collective-permute-start.22 = (bf16[736,128]{1,0:T(8,128)(2,1)S(1)}, bf16[736,128]{1,0:T(8,128)(2,1)S(1)}, u32[]{:S(2)}, u32[]{:S(2)}) collective-permute-start(bf16[736,128]{1,0:T(8,128)(2,1)S(1)} %get-tuple-element.247), channel_id=1, source_target_pairs={{0,1},{1,0},{2,3},{3,2},{4,5},{5,4},{6,7},{7,6},{8,9},{9,8},{10,11... | collective-permute-start | bytes 565256 | tf_op jit(solution)/shard_map/ppermute | solution.py:824
  138.6 11.2 %collective-permute-start.23 = (bf16[736,128]{1,0:T(8,128)(2,1)S(1)}, bf16[736,128]{1,0:T(8,128)(2,1)S(1)}, u32[]{:S(2)}, u32[]{:S(2)}) collective-permute-start(bf16[736,128]{1,0:T(8,128)(2,1)S(1)} %get-tuple-element.248), channel_id=1, source_target_pairs={{0,2},{1,3},{2,0},{3,1},{4,6},{5,7},{6,4},{7,5},{8,10},{9,11},{10,... | collective-permute-start | bytes 565256 | tf_op jit(solution)/shard_map/ppermute | solution.py:824
  142.9 22.1 %collective-permute-start.48 = (bf16[1152,128]{1,0:T(8,128)(2,1)S(1)}, bf16[1152,128]{1,0:T(8,128)(2,1)S(1)}, u32[]{:S(2)}, u32[]{:S(2)}) collective-permute-start(bf16[1152,128]{1,0:T(8,128)(2,1)S(1)} %get-tuple-element.274.refs_0_), channel_id=1, source_target_pairs={{0,24},{4,28},{8,16},{12,20},{16,8},{20,12},{24,0},{28,4},{1,25},{... | collective-permute-start | bytes 884744 | tf_op jit(solution)/shard_map/ppermute | solution.py:824
  149.9 20.5 %collective-permute-start.49 = (bf16[1152,128]{1,0:T(8,128)(2,1)S(1)}, bf16[1152,128]{1,0:T(8,128)(2,1)S(1)}, u32[]{:S(2)}, u32[]{:S(2)}) collective-permute-start(bf16[1152,128]{1,0:T(8,128)(2,1)S(1)} %get-tuple-element.274.refs_0_), channel_id=1, source_target_pairs={{0,4},{4,0},{8,12},{12,8},{16,20},{20,16},{24,28},{28,24},{1,5},{5... | collective-permute-start | bytes 884744 | tf_op jit(solution)/shard_map/ppermute | solution.py:824
  173.4 10.4 %collective-permute-start.50 = (bf16[1152,128]{1,0:T(8,128)(2,1)S(1)}, bf16[1152,128]{1,0:T(8,128)(2,1)S(1)}, u32[]{:S(2)}, u32[]{:S(2)}) collective-permute-start(bf16[1152,128]{1,0:T(8,128)(2,1)S(1)} %collective-permute-done.46.refs_1_), channel_id=1, source_target_pairs={{0,4},{4,0},{8,12},{12,8},{16,20},{20,16},{24,28},{28,24},{1,5},{5... | collective-permute-start | bytes 884744 | tf_op jit(solution)/shard_map/ppermute | solution.py:824
  (70 other events, 848.5 us)

commit v3 on v2

--- a/solution.py
+++ b/solution.py
@@ -8,6 +8,7 @@
 from jax.sharding import PartitionSpec as P
 
 MB = 16
+GROUP = 3
 EPSILON = 1e-06
 BASE_RATE = 0.1
 F32 = jnp.float32
@@ -36,6 +37,10 @@
 
 def sum_rows(values):
     return jnp.sum(values, 0, keepdims=True)
+
+
+def row_of(ref):
+    return ref[...].astype(F32).reshape(1, ref.shape[0])
 
 
 def column_of(row):
@@ -60,7 +65,7 @@
     seg_ref,
     live_ref,
     tok_ref,
-    gains_ref,
+    gain1_ref,
     wq_hbm,
     wk_hbm,
     wv_hbm,
@@ -74,6 +79,7 @@
     ig_ref,
     ib_ref,
     wo_hbm,
+    gain2_ref,
     pair_ref,
     normed_two_ref,
     *refs,
@@ -107,7 +113,7 @@
     length, width = tok_ref.shape[1], tok_ref.shape[2]
     copies = [
         pltpu.make_async_copy(w, weights_s.at[i], sems.at[i])
-        for i, w in enumerate((wq_hbm, wk_hbm, wv_hbm, wg_hbm, wo_hbm))
+        for i, w in enumerate((wk_hbm, wv_hbm, wq_hbm, wg_hbm, wo_hbm))
     ]
     for copy in copies:
         copy.start()
@@ -123,7 +129,7 @@
     blocks = length // MB
     tok = tok_ref[0].astype(F32)
     spread = lax.rsqrt(mean_last(tok * tok) + EPSILON)
-    normed = low(tok * spread * gains_ref[0:1].astype(F32))
+    normed = low(tok * spread * row_of(gain1_ref))
     pair_ref[0] = normed
     seg_row = seg_ref[...].astype(F32)
     live = column_of(live_ref[...].astype(F32))
@@ -135,52 +141,38 @@
     fcol_ref[...] = jnp.zeros(fcol_ref.shape, F32)
     fcol_ref[:, 0:heads] = rates * (1.0 - sig)
     erow_ref[...] = jnp.transpose(ecol_ref[...])[0 : erow_ref.shape[0]]
-    for i, to in enumerate((q_s, k_s, v_s)):
+
+    def project(i, to):
         copies[i].wait()
         whole = dot(normed, weights_s[i])
         for h in range(heads):
             to[h] = whole[:, h * head : (h + 1) * head]
+
+    project(0, k_s)
+    project(1, v_s)
     b1f[...] = b1_ref[...].astype(F32)
     b2f[...] = b2_ref[...].astype(F32)
     igf[...] = ig_ref[...].astype(F32)
     ibf[...] = ib_ref[...].astype(F32)
     for h in range(heads):
-        qk_ref[h, 0:length] = low(q_s[h])
         qk_ref[h, length : 2 * length] = low(k_s[h])
 
     def step(b, carry):
         here = pl.multiple_of(b * MB, MB)
         before = jnp.maximum(here - 1, 0)
         fresh = (b == 0) | (seg_smem[0, here] != seg_smem[0, before])
-
-        @pl.when(fresh)
-        def _():
-            for h in range(heads):
-                first = w1_ref[h]
-                second = w2t_ref[h]
-                w1_s[h] = first.astype(F32)
-                w1b_s[h] = first
-                w2_s[h] = second.astype(F32)
-                w2s_ref[b, h] = second
-                b1_s[h] = b1f[h : h + 1]
-                b2_s[h] = b2f[h : h + 1]
-
-        @pl.when(jnp.logical_not(fresh))
-        def _():
-            for h in range(heads):
-                w2s_ref[b, h] = low(w2_s[h])
 
         ds = pl.ds(here, MB)
         rng = range(heads)
         k = [k_s[h, ds, :] for h in rng]
         v = [v_s[h, ds, :] for h in rng]
         e = [ecol_ref[ds, h : h + 1] for h in rng]
-        w1 = [w1b_s[h] for h in rng]
-        w2 = [w2s_ref[b, h] for h in rng]
-        w1f = [w1_s[h] for h in rng]
-        w2f = [w2_s[h] for h in rng]
-        b1 = [b1_s[h] for h in rng]
-        b2 = [b2_s[h] for h in rng]
+        w1f = [jnp.where(fresh, w1_ref[h].astype(F32), w1_s[h]) for h in rng]
+        w2f = [jnp.where(fresh, w2t_ref[h].astype(F32), w2_s[h]) for h in rng]
+        w1 = [low(w1f[h]) for h in rng]
+        w2 = [low(w2f[h]) for h in rng]
+        b1 = [jnp.where(fresh, b1f[h : h + 1], b1_s[h]) for h in rng]
+        b2 = [jnp.where(fresh, b2f[h : h + 1], b2_s[h]) for h in rng]
         g = [igf[h : h + 1] for h in rng]
         gb = [ibf[h : h + 1] for h in rng]
         parts = [gelu_parts(dot(low(k[h]), w1[h]) + b1[h]) for h in rng]
@@ -203,7 +195,7 @@
         for h in rng:
             w1n = w1f[h] - up1[h]
             w1_s[h] = w1n
-            w1b_s[h] = low(w1n)
+            w2s_ref[b, h] = w2[h]
             w2_s[h] = w2f[h] - up2[h]
             b1_s[h] = b1[h] - sum_rows(d1[h] * e[h])
             b2_s[h] = b2[h] - sum_rows(ed2[h])
@@ -211,37 +203,54 @@
             slope1_ref[h, ds, :] = low(parts[h][1])
             curve1_ref[h, ds, :] = low(back[h] * parts[h][2])
             d1_ref[h, ds, :] = d1b[h]
-            d2_ref[h, ds, :] = d2[h]
-            n_ref[h, ds, :] = n[h]
-            s_ref[h, ds, :] = s[h]
-            fit_ref[h, ds, :] = fit[h]
+            d2_ref[h, ds, :] = low(d2[h])
+            n_ref[h, ds, :] = low(n[h])
+            s_ref[ds, h : h + 1] = s[h]
+            fit_ref[h, ds, :] = low(fit[h])
         return carry
 
-    save(3, 4, 5, 6)
-    lax.fori_loop(0, blocks, step, 0)
+    save(4, 5, 6)
+    lax.fori_loop(0, blocks, step, 0, unroll=4)
     save(7, 8, 10, 11, 12, 13, 14, 15)
+    project(2, q_s)
+    for h in range(heads):
+        qk_ref[h, 0:length] = low(q_s[h])
+    save(3)
     inclusive, _ = segment_masks(seg_row)
-    for h in range(heads):
-        queries = qk_ref[h, 0:length]
-        keys = qk_ref[h, length : 2 * length]
-        key_act = act_ref[h, length : 2 * length]
-        er = erow_ref[h : h + 1, :]
-        p1 = (dot(queries, keys, 1, 1) + 1.0) * inclusive
-        p1_ref[h] = low(p1)
-        zq1 = dot(queries, w1_ref[h]) + b1f[h : h + 1] - dot(low(p1 * er), d1_ref[h])
-        aq, slope, _ = gelu_parts(zq1)
-        aqb = low(aq)
-        act_ref[h, 0:length] = aqb
-        slopeq_ref[h] = low(slope)
-        p2 = (dot(aqb, key_act, 1, 1) + 1.0) * inclusive
-        p2_ref[h] = low(p2)
-        zq2 = dot(aqb, w2t_ref[h], 1, 1) + b2f[h : h + 1] - dot(low(p2 * er), low(d2_ref[h]))
-        c = zq2 - mean_last(zq2)
-        s = lax.rsqrt(mean_last(c * c) + EPSILON)
-        n = c * s
-        nq_ref[h] = n
-        sq_ref[h] = s
-        out_s[:, h * head : (h + 1) * head] = q_s[h] + igf[h : h + 1] * n + ibf[h : h + 1]
+    for start in range(0, heads, GROUP):
+        rng = range(start, start + GROUP)
+        every = range(GROUP)
+        queries = [qk_ref[h, 0:length] for h in rng]
+        keys = [qk_ref[h, length : 2 * length] for h in rng]
+        key_act = [act_ref[h, length : 2 * length] for h in rng]
+        er = [erow_ref[h : h + 1, :] for h in rng]
+        p1 = [(dot(queries[i], keys[i], 1, 1) + 1.0) * inclusive for i in every]
+        zq1 = [
+            dot(queries[i], w1_ref[h]) + b1f[h : h + 1] - dot(low(p1[i] * er[i]), d1_ref[h])
+            for i, h in enumerate(rng)
+        ]
+        parts = [gelu_parts(x) for x in zq1]
+        aq = [low(x[0]) for x in parts]
+        p2 = [(dot(aq[i], key_act[i], 1, 1) + 1.0) * inclusive for i in every]
+        zq2 = [
+            dot(aq[i], w2t_ref[h], 1, 1)
+            + b2f[h : h + 1]
+            - dot(low(p2[i] * er[i]), d2_ref[h])
+            for i, h in enumerate(rng)
+        ]
+        c = [z - mean_last(z) for z in zq2]
+        s = [lax.rsqrt(mean_last(x * x) + EPSILON) for x in c]
+        n = [c[i] * s[i] for i in every]
+        for i, h in enumerate(rng):
+            p1_ref[h] = low(p1[i])
+            p2_ref[h] = low(p2[i])
+            act_ref[h, 0:length] = aq[i]
+            slopeq_ref[h] = low(parts[i][1])
+            nq_ref[h] = low(n[i])
+            sq_ref[:, h : h + 1] = s[i]
+            out_s[:, h * head : (h + 1) * head] = (
+                q_s[h] + igf[h : h + 1] * n[i] + ibf[h : h + 1]
+            )
     save(9, 16, 17, 18, 19, 20)
     inner_out = out_s[...]
     copies[3].wait()
@@ -254,7 +263,7 @@
     resid = tok + dot(gated, weights_s[4])
     resid_ref[...] = resid
     spread_two = lax.rsqrt(mean_last(resid * resid) + EPSILON)
-    normed_two_ref[...] = low(resid * spread_two * gains_ref[1:2].astype(F32))
+    normed_two_ref[...] = low(resid * spread_two * row_of(gain2_ref))
     save(0, 1, 2)
     for copy in saves:
         copy.wait()
@@ -309,14 +318,14 @@
 
 def between_kernel(parts, *refs):
     pieces = refs[0:parts]
-    resid_ref, cot_ref, gains_ref, wo_ref, gelu_ref, slope_ref = refs[parts : parts + 6]
+    resid_ref, cot_ref, gain2_ref, wo_ref, gelu_ref, slope_ref = refs[parts : parts + 6]
     resid_grad_ref, go_ref, pair_ref, gain_grad_ref = refs[parts + 6 :]
     grad = pieces[0][...].astype(F32)
     for piece in pieces[1:]:
         grad = grad + piece[...].astype(F32)
     resid = resid_ref[...]
     spread = lax.rsqrt(mean_last(resid * resid) + EPSILON)
-    scaled = gains_ref[1:2].astype(F32) * grad
+    scaled = row_of(gain2_ref) * grad
     grad_resid = (
         cot_ref[0].astype(F32)
         + spread * scaled
@@ -384,22 +393,35 @@
     top, bottom = slice(0, length), slice(length, 2 * length)
     igf[...] = ig_ref[...].astype(F32)
     inclusive, strict = segment_masks(seg_ref[...].astype(F32))
-    for h in range(heads):
-        g = igf[h : h + 1]
-        er = erow_ref[h : h + 1, :]
-        go = go_ref[:, h * head : (h + 1) * head]
-        n = nq_ref[h]
-        x = go * g
-        hq2 = low(sq_ref[h] * (x - mean_last(x) - n * mean_last(x * n)))
-        hh2_s[h, top] = hq2
-        t2_s[h] = dot(p2_ref[h], hq2, 0, 0)
-        mix = low(-dot(hq2, low(d2_ref[h]), 1, 1) * (inclusive * er))
-        aq = act_ref[h, top]
-        gaq = dot(hq2, w2t_ref[h]) + dot(mix, act_ref[h, bottom])
-        ga_s[h] = dot(mix, aq, 0, 0)
-        hq1 = low(gaq * slopeq_ref[h].astype(F32))
-        hh1_s[h, top] = hq1
-        t1_s[h] = dot(p1_ref[h], hq1, 0, 0)
+    for first in range(0, heads, GROUP):
+        rng = range(first, first + GROUP)
+        every = range(GROUP)
+        g = [igf[h : h + 1] for h in rng]
+        weigh = [inclusive * erow_ref[h : h + 1, :] for h in rng]
+        n = [nq_ref[h].astype(F32) for h in rng]
+        x = [go_ref[:, h * head : (h + 1) * head] * igf[h : h + 1] for h in rng]
+        mx = [mean_last(x[i]) for i in every]
+        mxn = [mean_last(x[i] * n[i]) for i in every]
+        hq2 = [
+            low(sq_ref[:, h : h + 1] * (x[i] - mx[i] - n[i] * mxn[i]))
+            for i, h in enumerate(rng)
+        ]
+        aq = [act_ref[h, top] for h in rng]
+        ak = [act_ref[h, bottom] for h in rng]
+        t2 = [dot(p2_ref[h], hq2[i], 0, 0) for i, h in enumerate(rng)]
+        mix = [
+            low(-dot(hq2[i], d2_ref[h], 1, 1) * weigh[i]) for i, h in enumerate(rng)
+        ]
+        gaq = [dot(hq2[i], w2t_ref[h]) + dot(mix[i], ak[i]) for i, h in enumerate(rng)]
+        ga = [dot(mix[i], aq[i], 0, 0) for i in every]
+        hq1 = [low(gaq[i] * slopeq_ref[h].astype(F32)) for i, h in enumerate(rng)]
+        t1 = [dot(p1_ref[h], hq1[i], 0, 0) for i, h in enumerate(rng)]
+        for i, h in enumerate(rng):
+            hh2_s[h, top] = hq2[i]
+            t2_s[h] = t2[i]
+            ga_s[h] = ga[i]
+            hh1_s[h, top] = hq1[i]
+            t1_s[h] = t1[i]
     ge_s[...] = jnp.zeros(ge_s.shape, F32)
 
     def step(i, carry):
@@ -407,11 +429,6 @@
         here = pl.multiple_of(b * MB, MB)
         after = jnp.minimum(here + MB, length - 1)
         fresh = (i == 0) | (seg_smem[0, after] != seg_smem[0, after - 1])
-
-        @pl.when(fresh)
-        def _():
-            for ref in (gw1_s, gw1b_s, gb1_s, gw2_s, gw2b_s, gb2_s):
-                ref[...] = jnp.zeros(ref.shape, ref.dtype)
 
         ds = pl.ds(here, MB)
         ds_low = pl.ds(length + here, MB)
@@ -420,17 +437,17 @@
         act = [act_ref[h, ds_low, :] for h in rng]
         e = [ecol_ref[ds, h : h + 1] for h in rng]
         w2 = [w2s_ref[b, h] for h in rng]
-        gw1b = [gw1b_s[h] for h in rng]
-        gw2b = [gw2b_s[h] for h in rng]
-        gw1 = [gw1_s[h] for h in rng]
-        gw2 = [gw2_s[h] for h in rng]
-        gb1 = [gb1_s[h] for h in rng]
-        gb2 = [gb2_s[h] for h in rng]
+        gw1 = [jnp.where(fresh, 0.0, gw1_s[h]) for h in rng]
+        gw2 = [jnp.where(fresh, 0.0, gw2_s[h]) for h in rng]
+        gw1b = [low(x) for x in gw1]
+        gw2b = [low(x) for x in gw2]
+        gb1 = [jnp.where(fresh, 0.0, gb1_s[h]) for h in rng]
+        gb2 = [jnp.where(fresh, 0.0, gb2_s[h]) for h in rng]
         d1 = [d1_ref[h, ds, :].astype(F32) for h in rng]
-        d2 = [d2_ref[h, ds, :] for h in rng]
-        n = [n_ref[h, ds, :] for h in rng]
-        s = [s_ref[h, ds, :] for h in rng]
-        fit = [fit_ref[h, ds, :] for h in rng]
+        d2 = [d2_ref[h, ds, :].astype(F32) for h in rng]
+        n = [n_ref[h, ds, :].astype(F32) for h in rng]
+        s = [s_ref[ds, h : h + 1] for h in rng]
+        fit = [fit_ref[h, ds, :].astype(F32) for h in rng]
         slope = [slope1_ref[h, ds, :].astype(F32) for h in rng]
         curve = [curve1_ref[h, ds, :].astype(F32) for h in rng]
         g = [igf[h : h + 1] for h in rng]
@@ -465,9 +482,7 @@
             w1n = gw1[h] + up1[h]
             w2n = gw2[h] + up2[h]
             gw1_s[h] = w1n
-            gw1b_s[h] = low(w1n)
             gw2_s[h] = w2n
-            gw2b_s[h] = low(w2n)
             gb1_s[h] = gb1[h] + sum_rows(h1f[h])
             gb2_s[h] = gb2[h] + sum_rows(h2[h].astype(F32))
             u_s[h, ds, :] = u[h]
@@ -479,49 +494,54 @@
             )
         return carry
 
-    lax.fori_loop(0, blocks, step, 0)
+    lax.fori_loop(0, blocks, step, 0, unroll=4)
     small_ref[...] = jnp.zeros(small_ref.shape, F32)
     core = ids_smem[0]
     pad = small_ref.shape[0] // 2
-    for h in range(heads):
-        cols = slice(h * head, (h + 1) * head)
-        rows = slice(h * head, (h + 1) * head)
-        g = igf[h : h + 1]
-        er = erow_ref[h : h + 1, :]
-        hh1 = hh1_s[h]
-        hh2 = hh2_s[h]
-        qk = qk_ref[h]
-        keys = qk_ref[h, bottom]
-        both = dot(hh1, d1_ref[h], 1, 1)
-        mixq = low(-both[top] * (inclusive * er))
-        mixk = low(-both[bottom] * (strict * er))
-        direct = dot(hh1, w1_ref[h], 1, 1)
-        share = share_s[h]
-        spread = dot(mixq, qk_ref[h, top], 0, 0) + dot(mixk, keys, 0, 0)
-        go = go_ref[:, cols]
-        triple_ref[0, :, cols] = low(go + direct[top] + dot(mixq, keys))
-        triple_ref[1, :, cols] = low(g * share + direct[bottom] + dot(mixk, keys) + spread)
-        triple_ref[2, :, cols] = low(-g * share)
-        first = low(dot(qk, hh1, 0, 0))
-        second = low(dot(hh2, act_ref[h], 0, 0) + dot(low(d2_ref[h]), u_s[h], 0, 0))
-
-        @pl.when(core == 0)
-        def _(first=first, second=second, rows=rows):
-            kept_ref[rows] = first
-            sent_ref[rows] = second
-
-        @pl.when(core != 0)
-        def _(first=first, second=second, rows=rows):
-            kept_ref[rows] = second
-            sent_ref[rows] = first
-
-        small_ref[h : h + 1] = sum_rows(hh1.astype(F32))
-        row = slice(pad + h, pad + h + 1)
-        small_ref[row, 0:head] = sum_rows(hh2.astype(F32))
-        small_ref[row, head : 2 * head] = sum_rows(go * nq_ref[h]) + sum_rows(
-            share * (fit_ref[h] + g * n_ref[h])
-        )
-        small_ref[row, 2 * head : 3 * head] = sum_rows(go) + g * sum_rows(share)
+    for start in range(0, heads, GROUP):
+        rng = range(start, start + GROUP)
+        every = range(GROUP)
+        cols = [slice(h * head, (h + 1) * head) for h in rng]
+        g = [igf[h : h + 1] for h in rng]
+        er = [erow_ref[h : h + 1, :] for h in rng]
+        hh1 = [hh1_s[h] for h in rng]
+        hh2 = [hh2_s[h] for h in rng]
+        qk = [qk_ref[h] for h in rng]
+        keys = [qk_ref[h, bottom] for h in rng]
+        share = [share_s[h] for h in rng]
+        go = [go_ref[:, cols[i]] for i in every]
+        both = [dot(hh1[i], d1_ref[h], 1, 1) for i, h in enumerate(rng)]
+        direct = [dot(hh1[i], w1_ref[h], 1, 1) for i, h in enumerate(rng)]
+        mixq = [low(-both[i][top] * (inclusive * er[i])) for i in every]
+        mixk = [low(-both[i][bottom] * (strict * er[i])) for i in every]
+        first = [low(dot(qk[i], hh1[i], 0, 0)) for i in every]
+        second = [
+            low(dot(hh2[i], act_ref[h], 0, 0) + dot(d2_ref[h], u_s[h], 0, 0))
+            for i, h in enumerate(rng)
+        ]
+        gq = [low(go[i] + direct[i][top] + dot(mixq[i], keys[i])) for i in every]
+        spread = [
+            dot(mixq[i], qk_ref[h, top], 0, 0) + dot(mixk[i], keys[i], 0, 0)
+            for i, h in enumerate(rng)
+        ]
+        gk = [
+            low(g[i] * share[i] + direct[i][bottom] + dot(mixk[i], keys[i]) + spread[i])
+            for i in every
+        ]
+        for i, h in enumerate(rng):
+            triple_ref[0, :, cols[i]] = gq[i]
+            triple_ref[1, :, cols[i]] = gk[i]
+            triple_ref[2, :, cols[i]] = low(-g[i] * share[i])
+            kept_ref[cols[i]] = jnp.where(core == 0, first[i], second[i])
+            sent_ref[cols[i]] = jnp.where(core == 0, second[i], first[i])
+            small_ref[h : h + 1] = sum_rows(hh1[i].astype(F32))
+            row = slice(pad + h, pad + h + 1)
+            small_ref[row, 0:head] = sum_rows(hh2[i].astype(F32))
+            small_ref[row, head : 2 * head] = sum_rows(
+                go[i] * nq_ref[h].astype(F32)
+                + share[i] * (fit_ref[h].astype(F32) + g[i] * n_ref[h].astype(F32))
+            )
+            small_ref[row, 2 * head : 3 * head] = sum_rows(go[i]) + g[i] * sum_rows(share[i])
     grad_rates = ge_s[...] * fcol_ref[...]
     gr_ref[...] = low(grad_rates)
     total = jnp.broadcast_to(sum_rows(grad_rates), (grad_rates.shape[1], grad_rates.shape[1]))
@@ -545,9 +565,17 @@
     return jnp.where(core == 0, values[:, 0:half], values[:, half:])
 
 
+def put_halves(ids_smem, kept_ref, sent_ref, put):
+    core, chip = ids_smem[0], ids_smem[1]
+    first, second = 1 + core, 2 - core
+    put(kept_ref.at[0], chip)
+    put(kept_ref.at[1], lax.bitwise_xor(chip, second))
+    put(sent_ref.at[0], lax.bitwise_xor(chip, first))
+    put(sent_ref.at[1], lax.bitwise_xor(chip, 3))
+
+
 def gate_weights_kernel(
     feats,
-    chips,
     ids_smem,
     mine_ref,
     other_ref,
@@ -557,11 +585,13 @@
     kept_ref,
     got_ref,
     part_ref,
-    *refs,
+    kept_out,
+    sent_out,
+    pieces_s,
+    left_s,
+    right_s,
 ):
-    outs = refs[0:chips]
-    pieces_s, left_s, right_s = refs[chips:]
-    core, chip = ids_smem[0], ids_smem[1]
+    core = ids_smem[0]
     length = mine_ref.shape[1]
     for i in range(2):
         left_s[i, 0:length] = mine_ref[i]
@@ -572,17 +602,19 @@
         put_matrix(pieces_s, low(dot(left_s[i], right_s[i], 0, 0)), i, 2, feats)
     count, _, half = kept_ref.shape
     chunks = half // 128
-    before = outs[0].shape[0] - pieces_s.shape[1]
+    before = kept_out.shape[1] - pieces_s.shape[1]
     rows = before // (count * chunks)
-    for s, out in enumerate(outs):
-        place = lax.bitwise_xor(chip, s)
-        at = pl.ds(pl.multiple_of(place * rows, 16), rows)
+
+    def put(out, place):
+        at = pl.ds(pl.multiple_of(place * rows, rows), rows)
         for i in range(count):
             both = low(kept_ref[i, at, :].astype(F32) + got_ref[i, at, :].astype(F32))
             for l in range(chunks):
                 row = (i * chunks + l) * rows
                 out[row : row + rows] = both[:, l * 128 : (l + 1) * 128]
         out[before:] = pieces_s[place]
+
+    put_halves(ids_smem, kept_out, sent_out, put)
     part_ref[...] = dot(grads_ref[0], wg_ref[...], 1, 1)
 
 
@@ -597,7 +629,7 @@
     wr_ref,
     part_ref,
     tok_ref,
-    gains_ref,
+    gain1_ref,
     resid_grad_ref,
     small_ref,
     gain_two_ref,
@@ -611,7 +643,7 @@
     grad = grad + dot(gr[:, 0:heads], wr_ref[...])
     tok = tok_ref[0].astype(F32)
     spread = lax.rsqrt(mean_last(tok * tok) + EPSILON)
-    scaled = gains_ref[0:1].astype(F32) * grad
+    scaled = row_of(gain1_ref) * grad
     grad_ref[0] = (
         resid_grad_ref[...]
         + spread * scaled
@@ -634,30 +666,37 @@
     small_out[at : at + small_ref.shape[0]] = low(small_ref[...])
 
 
-def tails_kernel(ids_smem, kept_ref, got_ref, small_ref, *refs):
-    outs, tails_s = refs[:-1], refs[-1]
-    chips = len(outs)
+def tails_kernel(ids_smem, kept_ref, got_ref, kept_out, sent_out, tails_s):
+    chips = tails_s.shape[0]
     inner = low(kept_ref[...].astype(F32) + got_ref[...].astype(F32))
     rows = inner.shape[0] // chips
-    extra = small_ref.shape[0] // chips
     for j in range(chips):
-        at = 0
         for l in range(2):
-            cols = slice(l * 128, (l + 1) * 128)
-            tails_s[j, at : at + rows] = inner[j * rows : (j + 1) * rows, cols]
-            at += rows
-            tails_s[j, at : at + extra] = small_ref[j * extra : (j + 1) * extra, cols]
-            at += extra
-    for s, out in enumerate(outs):
-        out[...] = tails_s[lax.bitwise_xor(ids_smem[1], s)]
+            tails_s[j, l * rows : (l + 1) * rows] = inner[
+                j * rows : (j + 1) * rows, l * 128 : (l + 1) * 128
+            ]
+
+    def put(out, place):
+        out[...] = tails_s[place]
+
+    put_halves(ids_smem, kept_out, sent_out, put)
 
 
 def late_weights_kernel(
-    feats, ids_smem, mine_ref, other_ref, triple_ref, other_triple_ref, *refs
+    feats,
+    ids_smem,
+    mine_ref,
+    other_ref,
+    triple_ref,
+    other_triple_ref,
+    small_ref,
+    kept_out,
+    sent_out,
+    pieces_s,
+    left_s,
+    right_s,
 ):
-    pieces_s, left_s, right_s = refs[-3:]
-    outs = refs[:-3]
-    core, chip = ids_smem[0], ids_smem[1]
+    core = ids_smem[0]
     length = mine_ref.shape[1]
     left_s[0:length] = mine_ref[0]
     left_s[length : 2 * length] = other_ref[0]
@@ -666,8 +705,33 @@
         right_s[i, length : 2 * length] = core_columns(core, other_triple_ref[i])
     for i in range(3):
         put_matrix(pieces_s, low(dot(left_s[...], right_s[i], 0, 0)), i, 3, feats)
-    for s, out in enumerate(outs):
-        out[...] = pieces_s[lax.bitwise_xor(chip, s)]
+    chips, most, _ = pieces_s.shape
+    extra = small_ref.shape[0] // chips
+    for j in range(chips):
+        for l in range(2):
+            at = most - (2 - l) * extra
+            pieces_s[j, at : at + extra] = small_ref[
+                j * extra : (j + 1) * extra, l * 128 : (l + 1) * 128
+            ]
+
+    def put(out, place):
+        out[...] = pieces_s[place]
+
+    put_halves(ids_smem, kept_out, sent_out, put)
+
+
+def mixed_kernel(feats, resid_ref, *refs):
+    kept_ref, got_ref, mixed_ref, stay_ref, go_ref = refs[feats:]
+    total = resid_ref[...]
+    for ref in refs[0:feats]:
+        total = total + ref[...].astype(F32)
+    mixed_ref[0] = low(total)
+    add_kernel(kept_ref, got_ref, stay_ref, go_ref)
+
+
+def add_kernel(kept_ref, got_ref, stay_ref, go_ref):
+    stay_ref[...] = low(kept_ref[0].astype(F32) + got_ref[0].astype(F32))
+    go_ref[...] = low(kept_ref[1].astype(F32) + got_ref[1].astype(F32))
 
 
 def sum_at(refs, at):
@@ -677,17 +741,33 @@
     return low(value)
 
 
-def cut_feat_kernel(chips, ids_smem, *refs):
-    parts, outs = refs[0:chips], refs[chips:]
-    rows = outs[0].shape[0]
+def cut_feat_kernel(common, ids_smem, *refs):
+    parts, outs = refs[0:2], refs[2:]
+    rows = outs[0].shape[0] - common
+    shared = sum_at(parts, (slice(rows * len(outs), rows * len(outs) + common), slice(None)))
     for s, out in enumerate(outs):
         at = pl.ds(pl.multiple_of(lax.bitwise_xor(ids_smem[2], s) * rows, 16), rows)
-        out[...] = sum_at(parts, (at, slice(None)))
-
-
-def middle_kernel(chips, ids_smem, *refs):
-    pair, tail = refs[0:chips], refs[chips : 2 * chips]
-    total_ref, outs = refs[2 * chips], refs[2 * chips + 1 :]
+        out[0:rows] = sum_at(parts, (at, slice(None)))
+        out[rows:] = shared
+
+
+def sum_kernel(*refs):
+    values = [ref[...].astype(F32) for ref in refs[:-1]]
+    while len(values) > 1:
+        values = [values[i] + values[i + 1] for i in range(0, len(values), 2)]
+    refs[-1][...] = low(values[0])
+
+
+def join_kernel(*refs):
+    total_ref, out_ref = refs[-2:]
+    rows = refs[0].shape[0]
+    sum_kernel(*refs[:-2], out_ref.at[0:rows])
+    out_ref[rows:] = total_ref[...]
+
+
+def middle_kernel(ids_smem, *refs):
+    pair, tail = refs[0:2], refs[2:4]
+    total_ref, outs = refs[4], refs[5:]
     before = total_ref.shape[0]
     rows = (pair[0].shape[0] - before) // len(outs)
     shared = sum_at(tail, (slice(None), slice(None)))
@@ -698,72 +778,84 @@
     total_ref[...] = sum_at(pair, (slice(0, before), slice(None)))
 
 
-def take_matrices(ids_smem, pieces, outs, start=0):
+def take_matrices(ids_smem, pieces, outs, start=0, order=None):
     core, chip = ids_smem[0], ids_smem[1]
     chunks = outs[0].shape[1] // 256
     rows = outs[0].shape[0] // len(pieces)
     for s, both in enumerate(pieces):
-        at = pl.ds(pl.multiple_of(lax.bitwise_xor(chip, s) * rows, 16), rows)
+        ats = [
+            pl.ds(pl.multiple_of(lax.bitwise_xor(chip, d) * rows, 16), rows)
+            for d in (order[s] if order else (s, s))
+        ]
         for i, out in enumerate(outs):
             for l in range(chunks):
                 row = start + (i * chunks + l) * rows
                 mine = both[0][row : row + rows, :].astype(F32)
                 other = both[1][row : row + rows, :].astype(F32)
+                low_cols = slice(l * 128, (l + 1) * 128)
+                high_cols = slice((chunks + l) * 128, (chunks + l + 1) * 128)
 
                 @pl.when(core == 0)
-                def _(out=out, at=at, l=l, mine=mine, other=other):
-                    out[at, l * 128 : (l + 1) * 128] = mine
-                    out[at, (chunks + l) * 128 : (chunks + l + 1) * 128] = other
+                def _(out=out, ats=ats, mine=mine, other=other, a=low_cols, b=high_cols):
+                    out[ats[0], a] = mine
+                    out[ats[1], b] = other
 
                 @pl.when(core != 0)
-                def _(out=out, at=at, l=l, mine=mine, other=other):
-                    out[at, l * 128 : (l + 1) * 128] = other
-                    out[at, (chunks + l) * 128 : (chunks + l + 1) * 128] = mine
-
-
-def ffn_totals_kernel(chips, ids_smem, *refs):
-    pieces = [(refs[s], refs[chips + s]) for s in range(chips)]
-    gate_ref, up_ref, down_ref, down_s = refs[2 * chips :]
-    take_matrices(ids_smem, pieces, (gate_ref, up_ref, down_s))
-    down_ref[...] = jnp.transpose(down_s[...])
-
-
-def early_totals_kernel(chips, feats, heads, head, ids_smem, *refs):
-    pieces = [(refs[s], refs[chips + s]) for s in range(chips)]
-    wg_ref, wo_ref, first_ref, second_ref = refs[2 * chips : 2 * chips + 4]
-    (rate_ref, norm1_ref, norm2_ref, b1_ref, b2_ref, ig_ref, ib_ref, br_ref, small_s) = refs[
-        2 * chips + 4 :
-    ]
-    core, chip, feat = ids_smem[0], ids_smem[1], ids_smem[2]
-    take_matrices(ids_smem, pieces, (wg_ref, wo_ref))
-    rows = first_ref.shape[0] // chips
-    extra = small_s.shape[0] // chips
-    start = 2 * (wg_ref.shape[0] // chips) * (wg_ref.shape[1] // 256)
+                def _(out=out, ats=ats, mine=mine, other=other, a=low_cols, b=high_cols):
+                    out[ats[0], b] = mine
+                    out[ats[1], a] = other
+
+
+def early_totals_kernel(ids_smem, *refs):
+    core, chip = ids_smem[0], ids_smem[1]
+    first, second = 1 + core, 2 - core
+    pieces = [(refs[s], refs[4 + s]) for s in range(4)]
+    order = [(0, 0), (second, first), (first, second), (3, 3)]
+    gate_ref, up_ref, down_ref, wg_ref, wo_ref, first_ref, second_ref, down_s = refs[8:]
+    take_matrices(ids_smem, pieces, (wg_ref, wo_ref), order=order)
+    rows = first_ref.shape[0] // 4
+    start = 2 * (wg_ref.shape[0] // 4) * (wg_ref.shape[1] // 256)
     for s, both in enumerate(pieces):
-        place = lax.bitwise_xor(chip, s)
-        at = pl.ds(pl.multiple_of(place * rows, 16), rows)
-        at_small = pl.ds(pl.multiple_of(place * extra, 16), extra)
-        row = start
+        ats = [
+            pl.ds(pl.multiple_of(lax.bitwise_xor(chip, d) * rows, 16), rows) for d in order[s]
+        ]
         for l in range(2):
             cols = slice(l * 128, (l + 1) * 128)
+            row = start + l * rows
             mine = both[0][row : row + rows].astype(F32)
             other = both[1][row : row + rows].astype(F32)
-            row += rows
 
             @pl.when(core == 0)
-            def _(at=at, cols=cols, mine=mine, other=other):
-                first_ref[at, cols] = mine
-                second_ref[at, cols] = other
+            def _(ats=ats, cols=cols, mine=mine, other=other):
+                first_ref[ats[0], cols] = mine
+                second_ref[ats[1], cols] = other
 
             @pl.when(core != 0)
-            def _(at=at, cols=cols, mine=mine, other=other):
-                first_ref[at, cols] = other
-                second_ref[at, cols] = mine
-
-            small_s[at_small, cols] = both[0][row : row + extra].astype(F32) + both[1][
-                row : row + extra
-            ].astype(F32)
-            row += extra
+            def _(ats=ats, cols=cols, mine=mine, other=other):
+                first_ref[ats[1], cols] = other
+                second_ref[ats[0], cols] = mine
+
+    take_matrices(ids_smem, pieces, (gate_ref, up_ref, down_s), start + 2 * rows, order)
+    down_ref[...] = jnp.transpose(down_s[...])
+
+
+def late_totals_kernel(chips, feats, heads, head, ids_smem, *refs):
+    pieces = [(refs[s], refs[chips + s]) for s in range(chips)]
+    matrices = refs[2 * chips : 2 * chips + 3]
+    (rate_ref, norm1_ref, norm2_ref, b1_ref, b2_ref, ig_ref, ib_ref, br_ref, small_s) = refs[
+        2 * chips + 3 :
+    ]
+    chip, feat = ids_smem[1], ids_smem[2]
+    take_matrices(ids_smem, pieces, matrices)
+    extra = small_s.shape[0] // chips
+    most = refs[0].shape[0]
+    for s, both in enumerate(pieces):
+        at = pl.ds(pl.multiple_of(lax.bitwise_xor(chip, s) * extra, 16), extra)
+        for l in range(2):
+            row = most - (2 - l) * extra
+            small_s[at, l * 128 : (l + 1) * 128] = both[0][row : row + extra].astype(
+                F32
+            ) + both[1][row : row + extra].astype(F32)
     share = rate_ref.shape[1]
     block = small_s[pl.ds(pl.multiple_of(feat * 16, 16), 16), :]
     rate_ref[...] = block[0:heads, 0:share]
@@ -775,19 +867,31 @@
     b2_ref[...] = packed[:, 0:head]
     ig_ref[...] = packed[:, head : 2 * head]
     ib_ref[...] = packed[:, 2 * head : 3 * head]
-    br_ref[...] = packed[:, 3 * head : 3 * head + 1]
-
-
-def late_totals_kernel(chips, ids_smem, *refs):
-    pieces = [(refs[s], refs[chips + s]) for s in range(chips)]
-    take_matrices(ids_smem, pieces, refs[2 * chips : 2 * chips + 3])
+    br_ref[...] = jnp.transpose(small_s[at + 16 : at + 32, 128:])[3 * head - 128 : 3 * head - 127, 0:heads]
 
 
 def held(values):
     return pltpu.with_memory_space_constraint(values, pltpu.VMEM)
 
 
-def call(kernel, outs, inputs, scratch=(), smem=0, us=1.0, plain=(), loose=(), keep=True, mib=24):
+def in_order():
+    last = []
+
+    def ordered(kernel, outs, inputs, scratch=(), **options):
+        inputs = list(inputs)
+        at = options.get("smem", 0)
+        if last:
+            inputs[at], _ = lax.optimization_barrier((inputs[at], last.pop()))
+        found = call(kernel, outs, inputs, scratch, **options)
+        last.append(found[0])
+        return found
+
+    return ordered
+
+
+def call(
+    kernel, outs, inputs, scratch=(), smem=0, cover=True, plain=(), loose=(), keep=True, mib=24
+):
     specs, placed = [], []
     for i, x in enumerate(inputs):
         if i < smem:
@@ -814,7 +918,7 @@
         ],
         scratch_shapes=[pltpu.VMEM(*x) if isinstance(x, tuple) else x for x in scratch],
         cost_estimate=pl.CostEstimate(
-            flops=int(us * 1e10), bytes_accessed=int(us * 3e7), transcendentals=0
+            flops=int(2e10 if cover else 1e6), bytes_accessed=int(2e7 if cover else 1e3), transcendentals=0
         ),
         compiler_params=pltpu.CompilerParams(vmem_limit_bytes=mib * 2**20),
     )(*placed)
@@ -865,15 +969,21 @@
     return [values[0]] + [exchange(values[s], "feat", feats, s) for s in range(1, feats)]
 
 
+def first_axis(values, rows):
+    return lax.ppermute(values, "rows", [(i, i ^ (2 << (i & 1))) for i in range(rows)])
+
+
+def second_axis(values, rows):
+    return lax.ppermute(values, "rows", [(i, i ^ (4 >> (i & 1))) for i in range(rows)])
+
+
+def halved(launch, kept, got, rows, cover):
+    stay, go = launch(add_kernel, [(kept.shape[1:], BF16)] * 2, [kept, got], cover=cover)
+    return stay, second_axis(go, rows)
+
+
 def other_core(values, rows):
     return exchange(values, "rows", rows, 1)
-
-
-def sum_low(values):
-    values = [v.astype(F32) for v in values]
-    while len(values) > 1:
-        values = [values[i] + values[i + 1] for i in range(0, len(values), 2)]
-    return low(values[0])
 
 
 def scatter_rows(values, size, dim):
@@ -923,16 +1033,15 @@
     ffn_up,
     ffn_down,
 ):
+    launch = in_order()
     _, length, width = tokens.shape
     heads, head, inner = inner_w1.shape
     hidden = ffn_gate.shape[1]
     blocks = length // MB
     chips = rows // 2
-    gains = jnp.stack([norm1_gain, norm2_gain])
     line = (length, width)
     wide = (heads, length, inner)
     slim = (heads, length, head)
-    thin = (heads, length, 1)
     square = (heads, length, length)
     state = (heads, head, inner)
     w2t = jnp.transpose(inner_w2, (0, 2, 1))
@@ -953,18 +1062,18 @@
         (wide, BF16),
         ((heads, 2 * length, inner), BF16),
         (wide, BF16),
-        (slim, F32),
-        (slim, F32),
-        (thin, F32),
-        (slim, F32),
+        (slim, BF16),
+        (slim, BF16),
+        ((length, 128), F32),
+        (slim, BF16),
         ((blocks,) + state, BF16),
         (square, BF16),
         (square, BF16),
         (wide, BF16),
-        (slim, F32),
-        (thin, F32),
+        (slim, BF16),
+        ((length, 128), F32),
     ]
-    saved = call(
+    saved = launch(
         forward_kernel,
         [((2,) + line, BF16), (line, BF16)] + kept,
         [
@@ -972,7 +1081,7 @@
             seg_ids,
             pad_mask,
             tokens,
-            gains,
+            norm1_gain,
             w_query,
             w_key,
             w_value,
@@ -986,6 +1095,7 @@
             inner_gain,
             inner_bias,
             w_out,
+            norm2_gain,
         ],
         kept
         + [
@@ -1006,8 +1116,7 @@
             pltpu.SemaphoreType.DMA((5 + len(kept),)),
         ],
         smem=1,
-        us=20,
-        plain=range(18),
+        plain=range(19),
         loose=(5, 6, 7, 8, 17),
         keep=[True, True] + [None] * len(kept),
         mib=48,
@@ -1017,31 +1126,39 @@
     rest = saved[9:]
     normed_two, *cots = lax.optimization_barrier([normed_two] + cots)
     blocks_in = [normed_two]
+    acts, ggs, gus, pieces = [], [], [], []
     for s in range(1, feats):
-        nearest = s & -s
-        blocks_in.append(exchange(blocks_in[s ^ nearest], "feat", feats, nearest))
-    acts, ggs, gus, pieces = [], [], [], []
+        if s & (s - 1) == 0:
+            blocks_in.append(exchange(normed_two, "feat", feats, s))
+        else:
+            blocks_in.append(None)
     for s in range(feats):
-        act, gg, gu, gx = call(
+        if blocks_in[s] is None:
+            nearest = s & -s
+            held_back, _ = lax.optimization_barrier((blocks_in[s ^ nearest], pieces[1]))
+            blocks_in[s] = exchange(held_back, "feat", feats, nearest)
+        act, gg, gu, gx = launch(
             ffn_kernel,
             [((length, hidden), BF16)] * 3 + [(line, BF16)],
             [blocks_in[s], cots[s], ffn_gate, ffn_up, ffn_down],
-            us=1.5,
         )
         acts.append(act)
         ggs.append(gg)
         gus.append(gu)
-        pieces.append(gx if s == 0 else exchange(gx, "feat", feats, s))
+        pieces.append(gx)
+    if feats > 2:
+        pieces[1], _ = lax.optimization_barrier((pieces[1], acts[2]))
+    pieces = across_feats(pieces, feats)
+
     def between(pieces):
-        return call(
+        return launch(
             partial(between_kernel, feats),
             [(line, F32), (line, F32), ((2,) + line, BF16), ((1, width), F32)],
-            pieces + [resid, cotangent, gains, w_out, gelu_gate, gate_slope],
-            us=1,
+            pieces + [resid, cotangent, norm2_gain, w_out, gelu_gate, gate_slope],
         )
 
     def inner_backward(grad_inner_out):
-        return call(
+        return launch(
             backward_kernel,
             [
                 ((3,) + line, BF16),
@@ -1071,157 +1188,156 @@
                 ((heads, 1, head), F32),
             ],
             smem=2,
-            us=22,
         )
 
     step = 16 * chips
     small_rows = -(-(16 * feats + 32) // step) * step
 
     def finish(triple, grad_rates, small, part, grad_resid, grad_gain_two):
-        return call(
+        return launch(
             partial(input_kernel, feats),
             [((1,) + line, F32), ((small_rows, inner), BF16)],
             [triple, grad_rates, pair, w_query, w_key, w_value, w_rate_t, part]
-            + [tokens, gains, grad_resid, small, grad_gain_two],
-            us=2,
+            + [tokens, norm1_gain, grad_resid, small, grad_gain_two],
             keep=(False, True),
+            cover=False,
         )
 
-    if (width // feats) % step or hidden % 256 or width % 256:
+    if chips != 4 or (width // feats) % step or hidden % 256 or width % 256:
         grad_resid, grad_inner_out, grad_pair, grad_gain_two = between(pieces)
         out, grads = plain_totals(
             rows, feats, blocks_in, cots, acts, ggs, gus, ffn_down, pair, grad_pair, w_gate
         )
         triple, grad_rates, kept, sent, small = inner_backward(grad_inner_out)
-        grad_tokens, small = finish(triple, grad_rates, small, grads.pop(), grad_resid, grad_gain_two)
+        out = across_feats(out, feats)
+        mixed = low(resid + sum(x.astype(F32) for x in out))[None]
+        grad_tokens, small = finish(
+            triple, grad_rates, small, grads.pop(), grad_resid, grad_gain_two
+        )
         late = plain_late_totals(rows, feats, pair, triple, kept, sent, small, state)
-        mixed = low(resid + sum(x.astype(F32) for x in across_feats(out, feats)))
         return arrange(mixed, grad_tokens, grads, late, state)
-    ffn = call(
+    ffn = launch(
         partial(ffn_weights_kernel, feats),
         [((3, width, hidden // 2), BF16)] * 2 + [(line, BF16)] * feats,
         [ids] + blocks_in + cots + acts + ggs + gus + [ffn_down],
         [((feats * length, width), BF16)] * 2 + [((feats * length, hidden), BF16)] * 3,
         smem=1,
-        us=4,
-    )
-    pieces, ffn_kept = lax.optimization_barrier((pieces, ffn[0]))
+    )
     grad_resid, grad_inner_out, grad_pair, grad_gain_two = between(pieces)
+    ffn_sent, _ = lax.optimization_barrier((ffn[1], grad_pair))
     pair_other = other_core(pair, rows)
     half = width // 2
     per = width // (feats * chips) * (half // 128)
     ffn_rows = 3 * (width // chips) * (hidden // 256)
-    part, *early = call(
-        partial(gate_weights_kernel, feats, chips),
-        [(line, F32)] + [((ffn_rows + feats * 2 * per, 128), BF16)] * chips,
+    part, early, early_sent = launch(
+        partial(gate_weights_kernel, feats),
+        [(line, F32)] + [((2, ffn_rows + feats * 2 * per, 128), BF16)] * 2,
         [ids, pair, pair_other, grad_pair, other_core(grad_pair, rows), w_gate]
-        + [ffn_kept, other_core(ffn[1], rows)],
+        + [ffn[0], other_core(ffn_sent, rows)],
         [
             ((chips, feats * 2 * per, 128), BF16),
             ((2, 2 * length, width), BF16),
             ((2, 2 * length, half), BF16),
         ],
         smem=1,
-        us=2,
-    )
-    grad_inner_out, early, out = lax.optimization_barrier((grad_inner_out, early, ffn[2:]))
-    early = across_chips(early, rows)
+    )
+    early_got = first_axis(early_sent, rows)
+    out, _ = lax.optimization_barrier((ffn[2:], part))
     out = across_feats(out, feats)
     triple, grad_rates, kept, sent, small = inner_backward(grad_inner_out)
     triple_other = other_core(triple, rows)
-    got = other_core(sent, rows)
-    small, early, out = lax.optimization_barrier((small, early, out))
-    grad_tokens, small = finish(
-        triple, grad_rates, small, part, grad_resid, grad_gain_two
-    )
-    mixed = low(resid + sum(x.astype(F32) for x in out))
-    tail = 2 * (heads * head + small_rows) // chips
-    tails = call(
+    inner_got = other_core(sent, rows)
+    mixed, early, early_sent = launch(
+        partial(mixed_kernel, feats),
+        [((1,) + line, BF16)] + [(early.shape[1:], BF16)] * 2,
+        [resid] + out + [early, early_got],
+        keep=(False, True, True),
+    )
+    early_got = second_axis(early_sent, rows)
+    tail = 2 * heads * head // chips
+    tails, tails_sent = launch(
         tails_kernel,
-        [((tail, 128), BF16)] * chips,
-        [ids, kept, got, small],
+        [((2, tail, 128), BF16)] * 2,
+        [ids, kept, inner_got],
         [((chips, tail, 128), BF16)],
         smem=1,
-        us=1,
-    )
-    tails, triple = lax.optimization_barrier((tails, triple))
-    tails = across_chips(tails, rows)
-    late = call(
+        cover=False,
+    )
+    tails_got = first_axis(tails_sent, rows)
+    grad_tokens, small = finish(triple, grad_rates, small, part, grad_resid, grad_gain_two)
+    tails, tails_got = halved(launch, tails, tails_got, rows, False)
+    early_got, small = lax.optimization_barrier((early_got, small))
+    common = 2 * small_rows // chips
+    late, late_sent = launch(
         partial(late_weights_kernel, feats),
-        [((feats * 3 * per, 128), BF16)] * chips,
-        [ids, pair, pair_other, triple, triple_other],
+        [((2, feats * 3 * per + common, 128), BF16)] * 2,
+        [ids, pair, pair_other, triple, triple_other, small],
         [
-            ((chips, feats * 3 * per, 128), BF16),
+            ((chips, feats * 3 * per + common, 128), BF16),
             ((2 * length, width), BF16),
             ((3, 2 * length, half), BF16),
         ],
         smem=1,
-        us=2,
-    )
-    late = across_chips(late, rows)
-    ffn_total, *cut = call(
-        partial(middle_kernel, chips),
+    )
+    late_got = first_axis(late_sent, rows)
+    ffn_total, *cut = launch(
+        middle_kernel,
         [((ffn_rows, 128), BF16)] + [((2 * per + tail, 128), BF16)] * feats,
-        [ids] + early + tails,
+        [ids, early, early_got, tails, tails_got],
         smem=1,
-        us=1,
-    )
-    ffn_total = across_chips([ffn_total] * chips, rows)
-    ffn_total += [other_core(x, rows) for x in ffn_total]
-    joined = sum_low(across_feats(cut, feats))
-    joined = across_chips([joined] * chips, rows)
-    joined += [other_core(x, rows) for x in joined]
-    late_cut = call(
-        partial(cut_feat_kernel, chips),
-        [((3 * per, 128), BF16)] * feats,
-        [ids] + late,
+    )
+    cut = across_feats(cut, feats)
+    late, late_got = halved(launch, late, late_got, rows, True)
+    (joined,) = launch(
+        join_kernel, [((2 * per + tail + ffn_rows, 128), BF16)], cut + [ffn_total]
+    )
+    late_cut = launch(
+        partial(cut_feat_kernel, common),
+        [((3 * per + common, 128), BF16)] * feats,
+        [ids, late, late_got],
         smem=1,
-        us=1,
-    )
-    late_total = sum_low(across_feats(late_cut, feats))
+        cover=False,
+    )
+    joined, late_cut = lax.optimization_barrier((joined, late_cut))
+    late_cut = across_feats(late_cut, feats)
+    near = second_axis(joined, rows)
+    joined = [joined, near, first_axis(joined, rows), first_axis(near, rows)]
+    (late_total,) = launch(sum_kernel, [((3 * per + common, 128), BF16)], late_cut)
     late = across_chips([late_total] * chips, rows)
     late += [other_core(x, rows) for x in late]
+    joined += [other_core(x, rows) for x in joined]
     share = (width // feats, width)
-    ffn = call(
-        partial(ffn_totals_kernel, chips),
-        [((width, hidden), F32)] * 2 + [((hidden, width), F32)],
-        [ids] + ffn_total,
-        [((width, hidden), F32)],
-        smem=1,
-        us=3,
-        keep=False,
-    )
-    early = call(
-        partial(early_totals_kernel, chips, feats, heads, head),
-        [(share, F32)] * 2
-        + [((heads * head, inner), F32)] * 2
+    late = launch(
+        partial(late_totals_kernel, chips, feats, heads, head),
+        [(share, F32)] * 3
         + [((heads, width // feats), F32)]
         + [((1, width // feats), F32)] * 2
         + [((heads, inner), F32)]
         + [((heads, head), F32)] * 3
-        + [((heads, 1), F32)],
-        [ids] + joined,
+        + [((1, heads), F32)],
+        [ids] + late,
         [((small_rows, inner), F32)],
         smem=1,
-        us=3,
         keep=False,
     )
-    late = call(
-        partial(late_totals_kernel, chips),
-        [(share, F32)] * 3,
-        [ids] + late,
+    early = launch(
+        early_totals_kernel,
+        [((width, hidden), F32)] * 2
+        + [((hidden, width), F32)]
+        + [(share, F32)] * 2
+        + [((heads * head, inner), F32)] * 2,
+        [ids] + joined,
+        [((width, hidden), F32)],
         smem=1,
-        us=2,
         keep=False,
     )
-    return arrange(
-        mixed, grad_tokens, list(ffn) + list(early[0:2]), list(late) + list(early[2:]), state
-    )
+    early, late = list(early), list(late)
+    return arrange(mixed, grad_tokens, early[0:5], late[0:3] + early[5:7] + late[3:], state)
 
 
 def arrange(mixed, grad_tokens, early, late, state):
     return (
-        mixed[None],
+        mixed,
         grad_tokens,
         late[6][0],
         late[0],
@@ -1229,7 +1345,7 @@
         late[2],
         early[3],
         jnp.transpose(late[5]),
-        late[12][:, 0],
+        late[12][0],
         late[3].reshape(state),
         late[8],
         jnp.transpose(late[4].reshape(state), (0, 2, 1)),
@@ -1303,7 +1419,7 @@
         packed[:, 0:head],
         packed[:, head : 2 * head],
         packed[:, 2 * head : 3 * head],
-        packed[:, 3 * head : 3 * head + 1],
+        packed[:, 3 * head : 3 * head + 1].reshape(1, heads),
     ]
 
 

time: 190 us -> 163 us (0.86)
  Pallas kernels: 76.8 us -> 61.9 us
  starting transfers between devices: 55.8 us -> 46.3 us
  other arithmetic: 3.99 us -> 0.08 us
    ppermute x0 -> x9, waiting for transfers between devices: none -> 23.1 us  [the longest x5 11.8 us: first_axis(): lax.ppermute(values, 'rows', [(i, i ^ 2 << (i & 1)) for i in range(rows)])]
    ppermute x53 -> x34, waiting for transfers between devices: 50.3 us -> 28.1 us  [exchange(): return lax.ppermute(values, axis, [(i, i ^ distance) for i in range(size)])]
    ppermute x53 -> x34, starting transfers between devices: 55.8 us -> 37.2 us  [exchange(): return lax.ppermute(values, axis, [(i, i ^ distance) for i in range(size)])]
    pallas_call x17 -> x21, Pallas kernels: 76.8 us -> 61.9 us  [call(): pl.pallas_call(kernel, out_shape=[pltpu.VMEM(s, d) if k else pltpu.HBM(s,...]
    ppermute x0 -> x9, starting transfers between devices: none -> 9.11 us  [the longest x4 5.47 us: second_axis(): lax.ppermute(values, 'rows', [(i, i ^ 4 >> (i & 1)) for i in range(rows)])]
  transfers between devices with their start and end apart: 53 -> 43, of which waited for: 14 -> 17; matrix products, arithmetic and copies ran while one was open for 3% -> 0% of each run, Pallas kernels for 38% -> 33%
where the time goes in v3:
time: 163 us
  Pallas kernels  61.9 us (38%)
  waiting for transfers between devices  51.2 us (31%)
  starting transfers between devices  46.3 us (28%)
  local copies, waits for them, and re-layouts  1.81 us (1%)
    pallas_call x21, Pallas kernels, call(): pl.pallas_call(kernel, out_shape=[pltpu.VMEM(s, d) if k else pltpu.HBM(s,...  61.9 us
    ppermute x34, starting transfers between devices, exchange(): return lax.ppermute(values, axis, [(i, i ^ distance) for i in range(size)])  37.2 us
    ppermute x34, waiting for transfers between devices, exchange(): return lax.ppermute(values, axis, [(i, i ^ distance) for i in range(size)])  28.1 us
    ppermute x5, waiting for transfers between devices, first_axis(): lax.ppermute(values, 'rows', [(i, i ^ 2 << (i & 1)) for i in range(rows)])  11.8 us
    ppermute x4, waiting for transfers between devices, second_axis(): lax.ppermute(values, 'rows', [(i, i ^ 4 >> (i & 1)) for i in range(rows)])  11.4 us
    ppermute x4, starting transfers between devices, second_axis(): lax.ppermute(values, 'rows', [(i, i ^ 4 >> (i & 1)) for i in range(rows)])  5.47 us
    ppermute x5, starting transfers between devices, first_axis(): lax.ppermute(values, 'rows', [(i, i ^ 2 << (i & 1)) for i in range(rows)])  3.63 us
  transfers between devices with their start and end apart: 43, of which 17 were waited for; matrix products, arithmetic and copies ran while one was open for 0% of the time, Pallas kernels for 33%

profile of v3, /device:TPU:0, one launch (start us, length us, event | category | flops | bytes accessed | tf_op | source)
XLA Modules:
  0.0 162.6 jit_solution(14309906626674518226)
XLA Ops:
  0.7 3.1 %collective-permute-start = (bf16[128,768]{1,0:T(8,128)(2,1)}, bf16[128,768]{1,0:T(8,128)(2,1)S(1)}, u32[]{:S(2)}, u32[]{:S(2)}) collective-permute-start(bf16[128,768]{1,0:T(8,128)(2,1)} %bitcast.19), channel_id=1, source_target_pairs={{0,1},{1,0},{2,3},{3,2},{4,5},{5,4},{6,7},{7,6},{8,9},{9,8},{10,11... | collective-permute-start | bytes 589832 | tf_op jit(solution)/shard_map/ppermute | solution.py:928
  3.7 2.6 %collective-permute-start.1 = (bf16[128,768]{1,0:T(8,128)(2,1)}, bf16[128,768]{1,0:T(8,128)(2,1)S(1)}, u32[]{:S(2)}, u32[]{:S(2)}) collective-permute-start(bf16[128,768]{1,0:T(8,128)(2,1)} %bitcast.20), channel_id=1, source_target_pairs={{0,2},{1,3},{2,0},{3,1},{4,6},{5,7},{6,4},{7,5},{8,10},{9,11},{10,... | collective-permute-start | bytes 589832 | tf_op jit(solution)/shard_map/ppermute | solution.py:928
  6.4 19.3 %shard_map.365 = (bf16[2,128,768]{2,1,0:T(8,128)(2,1)S(1)}, bf16[128,768]{1,0:T(8,128)(2,1)S(1)}, f32[128,768]{1,0:T(8,128)}, f32[128,768]{1,0:T(8,128)}, f32[12...) custom-call(s32[1,128]{1,0:T(1,128)} %seg_ref.2, ...), custom_call_target="tpu_custom_call" | custom-call | flops 20000000000 | bytes 20000000 | tf_op jit(solution)/shard_map/pallas_call | solution.py:910
  27.3 3.5 %collective-permute-start.3 = (bf16[128,768]{1,0:T(8,128)(2,1)}, bf16[128,768]{1,0:T(8,128)(2,1)S(1)}, u32[]{:S(2)}, u32[]{:S(2)}) collective-permute-start(bf16[128,768]{1,0:T(8,128)(2,1)} %copy-done.14), channel_id=1, source_target_pairs={{0,2},{1,3},{2,0},{3,1},{4,6},{5,7},{6,4},{7,5},{8,10},{9,11},{10,... | collective-permute-start | bytes 589832 | tf_op jit(solution)/shard_map/ppermute | solution.py:928
  33.1 3.6 %collective-permute-done.4.x_ref.refs_1_ = bf16[128,768]{1,0:T(8,128)(2,1)S(1)} collective-permute-done((bf16[128,768]{1,0:T(8,128)(2,1)}, bf16[128,768]{1,0:T(8,128)(2,1)S(1)}, u32[]{:S(2)}, u32[]{:S(2)}) %collective-permute-start.4) | collective-permute-done | bytes 196640 | tf_op jit(solution)/shard_map/ppermute | solution.py:928
  40.7 1.9 %collective-permute-start.6 = (bf16[128,768]{1,0:T(8,128)(2,1)S(1)}, bf16[128,768]{1,0:T(8,128)(2,1)S(1)}, u32[]{:S(2)}, u32[]{:S(2)}) collective-permute-start(bf16[128,768]{1,0:T(8,128)(2,1)S(1)} %get-tuple-element.186), channel_id=1, source_target_pairs={{0,1},{1,0},{2,3},{3,2},{4,5},{5,4},{6,7},{7,6},{8,9},{9,8},{10,11... | collective-permute-start | bytes 589832 | tf_op jit(solution)/shard_map/ppermute | solution.py:928
  43.5 4.7 %collective-permute-done.5.x_ref.refs_3_ = bf16[128,768]{1,0:T(8,128)(2,1)S(1)} collective-permute-done((bf16[128,768]{1,0:T(8,128)(2,1)S(1)}, bf16[128,768]{1,0:T(8,128)(2,1)S(1)}, u32[]{:S(2)}, u32[]{:S(2)}) %collective-permute-start.5) | collective-permute-done | bytes 196640 | tf_op jit(solution)/shard_map/ppermute | solution.py:928
  49.5 3.5 %collective-permute-start.8 = (bf16[128,768]{1,0:T(8,128)(2,1)S(1)}, bf16[128,768]{1,0:T(8,128)(2,1)S(1)}, u32[]{:S(2)}, u32[]{:S(2)}) collective-permute-start(bf16[128,768]{1,0:T(8,128)(2,1)S(1)} %get-tuple-element.188), channel_id=1, source_target_pairs={{0,3},{1,2},{2,1},{3,0},{4,7},{5,6},{6,5},{7,4},{8,11},{9,10},{10,... | collective-permute-start | bytes 589832 | tf_op jit(solution)/shard_map/ppermute | solution.py:928
  53.0 3.3 %shard_map.370 = (bf16[3,768,256]{2,1,0:T(8,128)(2,1)S(1)}, bf16[3,768,256]{2,1,0:T(8,128)(2,1)S(1)}, bf16[128,768]{1,0:T(8,128)(2,1)S(1)}, bf16[128,768]{1,0:T(...) custom-call(s32[3]{0:T(128)S(1)} %pad_add_fusion.ids_smem, bf16[128,768]{1,0:T(8,128)(2,1)S(1)} %copy-done.16, ...), custom_call_target="tpu_custom_call" | custom-call | flops 20000000000 | bytes 20000000 | tf_op jit(solution)/shard_map/pallas_call | solution.py:910
  56.4 2.9 %collective-permute-done.7.refs_2_ = bf16[128,768]{1,0:T(8,128)(2,1)S(1)} collective-permute-done((bf16[128,768]{1,0:T(8,128)(2,1)S(1)}, bf16[128,768]{1,0:T(8,128)(2,1)S(1)}, u32[]{:S(2)}, u32[]{:S(2)}) %collective-permute-start.7) | collective-permute-done | bytes 196640 | tf_op jit(solution)/shard_map/ppermute | solution.py:928
  60.9 2.6 %collective-permute-done.9.other_ref = bf16[2,128,768]{2,1,0:T(8,128)(2,1)S(1)} collective-permute-done((bf16[2,128,768]{2,1,0:T(8,128)(2,1)S(1)}, bf16[2,128,768]{2,1,0:T(8,128)(2,1)S(1)}, u32[]{:S(2)}, u32[]{:S(2)}) %collective-permute-start.9) | collective-permute-done | bytes 393248 | tf_op jit(solution)/shard_map/ppermute | solution.py:928
  65.9 2.7 %collective-permute-start.12 = (bf16[128,768]{1,0:T(8,128)(2,1)S(1)}, bf16[128,768]{1,0:T(8,128)(2,1)S(1)}, u32[]{:S(2)}, u32[]{:S(2)}) collective-permute-start(bf16[128,768]{1,0:T(8,128)(2,1)S(1)} %get-tuple-element.224), channel_id=1, source_target_pairs={{0,1},{1,0},{2,3},{3,2},{4,5},{5,4},{6,7},{7,6},{8,9},{9,8},{10,11... | collective-permute-start | bytes 589832 | tf_op jit(solution)/shard_map/ppermute | solution.py:928
  72.7 17.5 %shard_map.373 = (bf16[3,128,768]{2,1,0:T(8,128)(2,1)S(1)}, bf16[128,128]{1,0:T(8,128)(2,1)S(1)}, bf16[768,256]{1,0:T(8,128)(2,1)S(1)}, bf16[768,256]{1,0:T(8,128)(2,1)S(1)}, f32[32,256]{1,0:T(8,128)S(1)}) custom-call(s32[3]{0:T(128)S(1)} %pad_add_fusion.ids_smem, s32[1,128]{1,0:T(1,128)S(1)} %copy-done.19, s32[1,128]{1,0:T(1,128)S(1)} %copy-done.19, ...), custom_call_target="tpu_custom_call" | custom-call | flops 20000000000 | bytes 20000000 | tf_op jit(solution)/shard_map/pallas_call | solution.py:910
  94.5 2.3 %shard_map.376 = (f32[1,128,768]{2,1,0:T(8,128)}, bf16[128,256]{1,0:T(8,128)(2,1)S(1)}) custom-call(bf16[3,128,768]{2,1,0:T(8,128)(2,1)S(1)} %get-tuple-element.234.triple_ref, bf16[128,128]{1,0:T(8,128)(2,1)S(1)} %get-tuple-element.235.gr_ref, bf16[2,128,768]{2,1,0:T(8,128)(2,1)S(1)} %get-tuple-element.243.mine_ref.pair_ref, bf16[768,768]{1,0:T(8,128)(2,1)S(1)} %copy-done, ...), custom_call_target="tpu_custom_call" | custom-call | flops 1000000 | bytes 1000 | tf_op jit(solution)/shard_map/pallas_call | solution.py:910
  96.7 4.9 %collective-permute-done.17.got_ref = bf16[2,384,128]{2,1,0:T(8,128)(2,1)S(1)} collective-permute-done((bf16[2,384,128]{2,1,0:T(8,128)(2,1)S(1)}, bf16[2,384,128]{2,1,0:T(8,128)(2,1)S(1)}, u32[]{:S(2)}, u32[]{:S(2)}) %collective-permute-start.17) | collective-permute-done | bytes 196640 | tf_op jit(solution)/shard_map/ppermute | solution.py:973
  111.5 6.9 %collective-permute-done.21.got_ref = bf16[2,1792,128]{2,1,0:T(8,128)(2,1)S(1)} collective-permute-done((bf16[2,1792,128]{2,1,0:T(8,128)(2,1)S(1)}, bf16[2,1792,128]{2,1,0:T(8,128)(2,1)S(1)}, u32[]{:S(2)}, u32[]{:S(2)}) %collective-permute-start.21) | collective-permute-done | bytes 917536 | tf_op jit(solution)/shard_map/ppermute | solution.py:973
  120.2 3.4 %collective-permute-done.23.refs_2_ = bf16[672,128]{1,0:T(8,128)(2,1)S(1)} collective-permute-done((bf16[672,128]{1,0:T(8,128)(2,1)S(1)}, bf16[672,128]{1,0:T(8,128)(2,1)S(1)}, u32[]{:S(2)}, u32[]{:S(2)}) %collective-permute-start.23) | collective-permute-done | bytes 172064 | tf_op jit(solution)/shard_map/ppermute | solution.py:928
  123.7 3.4 %collective-permute-done.25.refs_1_ = bf16[1792,128]{1,0:T(8,128)(2,1)S(1)} collective-permute-done((bf16[1792,128]{1,0:T(8,128)(2,1)S(1)}, bf16[1792,128]{1,0:T(8,128)(2,1)S(1)}, u32[]{:S(2)}, u32[]{:S(2)}) %collective-permute-start.25) | collective-permute-done | bytes 458784 | tf_op jit(solution)/shard_map/ppermute | solution.py:977
  134.3 6.4 %collective-permute-done.36.refs_1_ = bf16[1824,128]{1,0:T(8,128)(2,1)S(1)} collective-permute-done((bf16[1824,128]{1,0:T(8,128)(2,1)S(1)}, bf16[1824,128]{1,0:T(8,128)(2,1)S(1)}, u32[]{:S(2)}, u32[]{:S(2)}) %collective-permute-start.36) | collective-permute-done | bytes 466976 | tf_op jit(solution)/shard_map/ppermute | solution.py:977
  140.8 2.1 %collective-permute-start.29 = (bf16[496,128]{1,0:T(8,128)(2,1)S(1)}, bf16[496,128]{1,0:T(8,128)(2,1)S(1)}, u32[]{:S(2)}, u32[]{:S(2)}) collective-permute-start(bf16[496,128]{1,0:T(8,128)(2,1)S(1)} %shard_map.383.refs_0_), channel_id=1, source_target_pairs={{0,8},{4,12},{8,0},{12,4},{16,24},{20,28},{24,16},{28,20},{1,9},{5... | collective-permute-start | bytes 380936 | tf_op jit(solution)/shard_map/ppermute | solution.py:928
  142.9 2.1 %collective-permute-start.30 = (bf16[496,128]{1,0:T(8,128)(2,1)S(1)}, bf16[496,128]{1,0:T(8,128)(2,1)S(1)}, u32[]{:S(2)}, u32[]{:S(2)}) collective-permute-start(bf16[496,128]{1,0:T(8,128)(2,1)S(1)} %shard_map.383.refs_0_), channel_id=1, source_target_pairs={{0,16},{4,20},{8,24},{12,28},{16,0},{20,4},{24,8},{28,12},{1,17},{... | collective-permute-start | bytes 380936 | tf_op jit(solution)/shard_map/ppermute | solution.py:928
  145.0 6.4 %collective-permute-done.29.refs_1_ = bf16[496,128]{1,0:T(8,128)(2,1)S(1)} collective-permute-done((bf16[496,128]{1,0:T(8,128)(2,1)S(1)}, bf16[496,128]{1,0:T(8,128)(2,1)S(1)}, u32[]{:S(2)}, u32[]{:S(2)}) %collective-permute-start.29) | collective-permute-done | bytes 127008 | tf_op jit(solution)/shard_map/ppermute | solution.py:928
  155.6 2.2 %shard_map.384 = (f32[192,768]{1,0:T(8,128)}, f32[192,768]{1,0:T(8,128)}, f32[192,768]{1,0:T(8,128)}, f32[12,192]{1,0:T(8,128)}, f32[1,192]{1,0:T(1,128)}, /*ind...) custom-call(s32[3]{0:T(128)S(1)} %pad_add_fusion.ids_smem, ...), custom_call_target="tpu_custom_call" | custom-call | flops 20000000000 | bytes 20000000 | tf_op jit(solution)/shard_map/pallas_call | solution.py:910
  158.1 4.6 %shard_map.385 = (f32[768,512]{1,0:T(8,128)}, f32[768,512]{1,0:T(8,128)}, f32[512,768]{1,0:T(8,128)}, f32[192,768]{1,0:T(8,128)}, f32[192,768]{1,0:T(8,128)}, /*index=5*/f32[768,256]{1,0:T(8,128)}, f32[768,256]{1,0:T(8,128)}) custom-call(s32[3]{0:T(128)S(1)} %pad_add_fusion.ids_smem, bf16[1824,128]{1,0:T(8,128)(2,1)S(1)} %shard_map.381.refs_0_, ...), custom_call_target="tpu_custom_call" | custom-call | flops 20000000000 | bytes 20000000 | tf_op jit(solution)/shard_map/pallas_call | solution.py:910
  (166 shorter events, 45.6 us)
Async XLA Ops:
  0.7 25.7 %collective-permute-start = (bf16[128,768]{1,0:T(8,128)(2,1)}, bf16[128,768]{1,0:T(8,128)(2,1)S(1)}, u32[]{:S(2)}, u32[]{:S(2)}) collective-permute-start(bf16[128,768]{1,0:T(8,128)(2,1)} %bitcast.19), channel_id=1, source_target_pairs={{0,1},{1,0},{2,3},{3,2},{4,5},{5,4},{6,7},{7,6},{8,9},{9,8},{10,11... | collective-permute-start | bytes 589832 | tf_op jit(solution)/shard_map/ppermute | solution.py:928
  3.7 22.6 %collective-permute-start.1 = (bf16[128,768]{1,0:T(8,128)(2,1)}, bf16[128,768]{1,0:T(8,128)(2,1)S(1)}, u32[]{:S(2)}, u32[]{:S(2)}) collective-permute-start(bf16[128,768]{1,0:T(8,128)(2,1)} %bitcast.20), channel_id=1, source_target_pairs={{0,2},{1,3},{2,0},{3,1},{4,6},{5,7},{6,4},{7,5},{8,10},{9,11},{10,... | collective-permute-start | bytes 589832 | tf_op jit(solution)/shard_map/ppermute | solution.py:928
  6.3 20.0 %collective-permute-start.2 = (bf16[128,768]{1,0:T(8,128)(2,1)}, bf16[128,768]{1,0:T(8,128)(2,1)S(1)}, u32[]{:S(2)}, u32[]{:S(2)}) collective-permute-start(bf16[128,768]{1,0:T(8,128)(2,1)} %bitcast.21), channel_id=1, source_target_pairs={{0,3},{1,2},{2,1},{3,0},{4,7},{5,6},{6,5},{7,4},{8,11},{9,10},{10,... | collective-permute-start | bytes 589832 | tf_op jit(solution)/shard_map/ppermute | solution.py:928
  26.4 10.3 %collective-permute-start.4 = (bf16[128,768]{1,0:T(8,128)(2,1)}, bf16[128,768]{1,0:T(8,128)(2,1)S(1)}, u32[]{:S(2)}, u32[]{:S(2)}) collective-permute-start(bf16[128,768]{1,0:T(8,128)(2,1)} %copy-done.14), channel_id=1, source_target_pairs={{0,1},{1,0},{2,3},{3,2},{4,5},{5,4},{6,7},{7,6},{8,9},{9,8},{10,11... | collective-permute-start | bytes 589832 | tf_op jit(solution)/shard_map/ppermute | solution.py:928
  27.3 11.9 %collective-permute-start.3 = (bf16[128,768]{1,0:T(8,128)(2,1)}, bf16[128,768]{1,0:T(8,128)(2,1)S(1)}, u32[]{:S(2)}, u32[]{:S(2)}) collective-permute-start(bf16[128,768]{1,0:T(8,128)(2,1)} %copy-done.14), channel_id=1, source_target_pairs={{0,2},{1,3},{2,0},{3,1},{4,6},{5,7},{6,4},{7,5},{8,10},{9,11},{10,... | collective-permute-start | bytes 589832 | tf_op jit(solution)/shard_map/ppermute | solution.py:928
  40.7 15.6 %collective-permute-start.6 = (bf16[128,768]{1,0:T(8,128)(2,1)S(1)}, bf16[128,768]{1,0:T(8,128)(2,1)S(1)}, u32[]{:S(2)}, u32[]{:S(2)}) collective-permute-start(bf16[128,768]{1,0:T(8,128)(2,1)S(1)} %get-tuple-element.186), channel_id=1, source_target_pairs={{0,1},{1,0},{2,3},{3,2},{4,5},{5,4},{6,7},{7,6},{8,9},{9,8},{10,11... | collective-permute-start | bytes 589832 | tf_op jit(solution)/shard_map/ppermute | solution.py:928
  42.6 16.6 %collective-permute-start.7 = (bf16[128,768]{1,0:T(8,128)(2,1)S(1)}, bf16[128,768]{1,0:T(8,128)(2,1)S(1)}, u32[]{:S(2)}, u32[]{:S(2)}) collective-permute-start(bf16[128,768]{1,0:T(8,128)(2,1)S(1)} %get-tuple-element.187), channel_id=1, source_target_pairs={{0,2},{1,3},{2,0},{3,1},{4,6},{5,7},{6,4},{7,5},{8,10},{9,11},{10,... | collective-permute-start | bytes 589832 | tf_op jit(solution)/shard_map/ppermute | solution.py:928
  49.5 9.7 %collective-permute-start.8 = (bf16[128,768]{1,0:T(8,128)(2,1)S(1)}, bf16[128,768]{1,0:T(8,128)(2,1)S(1)}, u32[]{:S(2)}, u32[]{:S(2)}) collective-permute-start(bf16[128,768]{1,0:T(8,128)(2,1)S(1)} %get-tuple-element.188), channel_id=1, source_target_pairs={{0,3},{1,2},{2,1},{3,0},{4,7},{5,6},{6,5},{7,4},{8,11},{9,10},{10,... | collective-permute-start | bytes 589832 | tf_op jit(solution)/shard_map/ppermute | solution.py:928
  65.9 24.4 %collective-permute-start.12 = (bf16[128,768]{1,0:T(8,128)(2,1)S(1)}, bf16[128,768]{1,0:T(8,128)(2,1)S(1)}, u32[]{:S(2)}, u32[]{:S(2)}) collective-permute-start(bf16[128,768]{1,0:T(8,128)(2,1)S(1)} %get-tuple-element.224), channel_id=1, source_target_pairs={{0,1},{1,0},{2,3},{3,2},{4,5},{5,4},{6,7},{7,6},{8,9},{9,8},{10,11... | collective-permute-start | bytes 589832 | tf_op jit(solution)/shard_map/ppermute | solution.py:928
  68.6 21.7 %collective-permute-start.13 = (bf16[128,768]{1,0:T(8,128)(2,1)S(1)}, bf16[128,768]{1,0:T(8,128)(2,1)S(1)}, u32[]{:S(2)}, u32[]{:S(2)}) collective-permute-start(bf16[128,768]{1,0:T(8,128)(2,1)S(1)} %get-tuple-element.225), channel_id=1, source_target_pairs={{0,2},{1,3},{2,0},{3,1},{4,6},{5,7},{6,4},{7,5},{8,10},{9,11},{10,... | collective-permute-start | bytes 589832 | tf_op jit(solution)/shard_map/ppermute | solution.py:928
  69.2 21.2 %collective-permute-start.14 = (bf16[128,768]{1,0:T(8,128)(2,1)S(1)}, bf16[128,768]{1,0:T(8,128)(2,1)S(1)}, u32[]{:S(2)}, u32[]{:S(2)}) collective-permute-start(bf16[128,768]{1,0:T(8,128)(2,1)S(1)} %get-tuple-element.226), channel_id=1, source_target_pairs={{0,3},{1,2},{2,1},{3,0},{4,7},{5,6},{6,5},{7,4},{8,11},{9,10},{10,... | collective-permute-start | bytes 589832 | tf_op jit(solution)/shard_map/ppermute | solution.py:928
  71.0 19.3 %collective-permute-start.15 = (bf16[2,2304,128]{2,1,0:T(8,128)(2,1)S(1)}, bf16[2,2304,128]{2,1,0:T(8,128)(2,1)S(1)}, u32[]{:S(2)}, u32[]{:S(2)}) collective-permute-start(bf16[2,2304,128]{2,1,0:T(8,128)(2,1)S(1)} %get-tuple-element.228), channel_id=1, source_target_pairs={{0,8},{4,20},{8,0},{12,28},{16,24},{20,4},{24,16},{28,12},{1,9},{5... | collective-permute-start | bytes 3538952 | tf_op jit(solution)/shard_map/ppermute | solution.py:973
  91.4 12.0 %collective-permute-start.19 = (bf16[2304,128]{1,0:T(8,128)(2,1)S(1)}, bf16[2304,128]{1,0:T(8,128)(2,1)S(1)}, u32[]{:S(2)}, u32[]{:S(2)}) collective-permute-start(bf16[2304,128]{1,0:T(8,128)(2,1)S(1)} %get-tuple-element.244), channel_id=1, source_target_pairs={{0,16},{4,12},{8,24},{12,4},{16,0},{20,28},{24,8},{28,20},{1,17},{... | collective-permute-start | bytes 1769480 | tf_op jit(solution)/shard_map/ppermute | solution.py:977
  92.9 10.5 %collective-permute-start.18 = (bf16[3,128,768]{2,1,0:T(8,128)(2,1)S(1)}, bf16[3,128,768]{2,1,0:T(8,128)(2,1)S(1)}, u32[]{:S(2)}, u32[]{:S(2)}) collective-permute-start(bf16[3,128,768]{2,1,0:T(8,128)(2,1)S(1)} %get-tuple-element.234.triple_ref), channel_id=1, source_target_pairs={{0,4},{4,0},{8,12},{12,8},{16,20},{20,16},{24,28},{28,24},{1,5},{5... | collective-permute-start | bytes 1769480 | tf_op jit(solution)/shard_map/ppermute | solution.py:928
  104.9 13.5 %collective-permute-start.21 = (bf16[2,1792,128]{2,1,0:T(8,128)(2,1)S(1)}, bf16[2,1792,128]{2,1,0:T(8,128)(2,1)S(1)}, u32[]{:S(2)}, u32[]{:S(2)}) collective-permute-start(bf16[2,1792,128]{2,1,0:T(8,128)(2,1)S(1)} %get-tuple-element.254), channel_id=1, source_target_pairs={{0,8},{4,20},{8,0},{12,28},{16,24},{20,4},{24,16},{28,12},{1,9},{5... | collective-permute-start | bytes 2752520 | tf_op jit(solution)/shard_map/ppermute | solution.py:973
  107.0 13.2 %collective-permute-start.22 = (bf16[672,128]{1,0:T(8,128)(2,1)S(1)}, bf16[672,128]{1,0:T(8,128)(2,1)S(1)}, u32[]{:S(2)}, u32[]{:S(2)}) collective-permute-start(bf16[672,128]{1,0:T(8,128)(2,1)S(1)} %get-tuple-element.257), channel_id=1, source_target_pairs={{0,1},{1,0},{2,3},{3,2},{4,5},{5,4},{6,7},{7,6},{8,9},{9,8},{10,11... | collective-permute-start | bytes 516104 | tf_op jit(solution)/shard_map/ppermute | solution.py:928
  108.1 15.5 %collective-permute-start.23 = (bf16[672,128]{1,0:T(8,128)(2,1)S(1)}, bf16[672,128]{1,0:T(8,128)(2,1)S(1)}, u32[]{:S(2)}, u32[]{:S(2)}) collective-permute-start(bf16[672,128]{1,0:T(8,128)(2,1)S(1)} %get-tuple-element.258), channel_id=1, source_target_pairs={{0,2},{1,3},{2,0},{3,1},{4,6},{5,7},{6,4},{7,5},{8,10},{9,11},{10,... | collective-permute-start | bytes 516104 | tf_op jit(solution)/shard_map/ppermute | solution.py:928
  109.6 14.0 %collective-permute-start.24 = (bf16[672,128]{1,0:T(8,128)(2,1)S(1)}, bf16[672,128]{1,0:T(8,128)(2,1)S(1)}, u32[]{:S(2)}, u32[]{:S(2)}) collective-permute-start(bf16[672,128]{1,0:T(8,128)(2,1)S(1)} %get-tuple-element.259), channel_id=1, source_target_pairs={{0,3},{1,2},{2,1},{3,0},{4,7},{5,6},{6,5},{7,4},{8,11},{9,10},{10,... | collective-permute-start | bytes 516104 | tf_op jit(solution)/shard_map/ppermute | solution.py:928
  127.8 12.9 %collective-permute-start.36 = (bf16[1824,128]{1,0:T(8,128)(2,1)S(1)}, bf16[1824,128]{1,0:T(8,128)(2,1)S(1)}, u32[]{:S(2)}, u32[]{:S(2)}) collective-permute-start(bf16[1824,128]{1,0:T(8,128)(2,1)S(1)} %shard_map.381.refs_0_), channel_id=1, source_target_pairs={{0,16},{4,12},{8,24},{12,4},{16,0},{20,28},{24,8},{28,20},{1,17},{... | collective-permute-start | bytes 1400840 | tf_op jit(solution)/shard_map/ppermute | solution.py:977
  129.4 11.3 %collective-permute-start.26 = (bf16[496,128]{1,0:T(8,128)(2,1)S(1)}, bf16[496,128]{1,0:T(8,128)(2,1)S(1)}, u32[]{:S(2)}, u32[]{:S(2)}) collective-permute-start(bf16[496,128]{1,0:T(8,128)(2,1)S(1)} %get-tuple-element.268), channel_id=1, source_target_pairs={{0,1},{1,0},{2,3},{3,2},{4,5},{5,4},{6,7},{7,6},{8,9},{9,8},{10,11... | collective-permute-start | bytes 380936 | tf_op jit(solution)/shard_map/ppermute | solution.py:928
  130.4 10.3 %collective-permute-start.27 = (bf16[496,128]{1,0:T(8,128)(2,1)S(1)}, bf16[496,128]{1,0:T(8,128)(2,1)S(1)}, u32[]{:S(2)}, u32[]{:S(2)}) collective-permute-start(bf16[496,128]{1,0:T(8,128)(2,1)S(1)} %get-tuple-element.269), channel_id=1, source_target_pairs={{0,2},{1,3},{2,0},{3,1},{4,6},{5,7},{6,4},{7,5},{8,10},{9,11},{10,... | collective-permute-start | bytes 380936 | tf_op jit(solution)/shard_map/ppermute | solution.py:928
  133.8 21.3 %collective-permute-start.37 = (bf16[1824,128]{1,0:T(8,128)(2,1)S(1)}, bf16[1824,128]{1,0:T(8,128)(2,1)S(1)}, u32[]{:S(2)}, u32[]{:S(2)}) collective-permute-start(bf16[1824,128]{1,0:T(8,128)(2,1)S(1)} %shard_map.381.refs_0_), channel_id=1, source_target_pairs={{0,8},{4,20},{8,0},{12,28},{16,24},{20,4},{24,16},{28,12},{1,9},{5... | collective-permute-start | bytes 1400840 | tf_op jit(solution)/shard_map/ppermute | solution.py:973
  140.7 14.7 %collective-permute-start.38 = (bf16[1824,128]{1,0:T(8,128)(2,1)S(1)}, bf16[1824,128]{1,0:T(8,128)(2,1)S(1)}, u32[]{:S(2)}, u32[]{:S(2)}) collective-permute-start(bf16[1824,128]{1,0:T(8,128)(2,1)S(1)} %collective-permute-done.36.refs_1_), channel_id=1, source_target_pairs={{0,8},{4,20},{8,0},{12,28},{16,24},{20,4},{24,16},{28,12},{1,9},{5... | collective-permute-start | bytes 1400840 | tf_op jit(solution)/shard_map/ppermute | solution.py:973
  140.8 10.6 %collective-permute-start.29 = (bf16[496,128]{1,0:T(8,128)(2,1)S(1)}, bf16[496,128]{1,0:T(8,128)(2,1)S(1)}, u32[]{:S(2)}, u32[]{:S(2)}) collective-permute-start(bf16[496,128]{1,0:T(8,128)(2,1)S(1)} %shard_map.383.refs_0_), channel_id=1, source_target_pairs={{0,8},{4,12},{8,0},{12,4},{16,24},{20,28},{24,16},{28,20},{1,9},{5... | collective-permute-start | bytes 380936 | tf_op jit(solution)/shard_map/ppermute | solution.py:928
  (60 other events, 521.4 us)

commit v4 on v3

--- a/solution.py
+++ b/solution.py
@@ -8,7 +8,8 @@
 from jax.sharding import PartitionSpec as P
 
 MB = 16
-GROUP = 3
+FORWARD_HEADS = 6
+BACKWARD_HEADS = 3
 EPSILON = 1e-06
 BASE_RATE = 0.1
 F32 = jnp.float32
@@ -109,7 +110,8 @@
         nq_ref,
         sq_ref,
     ) = kept
-    q_s, k_s, v_s, out_s, w1_s, w1b_s, b1_s, w2_s, b2_s, b1f, b2f, igf, ibf, weights_s, sems = scratch
+    q_s, k_s, v_s, out_s, base_s, mix_s, w2_s, b2_s = scratch[0:8]
+    b1f, b2f, igf, ibf, weights_s, sems, state_sems = scratch[8:]
     length, width = tok_ref.shape[1], tok_ref.shape[2]
     copies = [
         pltpu.make_async_copy(w, weights_s.at[i], sems.at[i])
@@ -117,9 +119,11 @@
     ]
     for copy in copies:
         copy.start()
-    saves = [
-        pltpu.make_async_copy(kept[i], outs[i], sems.at[len(copies) + i]) for i in range(saved)
-    ]
+    saves = {
+        i: pltpu.make_async_copy(kept[i], outs[i], sems.at[len(copies) + i])
+        for i in range(saved)
+        if i != 15
+    }
 
     def save(*indices):
         for i in indices:
@@ -157,6 +161,13 @@
     for h in range(heads):
         qk_ref[h, length : 2 * length] = low(k_s[h])
 
+    d1_ref[...] = jnp.zeros(d1_ref.shape, BF16)
+    inclusive, strict = segment_masks(seg_row)
+    for h in range(heads):
+        keys = qk_ref[h, length : 2 * length]
+        mix_s[h] = low((dot(keys, keys, 1, 1) + 1.0) * (strict * erow_ref[h : h + 1, :]))
+        base_s[h] = dot(keys, w1_ref[h]) + b1f[h : h + 1]
+
     def step(b, carry):
         here = pl.multiple_of(b * MB, MB)
         before = jnp.maximum(here - 1, 0)
@@ -167,15 +178,12 @@
         k = [k_s[h, ds, :] for h in rng]
         v = [v_s[h, ds, :] for h in rng]
         e = [ecol_ref[ds, h : h + 1] for h in rng]
-        w1f = [jnp.where(fresh, w1_ref[h].astype(F32), w1_s[h]) for h in rng]
         w2f = [jnp.where(fresh, w2t_ref[h].astype(F32), w2_s[h]) for h in rng]
-        w1 = [low(w1f[h]) for h in rng]
         w2 = [low(w2f[h]) for h in rng]
-        b1 = [jnp.where(fresh, b1f[h : h + 1], b1_s[h]) for h in rng]
         b2 = [jnp.where(fresh, b2f[h : h + 1], b2_s[h]) for h in rng]
         g = [igf[h : h + 1] for h in rng]
         gb = [ibf[h : h + 1] for h in rng]
-        parts = [gelu_parts(dot(low(k[h]), w1[h]) + b1[h]) for h in rng]
+        parts = [gelu_parts(base_s[h, ds, :] - dot(mix_s[h, ds, :], d1_ref[h])) for h in rng]
         act = [low(parts[h][0]) for h in rng]
         z2 = [dot(act[h], w2[h], 1, 1) + b2[h] for h in rng]
         c = [z - mean_last(z) for z in z2]
@@ -190,14 +198,10 @@
         d1 = [back[h] * parts[h][1] for h in rng]
         d1b = [low(d1[h]) for h in rng]
         ed2 = [d2[h] * e[h] for h in rng]
-        up1 = [dot(low(k[h] * e[h]), d1b[h], 0, 0) for h in rng]
         up2 = [dot(low(ed2[h]), act[h], 0, 0) for h in rng]
         for h in rng:
-            w1n = w1f[h] - up1[h]
-            w1_s[h] = w1n
             w2s_ref[b, h] = w2[h]
             w2_s[h] = w2f[h] - up2[h]
-            b1_s[h] = b1[h] - sum_rows(d1[h] * e[h])
             b2_s[h] = b2[h] - sum_rows(ed2[h])
             act_ref[h, pl.ds(length + here, MB), :] = act[h]
             slope1_ref[h, ds, :] = low(parts[h][1])
@@ -207,19 +211,19 @@
             n_ref[h, ds, :] = low(n[h])
             s_ref[ds, h : h + 1] = s[h]
             fit_ref[h, ds, :] = low(fit[h])
+        pltpu.make_async_copy(w2s_ref.at[b], outs[15].at[b], state_sems.at[b]).start()
         return carry
 
     save(4, 5, 6)
     lax.fori_loop(0, blocks, step, 0, unroll=4)
-    save(7, 8, 10, 11, 12, 13, 14, 15)
+    save(7, 8, 10, 11, 12, 13, 14)
     project(2, q_s)
     for h in range(heads):
         qk_ref[h, 0:length] = low(q_s[h])
     save(3)
-    inclusive, _ = segment_masks(seg_row)
-    for start in range(0, heads, GROUP):
-        rng = range(start, start + GROUP)
-        every = range(GROUP)
+    for start in range(0, heads, FORWARD_HEADS):
+        rng = range(start, start + FORWARD_HEADS)
+        every = range(FORWARD_HEADS)
         queries = [qk_ref[h, 0:length] for h in rng]
         keys = [qk_ref[h, length : 2 * length] for h in rng]
         key_act = [act_ref[h, length : 2 * length] for h in rng]
@@ -265,8 +269,10 @@
     spread_two = lax.rsqrt(mean_last(resid * resid) + EPSILON)
     normed_two_ref[...] = low(resid * spread_two * row_of(gain2_ref))
     save(0, 1, 2)
-    for copy in saves:
+    for copy in saves.values():
         copy.wait()
+    for b in range(blocks):
+        pltpu.make_async_copy(w2s_ref.at[b], outs[15].at[b], state_sems.at[b]).wait()
 
 
 def ffn_kernel(x_ref, c_ref, wg_ref, wu_ref, wd_ref, act_ref, gg_ref, gu_ref, gx_ref):
@@ -380,11 +386,8 @@
     u_s,
     share_s,
     ge_s,
-    gw1_s,
-    gw1b_s,
-    gb1_s,
+    mix_s,
     gw2_s,
-    gw2b_s,
     gb2_s,
 ):
     length = go_ref.shape[0]
@@ -393,9 +396,9 @@
     top, bottom = slice(0, length), slice(length, 2 * length)
     igf[...] = ig_ref[...].astype(F32)
     inclusive, strict = segment_masks(seg_ref[...].astype(F32))
-    for first in range(0, heads, GROUP):
-        rng = range(first, first + GROUP)
-        every = range(GROUP)
+    for first in range(0, heads, BACKWARD_HEADS):
+        rng = range(first, first + BACKWARD_HEADS)
+        every = range(BACKWARD_HEADS)
         g = [igf[h : h + 1] for h in rng]
         weigh = [inclusive * erow_ref[h : h + 1, :] for h in rng]
         n = [nq_ref[h].astype(F32) for h in rng]
@@ -423,6 +426,11 @@
             hh1_s[h, top] = hq1[i]
             t1_s[h] = t1[i]
     ge_s[...] = jnp.zeros(ge_s.shape, F32)
+    earlier = jnp.transpose(strict)
+    for h in range(heads):
+        keys = qk_ref[h, bottom]
+        mix_s[h] = low((dot(keys, keys, 1, 1) + 1.0) * earlier)
+    hh1_s[:, bottom, :] = jnp.zeros(hh1_s[:, bottom, :].shape, BF16)
 
     def step(i, carry):
         b = blocks - 1 - i
@@ -433,15 +441,11 @@
         ds = pl.ds(here, MB)
         ds_low = pl.ds(length + here, MB)
         rng = range(heads)
-        k = [qk_ref[h, ds_low, :] for h in rng]
         act = [act_ref[h, ds_low, :] for h in rng]
         e = [ecol_ref[ds, h : h + 1] for h in rng]
         w2 = [w2s_ref[b, h] for h in rng]
-        gw1 = [jnp.where(fresh, 0.0, gw1_s[h]) for h in rng]
         gw2 = [jnp.where(fresh, 0.0, gw2_s[h]) for h in rng]
-        gw1b = [low(x) for x in gw1]
         gw2b = [low(x) for x in gw2]
-        gb1 = [jnp.where(fresh, 0.0, gb1_s[h]) for h in rng]
         gb2 = [jnp.where(fresh, 0.0, gb2_s[h]) for h in rng]
         d1 = [d1_ref[h, ds, :].astype(F32) for h in rng]
         d2 = [d2_ref[h, ds, :].astype(F32) for h in rng]
@@ -452,7 +456,7 @@
         curve = [curve1_ref[h, ds, :].astype(F32) for h in rng]
         g = [igf[h : h + 1] for h in rng]
         share = [g[h] * fit[h] for h in rng]
-        t1 = [t1_s[h, ds, :] + dot(k[h], gw1b[h]) + gb1[h] for h in rng]
+        t1 = [t1_s[h, ds, :] + dot(mix_s[h, ds, :], hh1_s[h, bottom]) for h in rng]
         t2 = [t2_s[h, ds, :] + dot(act[h], gw2b[h], 1, 1) + gb2[h] for h in rng]
         g1 = [-e[h] * t1[h] for h in rng]
         u = [low(g1[h] * slope[h]) for h in rng]
@@ -474,16 +478,12 @@
         ga = [ga[h] + dot(h2[h], w2[h]) for h in rng]
         h1f = [ga[h] * slope[h] + g1[h] * curve[h] for h in rng]
         h1 = [low(x) for x in h1f]
-        up1 = [dot(k[h], h1[h], 0, 0) for h in rng]
         up2 = [
             dot(low(d2[h]), u[h], 0, 0) + dot(h2[h], act[h], 0, 0) for h in rng
         ]
         for h in rng:
-            w1n = gw1[h] + up1[h]
             w2n = gw2[h] + up2[h]
-            gw1_s[h] = w1n
             gw2_s[h] = w2n
-            gb1_s[h] = gb1[h] + sum_rows(h1f[h])
             gb2_s[h] = gb2[h] + sum_rows(h2[h].astype(F32))
             u_s[h, ds, :] = u[h]
             hh1_s[h, ds_low, :] = h1[h]
@@ -498,9 +498,9 @@
     small_ref[...] = jnp.zeros(small_ref.shape, F32)
     core = ids_smem[0]
     pad = small_ref.shape[0] // 2
-    for start in range(0, heads, GROUP):
-        rng = range(start, start + GROUP)
-        every = range(GROUP)
+    for start in range(0, heads, BACKWARD_HEADS):
+        rng = range(start, start + BACKWARD_HEADS)
+        every = range(BACKWARD_HEADS)
         cols = [slice(h * head, (h + 1) * head) for h in rng]
         g = [igf[h : h + 1] for h in rng]
         er = [erow_ref[h : h + 1, :] for h in rng]
@@ -811,10 +811,16 @@
     first, second = 1 + core, 2 - core
     pieces = [(refs[s], refs[4 + s]) for s in range(4)]
     order = [(0, 0), (second, first), (first, second), (3, 3)]
-    gate_ref, up_ref, down_ref, wg_ref, wo_ref, first_ref, second_ref, down_s = refs[8:]
-    take_matrices(ids_smem, pieces, (wg_ref, wo_ref), order=order)
+    outs, kept, down_s, sems = refs[8:15], refs[15:22], refs[22], refs[23]
+    gate_ref, up_ref, down_ref, wg_ref, wo_ref, first_ref, second_ref = kept
+    saves = [pltpu.make_async_copy(kept[i], outs[i], sems.at[i]) for i in range(7)]
     rows = first_ref.shape[0] // 4
     start = 2 * (wg_ref.shape[0] // 4) * (wg_ref.shape[1] // 256)
+    take_matrices(ids_smem, pieces, (gate_ref, up_ref, down_s), start + 2 * rows, order)
+    saves[0].start()
+    saves[1].start()
+    down_ref[...] = jnp.transpose(down_s[...])
+    saves[2].start()
     for s, both in enumerate(pieces):
         ats = [
             pl.ds(pl.multiple_of(lax.bitwise_xor(chip, d) * rows, 16), rows) for d in order[s]
@@ -835,8 +841,13 @@
                 first_ref[ats[1], cols] = other
                 second_ref[ats[0], cols] = mine
 
-    take_matrices(ids_smem, pieces, (gate_ref, up_ref, down_s), start + 2 * rows, order)
-    down_ref[...] = jnp.transpose(down_s[...])
+    saves[5].start()
+    saves[6].start()
+    take_matrices(ids_smem, pieces, (wg_ref, wo_ref), order=order)
+    saves[3].start()
+    saves[4].start()
+    for copy in saves:
+        copy.wait()
 
 
 def late_totals_kernel(chips, feats, heads, head, ids_smem, *refs):
@@ -890,7 +901,7 @@
 
 
 def call(
-    kernel, outs, inputs, scratch=(), smem=0, cover=True, plain=(), loose=(), keep=True, mib=24
+    kernel, outs, inputs, scratch=(), smem=0, cover=1, plain=(), loose=(), keep=True, mib=24
 ):
     specs, placed = [], []
     for i, x in enumerate(inputs):
@@ -918,7 +929,7 @@
         ],
         scratch_shapes=[pltpu.VMEM(*x) if isinstance(x, tuple) else x for x in scratch],
         cost_estimate=pl.CostEstimate(
-            flops=int(2e10 if cover else 1e6), bytes_accessed=int(2e7 if cover else 1e3), transcendentals=0
+            flops=int(2e10 * cover + 1e6), bytes_accessed=int(2e7 * cover + 1e3), transcendentals=0
         ),
         compiler_params=pltpu.CompilerParams(vmem_limit_bytes=mib * 2**20),
     )(*placed)
@@ -1103,9 +1114,8 @@
             (slim, F32),
             (slim, F32),
             (line, F32),
-            (state, F32),
-            (state, BF16),
-            ((heads, 1, inner), F32),
+            (wide, F32),
+            (square, BF16),
             (state, F32),
             ((heads, 1, head), F32),
             ((heads, inner), F32),
@@ -1114,6 +1124,7 @@
             ((heads, head), F32),
             ((5, width, width), BF16),
             pltpu.SemaphoreType.DMA((5 + len(kept),)),
+            pltpu.SemaphoreType.DMA((blocks,)),
         ],
         smem=1,
         plain=range(19),
@@ -1147,7 +1158,7 @@
         gus.append(gu)
         pieces.append(gx)
     if feats > 2:
-        pieces[1], _ = lax.optimization_barrier((pieces[1], acts[2]))
+        pieces[1], _ = lax.optimization_barrier((pieces[1], acts[3]))
     pieces = across_feats(pieces, feats)
 
     def between(pieces):
@@ -1180,11 +1191,8 @@
                 (wide, BF16),
                 (slim, F32),
                 ((length, 128), F32),
+                (square, BF16),
                 (state, F32),
-                (state, BF16),
-                ((heads, 1, inner), F32),
-                (state, F32),
-                (state, BF16),
                 ((heads, 1, head), F32),
             ],
             smem=2,
@@ -1200,7 +1208,7 @@
             [triple, grad_rates, pair, w_query, w_key, w_value, w_rate_t, part]
             + [tokens, norm1_gain, grad_resid, small, grad_gain_two],
             keep=(False, True),
-            cover=False,
+            cover=0,
         )
 
     if chips != 4 or (width // feats) % step or hidden % 256 or width % 256:
@@ -1253,7 +1261,6 @@
         [resid] + out + [early, early_got],
         keep=(False, True, True),
     )
-    early_got = second_axis(early_sent, rows)
     tail = 2 * heads * head // chips
     tails, tails_sent = launch(
         tails_kernel,
@@ -1261,12 +1268,13 @@
         [ids, kept, inner_got],
         [((chips, tail, 128), BF16)],
         smem=1,
-        cover=False,
+        cover=0,
     )
     tails_got = first_axis(tails_sent, rows)
+    early_sent, _ = lax.optimization_barrier((early_sent, tails_sent))
+    early_got = second_axis(early_sent, rows)
     grad_tokens, small = finish(triple, grad_rates, small, part, grad_resid, grad_gain_two)
-    tails, tails_got = halved(launch, tails, tails_got, rows, False)
-    early_got, small = lax.optimization_barrier((early_got, small))
+    tails, tails_got = halved(launch, tails, tails_got, rows, 0)
     common = 2 * small_rows // chips
     late, late_sent = launch(
         partial(late_weights_kernel, feats),
@@ -1278,6 +1286,7 @@
             ((3, 2 * length, half), BF16),
         ],
         smem=1,
+        cover=2,
     )
     late_got = first_axis(late_sent, rows)
     ffn_total, *cut = launch(
@@ -1287,7 +1296,7 @@
         smem=1,
     )
     cut = across_feats(cut, feats)
-    late, late_got = halved(launch, late, late_got, rows, True)
+    late, late_got = halved(launch, late, late_got, rows, 1)
     (joined,) = launch(
         join_kernel, [((2 * per + tail + ffn_rows, 128), BF16)], cut + [ffn_total]
     )
@@ -1296,7 +1305,7 @@
         [((3 * per + common, 128), BF16)] * feats,
         [ids, late, late_got],
         smem=1,
-        cover=False,
+        cover=0,
     )
     joined, late_cut = lax.optimization_barrier((joined, late_cut))
     late_cut = across_feats(late_cut, feats)
@@ -1320,16 +1329,19 @@
         smem=1,
         keep=False,
     )
-    early = launch(
-        early_totals_kernel,
+    kept = (
         [((width, hidden), F32)] * 2
         + [((hidden, width), F32)]
         + [(share, F32)] * 2
-        + [((heads * head, inner), F32)] * 2,
+        + [((heads * head, inner), F32)] * 2
+    )
+    early = launch(
+        early_totals_kernel,
+        kept,
         [ids] + joined,
-        [((width, hidden), F32)],
+        kept + [((width, hidden), F32), pltpu.SemaphoreType.DMA((len(kept),))],
         smem=1,
-        keep=False,
+        keep=[None] * len(kept),
     )
     early, late = list(early), list(late)
     return arrange(mixed, grad_tokens, early[0:5], late[0:3] + early[5:7] + late[3:], state)

time: 163 us -> 156 us (0.957)
  Pallas kernels: 61.9 us -> 57.2 us
  starting transfers between devices: 46.3 us -> 41.6 us
  waiting for transfers between devices: 51.2 us -> 53.6 us
    pallas_call x21, Pallas kernels: 61.9 us -> 57.2 us  [call(): pl.pallas_call(kernel, out_shape=[pltpu.VMEM(s, d) if k else pltpu.HBM(s,...]
    ppermute x5, waiting for transfers between devices: 11.8 us -> 7.91 us  [first_axis(): lax.ppermute(values, 'rows', [(i, i ^ 2 << (i & 1)) for i in range(rows)])]
    ppermute x34, waiting for transfers between devices: 28.1 us -> 31.3 us  [exchange(): return lax.ppermute(values, axis, [(i, i ^ distance) for i in range(size)])]
    ppermute x4, waiting for transfers between devices: 11.4 us -> 14.4 us  [second_axis(): lax.ppermute(values, 'rows', [(i, i ^ 4 >> (i & 1)) for i in range(rows)])]
    ppermute x34, starting transfers between devices: 37.2 us -> 34.4 us  [exchange(): return lax.ppermute(values, axis, [(i, i ^ distance) for i in range(size)])]
  transfers between devices with their start and end apart: 43 -> 43, of which waited for: 17 -> 20; matrix products, arithmetic and copies ran while one was open for 0% -> 0% of each run, Pallas kernels for 33% -> 32%
where the time goes in v4:
time: 156 us
  Pallas kernels  57.2 us (37%)
  waiting for transfers between devices  53.6 us (34%)
  starting transfers between devices  41.6 us (27%)
  local copies, waits for them, and re-layouts  1.81 us (1%)
    pallas_call x21, Pallas kernels, call(): pl.pallas_call(kernel, out_shape=[pltpu.VMEM(s, d) if k else pltpu.HBM(s,...  57.2 us
    ppermute x34, starting transfers between devices, exchange(): return lax.ppermute(values, axis, [(i, i ^ distance) for i in range(size)])  34.4 us
    ppermute x34, waiting for transfers between devices, exchange(): return lax.ppermute(values, axis, [(i, i ^ distance) for i in range(size)])  31.3 us
    ppermute x4, waiting for transfers between devices, second_axis(): lax.ppermute(values, 'rows', [(i, i ^ 4 >> (i & 1)) for i in range(rows)])  14.4 us
    ppermute x5, waiting for transfers between devices, first_axis(): lax.ppermute(values, 'rows', [(i, i ^ 2 << (i & 1)) for i in range(rows)])  7.91 us
    ppermute x4, starting transfers between devices, second_axis(): lax.ppermute(values, 'rows', [(i, i ^ 4 >> (i & 1)) for i in range(rows)])  3.98 us
    ppermute x5, starting transfers between devices, first_axis(): lax.ppermute(values, 'rows', [(i, i ^ 2 << (i & 1)) for i in range(rows)])  3.21 us
  transfers between devices with their start and end apart: 43, of which 20 were waited for; matrix products, arithmetic and copies ran while one was open for 0% of the time, Pallas kernels for 32%

profile of v4, /device:TPU:0, one launch (start us, length us, event | category | flops | bytes accessed | tf_op | source)
XLA Modules:
  0.0 155.7 jit_solution(16937917785158023033)
XLA Ops:
  0.7 3.1 %collective-permute-start = (bf16[128,768]{1,0:T(8,128)(2,1)}, bf16[128,768]{1,0:T(8,128)(2,1)S(1)}, u32[]{:S(2)}, u32[]{:S(2)}) collective-permute-start(bf16[128,768]{1,0:T(8,128)(2,1)} %bitcast.19), channel_id=1, source_target_pairs={{0,1},{1,0},{2,3},{3,2},{4,5},{5,4},{6,7},{7,6},{8,9},{9,8},{10,11... | collective-permute-start | bytes 589832 | tf_op jit(solution)/shard_map/ppermute | solution.py:939
  3.7 2.6 %collective-permute-start.1 = (bf16[128,768]{1,0:T(8,128)(2,1)}, bf16[128,768]{1,0:T(8,128)(2,1)S(1)}, u32[]{:S(2)}, u32[]{:S(2)}) collective-permute-start(bf16[128,768]{1,0:T(8,128)(2,1)} %bitcast.20), channel_id=1, source_target_pairs={{0,2},{1,3},{2,0},{3,1},{4,6},{5,7},{6,4},{7,5},{8,10},{9,11},{10,... | collective-permute-start | bytes 589832 | tf_op jit(solution)/shard_map/ppermute | solution.py:939
  6.4 16.3 %shard_map.365 = (bf16[2,128,768]{2,1,0:T(8,128)(2,1)S(1)}, bf16[128,768]{1,0:T(8,128)(2,1)S(1)}, f32[128,768]{1,0:T(8,128)}, f32[128,768]{1,0:T(8,128)}, f32[12...) custom-call(s32[1,128]{1,0:T(1,128)} %seg_ref.2, ...), custom_call_target="tpu_custom_call" | custom-call | flops 20000999424 | bytes 20001000 | tf_op jit(solution)/shard_map/pallas_call | solution.py:921
  24.5 3.4 %collective-permute-start.3 = (bf16[128,768]{1,0:T(8,128)(2,1)}, bf16[128,768]{1,0:T(8,128)(2,1)S(1)}, u32[]{:S(2)}, u32[]{:S(2)}) collective-permute-start(bf16[128,768]{1,0:T(8,128)(2,1)} %copy-done.14), channel_id=1, source_target_pairs={{0,2},{1,3},{2,0},{3,1},{4,6},{5,7},{6,4},{7,5},{8,10},{9,11},{10,... | collective-permute-start | bytes 589832 | tf_op jit(solution)/shard_map/ppermute | solution.py:939
  30.2 3.6 %collective-permute-done.4.x_ref.refs_1_ = bf16[128,768]{1,0:T(8,128)(2,1)S(1)} collective-permute-done((bf16[128,768]{1,0:T(8,128)(2,1)}, bf16[128,768]{1,0:T(8,128)(2,1)S(1)}, u32[]{:S(2)}, u32[]{:S(2)}) %collective-permute-start.4) | collective-permute-done | bytes 196640 | tf_op jit(solution)/shard_map/ppermute | solution.py:939
  37.8 2.7 %collective-permute-start.7 = (bf16[128,768]{1,0:T(8,128)(2,1)S(1)}, bf16[128,768]{1,0:T(8,128)(2,1)S(1)}, u32[]{:S(2)}, u32[]{:S(2)}) collective-permute-start(bf16[128,768]{1,0:T(8,128)(2,1)S(1)} %get-tuple-element.186), channel_id=1, source_target_pairs={{0,2},{1,3},{2,0},{3,1},{4,6},{5,7},{6,4},{7,5},{8,10},{9,11},{10,... | collective-permute-start | bytes 589832 | tf_op jit(solution)/shard_map/ppermute | solution.py:939
  40.5 4.9 %collective-permute-done.5.x_ref.refs_3_ = bf16[128,768]{1,0:T(8,128)(2,1)S(1)} collective-permute-done((bf16[128,768]{1,0:T(8,128)(2,1)S(1)}, bf16[128,768]{1,0:T(8,128)(2,1)S(1)}, u32[]{:S(2)}, u32[]{:S(2)}) %collective-permute-start.5) | collective-permute-done | bytes 196640 | tf_op jit(solution)/shard_map/ppermute | solution.py:939
  48.4 3.3 %shard_map.370 = (bf16[3,768,256]{2,1,0:T(8,128)(2,1)S(1)}, bf16[3,768,256]{2,1,0:T(8,128)(2,1)S(1)}, bf16[128,768]{1,0:T(8,128)(2,1)S(1)}, bf16[128,768]{1,0:T(...) custom-call(s32[3]{0:T(128)S(1)} %pad_add_fusion.ids_smem, bf16[128,768]{1,0:T(8,128)(2,1)S(1)} %copy-done.16, ...), custom_call_target="tpu_custom_call" | custom-call | flops 20000999424 | bytes 20001000 | tf_op jit(solution)/shard_map/pallas_call | solution.py:921
  51.8 3.8 %collective-permute-done.6.refs_1_ = bf16[128,768]{1,0:T(8,128)(2,1)S(1)} collective-permute-done((bf16[128,768]{1,0:T(8,128)(2,1)S(1)}, bf16[128,768]{1,0:T(8,128)(2,1)S(1)}, u32[]{:S(2)}, u32[]{:S(2)}) %collective-permute-start.6) | collective-permute-done | bytes 196640 | tf_op jit(solution)/shard_map/ppermute | solution.py:939
  57.2 2.6 %collective-permute-done.9.other_ref = bf16[2,128,768]{2,1,0:T(8,128)(2,1)S(1)} collective-permute-done((bf16[2,128,768]{2,1,0:T(8,128)(2,1)S(1)}, bf16[2,128,768]{2,1,0:T(8,128)(2,1)S(1)}, u32[]{:S(2)}, u32[]{:S(2)}) %collective-permute-start.9) | collective-permute-done | bytes 393248 | tf_op jit(solution)/shard_map/ppermute | solution.py:939
  68.3 16.1 %shard_map.373 = (bf16[3,128,768]{2,1,0:T(8,128)(2,1)S(1)}, bf16[128,128]{1,0:T(8,128)(2,1)S(1)}, bf16[768,256]{1,0:T(8,128)(2,1)S(1)}, bf16[768,256]{1,0:T(8,128)(2,1)S(1)}, f32[32,256]{1,0:T(8,128)S(1)}) custom-call(s32[3]{0:T(128)S(1)} %pad_add_fusion.ids_smem, s32[1,128]{1,0:T(1,128)S(1)} %copy-done.19, s32[1,128]{1,0:T(1,128)S(1)} %copy-done.19, ...), custom_call_target="tpu_custom_call" | custom-call | flops 20000999424 | bytes 20001000 | tf_op jit(solution)/shard_map/pallas_call | solution.py:921
  90.0 2.3 %shard_map.376 = (f32[1,128,768]{2,1,0:T(8,128)}, bf16[128,256]{1,0:T(8,128)(2,1)S(1)}) custom-call(bf16[3,128,768]{2,1,0:T(8,128)(2,1)S(1)} %get-tuple-element.233.triple_ref, bf16[128,128]{1,0:T(8,128)(2,1)S(1)} %get-tuple-element.234.gr_ref, bf16[2,128,768]{2,1,0:T(8,128)(2,1)S(1)} %get-tuple-element.242.mine_ref.pair_ref, bf16[768,768]{1,0:T(8,128)(2,1)S(1)} %copy-done, ...), custom_call_target="tpu_custom_call" | custom-call | flops 1000000 | bytes 1000 | tf_op jit(solution)/shard_map/pallas_call | solution.py:921
  92.2 3.1 %collective-permute-done.17.got_ref = bf16[2,384,128]{2,1,0:T(8,128)(2,1)S(1)} collective-permute-done((bf16[2,384,128]{2,1,0:T(8,128)(2,1)S(1)}, bf16[2,384,128]{2,1,0:T(8,128)(2,1)S(1)}, u32[]{:S(2)}, u32[]{:S(2)}) %collective-permute-start.17) | collective-permute-done | bytes 196640 | tf_op jit(solution)/shard_map/ppermute | solution.py:984
  99.4 2.9 %collective-permute-done.20.refs_3_ = bf16[384,128]{1,0:T(8,128)(2,1)S(1)} collective-permute-done((bf16[384,128]{1,0:T(8,128)(2,1)S(1)}, bf16[384,128]{1,0:T(8,128)(2,1)S(1)}, u32[]{:S(2)}, u32[]{:S(2)}) %collective-permute-start.20) | collective-permute-done | bytes 98336 | tf_op jit(solution)/shard_map/ppermute | solution.py:988
  103.7 2.1 %collective-permute-start.23 = (bf16[672,128]{1,0:T(8,128)(2,1)S(1)}, bf16[672,128]{1,0:T(8,128)(2,1)S(1)}, u32[]{:S(2)}, u32[]{:S(2)}) collective-permute-start(bf16[672,128]{1,0:T(8,128)(2,1)S(1)} %get-tuple-element.256), channel_id=1, source_target_pairs={{0,2},{1,3},{2,0},{3,1},{4,6},{5,7},{6,4},{7,5},{8,10},{9,11},{10,... | collective-permute-start | bytes 516104 | tf_op jit(solution)/shard_map/ppermute | solution.py:939
  107.4 4.8 %collective-permute-done.21.got_ref = bf16[2,1792,128]{2,1,0:T(8,128)(2,1)S(1)} collective-permute-done((bf16[2,1792,128]{2,1,0:T(8,128)(2,1)S(1)}, bf16[2,1792,128]{2,1,0:T(8,128)(2,1)S(1)}, u32[]{:S(2)}, u32[]{:S(2)}) %collective-permute-start.21) | collective-permute-done | bytes 917536 | tf_op jit(solution)/shard_map/ppermute | solution.py:984
  112.7 5.8 %collective-permute-done.23.refs_2_ = bf16[672,128]{1,0:T(8,128)(2,1)S(1)} collective-permute-done((bf16[672,128]{1,0:T(8,128)(2,1)S(1)}, bf16[672,128]{1,0:T(8,128)(2,1)S(1)}, u32[]{:S(2)}, u32[]{:S(2)}) %collective-permute-start.23) | collective-permute-done | bytes 172064 | tf_op jit(solution)/shard_map/ppermute | solution.py:939
  118.7 2.3 %collective-permute-done.25.refs_1_ = bf16[1792,128]{1,0:T(8,128)(2,1)S(1)} collective-permute-done((bf16[1792,128]{1,0:T(8,128)(2,1)S(1)}, bf16[1792,128]{1,0:T(8,128)(2,1)S(1)}, u32[]{:S(2)}, u32[]{:S(2)}) %collective-permute-start.25) | collective-permute-done | bytes 458784 | tf_op jit(solution)/shard_map/ppermute | solution.py:988
  122.8 1.9 %collective-permute-start.27 = (bf16[496,128]{1,0:T(8,128)(2,1)S(1)}, bf16[496,128]{1,0:T(8,128)(2,1)S(1)}, u32[]{:S(2)}, u32[]{:S(2)}) collective-permute-start(bf16[496,128]{1,0:T(8,128)(2,1)S(1)} %get-tuple-element.267), channel_id=1, source_target_pairs={{0,2},{1,3},{2,0},{3,1},{4,6},{5,7},{6,4},{7,5},{8,10},{9,11},{10,... | collective-permute-start | bytes 380936 | tf_op jit(solution)/shard_map/ppermute | solution.py:939
  126.9 9.2 %collective-permute-done.36.refs_1_ = bf16[1824,128]{1,0:T(8,128)(2,1)S(1)} collective-permute-done((bf16[1824,128]{1,0:T(8,128)(2,1)S(1)}, bf16[1824,128]{1,0:T(8,128)(2,1)S(1)}, u32[]{:S(2)}, u32[]{:S(2)}) %collective-permute-start.36) | collective-permute-done | bytes 466976 | tf_op jit(solution)/shard_map/ppermute | solution.py:988
  136.2 2.1 %collective-permute-start.29 = (bf16[496,128]{1,0:T(8,128)(2,1)S(1)}, bf16[496,128]{1,0:T(8,128)(2,1)S(1)}, u32[]{:S(2)}, u32[]{:S(2)}) collective-permute-start(bf16[496,128]{1,0:T(8,128)(2,1)S(1)} %shard_map.383.refs_0_), channel_id=1, source_target_pairs={{0,8},{4,12},{8,0},{12,4},{16,24},{20,28},{24,16},{28,20},{1,9},{5... | collective-permute-start | bytes 380936 | tf_op jit(solution)/shard_map/ppermute | solution.py:939
  139.8 6.2 %collective-permute-done.29.refs_1_ = bf16[496,128]{1,0:T(8,128)(2,1)S(1)} collective-permute-done((bf16[496,128]{1,0:T(8,128)(2,1)S(1)}, bf16[496,128]{1,0:T(8,128)(2,1)S(1)}, u32[]{:S(2)}, u32[]{:S(2)}) %collective-permute-start.29) | collective-permute-done | bytes 127008 | tf_op jit(solution)/shard_map/ppermute | solution.py:939
  148.7 2.2 %shard_map.384 = (f32[192,768]{1,0:T(8,128)}, f32[192,768]{1,0:T(8,128)}, f32[192,768]{1,0:T(8,128)}, f32[12,192]{1,0:T(8,128)}, f32[1,192]{1,0:T(1,128)}, /*ind...) custom-call(s32[3]{0:T(128)S(1)} %pad_add_fusion.ids_smem, ...), custom_call_target="tpu_custom_call" | custom-call | flops 20000999424 | bytes 20001000 | tf_op jit(solution)/shard_map/pallas_call | solution.py:921
  151.3 4.2 %shard_map.385 = (f32[768,512]{1,0:T(8,128)}, f32[768,512]{1,0:T(8,128)}, f32[512,768]{1,0:T(8,128)}, f32[192,768]{1,0:T(8,128)}, f32[192,768]{1,0:T(8,128)}, /*index=5*/f32[768,256]{1,0:T(8,128)}, f32[768,256]{1,0:T(8,128)}) custom-call(s32[3]{0:T(128)S(1)} %pad_add_fusion.ids_smem, bf16[1824,128]{1,0:T(8,128)(2,1)S(1)} %shard_map.381.refs_0_, ...), custom_call_target="tpu_custom_call" | custom-call | flops 20000999424 | bytes 20001000 | tf_op jit(solution)/shard_map/pallas_call | solution.py:921
  (166 shorter events, 42.7 us)
Async XLA Ops:
  0.7 22.8 %collective-permute-start = (bf16[128,768]{1,0:T(8,128)(2,1)}, bf16[128,768]{1,0:T(8,128)(2,1)S(1)}, u32[]{:S(2)}, u32[]{:S(2)}) collective-permute-start(bf16[128,768]{1,0:T(8,128)(2,1)} %bitcast.19), channel_id=1, source_target_pairs={{0,1},{1,0},{2,3},{3,2},{4,5},{5,4},{6,7},{7,6},{8,9},{9,8},{10,11... | collective-permute-start | bytes 589832 | tf_op jit(solution)/shard_map/ppermute | solution.py:939
  3.7 19.7 %collective-permute-start.1 = (bf16[128,768]{1,0:T(8,128)(2,1)}, bf16[128,768]{1,0:T(8,128)(2,1)S(1)}, u32[]{:S(2)}, u32[]{:S(2)}) collective-permute-start(bf16[128,768]{1,0:T(8,128)(2,1)} %bitcast.20), channel_id=1, source_target_pairs={{0,2},{1,3},{2,0},{3,1},{4,6},{5,7},{6,4},{7,5},{8,10},{9,11},{10,... | collective-permute-start | bytes 589832 | tf_op jit(solution)/shard_map/ppermute | solution.py:939
  6.3 17.1 %collective-permute-start.2 = (bf16[128,768]{1,0:T(8,128)(2,1)}, bf16[128,768]{1,0:T(8,128)(2,1)S(1)}, u32[]{:S(2)}, u32[]{:S(2)}) collective-permute-start(bf16[128,768]{1,0:T(8,128)(2,1)} %bitcast.21), channel_id=1, source_target_pairs={{0,3},{1,2},{2,1},{3,0},{4,7},{5,6},{6,5},{7,4},{8,11},{9,10},{10,... | collective-permute-start | bytes 589832 | tf_op jit(solution)/shard_map/ppermute | solution.py:939
  23.5 10.3 %collective-permute-start.4 = (bf16[128,768]{1,0:T(8,128)(2,1)}, bf16[128,768]{1,0:T(8,128)(2,1)S(1)}, u32[]{:S(2)}, u32[]{:S(2)}) collective-permute-start(bf16[128,768]{1,0:T(8,128)(2,1)} %copy-done.14), channel_id=1, source_target_pairs={{0,1},{1,0},{2,3},{3,2},{4,5},{5,4},{6,7},{7,6},{8,9},{9,8},{10,11... | collective-permute-start | bytes 589832 | tf_op jit(solution)/shard_map/ppermute | solution.py:939
  24.5 11.8 %collective-permute-start.3 = (bf16[128,768]{1,0:T(8,128)(2,1)}, bf16[128,768]{1,0:T(8,128)(2,1)S(1)}, u32[]{:S(2)}, u32[]{:S(2)}) collective-permute-start(bf16[128,768]{1,0:T(8,128)(2,1)} %copy-done.14), channel_id=1, source_target_pairs={{0,2},{1,3},{2,0},{3,1},{4,6},{5,7},{6,4},{7,5},{8,10},{9,11},{10,... | collective-permute-start | bytes 589832 | tf_op jit(solution)/shard_map/ppermute | solution.py:939
  36.3 9.2 %collective-permute-start.5 = (bf16[128,768]{1,0:T(8,128)(2,1)S(1)}, bf16[128,768]{1,0:T(8,128)(2,1)S(1)}, u32[]{:S(2)}, u32[]{:S(2)}) collective-permute-start(bf16[128,768]{1,0:T(8,128)(2,1)S(1)} %collective-permute-done.3.x_ref.refs_2_), channel_id=1, source_target_pairs={{0,1},{1,0},{2,3},{3,2},{4,5},{5,4},{6,7},{7,6},{8,9},{9,8},{10,11... | collective-permute-start | bytes 589832 | tf_op jit(solution)/shard_map/ppermute | solution.py:939
  37.8 14.0 %collective-permute-start.7 = (bf16[128,768]{1,0:T(8,128)(2,1)S(1)}, bf16[128,768]{1,0:T(8,128)(2,1)S(1)}, u32[]{:S(2)}, u32[]{:S(2)}) collective-permute-start(bf16[128,768]{1,0:T(8,128)(2,1)S(1)} %get-tuple-element.186), channel_id=1, source_target_pairs={{0,2},{1,3},{2,0},{3,1},{4,6},{5,7},{6,4},{7,5},{8,10},{9,11},{10,... | collective-permute-start | bytes 589832 | tf_op jit(solution)/shard_map/ppermute | solution.py:939
  62.2 22.4 %collective-permute-start.12 = (bf16[128,768]{1,0:T(8,128)(2,1)S(1)}, bf16[128,768]{1,0:T(8,128)(2,1)S(1)}, u32[]{:S(2)}, u32[]{:S(2)}) collective-permute-start(bf16[128,768]{1,0:T(8,128)(2,1)S(1)} %get-tuple-element.223), channel_id=1, source_target_pairs={{0,1},{1,0},{2,3},{3,2},{4,5},{5,4},{6,7},{7,6},{8,9},{9,8},{10,11... | collective-permute-start | bytes 589832 | tf_op jit(solution)/shard_map/ppermute | solution.py:939
  63.8 21.3 %collective-permute-start.13 = (bf16[128,768]{1,0:T(8,128)(2,1)S(1)}, bf16[128,768]{1,0:T(8,128)(2,1)S(1)}, u32[]{:S(2)}, u32[]{:S(2)}) collective-permute-start(bf16[128,768]{1,0:T(8,128)(2,1)S(1)} %get-tuple-element.224), channel_id=1, source_target_pairs={{0,2},{1,3},{2,0},{3,1},{4,6},{5,7},{6,4},{7,5},{8,10},{9,11},{10,... | collective-permute-start | bytes 589832 | tf_op jit(solution)/shard_map/ppermute | solution.py:939
  64.9 20.1 %collective-permute-start.14 = (bf16[128,768]{1,0:T(8,128)(2,1)S(1)}, bf16[128,768]{1,0:T(8,128)(2,1)S(1)}, u32[]{:S(2)}, u32[]{:S(2)}) collective-permute-start(bf16[128,768]{1,0:T(8,128)(2,1)S(1)} %get-tuple-element.225), channel_id=1, source_target_pairs={{0,3},{1,2},{2,1},{3,0},{4,7},{5,6},{6,5},{7,4},{8,11},{9,10},{10,... | collective-permute-start | bytes 589832 | tf_op jit(solution)/shard_map/ppermute | solution.py:939
  66.6 18.4 %collective-permute-start.15 = (bf16[2,2304,128]{2,1,0:T(8,128)(2,1)S(1)}, bf16[2,2304,128]{2,1,0:T(8,128)(2,1)S(1)}, u32[]{:S(2)}, u32[]{:S(2)}) collective-permute-start(bf16[2,2304,128]{2,1,0:T(8,128)(2,1)S(1)} %get-tuple-element.227), channel_id=1, source_target_pairs={{0,8},{4,20},{8,0},{12,28},{16,24},{20,4},{24,16},{28,12},{1,9},{5... | collective-permute-start | bytes 3538952 | tf_op jit(solution)/shard_map/ppermute | solution.py:984
  84.5 12.8 %collective-permute-start.18 = (bf16[3,128,768]{2,1,0:T(8,128)(2,1)S(1)}, bf16[3,128,768]{2,1,0:T(8,128)(2,1)S(1)}, u32[]{:S(2)}, u32[]{:S(2)}) collective-permute-start(bf16[3,128,768]{2,1,0:T(8,128)(2,1)S(1)} %get-tuple-element.233.triple_ref), channel_id=1, source_target_pairs={{0,4},{4,0},{8,12},{12,8},{16,20},{20,16},{24,28},{28,24},{1,5},{5... | collective-permute-start | bytes 1769480 | tf_op jit(solution)/shard_map/ppermute | solution.py:939
  88.4 13.9 %collective-permute-start.19 = (bf16[2304,128]{1,0:T(8,128)(2,1)S(1)}, bf16[2304,128]{1,0:T(8,128)(2,1)S(1)}, u32[]{:S(2)}, u32[]{:S(2)}) collective-permute-start(bf16[2304,128]{1,0:T(8,128)(2,1)S(1)} %get-tuple-element.247), channel_id=1, source_target_pairs={{0,16},{4,12},{8,24},{12,4},{16,0},{20,28},{24,8},{28,20},{1,17},{... | collective-permute-start | bytes 1769480 | tf_op jit(solution)/shard_map/ppermute | solution.py:988
  98.8 13.5 %collective-permute-start.21 = (bf16[2,1792,128]{2,1,0:T(8,128)(2,1)S(1)}, bf16[2,1792,128]{2,1,0:T(8,128)(2,1)S(1)}, u32[]{:S(2)}, u32[]{:S(2)}) collective-permute-start(bf16[2,1792,128]{2,1,0:T(8,128)(2,1)S(1)} %get-tuple-element.252), channel_id=1, source_target_pairs={{0,8},{4,20},{8,0},{12,28},{16,24},{20,4},{24,16},{28,12},{1,9},{5... | collective-permute-start | bytes 2752520 | tf_op jit(solution)/shard_map/ppermute | solution.py:984
  103.0 9.8 %collective-permute-start.22 = (bf16[672,128]{1,0:T(8,128)(2,1)S(1)}, bf16[672,128]{1,0:T(8,128)(2,1)S(1)}, u32[]{:S(2)}, u32[]{:S(2)}) collective-permute-start(bf16[672,128]{1,0:T(8,128)(2,1)S(1)} %get-tuple-element.255), channel_id=1, source_target_pairs={{0,1},{1,0},{2,3},{3,2},{4,5},{5,4},{6,7},{7,6},{8,9},{9,8},{10,11... | collective-permute-start | bytes 516104 | tf_op jit(solution)/shard_map/ppermute | solution.py:939
  103.7 14.9 %collective-permute-start.23 = (bf16[672,128]{1,0:T(8,128)(2,1)S(1)}, bf16[672,128]{1,0:T(8,128)(2,1)S(1)}, u32[]{:S(2)}, u32[]{:S(2)}) collective-permute-start(bf16[672,128]{1,0:T(8,128)(2,1)S(1)} %get-tuple-element.256), channel_id=1, source_target_pairs={{0,2},{1,3},{2,0},{3,1},{4,6},{5,7},{6,4},{7,5},{8,10},{9,11},{10,... | collective-permute-start | bytes 516104 | tf_op jit(solution)/shard_map/ppermute | solution.py:939
  105.7 12.8 %collective-permute-start.24 = (bf16[672,128]{1,0:T(8,128)(2,1)S(1)}, bf16[672,128]{1,0:T(8,128)(2,1)S(1)}, u32[]{:S(2)}, u32[]{:S(2)}) collective-permute-start(bf16[672,128]{1,0:T(8,128)(2,1)S(1)} %get-tuple-element.257), channel_id=1, source_target_pairs={{0,3},{1,2},{2,1},{3,0},{4,7},{5,6},{6,5},{7,4},{8,11},{9,10},{10,... | collective-permute-start | bytes 516104 | tf_op jit(solution)/shard_map/ppermute | solution.py:939
  121.6 14.4 %collective-permute-start.36 = (bf16[1824,128]{1,0:T(8,128)(2,1)S(1)}, bf16[1824,128]{1,0:T(8,128)(2,1)S(1)}, u32[]{:S(2)}, u32[]{:S(2)}) collective-permute-start(bf16[1824,128]{1,0:T(8,128)(2,1)S(1)} %shard_map.381.refs_0_), channel_id=1, source_target_pairs={{0,16},{4,12},{8,24},{12,4},{16,0},{20,28},{24,8},{28,20},{1,17},{... | collective-permute-start | bytes 1400840 | tf_op jit(solution)/shard_map/ppermute | solution.py:988
  121.9 14.1 %collective-permute-start.26 = (bf16[496,128]{1,0:T(8,128)(2,1)S(1)}, bf16[496,128]{1,0:T(8,128)(2,1)S(1)}, u32[]{:S(2)}, u32[]{:S(2)}) collective-permute-start(bf16[496,128]{1,0:T(8,128)(2,1)S(1)} %get-tuple-element.266), channel_id=1, source_target_pairs={{0,1},{1,0},{2,3},{3,2},{4,5},{5,4},{6,7},{7,6},{8,9},{9,8},{10,11... | collective-permute-start | bytes 380936 | tf_op jit(solution)/shard_map/ppermute | solution.py:939
  122.8 13.3 %collective-permute-start.27 = (bf16[496,128]{1,0:T(8,128)(2,1)S(1)}, bf16[496,128]{1,0:T(8,128)(2,1)S(1)}, u32[]{:S(2)}, u32[]{:S(2)}) collective-permute-start(bf16[496,128]{1,0:T(8,128)(2,1)S(1)} %get-tuple-element.267), channel_id=1, source_target_pairs={{0,2},{1,3},{2,0},{3,1},{4,6},{5,7},{6,4},{7,5},{8,10},{9,11},{10,... | collective-permute-start | bytes 380936 | tf_op jit(solution)/shard_map/ppermute | solution.py:939
  124.6 11.4 %collective-permute-start.28 = (bf16[496,128]{1,0:T(8,128)(2,1)S(1)}, bf16[496,128]{1,0:T(8,128)(2,1)S(1)}, u32[]{:S(2)}, u32[]{:S(2)}) collective-permute-start(bf16[496,128]{1,0:T(8,128)(2,1)S(1)} %get-tuple-element.268), channel_id=1, source_target_pairs={{0,3},{1,2},{2,1},{3,0},{4,7},{5,6},{6,5},{7,4},{8,11},{9,10},{10,... | collective-permute-start | bytes 380936 | tf_op jit(solution)/shard_map/ppermute | solution.py:939
  126.3 21.7 %collective-permute-start.37 = (bf16[1824,128]{1,0:T(8,128)(2,1)S(1)}, bf16[1824,128]{1,0:T(8,128)(2,1)S(1)}, u32[]{:S(2)}, u32[]{:S(2)}) collective-permute-start(bf16[1824,128]{1,0:T(8,128)(2,1)S(1)} %shard_map.381.refs_0_), channel_id=1, source_target_pairs={{0,8},{4,20},{8,0},{12,28},{16,24},{20,4},{24,16},{28,12},{1,9},{5... | collective-permute-start | bytes 1400840 | tf_op jit(solution)/shard_map/ppermute | solution.py:984
  136.1 12.4 %collective-permute-start.38 = (bf16[1824,128]{1,0:T(8,128)(2,1)S(1)}, bf16[1824,128]{1,0:T(8,128)(2,1)S(1)}, u32[]{:S(2)}, u32[]{:S(2)}) collective-permute-start(bf16[1824,128]{1,0:T(8,128)(2,1)S(1)} %collective-permute-done.36.refs_1_), channel_id=1, source_target_pairs={{0,8},{4,20},{8,0},{12,28},{16,24},{20,4},{24,16},{28,12},{1,9},{5... | collective-permute-start | bytes 1400840 | tf_op jit(solution)/shard_map/ppermute | solution.py:984
  136.2 9.8 %collective-permute-start.29 = (bf16[496,128]{1,0:T(8,128)(2,1)S(1)}, bf16[496,128]{1,0:T(8,128)(2,1)S(1)}, u32[]{:S(2)}, u32[]{:S(2)}) collective-permute-start(bf16[496,128]{1,0:T(8,128)(2,1)S(1)} %shard_map.383.refs_0_), channel_id=1, source_target_pairs={{0,8},{4,12},{8,0},{12,4},{16,24},{20,28},{24,16},{28,20},{1,9},{5... | collective-permute-start | bytes 380936 | tf_op jit(solution)/shard_map/ppermute | solution.py:939
  (60 other events, 494.1 us)

commit v5 on v4

--- a/solution.py
+++ b/solution.py
@@ -545,7 +545,13 @@
     grad_rates = ge_s[...] * fcol_ref[...]
     gr_ref[...] = low(grad_rates)
     total = jnp.broadcast_to(sum_rows(grad_rates), (grad_rates.shape[1], grad_rates.shape[1]))
-    small_ref[pad : pad + heads, 3 * head : 3 * head + 1] = jnp.transpose(total)[0:heads, 0:1]
+    total = jnp.transpose(total)[0:heads, 0:1]
+    high = low(total).astype(F32)
+    slot = lax.broadcasted_iota(jnp.int32, (heads, head), 1)
+    mine = ids_smem[3]
+    small_ref[pad : pad + heads, 3 * head : 4 * head] = jnp.where(
+        slot == mine, high, 0.0
+    ) + jnp.where(slot == mine + head // 2, total - high, 0.0)
 
 
 def put_matrix(to_ref, values, index, count, feats):
@@ -878,7 +884,8 @@
     b2_ref[...] = packed[:, 0:head]
     ig_ref[...] = packed[:, head : 2 * head]
     ib_ref[...] = packed[:, 2 * head : 3 * head]
-    br_ref[...] = jnp.transpose(small_s[at + 16 : at + 32, 128:])[3 * head - 128 : 3 * head - 127, 0:heads]
+    turned = jnp.transpose(small_s[at + 16 : at + 32, 128:])
+    br_ref[...] = sum_rows(turned[3 * head - 128 :])[:, 0:heads]
 
 
 def held(values):
@@ -1059,7 +1066,10 @@
     w_rate_t = jnp.transpose(w_rate)
     place = lax.axis_index("rows")
     me = lax.axis_index("feat")
-    ids = jnp.stack([lax.bitwise_and(place, 1), lax.shift_right_logical(place, 1), me])
+    slot = lax.bitwise_and(place * feats + me, head // 2 - 1)
+    ids = jnp.stack(
+        [lax.bitwise_and(place, 1), lax.shift_right_logical(place, 1), me, slot]
+    )
     cots = across_feats([cotangent[0]] * feats, feats)
     kept = [
         (line, F32),
@@ -1307,14 +1317,15 @@
         smem=1,
         cover=0,
     )
-    joined, late_cut = lax.optimization_barrier((joined, late_cut))
     late_cut = across_feats(late_cut, feats)
     near = second_axis(joined, rows)
-    joined = [joined, near, first_axis(joined, rows), first_axis(near, rows)]
+    far = [first_axis(joined, rows), first_axis(near, rows)]
+    mirrored, late_cut[0] = lax.optimization_barrier((other_core(joined, rows), late_cut[0]))
+    joined = [joined, near] + far
     (late_total,) = launch(sum_kernel, [((3 * per + common, 128), BF16)], late_cut)
     late = across_chips([late_total] * chips, rows)
     late += [other_core(x, rows) for x in late]
-    joined += [other_core(x, rows) for x in joined]
+    joined += [mirrored] + [other_core(x, rows) for x in joined[1:]]
     share = (width // feats, width)
     late = launch(
         partial(late_totals_kernel, chips, feats, heads, head),
@@ -1431,7 +1442,7 @@
         packed[:, 0:head],
         packed[:, head : 2 * head],
         packed[:, 2 * head : 3 * head],
-        packed[:, 3 * head : 3 * head + 1].reshape(1, heads),
+        jnp.sum(packed[:, 3 * head :], 1)[None],
     ]
 
 

time: 156 us -> 153 us (0.981)
  waiting for transfers between devices: 53.6 us -> 49.5 us
    ppermute x4, waiting for transfers between devices: 14.4 us -> 5.07 us  [second_axis(): lax.ppermute(values, 'rows', [(i, i ^ 4 >> (i & 1)) for i in range(rows)])]
    ppermute x34, waiting for transfers between devices: 31.3 us -> 36.6 us  [exchange(): return lax.ppermute(values, axis, [(i, i ^ distance) for i in range(size)])]
  transfers between devices with their start and end apart: 43 -> 43, of which waited for: 20 -> 18; matrix products, arithmetic and copies ran while one was open for 0% -> 0% of each run, Pallas kernels for 32% -> 33%
where the time goes in v5:
time: 153 us; the launch traced here: 152 us
  Pallas kernels  56.7 us (37%)
  waiting for transfers between devices  49.5 us (32%)
  starting transfers between devices  42.9 us (28%)
  local copies, waits for them, and re-layouts  1.8 us (1%)
    pallas_call x21, Pallas kernels, call(): pl.pallas_call(kernel, out_shape=[pltpu.VMEM(s, d) if k else pltpu.HBM(s,...  56.7 us
    ppermute x34, waiting for transfers between devices, exchange(): return lax.ppermute(values, axis, [(i, i ^ distance) for i in range(size)])  36.6 us
    ppermute x34, starting transfers between devices, exchange(): return lax.ppermute(values, axis, [(i, i ^ distance) for i in range(size)])  34.4 us
    ppermute x5, waiting for transfers between devices, first_axis(): lax.ppermute(values, 'rows', [(i, i ^ 2 << (i & 1)) for i in range(rows)])  7.84 us
    ppermute x4, waiting for transfers between devices, second_axis(): lax.ppermute(values, 'rows', [(i, i ^ 4 >> (i & 1)) for i in range(rows)])  5.07 us
    ppermute x4, starting transfers between devices, second_axis(): lax.ppermute(values, 'rows', [(i, i ^ 4 >> (i & 1)) for i in range(rows)])  4.69 us
    ppermute x5, starting transfers between devices, first_axis(): lax.ppermute(values, 'rows', [(i, i ^ 2 << (i & 1)) for i in range(rows)])  3.79 us
  transfers between devices with their start and end apart: 43, of which 18 were waited for; matrix products, arithmetic and copies ran while one was open for 0% of the time, Pallas kernels for 33%

profile of v5, /device:TPU:0, one launch (start us, length us, event | category | flops | bytes accessed | tf_op | source)
XLA Modules:
  0.0 152.4 jit_solution(13034639384447366610)
XLA Ops:
  0.7 3.1 %collective-permute-start = (bf16[128,768]{1,0:T(8,128)(2,1)}, bf16[128,768]{1,0:T(8,128)(2,1)S(1)}, u32[]{:S(2)}, u32[]{:S(2)}) collective-permute-start(bf16[128,768]{1,0:T(8,128)(2,1)} %bitcast.20), channel_id=1, source_target_pairs={{0,1},{1,0},{2,3},{3,2},{4,5},{5,4},{6,7},{7,6},{8,9},{9,8},{10,11... | collective-permute-start | bytes 589832 | tf_op jit(solution)/shard_map/ppermute | solution.py:946
  3.7 2.6 %collective-permute-start.1 = (bf16[128,768]{1,0:T(8,128)(2,1)}, bf16[128,768]{1,0:T(8,128)(2,1)S(1)}, u32[]{:S(2)}, u32[]{:S(2)}) collective-permute-start(bf16[128,768]{1,0:T(8,128)(2,1)} %bitcast.21), channel_id=1, source_target_pairs={{0,2},{1,3},{2,0},{3,1},{4,6},{5,7},{6,4},{7,5},{8,10},{9,11},{10,... | collective-permute-start | bytes 589832 | tf_op jit(solution)/shard_map/ppermute | solution.py:946
  6.4 16.3 %shard_map.365 = (bf16[2,128,768]{2,1,0:T(8,128)(2,1)S(1)}, bf16[128,768]{1,0:T(8,128)(2,1)S(1)}, f32[128,768]{1,0:T(8,128)}, f32[128,768]{1,0:T(8,128)}, f32[12...) custom-call(s32[1,128]{1,0:T(1,128)} %seg_ref.2, ...), custom_call_target="tpu_custom_call" | custom-call | flops 20000999424 | bytes 20001000 | tf_op jit(solution)/shard_map/pallas_call | solution.py:928
  24.5 3.4 %collective-permute-start.3 = (bf16[128,768]{1,0:T(8,128)(2,1)}, bf16[128,768]{1,0:T(8,128)(2,1)S(1)}, u32[]{:S(2)}, u32[]{:S(2)}) collective-permute-start(bf16[128,768]{1,0:T(8,128)(2,1)} %copy-done.14), channel_id=1, source_target_pairs={{0,2},{1,3},{2,0},{3,1},{4,6},{5,7},{6,4},{7,5},{8,10},{9,11},{10,... | collective-permute-start | bytes 589832 | tf_op jit(solution)/shard_map/ppermute | solution.py:946
  30.2 3.6 %collective-permute-done.4.x_ref.refs_1_ = bf16[128,768]{1,0:T(8,128)(2,1)S(1)} collective-permute-done((bf16[128,768]{1,0:T(8,128)(2,1)}, bf16[128,768]{1,0:T(8,128)(2,1)S(1)}, u32[]{:S(2)}, u32[]{:S(2)}) %collective-permute-start.4) | collective-permute-done | bytes 196640 | tf_op jit(solution)/shard_map/ppermute | solution.py:946
  37.8 2.7 %collective-permute-start.7 = (bf16[128,768]{1,0:T(8,128)(2,1)S(1)}, bf16[128,768]{1,0:T(8,128)(2,1)S(1)}, u32[]{:S(2)}, u32[]{:S(2)}) collective-permute-start(bf16[128,768]{1,0:T(8,128)(2,1)S(1)} %get-tuple-element.183), channel_id=1, source_target_pairs={{0,2},{1,3},{2,0},{3,1},{4,6},{5,7},{6,4},{7,5},{8,10},{9,11},{10,... | collective-permute-start | bytes 589832 | tf_op jit(solution)/shard_map/ppermute | solution.py:946
  40.6 4.9 %collective-permute-done.5.x_ref.refs_3_ = bf16[128,768]{1,0:T(8,128)(2,1)S(1)} collective-permute-done((bf16[128,768]{1,0:T(8,128)(2,1)S(1)}, bf16[128,768]{1,0:T(8,128)(2,1)S(1)}, u32[]{:S(2)}, u32[]{:S(2)}) %collective-permute-start.5) | collective-permute-done | bytes 196640 | tf_op jit(solution)/shard_map/ppermute | solution.py:946
  48.4 3.3 %shard_map.370 = (bf16[3,768,256]{2,1,0:T(8,128)(2,1)S(1)}, bf16[3,768,256]{2,1,0:T(8,128)(2,1)S(1)}, bf16[128,768]{1,0:T(8,128)(2,1)S(1)}, bf16[128,768]{1,0:T(...) custom-call(s32[4]{0:T(128)S(1)} %pad_add_fusion.ids_smem, bf16[128,768]{1,0:T(8,128)(2,1)S(1)} %copy-done.15, ...), custom_call_target="tpu_custom_call" | custom-call | flops 20000999424 | bytes 20001000 | tf_op jit(solution)/shard_map/pallas_call | solution.py:928
  51.8 3.8 %collective-permute-done.6.refs_1_ = bf16[128,768]{1,0:T(8,128)(2,1)S(1)} collective-permute-done((bf16[128,768]{1,0:T(8,128)(2,1)S(1)}, bf16[128,768]{1,0:T(8,128)(2,1)S(1)}, u32[]{:S(2)}, u32[]{:S(2)}) %collective-permute-start.6) | collective-permute-done | bytes 196640 | tf_op jit(solution)/shard_map/ppermute | solution.py:946
  57.2 2.6 %collective-permute-done.9.other_ref = bf16[2,128,768]{2,1,0:T(8,128)(2,1)S(1)} collective-permute-done((bf16[2,128,768]{2,1,0:T(8,128)(2,1)S(1)}, bf16[2,128,768]{2,1,0:T(8,128)(2,1)S(1)}, u32[]{:S(2)}, u32[]{:S(2)}) %collective-permute-start.9) | collective-permute-done | bytes 393248 | tf_op jit(solution)/shard_map/ppermute | solution.py:946
  60.3 1.8 %shard_map.372 = (f32[128,768]{1,0:T(8,128)S(1)}, bf16[2,2304,128]{2,1,0:T(8,128)(2,1)S(1)}, bf16[2,2304,128]{2,1,0:T(8,128)(2,1)S(1)}) custom-call(s32[4]{0:T(128)S(1)} %pad_add_fusion.ids_smem, bf16[2,128,768]{2,1,0:T(8,128)(2,1)S(1)} %get-tuple-element.239.mine_ref.pair_ref, bf16[2,128,768]{2,1,0:T(8,128)(2,1)S(1)} %collective-permute-done.9.other_ref, ...), custom_call_target="tpu_custom_call" | custom-call | flops 20000999424 | bytes 20001000 | tf_op jit(solution)/shard_map/pallas_call | solution.py:928
  68.3 15.7 %shard_map.373 = (bf16[3,128,768]{2,1,0:T(8,128)(2,1)S(1)}, bf16[128,128]{1,0:T(8,128)(2,1)S(1)}, bf16[768,256]{1,0:T(8,128)(2,1)S(1)}, bf16[768,256]{1,0:T(8,128)(2,1)S(1)}, f32[32,256]{1,0:T(8,128)S(1)}) custom-call(s32[4]{0:T(128)S(1)} %pad_add_fusion.ids_smem, s32[1,128]{1,0:T(1,128)S(1)} %copy-done.18, s32[1,128]{1,0:T(1,128)S(1)} %copy-done.18, ...), custom_call_target="tpu_custom_call" | custom-call | flops 20000999424 | bytes 20001000 | tf_op jit(solution)/shard_map/pallas_call | solution.py:928
  89.5 2.3 %shard_map.376 = (f32[1,128,768]{2,1,0:T(8,128)}, bf16[128,256]{1,0:T(8,128)(2,1)S(1)}) custom-call(bf16[3,128,768]{2,1,0:T(8,128)(2,1)S(1)} %get-tuple-element.230.triple_ref, bf16[128,128]{1,0:T(8,128)(2,1)S(1)} %get-tuple-element.231.gr_ref, bf16[2,128,768]{2,1,0:T(8,128)(2,1)S(1)} %get-tuple-element.239.mine_ref.pair_ref, bf16[768,768]{1,0:T(8,128)(2,1)S(1)} %copy-done, ...), custom_call_target="tpu_custom_call" | custom-call | flops 1000000 | bytes 1000 | tf_op jit(solution)/shard_map/pallas_call | solution.py:928
  91.8 3.1 %collective-permute-done.17.got_ref = bf16[2,384,128]{2,1,0:T(8,128)(2,1)S(1)} collective-permute-done((bf16[2,384,128]{2,1,0:T(8,128)(2,1)S(1)}, bf16[2,384,128]{2,1,0:T(8,128)(2,1)S(1)}, u32[]{:S(2)}, u32[]{:S(2)}) %collective-permute-start.17) | collective-permute-done | bytes 196640 | tf_op jit(solution)/shard_map/ppermute | solution.py:991
  94.9 1.9 %collective-permute-start.20 = (bf16[384,128]{1,0:T(8,128)(2,1)S(1)}, bf16[384,128]{1,0:T(8,128)(2,1)S(1)}, u32[]{:S(2)}, u32[]{:S(2)}) collective-permute-start(bf16[384,128]{1,0:T(8,128)(2,1)S(1)} %get-tuple-element.245), channel_id=1, source_target_pairs={{0,16},{4,12},{8,24},{12,4},{16,0},{20,28},{24,8},{28,20},{1,17},{... | collective-permute-start | bytes 294920 | tf_op jit(solution)/shard_map/ppermute | solution.py:995
  98.9 2.9 %collective-permute-done.20.refs_3_ = bf16[384,128]{1,0:T(8,128)(2,1)S(1)} collective-permute-done((bf16[384,128]{1,0:T(8,128)(2,1)S(1)}, bf16[384,128]{1,0:T(8,128)(2,1)S(1)}, u32[]{:S(2)}, u32[]{:S(2)}) %collective-permute-start.20) | collective-permute-done | bytes 98336 | tf_op jit(solution)/shard_map/ppermute | solution.py:995
  103.2 2.1 %collective-permute-start.23 = (bf16[672,128]{1,0:T(8,128)(2,1)S(1)}, bf16[672,128]{1,0:T(8,128)(2,1)S(1)}, u32[]{:S(2)}, u32[]{:S(2)}) collective-permute-start(bf16[672,128]{1,0:T(8,128)(2,1)S(1)} %get-tuple-element.253), channel_id=1, source_target_pairs={{0,2},{1,3},{2,0},{3,1},{4,6},{5,7},{6,4},{7,5},{8,10},{9,11},{10,... | collective-permute-start | bytes 516104 | tf_op jit(solution)/shard_map/ppermute | solution.py:946
  107.0 4.8 %collective-permute-done.21.got_ref = bf16[2,1792,128]{2,1,0:T(8,128)(2,1)S(1)} collective-permute-done((bf16[2,1792,128]{2,1,0:T(8,128)(2,1)S(1)}, bf16[2,1792,128]{2,1,0:T(8,128)(2,1)S(1)}, u32[]{:S(2)}, u32[]{:S(2)}) %collective-permute-start.21) | collective-permute-done | bytes 917536 | tf_op jit(solution)/shard_map/ppermute | solution.py:991
  112.3 5.9 %collective-permute-done.23.refs_2_ = bf16[672,128]{1,0:T(8,128)(2,1)S(1)} collective-permute-done((bf16[672,128]{1,0:T(8,128)(2,1)S(1)}, bf16[672,128]{1,0:T(8,128)(2,1)S(1)}, u32[]{:S(2)}, u32[]{:S(2)}) %collective-permute-start.23) | collective-permute-done | bytes 172064 | tf_op jit(solution)/shard_map/ppermute | solution.py:946
  127.7 7.3 %collective-permute-done.28.refs_2_ = bf16[496,128]{1,0:T(8,128)(2,1)S(1)} collective-permute-done((bf16[496,128]{1,0:T(8,128)(2,1)S(1)}, bf16[496,128]{1,0:T(8,128)(2,1)S(1)}, u32[]{:S(2)}, u32[]{:S(2)}) %collective-permute-start.28) | collective-permute-done | bytes 127008 | tf_op jit(solution)/shard_map/ppermute | solution.py:946
  136.9 1.7 %collective-permute-start.32 = (bf16[496,128]{1,0:T(8,128)(2,1)S(1)}, bf16[496,128]{1,0:T(8,128)(2,1)S(1)}, u32[]{:S(2)}, u32[]{:S(2)}) collective-permute-start(bf16[496,128]{1,0:T(8,128)(2,1)S(1)} %shard_map.383.refs_0_), channel_id=1, source_target_pairs={{0,24},{4,28},{8,16},{12,20},{16,8},{20,12},{24,0},{28,4},{1,25},{... | collective-permute-start | bytes 380936 | tf_op jit(solution)/shard_map/ppermute | solution.py:946
  138.6 4.7 %collective-permute-done.30.refs_1_ = bf16[496,128]{1,0:T(8,128)(2,1)S(1)} collective-permute-done((bf16[496,128]{1,0:T(8,128)(2,1)S(1)}, bf16[496,128]{1,0:T(8,128)(2,1)S(1)}, u32[]{:S(2)}, u32[]{:S(2)}) %collective-permute-start.30) | collective-permute-done | bytes 127008 | tf_op jit(solution)/shard_map/ppermute | solution.py:946
  145.8 2.2 %shard_map.384 = (f32[192,768]{1,0:T(8,128)}, f32[192,768]{1,0:T(8,128)}, f32[192,768]{1,0:T(8,128)}, f32[12,192]{1,0:T(8,128)}, f32[1,192]{1,0:T(1,128)}, /*ind...) custom-call(s32[4]{0:T(128)S(1)} %pad_add_fusion.ids_smem, ...), custom_call_target="tpu_custom_call" | custom-call | flops 20000999424 | bytes 20001000 | tf_op jit(solution)/shard_map/pallas_call | solution.py:928
  148.0 4.2 %shard_map.385 = (f32[768,512]{1,0:T(8,128)}, f32[768,512]{1,0:T(8,128)}, f32[512,768]{1,0:T(8,128)}, f32[192,768]{1,0:T(8,128)}, f32[192,768]{1,0:T(8,128)}, /*index=5*/f32[768,256]{1,0:T(8,128)}, f32[768,256]{1,0:T(8,128)}) custom-call(s32[4]{0:T(128)S(1)} %pad_add_fusion.ids_smem, bf16[1824,128]{1,0:T(8,128)(2,1)S(1)} %shard_map.381.refs_0_, ...), custom_call_target="tpu_custom_call" | custom-call | flops 20000999424 | bytes 20001000 | tf_op jit(solution)/shard_map/pallas_call | solution.py:928
  (164 shorter events, 44.1 us)
Async XLA Ops:
  0.7 22.8 %collective-permute-start = (bf16[128,768]{1,0:T(8,128)(2,1)}, bf16[128,768]{1,0:T(8,128)(2,1)S(1)}, u32[]{:S(2)}, u32[]{:S(2)}) collective-permute-start(bf16[128,768]{1,0:T(8,128)(2,1)} %bitcast.20), channel_id=1, source_target_pairs={{0,1},{1,0},{2,3},{3,2},{4,5},{5,4},{6,7},{7,6},{8,9},{9,8},{10,11... | collective-permute-start | bytes 589832 | tf_op jit(solution)/shard_map/ppermute | solution.py:946
  3.7 19.7 %collective-permute-start.1 = (bf16[128,768]{1,0:T(8,128)(2,1)}, bf16[128,768]{1,0:T(8,128)(2,1)S(1)}, u32[]{:S(2)}, u32[]{:S(2)}) collective-permute-start(bf16[128,768]{1,0:T(8,128)(2,1)} %bitcast.21), channel_id=1, source_target_pairs={{0,2},{1,3},{2,0},{3,1},{4,6},{5,7},{6,4},{7,5},{8,10},{9,11},{10,... | collective-permute-start | bytes 589832 | tf_op jit(solution)/shard_map/ppermute | solution.py:946
  6.3 17.1 %collective-permute-start.2 = (bf16[128,768]{1,0:T(8,128)(2,1)}, bf16[128,768]{1,0:T(8,128)(2,1)S(1)}, u32[]{:S(2)}, u32[]{:S(2)}) collective-permute-start(bf16[128,768]{1,0:T(8,128)(2,1)} %bitcast.22), channel_id=1, source_target_pairs={{0,3},{1,2},{2,1},{3,0},{4,7},{5,6},{6,5},{7,4},{8,11},{9,10},{10,... | collective-permute-start | bytes 589832 | tf_op jit(solution)/shard_map/ppermute | solution.py:946
  23.5 10.3 %collective-permute-start.4 = (bf16[128,768]{1,0:T(8,128)(2,1)}, bf16[128,768]{1,0:T(8,128)(2,1)S(1)}, u32[]{:S(2)}, u32[]{:S(2)}) collective-permute-start(bf16[128,768]{1,0:T(8,128)(2,1)} %copy-done.14), channel_id=1, source_target_pairs={{0,1},{1,0},{2,3},{3,2},{4,5},{5,4},{6,7},{7,6},{8,9},{9,8},{10,11... | collective-permute-start | bytes 589832 | tf_op jit(solution)/shard_map/ppermute | solution.py:946
  24.5 11.8 %collective-permute-start.3 = (bf16[128,768]{1,0:T(8,128)(2,1)}, bf16[128,768]{1,0:T(8,128)(2,1)S(1)}, u32[]{:S(2)}, u32[]{:S(2)}) collective-permute-start(bf16[128,768]{1,0:T(8,128)(2,1)} %copy-done.14), channel_id=1, source_target_pairs={{0,2},{1,3},{2,0},{3,1},{4,6},{5,7},{6,4},{7,5},{8,10},{9,11},{10,... | collective-permute-start | bytes 589832 | tf_op jit(solution)/shard_map/ppermute | solution.py:946
  36.3 9.2 %collective-permute-start.5 = (bf16[128,768]{1,0:T(8,128)(2,1)S(1)}, bf16[128,768]{1,0:T(8,128)(2,1)S(1)}, u32[]{:S(2)}, u32[]{:S(2)}) collective-permute-start(bf16[128,768]{1,0:T(8,128)(2,1)S(1)} %collective-permute-done.3.x_ref.refs_2_), channel_id=1, source_target_pairs={{0,1},{1,0},{2,3},{3,2},{4,5},{5,4},{6,7},{7,6},{8,9},{9,8},{10,11... | collective-permute-start | bytes 589832 | tf_op jit(solution)/shard_map/ppermute | solution.py:946
  37.8 14.0 %collective-permute-start.7 = (bf16[128,768]{1,0:T(8,128)(2,1)S(1)}, bf16[128,768]{1,0:T(8,128)(2,1)S(1)}, u32[]{:S(2)}, u32[]{:S(2)}) collective-permute-start(bf16[128,768]{1,0:T(8,128)(2,1)S(1)} %get-tuple-element.183), channel_id=1, source_target_pairs={{0,2},{1,3},{2,0},{3,1},{4,6},{5,7},{6,4},{7,5},{8,10},{9,11},{10,... | collective-permute-start | bytes 589832 | tf_op jit(solution)/shard_map/ppermute | solution.py:946
  46.8 8.8 %collective-permute-start.6 = (bf16[128,768]{1,0:T(8,128)(2,1)S(1)}, bf16[128,768]{1,0:T(8,128)(2,1)S(1)}, u32[]{:S(2)}, u32[]{:S(2)}) collective-permute-start(bf16[128,768]{1,0:T(8,128)(2,1)S(1)} %get-tuple-element.182), channel_id=1, source_target_pairs={{0,1},{1,0},{2,3},{3,2},{4,5},{5,4},{6,7},{7,6},{8,9},{9,8},{10,11... | collective-permute-start | bytes 589832 | tf_op jit(solution)/shard_map/ppermute | solution.py:946
  46.9 8.7 %collective-permute-start.8 = (bf16[128,768]{1,0:T(8,128)(2,1)S(1)}, bf16[128,768]{1,0:T(8,128)(2,1)S(1)}, u32[]{:S(2)}, u32[]{:S(2)}) collective-permute-start(bf16[128,768]{1,0:T(8,128)(2,1)S(1)} %get-tuple-element.184), channel_id=1, source_target_pairs={{0,3},{1,2},{2,1},{3,0},{4,7},{5,6},{6,5},{7,4},{8,11},{9,10},{10,... | collective-permute-start | bytes 589832 | tf_op jit(solution)/shard_map/ppermute | solution.py:946
  62.2 21.9 %collective-permute-start.12 = (bf16[128,768]{1,0:T(8,128)(2,1)S(1)}, bf16[128,768]{1,0:T(8,128)(2,1)S(1)}, u32[]{:S(2)}, u32[]{:S(2)}) collective-permute-start(bf16[128,768]{1,0:T(8,128)(2,1)S(1)} %get-tuple-element.220), channel_id=1, source_target_pairs={{0,1},{1,0},{2,3},{3,2},{4,5},{5,4},{6,7},{7,6},{8,9},{9,8},{10,11... | collective-permute-start | bytes 589832 | tf_op jit(solution)/shard_map/ppermute | solution.py:946
  63.8 20.8 %collective-permute-start.13 = (bf16[128,768]{1,0:T(8,128)(2,1)S(1)}, bf16[128,768]{1,0:T(8,128)(2,1)S(1)}, u32[]{:S(2)}, u32[]{:S(2)}) collective-permute-start(bf16[128,768]{1,0:T(8,128)(2,1)S(1)} %get-tuple-element.221), channel_id=1, source_target_pairs={{0,2},{1,3},{2,0},{3,1},{4,6},{5,7},{6,4},{7,5},{8,10},{9,11},{10,... | collective-permute-start | bytes 589832 | tf_op jit(solution)/shard_map/ppermute | solution.py:946
  64.9 19.6 %collective-permute-start.14 = (bf16[128,768]{1,0:T(8,128)(2,1)S(1)}, bf16[128,768]{1,0:T(8,128)(2,1)S(1)}, u32[]{:S(2)}, u32[]{:S(2)}) collective-permute-start(bf16[128,768]{1,0:T(8,128)(2,1)S(1)} %get-tuple-element.222), channel_id=1, source_target_pairs={{0,3},{1,2},{2,1},{3,0},{4,7},{5,6},{6,5},{7,4},{8,11},{9,10},{10,... | collective-permute-start | bytes 589832 | tf_op jit(solution)/shard_map/ppermute | solution.py:946
  66.6 17.9 %collective-permute-start.15 = (bf16[2,2304,128]{2,1,0:T(8,128)(2,1)S(1)}, bf16[2,2304,128]{2,1,0:T(8,128)(2,1)S(1)}, u32[]{:S(2)}, u32[]{:S(2)}) collective-permute-start(bf16[2,2304,128]{2,1,0:T(8,128)(2,1)S(1)} %get-tuple-element.224), channel_id=1, source_target_pairs={{0,8},{4,20},{8,0},{12,28},{16,24},{20,4},{24,16},{28,12},{1,9},{5... | collective-permute-start | bytes 3538952 | tf_op jit(solution)/shard_map/ppermute | solution.py:991
  84.0 12.8 %collective-permute-start.18 = (bf16[3,128,768]{2,1,0:T(8,128)(2,1)S(1)}, bf16[3,128,768]{2,1,0:T(8,128)(2,1)S(1)}, u32[]{:S(2)}, u32[]{:S(2)}) collective-permute-start(bf16[3,128,768]{2,1,0:T(8,128)(2,1)S(1)} %get-tuple-element.230.triple_ref), channel_id=1, source_target_pairs={{0,4},{4,0},{8,12},{12,8},{16,20},{20,16},{24,28},{28,24},{1,5},{5... | collective-permute-start | bytes 1769480 | tf_op jit(solution)/shard_map/ppermute | solution.py:946
  88.0 13.9 %collective-permute-start.19 = (bf16[2304,128]{1,0:T(8,128)(2,1)S(1)}, bf16[2304,128]{1,0:T(8,128)(2,1)S(1)}, u32[]{:S(2)}, u32[]{:S(2)}) collective-permute-start(bf16[2304,128]{1,0:T(8,128)(2,1)S(1)} %get-tuple-element.244), channel_id=1, source_target_pairs={{0,16},{4,12},{8,24},{12,4},{16,0},{20,28},{24,8},{28,20},{1,17},{... | collective-permute-start | bytes 1769480 | tf_op jit(solution)/shard_map/ppermute | solution.py:995
  98.3 13.5 %collective-permute-start.21 = (bf16[2,1792,128]{2,1,0:T(8,128)(2,1)S(1)}, bf16[2,1792,128]{2,1,0:T(8,128)(2,1)S(1)}, u32[]{:S(2)}, u32[]{:S(2)}) collective-permute-start(bf16[2,1792,128]{2,1,0:T(8,128)(2,1)S(1)} %get-tuple-element.249), channel_id=1, source_target_pairs={{0,8},{4,20},{8,0},{12,28},{16,24},{20,4},{24,16},{28,12},{1,9},{5... | collective-permute-start | bytes 2752520 | tf_op jit(solution)/shard_map/ppermute | solution.py:991
  102.5 9.7 %collective-permute-start.22 = (bf16[672,128]{1,0:T(8,128)(2,1)S(1)}, bf16[672,128]{1,0:T(8,128)(2,1)S(1)}, u32[]{:S(2)}, u32[]{:S(2)}) collective-permute-start(bf16[672,128]{1,0:T(8,128)(2,1)S(1)} %get-tuple-element.252), channel_id=1, source_target_pairs={{0,1},{1,0},{2,3},{3,2},{4,5},{5,4},{6,7},{7,6},{8,9},{9,8},{10,11... | collective-permute-start | bytes 516104 | tf_op jit(solution)/shard_map/ppermute | solution.py:946
  103.2 14.9 %collective-permute-start.23 = (bf16[672,128]{1,0:T(8,128)(2,1)S(1)}, bf16[672,128]{1,0:T(8,128)(2,1)S(1)}, u32[]{:S(2)}, u32[]{:S(2)}) collective-permute-start(bf16[672,128]{1,0:T(8,128)(2,1)S(1)} %get-tuple-element.253), channel_id=1, source_target_pairs={{0,2},{1,3},{2,0},{3,1},{4,6},{5,7},{6,4},{7,5},{8,10},{9,11},{10,... | collective-permute-start | bytes 516104 | tf_op jit(solution)/shard_map/ppermute | solution.py:946
  105.3 12.8 %collective-permute-start.24 = (bf16[672,128]{1,0:T(8,128)(2,1)S(1)}, bf16[672,128]{1,0:T(8,128)(2,1)S(1)}, u32[]{:S(2)}, u32[]{:S(2)}) collective-permute-start(bf16[672,128]{1,0:T(8,128)(2,1)S(1)} %get-tuple-element.254), channel_id=1, source_target_pairs={{0,3},{1,2},{2,1},{3,0},{4,7},{5,6},{6,5},{7,4},{8,11},{9,10},{10,... | collective-permute-start | bytes 516104 | tf_op jit(solution)/shard_map/ppermute | solution.py:946
  118.3 8.8 %collective-permute-start.37 = (bf16[1824,128]{1,0:T(8,128)(2,1)S(1)}, bf16[1824,128]{1,0:T(8,128)(2,1)S(1)}, u32[]{:S(2)}, u32[]{:S(2)}) collective-permute-start(bf16[1824,128]{1,0:T(8,128)(2,1)S(1)} %shard_map.381.refs_0_), channel_id=1, source_target_pairs={{0,16},{4,12},{8,24},{12,4},{16,0},{20,28},{24,8},{28,20},{1,17},{... | collective-permute-start | bytes 1400840 | tf_op jit(solution)/shard_map/ppermute | solution.py:995
  122.4 12.5 %collective-permute-start.28 = (bf16[496,128]{1,0:T(8,128)(2,1)S(1)}, bf16[496,128]{1,0:T(8,128)(2,1)S(1)}, u32[]{:S(2)}, u32[]{:S(2)}) collective-permute-start(bf16[496,128]{1,0:T(8,128)(2,1)S(1)} %get-tuple-element.261), channel_id=1, source_target_pairs={{0,2},{1,3},{2,0},{3,1},{4,6},{5,7},{6,4},{7,5},{8,10},{9,11},{10,... | collective-permute-start | bytes 380936 | tf_op jit(solution)/shard_map/ppermute | solution.py:946
  123.9 11.1 %collective-permute-start.29 = (bf16[496,128]{1,0:T(8,128)(2,1)S(1)}, bf16[496,128]{1,0:T(8,128)(2,1)S(1)}, u32[]{:S(2)}, u32[]{:S(2)}) collective-permute-start(bf16[496,128]{1,0:T(8,128)(2,1)S(1)} %get-tuple-element.262), channel_id=1, source_target_pairs={{0,3},{1,2},{2,1},{3,0},{4,7},{5,6},{6,5},{7,4},{8,11},{9,10},{10,... | collective-permute-start | bytes 380936 | tf_op jit(solution)/shard_map/ppermute | solution.py:946
  125.6 13.0 %collective-permute-start.38 = (bf16[1824,128]{1,0:T(8,128)(2,1)S(1)}, bf16[1824,128]{1,0:T(8,128)(2,1)S(1)}, u32[]{:S(2)}, u32[]{:S(2)}) collective-permute-start(bf16[1824,128]{1,0:T(8,128)(2,1)S(1)} %shard_map.381.refs_0_), channel_id=1, source_target_pairs={{0,8},{4,20},{8,0},{12,28},{16,24},{20,4},{24,16},{28,12},{1,9},{5... | collective-permute-start | bytes 1400840 | tf_op jit(solution)/shard_map/ppermute | solution.py:991
  127.1 17.9 %collective-permute-start.39 = (bf16[1824,128]{1,0:T(8,128)(2,1)S(1)}, bf16[1824,128]{1,0:T(8,128)(2,1)S(1)}, u32[]{:S(2)}, u32[]{:S(2)}) collective-permute-start(bf16[1824,128]{1,0:T(8,128)(2,1)S(1)} %collective-permute-done.37.refs_1_), channel_id=1, source_target_pairs={{0,8},{4,20},{8,0},{12,28},{16,24},{20,4},{24,16},{28,12},{1,9},{5... | collective-permute-start | bytes 1400840 | tf_op jit(solution)/shard_map/ppermute | solution.py:991
  (59 other events, 498.0 us)

commit v6 on v5

--- a/solution.py
+++ b/solution.py
@@ -215,7 +215,7 @@
         return carry
 
     save(4, 5, 6)
-    lax.fori_loop(0, blocks, step, 0, unroll=4)
+    lax.fori_loop(0, blocks, step, 0, unroll=8)
     save(7, 8, 10, 11, 12, 13, 14)
     project(2, q_s)
     for h in range(heads):
@@ -1284,7 +1284,7 @@
     early_sent, _ = lax.optimization_barrier((early_sent, tails_sent))
     early_got = second_axis(early_sent, rows)
     grad_tokens, small = finish(triple, grad_rates, small, part, grad_resid, grad_gain_two)
-    tails, tails_got = halved(launch, tails, tails_got, rows, 0)
+    tails, tails_got = halved(launch, tails, tails_got, rows, 1)
     common = 2 * small_rows // chips
     late, late_sent = launch(
         partial(late_weights_kernel, feats),

time: 153 us -> 151 us (0.987)
  waiting for transfers between devices: 49.5 us -> 47.9 us
  transfers between devices with their start and end apart: 43 -> 43, of which waited for: 18 -> 17; matrix products, arithmetic and copies ran while one was open for 0% -> 0% of each run, Pallas kernels for 33% -> 32%
where the time goes in v6:
time: 151 us
  Pallas kernels  56.2 us (37%)
  waiting for transfers between devices  47.9 us (32%)
  starting transfers between devices  43.1 us (29%)
  local copies, waits for them, and re-layouts  1.8 us (1%)
  between operations  1.53 us (1%)
    pallas_call x21, Pallas kernels, call(): pl.pallas_call(kernel, out_shape=[pltpu.VMEM(s, d) if k else pltpu.HBM(s,...  56.2 us
    ppermute x34, waiting for transfers between devices, exchange(): return lax.ppermute(values, axis, [(i, i ^ distance) for i in range(size)])  35.3 us
    ppermute x34, starting transfers between devices, exchange(): return lax.ppermute(values, axis, [(i, i ^ distance) for i in range(size)])  35.3 us
    ppermute x5, waiting for transfers between devices, first_axis(): lax.ppermute(values, 'rows', [(i, i ^ 2 << (i & 1)) for i in range(rows)])  7.48 us
    ppermute x4, waiting for transfers between devices, second_axis(): lax.ppermute(values, 'rows', [(i, i ^ 4 >> (i & 1)) for i in range(rows)])  5.11 us
    ppermute x4, starting transfers between devices, second_axis(): lax.ppermute(values, 'rows', [(i, i ^ 4 >> (i & 1)) for i in range(rows)])  4.42 us
    ppermute x5, starting transfers between devices, first_axis(): lax.ppermute(values, 'rows', [(i, i ^ 2 << (i & 1)) for i in range(rows)])  3.44 us
  transfers between devices with their start and end apart: 43, of which 17 were waited for; matrix products, arithmetic and copies ran while one was open for 0% of the time, Pallas kernels for 32%

profile of v6, /device:TPU:0, one launch (start us, length us, event | category | flops | bytes accessed | tf_op | source)
XLA Modules:
  0.0 150.6 jit_solution(5687318484031291631)
XLA Ops:
  0.7 3.1 %collective-permute-start = (bf16[128,768]{1,0:T(8,128)(2,1)}, bf16[128,768]{1,0:T(8,128)(2,1)S(1)}, u32[]{:S(2)}, u32[]{:S(2)}) collective-permute-start(bf16[128,768]{1,0:T(8,128)(2,1)} %bitcast.20), channel_id=1, source_target_pairs={{0,1},{1,0},{2,3},{3,2},{4,5},{5,4},{6,7},{7,6},{8,9},{9,8},{10,11... | collective-permute-start | bytes 589832 | tf_op jit(solution)/shard_map/ppermute | solution.py:946
  3.7 2.6 %collective-permute-start.1 = (bf16[128,768]{1,0:T(8,128)(2,1)}, bf16[128,768]{1,0:T(8,128)(2,1)S(1)}, u32[]{:S(2)}, u32[]{:S(2)}) collective-permute-start(bf16[128,768]{1,0:T(8,128)(2,1)} %bitcast.21), channel_id=1, source_target_pairs={{0,2},{1,3},{2,0},{3,1},{4,6},{5,7},{6,4},{7,5},{8,10},{9,11},{10,... | collective-permute-start | bytes 589832 | tf_op jit(solution)/shard_map/ppermute | solution.py:946
  6.4 15.6 %shard_map.365 = (bf16[2,128,768]{2,1,0:T(8,128)(2,1)S(1)}, bf16[128,768]{1,0:T(8,128)(2,1)S(1)}, f32[128,768]{1,0:T(8,128)}, f32[128,768]{1,0:T(8,128)}, f32[12...) custom-call(s32[1,128]{1,0:T(1,128)} %seg_ref.2, ...), custom_call_target="tpu_custom_call" | custom-call | flops 20000999424 | bytes 20001000 | tf_op jit(solution)/shard_map/pallas_call | solution.py:928
  24.5 2.6 %collective-permute-start.3 = (bf16[128,768]{1,0:T(8,128)(2,1)}, bf16[128,768]{1,0:T(8,128)(2,1)S(1)}, u32[]{:S(2)}, u32[]{:S(2)}) collective-permute-start(bf16[128,768]{1,0:T(8,128)(2,1)} %copy-done.14), channel_id=1, source_target_pairs={{0,2},{1,3},{2,0},{3,1},{4,6},{5,7},{6,4},{7,5},{8,10},{9,11},{10,... | collective-permute-start | bytes 589832 | tf_op jit(solution)/shard_map/ppermute | solution.py:946
  29.4 3.5 %collective-permute-done.4.x_ref.refs_1_ = bf16[128,768]{1,0:T(8,128)(2,1)S(1)} collective-permute-done((bf16[128,768]{1,0:T(8,128)(2,1)}, bf16[128,768]{1,0:T(8,128)(2,1)S(1)}, u32[]{:S(2)}, u32[]{:S(2)}) %collective-permute-start.4) | collective-permute-done | bytes 196640 | tf_op jit(solution)/shard_map/ppermute | solution.py:946
  37.1 2.8 %collective-permute-start.7 = (bf16[128,768]{1,0:T(8,128)(2,1)S(1)}, bf16[128,768]{1,0:T(8,128)(2,1)S(1)}, u32[]{:S(2)}, u32[]{:S(2)}) collective-permute-start(bf16[128,768]{1,0:T(8,128)(2,1)S(1)} %get-tuple-element.183), channel_id=1, source_target_pairs={{0,2},{1,3},{2,0},{3,1},{4,6},{5,7},{6,4},{7,5},{8,10},{9,11},{10,... | collective-permute-start | bytes 589832 | tf_op jit(solution)/shard_map/ppermute | solution.py:946
  40.0 4.6 %collective-permute-done.5.x_ref.refs_3_ = bf16[128,768]{1,0:T(8,128)(2,1)S(1)} collective-permute-done((bf16[128,768]{1,0:T(8,128)(2,1)S(1)}, bf16[128,768]{1,0:T(8,128)(2,1)S(1)}, u32[]{:S(2)}, u32[]{:S(2)}) %collective-permute-start.5) | collective-permute-done | bytes 196640 | tf_op jit(solution)/shard_map/ppermute | solution.py:946
  46.0 2.1 %collective-permute-start.8 = (bf16[128,768]{1,0:T(8,128)(2,1)S(1)}, bf16[128,768]{1,0:T(8,128)(2,1)S(1)}, u32[]{:S(2)}, u32[]{:S(2)}) collective-permute-start(bf16[128,768]{1,0:T(8,128)(2,1)S(1)} %get-tuple-element.184), channel_id=1, source_target_pairs={{0,3},{1,2},{2,1},{3,0},{4,7},{5,6},{6,5},{7,4},{8,11},{9,10},{10,... | collective-permute-start | bytes 589832 | tf_op jit(solution)/shard_map/ppermute | solution.py:946
  48.1 3.1 %shard_map.370 = (bf16[3,768,256]{2,1,0:T(8,128)(2,1)S(1)}, bf16[3,768,256]{2,1,0:T(8,128)(2,1)S(1)}, bf16[128,768]{1,0:T(8,128)(2,1)S(1)}, bf16[128,768]{1,0:T(...) custom-call(s32[4]{0:T(128)S(1)} %pad_add_fusion.ids_smem, bf16[128,768]{1,0:T(8,128)(2,1)S(1)} %copy-done.15, ...), custom_call_target="tpu_custom_call" | custom-call | flops 20000999424 | bytes 20001000 | tf_op jit(solution)/shard_map/pallas_call | solution.py:928
  51.2 3.0 %collective-permute-done.6.refs_1_ = bf16[128,768]{1,0:T(8,128)(2,1)S(1)} collective-permute-done((bf16[128,768]{1,0:T(8,128)(2,1)S(1)}, bf16[128,768]{1,0:T(8,128)(2,1)S(1)}, u32[]{:S(2)}, u32[]{:S(2)}) %collective-permute-start.6) | collective-permute-done | bytes 196640 | tf_op jit(solution)/shard_map/ppermute | solution.py:946
  55.8 2.6 %collective-permute-done.9.other_ref = bf16[2,128,768]{2,1,0:T(8,128)(2,1)S(1)} collective-permute-done((bf16[2,128,768]{2,1,0:T(8,128)(2,1)S(1)}, bf16[2,128,768]{2,1,0:T(8,128)(2,1)S(1)}, u32[]{:S(2)}, u32[]{:S(2)}) %collective-permute-start.9) | collective-permute-done | bytes 393248 | tf_op jit(solution)/shard_map/ppermute | solution.py:946
  59.0 1.8 %shard_map.372 = (f32[128,768]{1,0:T(8,128)S(1)}, bf16[2,2304,128]{2,1,0:T(8,128)(2,1)S(1)}, bf16[2,2304,128]{2,1,0:T(8,128)(2,1)S(1)}) custom-call(s32[4]{0:T(128)S(1)} %pad_add_fusion.ids_smem, bf16[2,128,768]{2,1,0:T(8,128)(2,1)S(1)} %get-tuple-element.239.mine_ref.pair_ref, bf16[2,128,768]{2,1,0:T(8,128)(2,1)S(1)} %collective-permute-done.9.other_ref, ...), custom_call_target="tpu_custom_call" | custom-call | flops 20000999424 | bytes 20001000 | tf_op jit(solution)/shard_map/pallas_call | solution.py:928
  67.0 15.9 %shard_map.373 = (bf16[3,128,768]{2,1,0:T(8,128)(2,1)S(1)}, bf16[128,128]{1,0:T(8,128)(2,1)S(1)}, bf16[768,256]{1,0:T(8,128)(2,1)S(1)}, bf16[768,256]{1,0:T(8,128)(2,1)S(1)}, f32[32,256]{1,0:T(8,128)S(1)}) custom-call(s32[4]{0:T(128)S(1)} %pad_add_fusion.ids_smem, s32[1,128]{1,0:T(1,128)S(1)} %copy-done.18, s32[1,128]{1,0:T(1,128)S(1)} %copy-done.18, ...), custom_call_target="tpu_custom_call" | custom-call | flops 20000999424 | bytes 20001000 | tf_op jit(solution)/shard_map/pallas_call | solution.py:928
  87.5 2.3 %shard_map.376 = (f32[1,128,768]{2,1,0:T(8,128)}, bf16[128,256]{1,0:T(8,128)(2,1)S(1)}) custom-call(bf16[3,128,768]{2,1,0:T(8,128)(2,1)S(1)} %get-tuple-element.230.triple_ref, bf16[128,128]{1,0:T(8,128)(2,1)S(1)} %get-tuple-element.231.gr_ref, bf16[2,128,768]{2,1,0:T(8,128)(2,1)S(1)} %get-tuple-element.239.mine_ref.pair_ref, bf16[768,768]{1,0:T(8,128)(2,1)S(1)} %copy-done, ...), custom_call_target="tpu_custom_call" | custom-call | flops 1000000 | bytes 1000 | tf_op jit(solution)/shard_map/pallas_call | solution.py:928
  89.8 3.1 %collective-permute-done.17.got_ref = bf16[2,384,128]{2,1,0:T(8,128)(2,1)S(1)} collective-permute-done((bf16[2,384,128]{2,1,0:T(8,128)(2,1)S(1)}, bf16[2,384,128]{2,1,0:T(8,128)(2,1)S(1)}, u32[]{:S(2)}, u32[]{:S(2)}) %collective-permute-start.17) | collective-permute-done | bytes 196640 | tf_op jit(solution)/shard_map/ppermute | solution.py:991
  96.4 3.9 %collective-permute-done.20.refs_3_ = bf16[384,128]{1,0:T(8,128)(2,1)S(1)} collective-permute-done((bf16[384,128]{1,0:T(8,128)(2,1)S(1)}, bf16[384,128]{1,0:T(8,128)(2,1)S(1)}, u32[]{:S(2)}, u32[]{:S(2)}) %collective-permute-start.20) | collective-permute-done | bytes 98336 | tf_op jit(solution)/shard_map/ppermute | solution.py:995
  101.8 2.1 %collective-permute-start.23 = (bf16[672,128]{1,0:T(8,128)(2,1)S(1)}, bf16[672,128]{1,0:T(8,128)(2,1)S(1)}, u32[]{:S(2)}, u32[]{:S(2)}) collective-permute-start(bf16[672,128]{1,0:T(8,128)(2,1)S(1)} %get-tuple-element.253), channel_id=1, source_target_pairs={{0,2},{1,3},{2,0},{3,1},{4,6},{5,7},{6,4},{7,5},{8,10},{9,11},{10,... | collective-permute-start | bytes 516104 | tf_op jit(solution)/shard_map/ppermute | solution.py:946
  105.4 4.3 %collective-permute-done.21.got_ref = bf16[2,1792,128]{2,1,0:T(8,128)(2,1)S(1)} collective-permute-done((bf16[2,1792,128]{2,1,0:T(8,128)(2,1)S(1)}, bf16[2,1792,128]{2,1,0:T(8,128)(2,1)S(1)}, u32[]{:S(2)}, u32[]{:S(2)}) %collective-permute-start.21) | collective-permute-done | bytes 917536 | tf_op jit(solution)/shard_map/ppermute | solution.py:991
  110.3 5.9 %collective-permute-done.23.refs_2_ = bf16[672,128]{1,0:T(8,128)(2,1)S(1)} collective-permute-done((bf16[672,128]{1,0:T(8,128)(2,1)S(1)}, bf16[672,128]{1,0:T(8,128)(2,1)S(1)}, u32[]{:S(2)}, u32[]{:S(2)}) %collective-permute-start.23) | collective-permute-done | bytes 172064 | tf_op jit(solution)/shard_map/ppermute | solution.py:946
  119.2 2.0 %collective-permute-start.27 = (bf16[496,128]{1,0:T(8,128)(2,1)S(1)}, bf16[496,128]{1,0:T(8,128)(2,1)S(1)}, u32[]{:S(2)}, u32[]{:S(2)}) collective-permute-start(bf16[496,128]{1,0:T(8,128)(2,1)S(1)} %get-tuple-element.260), channel_id=1, source_target_pairs={{0,1},{1,0},{2,3},{3,2},{4,5},{5,4},{6,7},{7,6},{8,9},{9,8},{10,11... | collective-permute-start | bytes 380936 | tf_op jit(solution)/shard_map/ppermute | solution.py:946
  125.7 7.4 %collective-permute-done.28.refs_2_ = bf16[496,128]{1,0:T(8,128)(2,1)S(1)} collective-permute-done((bf16[496,128]{1,0:T(8,128)(2,1)S(1)}, bf16[496,128]{1,0:T(8,128)(2,1)S(1)}, u32[]{:S(2)}, u32[]{:S(2)}) %collective-permute-start.28) | collective-permute-done | bytes 127008 | tf_op jit(solution)/shard_map/ppermute | solution.py:946
  136.7 4.6 %collective-permute-done.30.refs_1_ = bf16[496,128]{1,0:T(8,128)(2,1)S(1)} collective-permute-done((bf16[496,128]{1,0:T(8,128)(2,1)S(1)}, bf16[496,128]{1,0:T(8,128)(2,1)S(1)}, u32[]{:S(2)}, u32[]{:S(2)}) %collective-permute-start.30) | collective-permute-done | bytes 127008 | tf_op jit(solution)/shard_map/ppermute | solution.py:946
  143.9 2.2 %shard_map.384 = (f32[192,768]{1,0:T(8,128)}, f32[192,768]{1,0:T(8,128)}, f32[192,768]{1,0:T(8,128)}, f32[12,192]{1,0:T(8,128)}, f32[1,192]{1,0:T(1,128)}, /*ind...) custom-call(s32[4]{0:T(128)S(1)} %pad_add_fusion.ids_smem, ...), custom_call_target="tpu_custom_call" | custom-call | flops 20000999424 | bytes 20001000 | tf_op jit(solution)/shard_map/pallas_call | solution.py:928
  146.2 4.2 %shard_map.385 = (f32[768,512]{1,0:T(8,128)}, f32[768,512]{1,0:T(8,128)}, f32[512,768]{1,0:T(8,128)}, f32[192,768]{1,0:T(8,128)}, f32[192,768]{1,0:T(8,128)}, /*index=5*/f32[768,256]{1,0:T(8,128)}, f32[768,256]{1,0:T(8,128)}) custom-call(s32[4]{0:T(128)S(1)} %pad_add_fusion.ids_smem, bf16[1824,128]{1,0:T(8,128)(2,1)S(1)} %shard_map.381.refs_0_, ...), custom_call_target="tpu_custom_call" | custom-call | flops 20000999424 | bytes 20001000 | tf_op jit(solution)/shard_map/pallas_call | solution.py:928
  (164 shorter events, 43.6 us)
Async XLA Ops:
  0.7 22.0 %collective-permute-start = (bf16[128,768]{1,0:T(8,128)(2,1)}, bf16[128,768]{1,0:T(8,128)(2,1)S(1)}, u32[]{:S(2)}, u32[]{:S(2)}) collective-permute-start(bf16[128,768]{1,0:T(8,128)(2,1)} %bitcast.20), channel_id=1, source_target_pairs={{0,1},{1,0},{2,3},{3,2},{4,5},{5,4},{6,7},{7,6},{8,9},{9,8},{10,11... | collective-permute-start | bytes 589832 | tf_op jit(solution)/shard_map/ppermute | solution.py:946
  3.7 19.0 %collective-permute-start.1 = (bf16[128,768]{1,0:T(8,128)(2,1)}, bf16[128,768]{1,0:T(8,128)(2,1)S(1)}, u32[]{:S(2)}, u32[]{:S(2)}) collective-permute-start(bf16[128,768]{1,0:T(8,128)(2,1)} %bitcast.21), channel_id=1, source_target_pairs={{0,2},{1,3},{2,0},{3,1},{4,6},{5,7},{6,4},{7,5},{8,10},{9,11},{10,... | collective-permute-start | bytes 589832 | tf_op jit(solution)/shard_map/ppermute | solution.py:946
  6.3 16.4 %collective-permute-start.2 = (bf16[128,768]{1,0:T(8,128)(2,1)}, bf16[128,768]{1,0:T(8,128)(2,1)S(1)}, u32[]{:S(2)}, u32[]{:S(2)}) collective-permute-start(bf16[128,768]{1,0:T(8,128)(2,1)} %bitcast.22), channel_id=1, source_target_pairs={{0,3},{1,2},{2,1},{3,0},{4,7},{5,6},{6,5},{7,4},{8,11},{9,10},{10,... | collective-permute-start | bytes 589832 | tf_op jit(solution)/shard_map/ppermute | solution.py:946
  22.7 10.1 %collective-permute-start.4 = (bf16[128,768]{1,0:T(8,128)(2,1)}, bf16[128,768]{1,0:T(8,128)(2,1)S(1)}, u32[]{:S(2)}, u32[]{:S(2)}) collective-permute-start(bf16[128,768]{1,0:T(8,128)(2,1)} %copy-done.14), channel_id=1, source_target_pairs={{0,1},{1,0},{2,3},{3,2},{4,5},{5,4},{6,7},{7,6},{8,9},{9,8},{10,11... | collective-permute-start | bytes 589832 | tf_op jit(solution)/shard_map/ppermute | solution.py:946
  24.5 11.0 %collective-permute-start.3 = (bf16[128,768]{1,0:T(8,128)(2,1)}, bf16[128,768]{1,0:T(8,128)(2,1)S(1)}, u32[]{:S(2)}, u32[]{:S(2)}) collective-permute-start(bf16[128,768]{1,0:T(8,128)(2,1)} %copy-done.14), channel_id=1, source_target_pairs={{0,2},{1,3},{2,0},{3,1},{4,6},{5,7},{6,4},{7,5},{8,10},{9,11},{10,... | collective-permute-start | bytes 589832 | tf_op jit(solution)/shard_map/ppermute | solution.py:946
  35.5 9.1 %collective-permute-start.5 = (bf16[128,768]{1,0:T(8,128)(2,1)S(1)}, bf16[128,768]{1,0:T(8,128)(2,1)S(1)}, u32[]{:S(2)}, u32[]{:S(2)}) collective-permute-start(bf16[128,768]{1,0:T(8,128)(2,1)S(1)} %collective-permute-done.3.x_ref.refs_2_), channel_id=1, source_target_pairs={{0,1},{1,0},{2,3},{3,2},{4,5},{5,4},{6,7},{7,6},{8,9},{9,8},{10,11... | collective-permute-start | bytes 589832 | tf_op jit(solution)/shard_map/ppermute | solution.py:946
  37.1 14.1 %collective-permute-start.7 = (bf16[128,768]{1,0:T(8,128)(2,1)S(1)}, bf16[128,768]{1,0:T(8,128)(2,1)S(1)}, u32[]{:S(2)}, u32[]{:S(2)}) collective-permute-start(bf16[128,768]{1,0:T(8,128)(2,1)S(1)} %get-tuple-element.183), channel_id=1, source_target_pairs={{0,2},{1,3},{2,0},{3,1},{4,6},{5,7},{6,4},{7,5},{8,10},{9,11},{10,... | collective-permute-start | bytes 589832 | tf_op jit(solution)/shard_map/ppermute | solution.py:946
  45.9 8.3 %collective-permute-start.6 = (bf16[128,768]{1,0:T(8,128)(2,1)S(1)}, bf16[128,768]{1,0:T(8,128)(2,1)S(1)}, u32[]{:S(2)}, u32[]{:S(2)}) collective-permute-start(bf16[128,768]{1,0:T(8,128)(2,1)S(1)} %get-tuple-element.182), channel_id=1, source_target_pairs={{0,1},{1,0},{2,3},{3,2},{4,5},{5,4},{6,7},{7,6},{8,9},{9,8},{10,11... | collective-permute-start | bytes 589832 | tf_op jit(solution)/shard_map/ppermute | solution.py:946
  60.8 22.1 %collective-permute-start.12 = (bf16[128,768]{1,0:T(8,128)(2,1)S(1)}, bf16[128,768]{1,0:T(8,128)(2,1)S(1)}, u32[]{:S(2)}, u32[]{:S(2)}) collective-permute-start(bf16[128,768]{1,0:T(8,128)(2,1)S(1)} %get-tuple-element.220), channel_id=1, source_target_pairs={{0,1},{1,0},{2,3},{3,2},{4,5},{5,4},{6,7},{7,6},{8,9},{9,8},{10,11... | collective-permute-start | bytes 589832 | tf_op jit(solution)/shard_map/ppermute | solution.py:946
  62.6 20.4 %collective-permute-start.13 = (bf16[128,768]{1,0:T(8,128)(2,1)S(1)}, bf16[128,768]{1,0:T(8,128)(2,1)S(1)}, u32[]{:S(2)}, u32[]{:S(2)}) collective-permute-start(bf16[128,768]{1,0:T(8,128)(2,1)S(1)} %get-tuple-element.221), channel_id=1, source_target_pairs={{0,2},{1,3},{2,0},{3,1},{4,6},{5,7},{6,4},{7,5},{8,10},{9,11},{10,... | collective-permute-start | bytes 589832 | tf_op jit(solution)/shard_map/ppermute | solution.py:946
  63.8 19.2 %collective-permute-start.14 = (bf16[128,768]{1,0:T(8,128)(2,1)S(1)}, bf16[128,768]{1,0:T(8,128)(2,1)S(1)}, u32[]{:S(2)}, u32[]{:S(2)}) collective-permute-start(bf16[128,768]{1,0:T(8,128)(2,1)S(1)} %get-tuple-element.222), channel_id=1, source_target_pairs={{0,3},{1,2},{2,1},{3,0},{4,7},{5,6},{6,5},{7,4},{8,11},{9,10},{10,... | collective-permute-start | bytes 589832 | tf_op jit(solution)/shard_map/ppermute | solution.py:946
  65.3 17.7 %collective-permute-start.15 = (bf16[2,2304,128]{2,1,0:T(8,128)(2,1)S(1)}, bf16[2,2304,128]{2,1,0:T(8,128)(2,1)S(1)}, u32[]{:S(2)}, u32[]{:S(2)}) collective-permute-start(bf16[2,2304,128]{2,1,0:T(8,128)(2,1)S(1)} %get-tuple-element.224), channel_id=1, source_target_pairs={{0,8},{4,20},{8,0},{12,28},{16,24},{20,4},{24,16},{28,12},{1,9},{5... | collective-permute-start | bytes 3538952 | tf_op jit(solution)/shard_map/ppermute | solution.py:991
  86.0 8.8 %collective-permute-start.18 = (bf16[3,128,768]{2,1,0:T(8,128)(2,1)S(1)}, bf16[3,128,768]{2,1,0:T(8,128)(2,1)S(1)}, u32[]{:S(2)}, u32[]{:S(2)}) collective-permute-start(bf16[3,128,768]{2,1,0:T(8,128)(2,1)S(1)} %get-tuple-element.230.triple_ref), channel_id=1, source_target_pairs={{0,4},{4,0},{8,12},{12,8},{16,20},{20,16},{24,28},{28,24},{1,5},{5... | collective-permute-start | bytes 1769480 | tf_op jit(solution)/shard_map/ppermute | solution.py:946
  86.8 13.5 %collective-permute-start.19 = (bf16[2304,128]{1,0:T(8,128)(2,1)S(1)}, bf16[2304,128]{1,0:T(8,128)(2,1)S(1)}, u32[]{:S(2)}, u32[]{:S(2)}) collective-permute-start(bf16[2304,128]{1,0:T(8,128)(2,1)S(1)} %get-tuple-element.244), channel_id=1, source_target_pairs={{0,16},{4,12},{8,24},{12,4},{16,0},{20,28},{24,8},{28,20},{1,17},{... | collective-permute-start | bytes 1769480 | tf_op jit(solution)/shard_map/ppermute | solution.py:995
  96.3 13.5 %collective-permute-start.21 = (bf16[2,1792,128]{2,1,0:T(8,128)(2,1)S(1)}, bf16[2,1792,128]{2,1,0:T(8,128)(2,1)S(1)}, u32[]{:S(2)}, u32[]{:S(2)}) collective-permute-start(bf16[2,1792,128]{2,1,0:T(8,128)(2,1)S(1)} %get-tuple-element.249), channel_id=1, source_target_pairs={{0,8},{4,20},{8,0},{12,28},{16,24},{20,4},{24,16},{28,12},{1,9},{5... | collective-permute-start | bytes 2752520 | tf_op jit(solution)/shard_map/ppermute | solution.py:991
  101.0 9.3 %collective-permute-start.22 = (bf16[672,128]{1,0:T(8,128)(2,1)S(1)}, bf16[672,128]{1,0:T(8,128)(2,1)S(1)}, u32[]{:S(2)}, u32[]{:S(2)}) collective-permute-start(bf16[672,128]{1,0:T(8,128)(2,1)S(1)} %get-tuple-element.252), channel_id=1, source_target_pairs={{0,1},{1,0},{2,3},{3,2},{4,5},{5,4},{6,7},{7,6},{8,9},{9,8},{10,11... | collective-permute-start | bytes 516104 | tf_op jit(solution)/shard_map/ppermute | solution.py:946
  101.8 14.5 %collective-permute-start.23 = (bf16[672,128]{1,0:T(8,128)(2,1)S(1)}, bf16[672,128]{1,0:T(8,128)(2,1)S(1)}, u32[]{:S(2)}, u32[]{:S(2)}) collective-permute-start(bf16[672,128]{1,0:T(8,128)(2,1)S(1)} %get-tuple-element.253), channel_id=1, source_target_pairs={{0,2},{1,3},{2,0},{3,1},{4,6},{5,7},{6,4},{7,5},{8,10},{9,11},{10,... | collective-permute-start | bytes 516104 | tf_op jit(solution)/shard_map/ppermute | solution.py:946
  103.9 12.3 %collective-permute-start.24 = (bf16[672,128]{1,0:T(8,128)(2,1)S(1)}, bf16[672,128]{1,0:T(8,128)(2,1)S(1)}, u32[]{:S(2)}, u32[]{:S(2)}) collective-permute-start(bf16[672,128]{1,0:T(8,128)(2,1)S(1)} %get-tuple-element.254), channel_id=1, source_target_pairs={{0,3},{1,2},{2,1},{3,0},{4,7},{5,6},{6,5},{7,4},{8,11},{9,10},{10,... | collective-permute-start | bytes 516104 | tf_op jit(solution)/shard_map/ppermute | solution.py:946
  110.0 8.5 %collective-permute-start.26 = (bf16[1792,128]{1,0:T(8,128)(2,1)S(1)}, bf16[1792,128]{1,0:T(8,128)(2,1)S(1)}, u32[]{:S(2)}, u32[]{:S(2)}) collective-permute-start(bf16[1792,128]{1,0:T(8,128)(2,1)S(1)} %get-tuple-element.256), channel_id=1, source_target_pairs={{0,16},{4,12},{8,24},{12,4},{16,0},{20,28},{24,8},{28,20},{1,17},{... | collective-permute-start | bytes 1376264 | tf_op jit(solution)/shard_map/ppermute | solution.py:995
  116.5 8.7 %collective-permute-start.37 = (bf16[1824,128]{1,0:T(8,128)(2,1)S(1)}, bf16[1824,128]{1,0:T(8,128)(2,1)S(1)}, u32[]{:S(2)}, u32[]{:S(2)}) collective-permute-start(bf16[1824,128]{1,0:T(8,128)(2,1)S(1)} %shard_map.381.refs_0_), channel_id=1, source_target_pairs={{0,16},{4,12},{8,24},{12,4},{16,0},{20,28},{24,8},{28,20},{1,17},{... | collective-permute-start | bytes 1400840 | tf_op jit(solution)/shard_map/ppermute | solution.py:995
  121.2 11.9 %collective-permute-start.28 = (bf16[496,128]{1,0:T(8,128)(2,1)S(1)}, bf16[496,128]{1,0:T(8,128)(2,1)S(1)}, u32[]{:S(2)}, u32[]{:S(2)}) collective-permute-start(bf16[496,128]{1,0:T(8,128)(2,1)S(1)} %get-tuple-element.261), channel_id=1, source_target_pairs={{0,2},{1,3},{2,0},{3,1},{4,6},{5,7},{6,4},{7,5},{8,10},{9,11},{10,... | collective-permute-start | bytes 380936 | tf_op jit(solution)/shard_map/ppermute | solution.py:946
  122.1 11.0 %collective-permute-start.29 = (bf16[496,128]{1,0:T(8,128)(2,1)S(1)}, bf16[496,128]{1,0:T(8,128)(2,1)S(1)}, u32[]{:S(2)}, u32[]{:S(2)}) collective-permute-start(bf16[496,128]{1,0:T(8,128)(2,1)S(1)} %get-tuple-element.262), channel_id=1, source_target_pairs={{0,3},{1,2},{2,1},{3,0},{4,7},{5,6},{6,5},{7,4},{8,11},{9,10},{10,... | collective-permute-start | bytes 380936 | tf_op jit(solution)/shard_map/ppermute | solution.py:946
  123.6 13.1 %collective-permute-start.38 = (bf16[1824,128]{1,0:T(8,128)(2,1)S(1)}, bf16[1824,128]{1,0:T(8,128)(2,1)S(1)}, u32[]{:S(2)}, u32[]{:S(2)}) collective-permute-start(bf16[1824,128]{1,0:T(8,128)(2,1)S(1)} %shard_map.381.refs_0_), channel_id=1, source_target_pairs={{0,8},{4,20},{8,0},{12,28},{16,24},{20,4},{24,16},{28,12},{1,9},{5... | collective-permute-start | bytes 1400840 | tf_op jit(solution)/shard_map/ppermute | solution.py:991
  125.2 18.0 %collective-permute-start.39 = (bf16[1824,128]{1,0:T(8,128)(2,1)S(1)}, bf16[1824,128]{1,0:T(8,128)(2,1)S(1)}, u32[]{:S(2)}, u32[]{:S(2)}) collective-permute-start(bf16[1824,128]{1,0:T(8,128)(2,1)S(1)} %collective-permute-done.37.refs_1_), channel_id=1, source_target_pairs={{0,8},{4,20},{8,0},{12,28},{16,24},{20,4},{24,16},{28,12},{1,9},{5... | collective-permute-start | bytes 1400840 | tf_op jit(solution)/shard_map/ppermute | solution.py:991
  (59 other events, 486.3 us)
